TPU v7x, 32 devices: a whole 2x2x4 slice. The times are simulated.
32 devices in a mesh: seq: 16 (over z, y, core), dp: 2 (over x).
Axes of the slice: x: 2, y: 2, z: 4, core: 2. Of those that a mesh axis runs over, the one named last changes fastest.
Arguments:
- probe_vectors: bfloat16 [2, 2048, 2048], P('dp', 'seq'), may hold values from -6 to 6
- lookup_vectors: bfloat16 [2, 2048, 2048], P('dp', 'seq'), may hold values from -6 to 6
- content_vectors: bfloat16 [2, 2048, 2048], P('dp', 'seq'), may hold values from -6 to 6
- result_cotangent: bfloat16 [2, 2048, 2048], P('dp', 'seq'), may hold values from -25 to 25
- logit_softness: float32 [16], replicated, may hold values from 0.7 to 1.2
- block_grouping: int32 [2, 16, 16, 1], P('dp'), may hold values from 0 to 1, as said below
- neighborhood_span: int32 [16], replicated, may hold values from 32 to 128
Outputs:
- query_grad: bfloat16 [2, 2048, 2048], P('dp', 'seq')
- key_grad: bfloat16 [2, 2048, 2048], P('dp', 'seq')
- value_grad: bfloat16 [2, 2048, 2048], P('dp', 'seq')
- temper_grad: float32 [16], replicated
Inputs may be any that keep to these rules, and one draw needn't show every extreme that they name: `block_grouping`: within one document and head no cluster holds more than 12 blocks, and some cluster holds exactly 12. Index j of seq owns the clusters c of head h with (h * 2 + c) // 2 == j; of the 1 block of one index of seq, at most 1 have for one head clusters owned by one index of seq, and that many is reached.
All inputs are finite; a program needn't handle non-finite values.
Results may differ from a plain program's by a relative error of at most 0.0076.
Values may be sent and summed in bfloat16 or wider, within the bound.
No kernel may reach another device: no remote copies, remote signals or barrier semaphores. Data moves between devices by JAX's collectives and lax.ppermute only.
A program may use at most 64 MiB of HBM per device.

v0:
```python
import math

import jax
import jax.numpy as jnp
from jax import lax
from jax.sharding import PartitionSpec as P

HD = 128
BLK = 128


blocked_score = -1e30


def shifted(value, axis, steps):
    count = lax.axis_size(axis)
    first, last = (max(0, -steps), min(count, count - steps))
    return lax.ppermute(value, axis, [(source, source + steps) for source in range(first, last)])


def lifted(array_in):
    return lax.optimization_barrier(array_in.astype(jnp.bfloat16)).astype(jnp.float32)


def head_major(tokens_in, block_len):
    token_count, feature_count = tokens_in.shape
    return tokens_in.reshape(
        token_count // block_len, block_len, feature_count // HD, HD
    ).transpose(2, 0, 1, 3)


def token_major(blocks_in):
    head_count, block_count, block_len, depth = blocks_in.shape
    return blocks_in.transpose(1, 2, 0, 3).reshape(1, block_count * block_len, head_count * depth)


def window_parts(query_block, prev_keys, prev_values, grad_block, usable, window_width, temper):
    block_len = query_block.shape[-2]
    inverse_root = 1.0 / math.sqrt(query_block.shape[-1])
    raw_scores = (
        jnp.einsum("...td,...sd->...ts", query_block, prev_keys, preferred_element_type=jnp.float32)
        * inverse_root
    )
    query_pos = lax.broadcasted_iota(jnp.int32, (block_len, block_len), 0)
    key_pos = lax.broadcasted_iota(jnp.int32, (block_len, block_len), 1)
    pair_mask = usable[..., None, None] & (
        key_pos > query_pos + block_len - window_width[..., None, None]
    )
    scores = temper[..., None, None] * raw_scores
    row_top = jnp.max(jnp.where(pair_mask, scores, blocked_score), axis=-1)
    weights = jnp.where(pair_mask, jnp.exp(scores - row_top[..., None]), 0.0)
    prob_grad = jnp.einsum(
        "...td,...sd->...ts", grad_block, prev_values, preferred_element_type=jnp.float32
    )
    return (
        raw_scores,
        pair_mask,
        prob_grad,
        row_top,
        jnp.sum(weights, axis=-1),
        jnp.sum(weights * prob_grad, axis=-1),
    )


def window_grads(
    raw_scores,
    pair_mask,
    prob_grad,
    query_block,
    prev_keys,
    grad_block,
    log_total,
    row_delta,
    temper,
):
    inverse_root = 1.0 / math.sqrt(query_block.shape[-1])
    scaling = (temper * inverse_root)[..., None, None]
    probability = jnp.where(
        pair_mask, jnp.exp(temper[..., None, None] * raw_scores - log_total[..., None]), 0.0
    )
    score_grad = probability * (prob_grad - row_delta[..., None])
    prob_low = probability.astype(jnp.bfloat16)
    grad_low = score_grad.astype(jnp.bfloat16)
    query_part = (
        jnp.einsum("...ts,...sd->...td", grad_low, prev_keys, preferred_element_type=jnp.float32)
        * scaling
    )
    key_part = (
        jnp.einsum("...ts,...td->...sd", grad_low, query_block, preferred_element_type=jnp.float32)
        * scaling
    )
    value_part = jnp.einsum(
        "...ts,...td->...sd", prob_low, grad_block, preferred_element_type=jnp.float32
    )
    temper_part = jnp.sum(score_grad * raw_scores, axis=(-2, -1))
    return (query_part, key_part, value_part, temper_part)


def cluster_pair(
    query_items,
    key_items,
    value_items,
    grad_items,
    live_items,
    temper,
    window_top,
    window_total,
    window_mass,
):
    item_count, block_len, depth = query_items.shape
    row_count = item_count * block_len
    group_rows = 4 * block_len
    inverse_root = 1.0 / math.sqrt(depth)
    scaling = temper * inverse_root
    query_rows = query_items.reshape(row_count, depth)
    key_rows = key_items.reshape(row_count, depth)
    value_rows = value_items.reshape(row_count, depth)
    grad_rows = grad_items.reshape(row_count, depth)
    key_item = jnp.arange(row_count) // block_len
    key_token = jnp.arange(row_count) % block_len
    live_rows = jnp.repeat(live_items, block_len)
    top_rows = window_top.reshape(row_count)
    total_rows = window_total.reshape(row_count)
    mass_rows = window_mass.reshape(row_count)

    def group_step(carry, start_row):
        key_acc, value_acc, temper_acc = carry
        query_group = lax.dynamic_slice_in_dim(query_rows, start_row, group_rows, 0)
        grad_group = lax.dynamic_slice_in_dim(grad_rows, start_row, group_rows, 0)
        group_live = lax.dynamic_slice_in_dim(live_rows, start_row, group_rows, 0)
        group_top = lax.dynamic_slice_in_dim(top_rows, start_row, group_rows, 0)
        group_total = lax.dynamic_slice_in_dim(total_rows, start_row, group_rows, 0)
        group_mass = lax.dynamic_slice_in_dim(mass_rows, start_row, group_rows, 0)
        query_item = (start_row + jnp.arange(group_rows)) // block_len
        query_token = jnp.arange(group_rows) % block_len
        earlier = (key_item[None, :] < query_item[:, None]) | (
            key_item[None, :] == query_item[:, None]
        ) & (key_token[None, :] <= query_token[:, None])
        pair_mask = group_live[:, None] & live_rows[None, :] & earlier
        raw_scores = (
            lax.dot_general(
                query_group, key_rows, (((1,), (1,)), ((), ())), preferred_element_type=jnp.float32
            )
            * inverse_root
        )
        scores = temper * raw_scores
        row_top = jnp.maximum(
            jnp.max(jnp.where(pair_mask, scores, blocked_score), axis=1), group_top
        )
        weights = jnp.where(pair_mask, jnp.exp(scores - row_top[:, None]), 0.0)
        row_total = jnp.sum(weights, axis=1) + group_total * jnp.exp(group_top - row_top)
        log_total = row_top + jnp.log(jnp.where(group_live, row_total, 1.0))
        probability = jnp.where(pair_mask, jnp.exp(scores - log_total[:, None]), 0.0)
        prob_grad = lax.dot_general(
            grad_group, value_rows, (((1,), (1,)), ((), ())), preferred_element_type=jnp.float32
        )
        row_delta = jnp.sum(probability * prob_grad, axis=1) + group_mass * jnp.exp(
            group_top - log_total
        )
        score_grad = probability * (prob_grad - row_delta[:, None])
        prob_low = probability.astype(jnp.bfloat16)
        grad_low = score_grad.astype(jnp.bfloat16)
        query_part = jnp.dot(grad_low, key_rows, preferred_element_type=jnp.float32) * scaling
        key_acc = (
            key_acc
            + lax.dot_general(
                grad_low, query_group, (((0,), (0,)), ((), ())), preferred_element_type=jnp.float32
            )
            * scaling
        )
        value_acc = value_acc + lax.dot_general(
            prob_low, grad_group, (((0,), (0,)), ((), ())), preferred_element_type=jnp.float32
        )
        temper_acc = temper_acc + jnp.sum(score_grad * raw_scores)
        return ((key_acc, value_acc, temper_acc), (query_part, log_total, row_delta))

    start_rows = jnp.arange(item_count // 4) * group_rows
    initial = (
        jnp.zeros((row_count, depth), jnp.float32),
        jnp.zeros((row_count, depth), jnp.float32),
        jnp.zeros((), jnp.float32),
    )
    (key_acc, value_acc, temper_acc), (query_part, log_total, row_delta) = lax.scan(
        group_step, initial, start_rows
    )
    return (
        query_part.reshape(item_count, block_len, depth),
        log_total.reshape(item_count, block_len),
        row_delta.reshape(item_count, block_len),
        key_acc.reshape(item_count, block_len, depth),
        value_acc.reshape(item_count, block_len, depth),
        temper_acc,
    )


def shards(
    probe_vectors,
    lookup_vectors,
    content_vectors,
    result_cotangent,
    logit_softness,
    block_grouping,
    neighborhood_span,
):
    seq_count = lax.axis_size("seq")
    position = lax.axis_index("seq")
    tokens = probe_vectors.shape[1]
    head_count = probe_vectors.shape[2] // HD
    local_blocks = tokens // BLK
    block_count = local_blocks * seq_count
    cluster_count = max(1, block_count // 8)
    capacity = min(12, block_count)
    owned_pairs = cluster_count * head_count // seq_count
    group_count = cluster_count // owned_pairs
    per_peer = max(1, local_blocks // group_count)
    cluster_ids = block_grouping[0, :, :, 0]
    query_home = head_major(probe_vectors[0], BLK)
    key_home = head_major(lookup_vectors[0], BLK)
    value_home = head_major(content_vectors[0], BLK)
    grad_home = head_major(result_cotangent[0], BLK)
    last_block = (lookup_vectors[0, tokens - BLK :], content_vectors[0, tokens - BLK :])
    prev_key_rows, prev_value_rows = shifted((last_block[0], last_block[1]), "seq", 1)
    prev_keys = jnp.concatenate([head_major(prev_key_rows, BLK), key_home[:, :-1]], axis=1)
    prev_values = jnp.concatenate([head_major(prev_value_rows, BLK), value_home[:, :-1]], axis=1)
    first_block = position * local_blocks
    before = jnp.concatenate(
        [jnp.full((head_count, 1), -1, jnp.int32), cluster_ids[:, :-1]], axis=1
    )
    my_ids = lax.dynamic_slice_in_dim(cluster_ids, first_block, local_blocks, 1)
    my_before = lax.dynamic_slice_in_dim(before, first_block, local_blocks, 1)
    global_block = first_block + jnp.arange(local_blocks)
    usable_home = (global_block[None, :] >= 1) & (my_before != my_ids)
    peer_index = jnp.arange(seq_count)
    peer_head = peer_index * owned_pairs // cluster_count
    slot_range = jnp.arange(per_peer)
    local_range = jnp.arange(local_blocks)
    owner_index = (jnp.arange(head_count)[:, None] * cluster_count + my_ids) // owned_pairs
    peer_ids = jnp.take(my_ids, peer_head, axis=0)
    goes = (peer_head[:, None] * cluster_count + peer_ids) // owned_pairs == peer_index[:, None]
    send_rank = jnp.cumsum(goes.astype(jnp.int32), axis=1) - 1
    send_pick = goes[:, None, :] & (send_rank[:, None, :] == slot_range[None, :, None])
    send_block = jnp.sum(jnp.where(send_pick, local_range[None, None, :], 0), axis=2)
    send_flat = peer_head[:, None] * local_blocks + send_block
    home_rank = jnp.take_along_axis(send_rank, owner_index, axis=0)
    home_pos = owner_index * per_peer + home_rank
    pair_index = position * owned_pairs + jnp.arange(owned_pairs)
    split_for_couple = pair_index // cluster_count
    pair_cluster = pair_index % cluster_count
    my_head = position * owned_pairs // cluster_count
    split_numbers = jnp.take(cluster_ids, my_head, axis=0)
    member = split_numbers[None, :] == pair_cluster[:, None]
    member_rank = jnp.cumsum(member.astype(jnp.int32), axis=1) - 1
    member_count = jnp.sum(member.astype(jnp.int32), axis=1)
    picked = member[:, None, :] & (member_rank[:, None, :] == jnp.arange(capacity)[None, :, None])
    member_block = jnp.sum(jnp.where(picked, jnp.arange(block_count)[None, None, :], 0), axis=2)
    live_members = jnp.arange(capacity)[None, :] < member_count[:, None]
    mine = (my_head * cluster_count + split_numbers) // owned_pairs == position
    mine_grid = mine.reshape(seq_count, local_blocks)
    recv_rank = jnp.cumsum(mine_grid.astype(jnp.int32), axis=1) - 1
    recv_pos = (peer_index[:, None] * per_peer + recv_rank).reshape(block_count)
    member_pos = jnp.take(recv_pos, member_block)
    couple_softness = jnp.take(logit_softness, split_for_couple)
    pair_onehot = (split_for_couple[:, None] == jnp.arange(head_count)[None, :]).astype(jnp.float32)
    slot_pair = my_head * cluster_count + split_numbers - position * owned_pairs
    same_cluster = split_numbers[:, None] == split_numbers[None, :]
    earlier_block = jnp.arange(block_count)[None, :] < jnp.arange(block_count)[:, None]
    slot_rank = jnp.sum((same_cluster & earlier_block).astype(jnp.int32), axis=1)
    back_pos = jnp.clip(slot_pair, 0, owned_pairs - 1) * capacity + jnp.clip(
        slot_rank, 0, capacity - 1
    )
    back_grid = back_pos.reshape(seq_count, local_blocks)
    back_pick = mine_grid[:, None, :] & (recv_rank[:, None, :] == slot_range[None, :, None])
    back_flat = jnp.sum(jnp.where(back_pick, back_grid[:, None, :], 0), axis=2)

    def to_peers(array_in):
        flat = array_in.reshape((head_count * local_blocks,) + array_in.shape[2:])
        return jnp.take(flat, send_flat, axis=0)

    def members(array_in):
        flat = array_in.reshape((seq_count * per_peer,) + array_in.shape[2:])
        return jnp.take(flat, member_pos, axis=0)

    def to_owner(array_in):
        flat = array_in.reshape((owned_pairs * capacity,) + array_in.shape[2:])
        return jnp.take(flat, back_flat, axis=0)

    def from_peers(array_in):
        flat = array_in.reshape((seq_count * per_peer,) + array_in.shape[2:])
        return jnp.take(flat, home_pos, axis=0)

    raw_w, mask_w, pgrad_w, top_w, total_w, mass_w = window_parts(
        query_home,
        prev_keys,
        prev_values,
        grad_home,
        usable_home,
        neighborhood_span[:, None],
        logit_softness[:, None],
    )
    arrived = (
        lax.all_to_all(to_peers(query_home), "seq", split_axis=0, concat_axis=0, tiled=True),
        lax.all_to_all(to_peers(key_home), "seq", split_axis=0, concat_axis=0, tiled=True),
        lax.all_to_all(to_peers(value_home), "seq", split_axis=0, concat_axis=0, tiled=True),
        lax.all_to_all(to_peers(grad_home), "seq", split_axis=0, concat_axis=0, tiled=True),
    )
    arrived_stats = (
        lax.all_to_all(to_peers(top_w), "seq", split_axis=0, concat_axis=0, tiled=True),
        lax.all_to_all(to_peers(total_w), "seq", split_axis=0, concat_axis=0, tiled=True),
        lax.all_to_all(to_peers(mass_w), "seq", split_axis=0, concat_axis=0, tiled=True),
    )
    query_m, key_m, value_m, grad_m = [members(item_in) for item_in in arrived]
    top_m, total_m, mass_m = [members(item_in) for item_in in arrived_stats]

    def split_pair(pair_inputs):
        query_i, key_i, value_i, grad_i, live_i, temper_i, top_i, total_i, mass_i = pair_inputs
        query_c, log_total, row_delta, key_c, value_c, temper_c = cluster_pair(
            query_i, key_i, value_i, grad_i, live_i, temper_i, top_i, total_i, mass_i
        )
        return (
            query_c.astype(jnp.bfloat16),
            key_c.astype(jnp.bfloat16),
            value_c.astype(jnp.bfloat16),
            log_total,
            row_delta,
            temper_c,
        )

    owner_results = lax.map(
        split_pair,
        (query_m, key_m, value_m, grad_m, live_members, couple_softness, top_m, total_m, mass_m),
    )
    returned = (
        lax.all_to_all(to_owner(owner_results[0]), "seq", split_axis=0, concat_axis=0, tiled=True),
        lax.all_to_all(to_owner(owner_results[1]), "seq", split_axis=0, concat_axis=0, tiled=True),
        lax.all_to_all(to_owner(owner_results[2]), "seq", split_axis=0, concat_axis=0, tiled=True),
    )
    returned_stats = (
        lax.all_to_all(to_owner(owner_results[3]), "seq", split_axis=0, concat_axis=0, tiled=True),
        lax.all_to_all(to_owner(owner_results[4]), "seq", split_axis=0, concat_axis=0, tiled=True),
    )
    query_cluster = from_peers(returned[0])
    key_cluster = from_peers(returned[1])
    value_cluster = from_peers(returned[2])
    log_home = from_peers(returned_stats[0])
    delta_home = from_peers(returned_stats[1])
    query_w, key_w, value_w, temper_w = window_grads(
        raw_w,
        mask_w,
        pgrad_w,
        query_home,
        prev_keys,
        grad_home,
        log_home,
        delta_home,
        logit_softness[:, None],
    )
    query_out = (query_cluster.astype(jnp.float32) + lifted(query_w)).astype(jnp.bfloat16)
    key_window = key_w.astype(jnp.bfloat16)
    value_window = value_w.astype(jnp.bfloat16)
    temper_local = jnp.sum(owner_results[5][:, None] * pair_onehot, axis=0) + jnp.sum(
        temper_w, axis=1
    )
    edge_keys, edge_values = shifted((key_window[:, 0], value_window[:, 0]), "seq", -1)
    key_next = jnp.concatenate([key_window[:, 1:], edge_keys[:, None]], axis=1)
    value_next = jnp.concatenate([value_window[:, 1:], edge_values[:, None]], axis=1)
    key_out = (key_cluster.astype(jnp.float32) + key_next.astype(jnp.float32)).astype(jnp.bfloat16)
    value_out = (value_cluster.astype(jnp.float32) + value_next.astype(jnp.float32)).astype(
        jnp.bfloat16
    )
    temper_total = lax.psum(temper_local, ("seq", "dp"))
    temper_grad = temper_total / (lax.axis_size("dp") * tokens * seq_count)
    return (token_major(query_out), token_major(key_out), token_major(value_out), temper_grad)


def solution(mesh):
    in_specs = (
        P("dp", "seq", None),
        P("dp", "seq", None),
        P("dp", "seq", None),
        P("dp", "seq", None),
        P(),
        P("dp", None, None, None),
        P(),
    )
    out_specs = (P("dp", "seq", None), P("dp", "seq", None), P("dp", "seq", None), P())
    return jax.shard_map(shards, mesh=mesh, in_specs=in_specs, out_specs=out_specs, check_vma=False)
```

profile of v0, /device:TPU:0, one launch (start us, length us, event | category | flops | bytes accessed | tf_op | source)
XLA Modules:
  0.0 406.3 jit_solution(12614558680634064290)
XLA Ops:
  5.9 5.3 %collective-permute-start.1 = (bf16[128,2048]{0,1:T(8,128)(2,1)S(1)}, bf16[128,2048]{0,1:T(8,128)(2,1)}, u32[]{:S(2)}, u32[]{:S(2)}) collective-permute-start(bf16[128,2048]{0,1:T(8,128)(2,1)S(1)} %bitcast.381), channel_id=1, source_target_pairs={{0,2},{2,4},{4,6},{6,8},{8,10},{10,12},{12,14},{14,16},{16,18},{18... | collective-permute-start | bytes 1572872 | tf_op jit(solution)/shard_map/ppermute | solution.py:18
  26.4 14.5 %all_to_all.60 = f32[16,1,128]{2,1,0:T(1,128)S(1)} all-to-all(f32[16,1,128]{2,1,0:T(1,128)S(1)} %bitcast.397), channel_id=1, replica_groups=mesh['seq'=16,'dp'=2] {'seq'}, dimensions={0} | all-to-all | bytes 16384 | tf_op jit(solution)/shard_map/all_to_all | solution.py:307
  46.3 4.4 %all-to-all-done.3 = f32[16,1,128]{2,1,0:T(1,128)S(1)} async-done(((f32[16,1,128]{2,1,0:T(1,128)}), f32[16,1,128]{2,1,0:T(1,128)S(1)}, u32[]{:S(2)}, u32[]{:S(2)}) %all-to-all-start.3) | async-done | bytes 8224 | tf_op jit(solution)/shard_map/all_to_all | solution.py:308
  55.3 5.2 %all-to-all-done.4 = f32[16,1,128]{2,1,0:T(1,128)S(1)} async-done(((f32[16,1,128]{2,1,0:T(1,128)}), f32[16,1,128]{2,1,0:T(1,128)S(1)}, u32[]{:S(2)}, u32[]{:S(2)}) %all-to-all-start.4) | async-done | bytes 8224 | tf_op jit(solution)/shard_map/all_to_all | solution.py:309
  65.7 12.8 %all-to-all-done.5 = bf16[16,1,128,128]{3,2,1,0:T(8,128)(2,1)S(1)} async-done(((bf16[16,1,128,128]{3,2,1,0:T(8,128)(2,1)}), bf16[16,1,128,128]{3,2,1,0:T(8,128)(2,1)S(1)}, u32[]{:S(2)}, u32[]{:S(2)}) %all-to-all-start.5) | async-done | bytes 524320 | tf_op jit(solution)/shard_map/all_to_all | solution.py:302
  78.5 4.0 all-to-all-start.6
  87.5 9.5 %all-to-all-done.6 = bf16[16,1,128,128]{3,2,1,0:T(8,128)(2,1)S(1)} async-done(((bf16[16,1,128,128]{3,2,1,0:T(8,128)(2,1)}), bf16[16,1,128,128]{3,2,1,0:T(8,128)(2,1)S(1)}, u32[]{:S(2)}, u32[]{:S(2)}) %all-to-all-start.6) | async-done | bytes 524320 | tf_op jit(solution)/shard_map/all_to_all | solution.py:303
  97.0 4.1 %all-to-all-start = ((bf16[16,1,128,128]{3,2,1,0:T(8,128)(2,1)}), bf16[16,1,128,128]{3,2,1,0:T(8,128)(2,1)S(1)}, u32[]{:S(2)}, u32[]{:S(2)}) async-start(bf16[16,1,128,128]{3,2,1,0:T(8,128)(2,1)} %get-tuple-element.847), calls=%async_computation | async-start | bytes 1048576 | tf_op jit(solution)/shard_map/all_to_all | solution.py:301
  103.2 12.3 %all-to-all-done = bf16[16,1,128,128]{3,2,1,0:T(8,128)(2,1)S(1)} async-done(((bf16[16,1,128,128]{3,2,1,0:T(8,128)(2,1)}), bf16[16,1,128,128]{3,2,1,0:T(8,128)(2,1)S(1)}, u32[]{:S(2)}, u32[]{:S(2)}) %all-to-all-start) | async-done | bytes 524320 | tf_op jit(solution)/shard_map/all_to_all | solution.py:301
  115.6 4.1 %all-to-all-start.1 = ((bf16[16,1,128,128]{3,2,1,0:T(8,128)(2,1)}), bf16[16,1,128,128]{3,2,1,0:T(8,128)(2,1)S(1)}, u32[]{:S(2)}, u32[]{:S(2)}) async-start(bf16[16,1,128,128]{3,2,1,0:T(8,128)(2,1)} %get-tuple-element.846), calls=%async_computation.1 | async-start | bytes 1048576 | tf_op jit(solution)/shard_map/all_to_all | solution.py:304
  126.7 7.5 %all-to-all-done.1 = bf16[16,1,128,128]{3,2,1,0:T(8,128)(2,1)S(1)} async-done(((bf16[16,1,128,128]{3,2,1,0:T(8,128)(2,1)}), bf16[16,1,128,128]{3,2,1,0:T(8,128)(2,1)S(1)}, u32[]{:S(2)}, u32[]{:S(2)}) %all-to-all-start.1) | async-done | bytes 524320 | tf_op jit(solution)/shard_map/all_to_all | solution.py:304
  137.8 144.2 %while.78 = (s32[]{:T(128)}, bf16[2,12,128,128]{3,2,1,0:T(8,128)(2,1)}, bf16[2,12,128,128]{3,2,1,0:T(8,128)(2,1)}, bf16[2,12,128,128]{3,2,1,0:T(8,128)(2,1)}, f3...) while((s32[]{:T(128)}, ...), condition=%wide.region_13.18_spmd, body=%wide.region_6.17_spmd.sunk | while | flops 1074954240 | bytes 115534976 | solution.py:328
  142.3 64.5 %while.79 = (s32[]{:T(128)}, f32[1536,128]{1,0:T(8,128)S(1)}, f32[1536,128]{1,0:T(8,128)S(1)}, f32[]{:T(128)}, bf16[3,512,128]{2,1,0:T(8,128)(2,1)}, /*index=5*/...) while((s32[]{:T(128)}, f32[1536,128]{1,0:T(8,128)S(1)}, ...), condition=%wide.region_12.16_spmd.clone.clone, body=%wide.region_7.15_spmd.clone.clone.sunk | while | flops 1074561024 | bytes 93417968 | solution.py:183
  157.7 3.8 convolution_add_fusion.2
  179.1 3.8 convolution_add_fusion.2
  214.4 64.5 %while.79 = (s32[]{:T(128)}, f32[1536,128]{1,0:T(8,128)S(1)}, f32[1536,128]{1,0:T(8,128)S(1)}, f32[]{:T(128)}, bf16[3,512,128]{2,1,0:T(8,128)(2,1)}, /*index=5*/...) while((s32[]{:T(128)}, f32[1536,128]{1,0:T(8,128)S(1)}, ...), condition=%wide.region_12.16_spmd.clone.clone, body=%wide.region_7.15_spmd.clone.clone.sunk | while | flops 1074561024 | bytes 93417968 | solution.py:183
  283.8 4.1 %all-to-all-start.9 = ((f32[16,1,128]{2,1,0:T(1,128)}), f32[16,1,128]{2,1,0:T(1,128)S(1)}, u32[]{:S(2)}, u32[]{:S(2)}) async-start(f32[16,1,128]{2,1,0:T(1,128)} %bitcast.104), calls=%async_computation.9 | async-start | bytes 16384 | tf_op jit(solution)/shard_map/all_to_all | solution.py:339
  294.2 5.2 %all-to-all-start.8 = ((f32[16,1,128]{2,1,0:T(1,128)}), f32[16,1,128]{2,1,0:T(1,128)S(1)}, u32[]{:S(2)}, u32[]{:S(2)}) async-start(f32[16,1,128]{2,1,0:T(1,128)} %bitcast.95), calls=%async_computation.8 | async-start | bytes 16384 | tf_op jit(solution)/shard_map/all_to_all | solution.py:338
  300.6 5.2 %all-to-all-done.8 = f32[16,1,128]{2,1,0:T(1,128)S(1)} async-done(((f32[16,1,128]{2,1,0:T(1,128)}), f32[16,1,128]{2,1,0:T(1,128)S(1)}, u32[]{:S(2)}, u32[]{:S(2)}) %all-to-all-start.8) | async-done | bytes 8224 | tf_op jit(solution)/shard_map/all_to_all | solution.py:338
  305.7 17.1 %all_to_all.61 = bf16[16,1,128,128]{3,2,1,0:T(8,128)(2,1)S(1)} all-to-all(bf16[16,1,128,128]{3,2,1,0:T(8,128)(2,1)S(1)} %get-tuple-element.823), channel_id=1, replica_groups=mesh['seq'=16,'dp'=2] {'seq'}, dimensions={0} | all-to-all | bytes 1048576 | tf_op jit(solution)/shard_map/all_to_all | solution.py:335
  322.8 4.0 all-to-all-start.7
  332.3 9.0 %all-to-all-done.7 = bf16[16,1,128,128]{3,2,1,0:T(8,128)(2,1)S(1)} async-done(((bf16[16,1,128,128]{3,2,1,0:T(8,128)(2,1)}), bf16[16,1,128,128]{3,2,1,0:T(8,128)(2,1)S(1)}, u32[]{:S(2)}, u32[]{:S(2)}) %all-to-all-start.7) | async-done | bytes 524320 | tf_op jit(solution)/shard_map/all_to_all | solution.py:333
  341.3 4.1 all-to-all-start.10
  351.4 45.6 %psum.7 = f32[16]{0:T(128)S(1)} all-reduce(f32[16]{0:T(128)S(1)} %add.523), channel_id=1, replica_groups=mesh['seq'=16,'dp'=2] {'seq','dp'}, use_global_device_ids=true, to_apply=%region_17.24 | all-reduce | flops 16 | bytes 128 | tf_op jit(solution)/shard_map/psum | solution.py:370
  (409 shorter events, 203.0 us)
Async XLA Ops:
  2.1 13.0 %collective-permute-start = (bf16[128,2048]{0,1:T(8,128)(2,1)S(1)}, bf16[128,2048]{0,1:T(8,128)(2,1)S(1)}, u32[]{:S(2)}, u32[]{:S(2)}) collective-permute-start(bf16[128,2048]{0,1:T(8,128)(2,1)S(1)} %bitcast.379), channel_id=1, source_target_pairs={{0,2},{2,4},{4,6},{6,8},{8,10},{10,12},{12,14},{14,16},{16,18},{18... | collective-permute-start | bytes 1572872 | tf_op jit(solution)/shard_map/ppermute | solution.py:18
  5.9 11.4 %collective-permute-start.1 = (bf16[128,2048]{0,1:T(8,128)(2,1)S(1)}, bf16[128,2048]{0,1:T(8,128)(2,1)}, u32[]{:S(2)}, u32[]{:S(2)}) collective-permute-start(bf16[128,2048]{0,1:T(8,128)(2,1)S(1)} %bitcast.381), channel_id=1, source_target_pairs={{0,2},{2,4},{4,6},{6,8},{8,10},{10,12},{12,14},{14,16},{16,18},{18... | collective-permute-start | bytes 1572872 | tf_op jit(solution)/shard_map/ppermute | solution.py:18
  15.1 67.8 %copy-start.27 = (pred[16]{0:T(512)(128)(4,1)}, pred[16]{0:T(512)(128)(4,1)S(1)}, u32[]{:S(2)}) copy-start(pred[16]{0:T(512)(128)(4,1)S(1)} %get-tuple-element.833) | copy-start | bytes 52
  40.9 9.8 %all-to-all-start.3 = ((f32[16,1,128]{2,1,0:T(1,128)}), f32[16,1,128]{2,1,0:T(1,128)S(1)}, u32[]{:S(2)}, u32[]{:S(2)}) async-start(f32[16,1,128]{2,1,0:T(1,128)} %bitcast.54), calls=%async_computation.3 | async-start | bytes 16384 | tf_op jit(solution)/shard_map/all_to_all | solution.py:308
  50.7 9.8 %all-to-all-start.4 = ((f32[16,1,128]{2,1,0:T(1,128)}), f32[16,1,128]{2,1,0:T(1,128)S(1)}, u32[]{:S(2)}, u32[]{:S(2)}) async-start(f32[16,1,128]{2,1,0:T(1,128)} %bitcast.64), calls=%async_computation.4 | async-start | bytes 16384 | tf_op jit(solution)/shard_map/all_to_all | solution.py:309
  60.5 18.0 %all-to-all-start.5 = ((bf16[16,1,128,128]{3,2,1,0:T(8,128)(2,1)}), bf16[16,1,128,128]{3,2,1,0:T(8,128)(2,1)S(1)}, u32[]{:S(2)}, u32[]{:S(2)}) async-start(bf16[16,1,128,128]{3,2,1,0:T(8,128)(2,1)} %get-tuple-element.839), calls=%async_computation.5 | async-start | bytes 1048576 | tf_op jit(solution)/shard_map/all_to_all | solution.py:302
  78.5 18.5 %all-to-all-start.6 = ((bf16[16,1,128,128]{3,2,1,0:T(8,128)(2,1)}), bf16[16,1,128,128]{3,2,1,0:T(8,128)(2,1)S(1)}, u32[]{:S(2)}, u32[]{:S(2)}) async-start(bf16[16,1,128,128]{3,2,1,0:T(8,128)(2,1)} %get-tuple-element.838), calls=%async_computation.6 | async-start | bytes 1048576 | tf_op jit(solution)/shard_map/all_to_all | solution.py:303
  97.0 18.6 %all-to-all-start = ((bf16[16,1,128,128]{3,2,1,0:T(8,128)(2,1)}), bf16[16,1,128,128]{3,2,1,0:T(8,128)(2,1)S(1)}, u32[]{:S(2)}, u32[]{:S(2)}) async-start(bf16[16,1,128,128]{3,2,1,0:T(8,128)(2,1)} %get-tuple-element.847), calls=%async_computation | async-start | bytes 1048576 | tf_op jit(solution)/shard_map/all_to_all | solution.py:301
  115.6 18.6 %all-to-all-start.1 = ((bf16[16,1,128,128]{3,2,1,0:T(8,128)(2,1)}), bf16[16,1,128,128]{3,2,1,0:T(8,128)(2,1)S(1)}, u32[]{:S(2)}, u32[]{:S(2)}) async-start(bf16[16,1,128,128]{3,2,1,0:T(8,128)(2,1)} %get-tuple-element.846), calls=%async_computation.1 | async-start | bytes 1048576 | tf_op jit(solution)/shard_map/all_to_all | solution.py:304
  137.8 144.2 %copy-start.22 = (s32[1024]{0:T(1024)S(1)}, s32[1024]{0:T(1024)}, u32[]{:S(2)}) copy-start(s32[1024]{0:T(1024)} %pad_clamp_fusion.1) | copy-start | bytes 12292
  137.8 145.3 %copy-start.26 = (pred[16]{0:T(512)(128)(4,1)S(1)}, pred[16]{0:T(512)(128)(4,1)}, u32[]{:S(2)}) copy-start(pred[16]{0:T(512)(128)(4,1)} %get-tuple-element.799) | copy-start | bytes 52
  283.8 10.4 %all-to-all-start.9 = ((f32[16,1,128]{2,1,0:T(1,128)}), f32[16,1,128]{2,1,0:T(1,128)S(1)}, u32[]{:S(2)}, u32[]{:S(2)}) async-start(f32[16,1,128]{2,1,0:T(1,128)} %bitcast.104), calls=%async_computation.9 | async-start | bytes 16384 | tf_op jit(solution)/shard_map/all_to_all | solution.py:339
  291.5 35.3 %copy-start.6 = (s32[16]{0:T(128)S(1)}, s32[16]{0:T(128)}, u32[]{:S(2)}) copy-start(s32[16]{0:T(128)} %copy-done.5) | copy-start | bytes 196
  291.5 35.4 %copy-start.35 = (s32[2]{0:T(128)S(1)}, s32[2]{0:T(128)}, u32[]{:S(2)}) copy-start(s32[2]{0:T(128)} %get-tuple-element.852) | copy-start | bytes 28
  291.5 36.6 %copy-start.23 = (pred[16]{0:T(512)(128)(4,1)S(1)}, pred[16]{0:T(512)(128)(4,1)}, u32[]{:S(2)}) copy-start(pred[16]{0:T(512)(128)(4,1)} %get-tuple-element.832) | copy-start | bytes 52
  291.5 36.7 %copy-start.25 = (f32[16]{0:T(128)S(1)}, f32[16]{0:T(128)}, u32[]{:S(2)}) copy-start(f32[16]{0:T(128)} %copy-done.24) | copy-start | bytes 196
  291.5 36.7 %copy-start.28 = (pred[16]{0:T(512)(128)(4,1)S(1)}, pred[16]{0:T(512)(128)(4,1)}, u32[]{:S(2)}) copy-start(pred[16]{0:T(512)(128)(4,1)} %copy-done.27) | copy-start | bytes 52
  291.6 36.7 %copy-start.32 = (s32[16]{0:T(128)S(1)}, s32[16]{0:T(128)}, u32[]{:S(2)}) copy-start(s32[16]{0:T(128)} %param.29) | copy-start | bytes 196
  291.6 36.6 %copy-start.34 = (s32[128]{0:T(128)S(1)}, s32[128]{0:T(128)}, u32[]{:S(2)}) copy-start(s32[128]{0:T(128)} %copy-done.33) | copy-start | bytes 1540
  294.2 11.5 %all-to-all-start.8 = ((f32[16,1,128]{2,1,0:T(1,128)}), f32[16,1,128]{2,1,0:T(1,128)S(1)}, u32[]{:S(2)}, u32[]{:S(2)}) async-start(f32[16,1,128]{2,1,0:T(1,128)} %bitcast.95), calls=%async_computation.8 | async-start | bytes 16384 | tf_op jit(solution)/shard_map/all_to_all | solution.py:338
  322.8 18.5 %all-to-all-start.7 = ((bf16[16,1,128,128]{3,2,1,0:T(8,128)(2,1)}), bf16[16,1,128,128]{3,2,1,0:T(8,128)(2,1)S(1)}, u32[]{:S(2)}, u32[]{:S(2)}) async-start(bf16[16,1,128,128]{3,2,1,0:T(8,128)(2,1)} %get-tuple-element.825), calls=%async_computation.7 | async-start | bytes 1048576 | tf_op jit(solution)/shard_map/all_to_all | solution.py:333
  330.9 67.3 %collective-permute-start.3 = (bf16[16,128,128]{2,1,0:T(8,128)(2,1)}, bf16[16,128,128]{2,1,0:T(8,128)(2,1)}, u32[]{:S(2)}, u32[]{:S(2)}) collective-permute-start(bf16[16,128,128]{2,1,0:T(8,128)(2,1)} %convolution_convert_fusion), channel_id=1, source_target_pairs={{2,0},{4,2},{6,4},{8,6},{10,8},{12,10},{14,12},{16,14},{18,16},{20... | collective-permute-start | bytes 1572872 | tf_op jit(solution)/shard_map/ppermute | solution.py:18
  341.3 60.4 %all-to-all-start.10 = ((bf16[16,1,128,128]{3,2,1,0:T(8,128)(2,1)}), bf16[16,1,128,128]{3,2,1,0:T(8,128)(2,1)S(1)}, u32[]{:S(2)}, u32[]{:S(2)}) async-start(bf16[16,1,128,128]{3,2,1,0:T(8,128)(2,1)} %get-tuple-element.824), calls=%async_computation.10 | async-start | bytes 1048576 | tf_op jit(solution)/shard_map/all_to_all | solution.py:334
  349.0 53.7 %collective-permute-start.2 = (bf16[16,128,128]{1,2,0:T(8,128)(2,1)}, bf16[16,128,128]{1,2,0:T(8,128)(2,1)}, u32[]{:S(2)}, u32[]{:S(2)}) collective-permute-start(bf16[16,128,128]{1,2,0:T(8,128)(2,1)} %fusion.37), channel_id=1, source_target_pairs={{2,0},{4,2},{6,4},{8,6},{10,8},{12,10},{14,12},{16,14},{18,16},{20... | collective-permute-start | bytes 1572872 | tf_op jit(solution)/shard_map/ppermute | solution.py:18
  (61 other events, 356.1 us)
where the time goes:
time: 409 us; the launch traced here: 406 us
  matrix products  82.7 us (20%)
  blocking collectives  77.2 us (19%)
  waiting for transfers between devices  66.6 us (16%)
  local copies, waits for them, and re-layouts  57.8 us (14%)
  other arithmetic  53.6 us (13%)
  starting transfers between devices  50.4 us (12%)
  loops' own time  16.5 us (4%)
    psum x1, blocking collectives, shards(): temper_total = lax.psum(temper_local, ('seq', 'dp'))  45.6 us
    dot_general x6, matrix products, group_step(): lax.dot_general(prob_low, grad_group, (((0,), (0,)), ((), ())), preferred...  22.9 us
    reduce_sum x6, other arithmetic, group_step(): temper_acc = temper_acc + jnp.sum(score_grad * raw_scores)  20 us
    all_to_all x1, blocking collectives, shards(): lax.all_to_all(to_owner(owner_results[2]), 'seq', split_axis=0, concat_ax...  17.1 us
    dot_general x6, matrix products, group_step(): lax.dot_general(grad_group, value_rows, (((1,), (1,)), ((), ())), preferr...  16.2 us
    another operation x2, loops' own time, cluster_pair(): lax.scan(group_step, initial, start_rows)  14.9 us
    all_to_all x1, blocking collectives, shards(): lax.all_to_all(to_peers(top_w), 'seq', split_axis=0, concat_axis=0, tiled...  14.5 us
    dot_general x6, matrix products, group_step(): lax.dot_general(grad_low, query_group, (((0,), (0,)), ((), ())), preferre...  13.2 us
  transfers between devices with their start and end apart: 14, of which 9 were waited for; matrix products, arithmetic and copies ran while one was open for 11% of the time, Pallas kernels for 0%

commit v1 on v0

--- a/solution.py
+++ b/solution.py
@@ -3,6 +3,8 @@
 import jax
 import jax.numpy as jnp
 from jax import lax
+from jax.experimental import pallas as pl
+from jax.experimental.pallas import tpu as pltpu
 from jax.sharding import PartitionSpec as P
 
 HD = 128
@@ -193,7 +195,7 @@
     )
 
 
-def shards(
+def clustered_shards(
     probe_vectors,
     lookup_vectors,
     content_vectors,
@@ -372,6 +374,261 @@
     return (token_major(query_out), token_major(key_out), token_major(value_out), temper_grad)
 
 
+TILE = 256
+EXTRA = 16
+VMEM_LIMIT = 56 * 1024 * 1024
+
+
+def pack_kernel(*refs):
+    arrays, packed_ref = refs[:-1], refs[-1]
+    for place, array_ref in enumerate(arrays):
+        for head in range(packed_ref.shape[0]):
+            packed_ref[head, place * BLK : (place + 1) * BLK, :] = array_ref[
+                0, :, head * HD : (head + 1) * HD
+            ]
+
+
+def packed(*arrays):
+    head_count = arrays[0].shape[2] // HD
+    out_shape = (head_count, len(arrays) * BLK, HD)
+    return pl.pallas_call(
+        pack_kernel,
+        out_shape=jax.ShapeDtypeStruct(out_shape, jnp.bfloat16),
+        cost_estimate=pl.CostEstimate(
+            flops=0, bytes_accessed=4 * math.prod(out_shape), transcendentals=0
+        ),
+        compiler_params=pltpu.CompilerParams(vmem_limit_bytes=VMEM_LIMIT),
+        name="pack_heads",
+    )(*arrays)
+
+
+def unpack_kernel(packed_ref, *out_refs):
+    for place, out_ref in enumerate(out_refs):
+        for head in range(packed_ref.shape[0]):
+            out_ref[0, :, head * HD : (head + 1) * HD] = packed_ref[
+                head, place * BLK : (place + 1) * BLK, :
+            ]
+
+
+def unpacked(array_in, count):
+    head_count = array_in.shape[0]
+    out_shape = (1, BLK, head_count * HD)
+    return pl.pallas_call(
+        unpack_kernel,
+        out_shape=[jax.ShapeDtypeStruct(out_shape, jnp.bfloat16)] * count,
+        cost_estimate=pl.CostEstimate(
+            flops=0, bytes_accessed=4 * count * math.prod(out_shape), transcendentals=0
+        ),
+        compiler_params=pltpu.CompilerParams(vmem_limit_bytes=VMEM_LIMIT),
+        name="unpack_heads",
+    )(array_in)
+
+
+def allowed_scores(scores, tile_key, tile_query, ids_ref, head, width):
+    per_tile = TILE // BLK
+    spread = lax.broadcasted_iota(jnp.int32, (BLK, BLK), 0) - lax.broadcasted_iota(
+        jnp.int32, (BLK, BLK), 1
+    )
+    rows = []
+    for sub_key in range(per_tile):
+        pieces = []
+        block_key = tile_key * per_tile + sub_key
+        for sub_query in range(per_tile):
+            block_query = tile_query * per_tile + sub_query
+            piece = scores[
+                sub_key * BLK : (sub_key + 1) * BLK, sub_query * BLK : (sub_query + 1) * BLK
+            ]
+            same = ids_ref[head, block_key] == ids_ref[head, block_query]
+            if block_key > block_query:
+                piece = jnp.full_like(piece, blocked_score)
+            elif block_key == block_query:
+                piece = jnp.where(spread <= 0, piece, blocked_score)
+            elif block_key == block_query - 1:
+                least = jnp.where(same, -BLK, BLK - width)
+                piece = jnp.where(spread > least, piece, blocked_score)
+            else:
+                piece = jnp.where(spread > jnp.where(same, -BLK, BLK), piece, blocked_score)
+            pieces.append(piece)
+        rows.append(jnp.concatenate(pieces, axis=1))
+    return jnp.concatenate(rows, axis=0)
+
+
+def dot_rows(left, right):
+    return lax.dot_general(
+        left, right, (((1,), (1,)), ((), ())), preferred_element_type=jnp.float32
+    )
+
+
+def dot_plain(left, right):
+    return lax.dot_general(
+        left, right, (((1,), (0,)), ((), ())), preferred_element_type=jnp.float32
+    )
+
+
+def attention_kernel(
+    softness_ref, ids_ref, span_ref, in_ref, out_ref,
+    query, key, value, grad, key_across, score, gradient, prob_low, grad_low,
+):
+    head = lax.axis_index("seq")
+    blocks = in_ref.shape[0]
+    tiles = blocks * BLK // TILE
+    temper = softness_ref[head]
+    width = span_ref[head]
+    scaling = temper * (1.0 / math.sqrt(HD))
+    to_log2 = scaling * math.log2(math.e)
+    for block in range(blocks):
+        rows = slice(block * BLK, (block + 1) * BLK)
+        query[rows, :] = in_ref[block, 0 * BLK : 1 * BLK, :]
+        key[rows, :] = in_ref[block, 1 * BLK : 2 * BLK, :]
+        value[rows, :] = in_ref[block, 2 * BLK : 3 * BLK, :]
+        grad[rows, :] = in_ref[block, 3 * BLK : 4 * BLK, :]
+        key_across[:, rows] = in_ref[block, 1 * BLK : 2 * BLK, :].T
+    temper_rows = jnp.zeros((1, HD), jnp.float32)
+    for tile in range(tiles):
+        here = slice(tile * TILE, (tile + 1) * TILE)
+        top = jnp.full((1, TILE), blocked_score, jnp.float32)
+        for other in range(tile + 1):
+            there = slice(other * TILE, (other + 1) * TILE)
+            raw = dot_rows(key[there, :], query[here, :]) * to_log2
+            raw = allowed_scores(raw, other, tile, ids_ref, head, width)
+            score[there, :] = raw
+            top = jnp.maximum(top, jnp.max(raw, axis=0, keepdims=True))
+        total = jnp.zeros((1, TILE), jnp.float32)
+        mass = jnp.zeros((1, TILE), jnp.float32)
+        for other in range(tile + 1):
+            there = slice(other * TILE, (other + 1) * TILE)
+            weight = jnp.exp2(score[there, :] - top)
+            towards = dot_rows(value[there, :], grad[here, :])
+            score[there, :] = weight
+            gradient[there, :] = towards
+            total += jnp.sum(weight, axis=0, keepdims=True)
+            mass += jnp.sum(weight * towards, axis=0, keepdims=True)
+        inverse = 1.0 / total
+        delta = mass * inverse
+        for other in range(tile + 1):
+            there = slice(other * TILE, (other + 1) * TILE)
+            probability = score[there, :] * inverse
+            prob_low[there, here] = probability.astype(jnp.bfloat16)
+            grad_low[there, here] = (probability * (gradient[there, :] - delta)).astype(
+                jnp.bfloat16
+            )
+        upto = slice(0, (tile + 1) * TILE)
+        query_part = dot_plain(key_across[:, upto], grad_low[upto, here]).T
+        temper_rows += jnp.sum(
+            query_part * query[here, :].astype(jnp.float32), axis=0, keepdims=True
+        )
+        query_part = (query_part * scaling).astype(jnp.bfloat16)
+        for sub in range(TILE // BLK):
+            out_ref[tile * (TILE // BLK) + sub, 0:BLK, :] = query_part[
+                sub * BLK : (sub + 1) * BLK, :
+            ]
+    for tile in range(tiles):
+        here = slice(tile * TILE, (tile + 1) * TILE)
+        onward = slice(tile * TILE, tiles * TILE)
+        key_part = (dot_plain(grad_low[here, onward], query[onward, :]) * scaling).astype(
+            jnp.bfloat16
+        )
+        value_part = dot_plain(prob_low[here, onward], grad[onward, :]).astype(jnp.bfloat16)
+        for sub in range(TILE // BLK):
+            block = tile * (TILE // BLK) + sub
+            part = slice(sub * BLK, (sub + 1) * BLK)
+            out_ref[block, BLK : 2 * BLK, :] = key_part[part, :]
+            out_ref[block, 2 * BLK : 3 * BLK, :] = value_part[part, :]
+    temper_sum = jnp.sum(temper_rows, axis=1, keepdims=True) * (1.0 / math.sqrt(HD))
+    spread = jnp.broadcast_to(temper_sum, (EXTRA, HD))
+    high = spread.astype(jnp.bfloat16).astype(jnp.float32)
+    middle = (spread - high).astype(jnp.bfloat16).astype(jnp.float32)
+    low = spread - high - middle
+    row = lax.broadcasted_iota(jnp.int32, (EXTRA, HD), 0)
+    pieces = jnp.where(row == 0, high, jnp.where(row == 1, middle, low)).astype(jnp.bfloat16)
+    for block in range(blocks):
+        out_ref[block, 3 * BLK : 3 * BLK + EXTRA, :] = pieces
+
+
+def attention(softness, ids, span, arrived):
+    blocks = arrived.shape[0]
+    length = blocks * BLK
+    out_shape = (blocks, 3 * BLK + EXTRA, HD)
+    smem = pl.BlockSpec(memory_space=pltpu.SMEM)
+    vmem = pl.BlockSpec(memory_space=pltpu.VMEM)
+    return pl.pallas_call(
+        attention_kernel,
+        out_shape=jax.ShapeDtypeStruct(out_shape, jnp.bfloat16),
+        in_specs=[smem, smem, smem, vmem],
+        out_specs=vmem,
+        scratch_shapes=[
+            pltpu.VMEM((length, HD), jnp.bfloat16),
+            pltpu.VMEM((length, HD), jnp.bfloat16),
+            pltpu.VMEM((length, HD), jnp.bfloat16),
+            pltpu.VMEM((length, HD), jnp.bfloat16),
+            pltpu.VMEM((HD, length), jnp.bfloat16),
+            pltpu.VMEM((length, TILE), jnp.float32),
+            pltpu.VMEM((length, TILE), jnp.float32),
+            pltpu.VMEM((length, length), jnp.bfloat16),
+            pltpu.VMEM((length, length), jnp.bfloat16),
+        ],
+        cost_estimate=pl.CostEstimate(
+            flops=5 * length * length * HD,
+            bytes_accessed=2 * (math.prod(out_shape) + math.prod(arrived.shape)),
+            transcendentals=length * length // 2,
+        ),
+        compiler_params=pltpu.CompilerParams(vmem_limit_bytes=VMEM_LIMIT),
+        name="head_attention",
+    )(softness, ids, span, arrived)
+
+
+def head_shards(
+    probe_vectors,
+    lookup_vectors,
+    content_vectors,
+    result_cotangent,
+    logit_softness,
+    block_grouping,
+    neighborhood_span,
+):
+    ids = block_grouping[0, :, :, 0]
+    dp_count = lax.axis_size("dp")
+    sent = packed(probe_vectors, lookup_vectors, content_vectors, result_cotangent)
+    arrived = lax.all_to_all(sent, "seq", split_axis=0, concat_axis=0, tiled=True)
+    owned = attention(logit_softness, ids, neighborhood_span, arrived)
+    back = lax.all_to_all(owned, "seq", split_axis=0, concat_axis=0, tiled=True)
+    pieces = back[:, 3 * BLK : 3 * BLK + 3, 0].astype(jnp.float32)
+    temper_local = jnp.sum(pieces, axis=1)
+    temper_total = temper_local
+    for step in range(1, dp_count):
+        pairs = [(source, (source + step) % dp_count) for source in range(dp_count)]
+        temper_total = temper_total + lax.ppermute(temper_local, "dp", pairs)
+    outs = unpacked(back, 3)
+    tokens = probe_vectors.shape[1] * lax.axis_size("seq")
+    return (*outs, temper_total / (dp_count * tokens))
+
+
+def shards(
+    probe_vectors,
+    lookup_vectors,
+    content_vectors,
+    result_cotangent,
+    logit_softness,
+    block_grouping,
+    neighborhood_span,
+):
+    head_count = probe_vectors.shape[2] // HD
+    one_block = probe_vectors.shape[1] == BLK
+    if head_count == lax.axis_size("seq") and one_block:
+        plan = head_shards
+    else:
+        plan = clustered_shards
+    return plan(
+        probe_vectors,
+        lookup_vectors,
+        content_vectors,
+        result_cotangent,
+        logit_softness,
+        block_grouping,
+        neighborhood_span,
+    )
+
+
 def solution(mesh):
     in_specs = (
         P("dp", "seq", None),

time: 409 us -> 121 us (0.30)
  matrix products: 82.7 us -> 0 us
  waiting for transfers between devices: 66.6 us -> 0.01 us
  local copies, waits for them, and re-layouts: 57.8 us -> 0.01 us
  other arithmetic: 53.6 us -> 0.72 us
  starting transfers between devices: 50.4 us -> 1.53 us
  blocking collectives: 77.2 us -> 99.7 us
  Pallas kernels: 0 us -> 18.4 us
  loops' own time: 16.5 us -> 0 us
    dot_general x35 -> x0, matrix products: 82.7 us -> none  [the longest x6 22.9 us: group_step(): lax.dot_general(prob_low, grad_group, (((0,), (0,)), ((), ())), preferred...]
    all_to_all x2, blocking collectives: 31.6 us -> 99.7 us  [the longest x1 54.8 us: head_shards(): lax.all_to_all(sent, 'seq', split_axis=0, concat_axis=0, tiled=True)]
    all_to_all x10 -> x0, waiting for transfers between devices: 66.6 us -> none  [the longest x1 12.8 us: shards(): lax.all_to_all(to_peers(key_home), 'seq', split_axis=0, concat_axis=0, ti...]
    psum x1 -> x0, blocking collectives: 45.6 us -> none  [shards(): temper_total = lax.psum(temper_local, ('seq', 'dp'))]
    all_to_all x10 -> x0, starting transfers between devices: 40.1 us -> none  [the longest x1 5.16 us: shards(): lax.all_to_all(to_owner(owner_results[3]), 'seq', split_axis=0, concat_ax...]
    reduce_sum x17 -> x1, other arithmetic: 33.6 us -> 0.2 us  [head_shards(): temper_local = jnp.sum(pieces, axis=1)]
    gather x35 -> x0, local copies, waits for them, and re-layouts: 24.6 us -> none  [the longest x5 6.47 us: to_owner(): return jnp.take(flat, back_flat, axis=0)]
    pallas_call x0 -> x3, Pallas kernels: none -> 18.4 us  [the longest x1 12.2 us: attention(): pl.pallas_call(attention_kernel, out_shape=jax.ShapeDtypeStruct(out_shape...]
  transfers between devices with their start and end apart: 14 -> 1, of which waited for: 9 -> 0; matrix products, arithmetic and copies ran while one was open for 11% -> 0% of each run, Pallas kernels for 0% -> 2%
where the time goes in v1:
time: 121 us
  blocking collectives  99.7 us (82%)
  Pallas kernels  18.4 us (15%)
  starting transfers between devices  1.53 us (1%)
    all_to_all x1, blocking collectives, head_shards(): lax.all_to_all(sent, 'seq', split_axis=0, concat_axis=0, tiled=True)  54.8 us
    all_to_all x1, blocking collectives, head_shards(): back = lax.all_to_all(owned, 'seq', split_axis=0, concat_axis=0, tiled=True)  44.9 us
    pallas_call x1, Pallas kernels, attention(): pl.pallas_call(attention_kernel, out_shape=jax.ShapeDtypeStruct(out_shape...  12.2 us
    pallas_call x1, Pallas kernels, packed(): pl.pallas_call(pack_kernel, out_shape=jax.ShapeDtypeStruct(out_shape, jnp...  3.18 us
    pallas_call x1, Pallas kernels, unpacked(): pl.pallas_call(unpack_kernel, out_shape=[jax.ShapeDtypeStruct(out_shape,...  2.98 us
  transfers between devices with their start and end apart: 1, of which 0 were waited for; matrix products, arithmetic and copies ran while one was open for 0% of the time, Pallas kernels for 2%

profile of v1, /device:TPU:0, one launch (start us, length us, event | category | flops | bytes accessed | tf_op | source)
XLA Modules:
  0.0 120.9 jit_solution(12420754935623321812)
XLA Ops:
  0.6 3.2 %pack_heads.1 = bf16[16,512,128]{2,1,0:T(8,128)(2,1)} custom-call(bf16[1,128,2048]{2,1,0:T(8,128)(2,1)} %refs_0_.1, bf16[1,128,2048]{2,1,0:T(8,128)(2,1)} %refs_1_.1, bf16[1,128,2048]{2,1,0:T(8,128)(2,1)} %refs_2_.1, bf16[1,128,2048]{2,1,0:T(8,128)(2,1)} %refs_3_.1), custom_call_target="tpu_custom_call" | custom-call | bytes 4194304 | tf_op jit(solution)/shard_map/pack_heads/pallas_call | solution.py:394
  3.8 54.8 %all_to_all.10.in_ref = bf16[16,512,128]{2,1,0:T(8,128)(2,1)} all-to-all(bf16[16,512,128]{2,1,0:T(8,128)(2,1)} %pack_heads.1), channel_id=1, replica_groups=mesh['seq'=16,'dp'=2] {'seq'}, dimensions={0} | all-to-all | bytes 4194304 | tf_op jit(solution)/shard_map/all_to_all | solution.py:592
  58.6 12.2 %head_attention.1 = bf16[16,400,128]{2,1,0:T(8,128)(2,1)} custom-call(f32[16]{0:T(128)} %softness_ref.1, s32[16,16]{1,0:T(8,128)} %bitcast.1, s32[16]{0:T(128)} %span_ref.1, bf16[16,512,128]{2,1,0:T(8,128)(2,1)} %all_to_all.10.in_ref), custom_call_target="tpu_custom_call" | custom-call | flops 2684354560 | bytes 3735552 | tf_op jit(solution)/shard_map/head_attention/pallas_call | solution.py:554
  70.8 44.9 %all_to_all.11.packed_ref = bf16[16,400,128]{2,1,0:T(8,128)(2,1)S(1)} all-to-all(bf16[16,400,128]{2,1,0:T(8,128)(2,1)} %head_attention.1), channel_id=1, replica_groups=mesh['seq'=16,'dp'=2] {'seq'}, dimensions={0} | all-to-all | bytes 3276800 | tf_op jit(solution)/shard_map/all_to_all | solution.py:594
  115.7 0.0 copy-start
  115.7 0.2 convert_reduce_fusion
  115.9 1.5 %collective-permute-start = (f32[16]{0:T(128)S(1)}, f32[16]{0:T(128)S(1)}, u32[]{:S(2)}, u32[]{:S(2)}) collective-permute-start(f32[16]{0:T(128)S(1)} %convert_reduce_fusion), channel_id=1, source_target_pairs={{0,1},{1,0},{2,3},{3,2},{4,5},{5,4},{6,7},{7,6},{8,9},{9,8},{10,11... | collective-permute-start | bytes 200 | tf_op jit(solution)/shard_map/ppermute | solution.py:600
  117.4 0.0 copy-done
  117.4 3.0 %unpack_heads.1 = (bf16[1,128,2048]{2,1,0:T(8,128)(2,1)}, bf16[1,128,2048]{2,1,0:T(8,128)(2,1)}, bf16[1,128,2048]{2,1,0:T(8,128)(2,1)}) custom-call(bf16[16,400,128]{2,1,0:T(8,128)(2,1)} %copy-done), custom_call_target="tpu_custom_call" | custom-call | bytes 3145728 | tf_op jit(solution)/shard_map/unpack_heads/pallas_call | solution.py:416
  120.4 0.0 collective-permute-done
  120.4 0.5 add_multiply_fusion
Async XLA Ops:
  115.7 1.7 %copy-start = (bf16[16,400,128]{2,1,0:T(8,128)(2,1)}, bf16[16,400,128]{2,1,0:T(8,128)(2,1)S(1)}, u32[]{:S(2)}) copy-start(bf16[16,400,128]{2,1,0:T(8,128)(2,1)S(1)} %all_to_all.11.packed_ref) | copy-start | bytes 4915204
  115.9 4.5 %collective-permute-start = (f32[16]{0:T(128)S(1)}, f32[16]{0:T(128)S(1)}, u32[]{:S(2)}, u32[]{:S(2)}) collective-permute-start(f32[16]{0:T(128)S(1)} %convert_reduce_fusion), channel_id=1, source_target_pairs={{0,1},{1,0},{2,3},{3,2},{4,5},{5,4},{6,7},{7,6},{8,9},{9,8},{10,11... | collective-permute-start | bytes 200 | tf_op jit(solution)/shard_map/ppermute | solution.py:600

commit v2 on v1

--- a/solution.py
+++ b/solution.py
@@ -1,3 +1,4 @@
+import functools
 import math
 
 import jax
@@ -379,49 +380,68 @@
 VMEM_LIMIT = 56 * 1024 * 1024
 
 
-def pack_kernel(*refs):
-    arrays, packed_ref = refs[:-1], refs[-1]
-    for place, array_ref in enumerate(arrays):
-        for head in range(packed_ref.shape[0]):
-            packed_ref[head, place * BLK : (place + 1) * BLK, :] = array_ref[
-                0, :, head * HD : (head + 1) * HD
-            ]
+def partner(step):
+    return lax.axis_index("seq") ^ step
+
+
+def columns_of(index):
+    return pl.ds(pl.multiple_of(index * HD, HD), HD)
+
+
+def rows_of(index):
+    return pl.ds(pl.multiple_of(index * BLK, BLK), BLK)
+
+
+def pack_kernel(*refs, count):
+    arrays, out_refs = refs[:count], refs[count:]
+    for step, out_ref in enumerate(out_refs):
+        head = partner(step)
+        for place, array_ref in enumerate(arrays):
+            out_ref[place * BLK : (place + 1) * BLK, :] = array_ref[0, :, columns_of(head)]
 
 
 def packed(*arrays):
     head_count = arrays[0].shape[2] // HD
-    out_shape = (head_count, len(arrays) * BLK, HD)
+    out_shape = (len(arrays) * BLK, HD)
     return pl.pallas_call(
-        pack_kernel,
-        out_shape=jax.ShapeDtypeStruct(out_shape, jnp.bfloat16),
+        functools.partial(pack_kernel, count=len(arrays)),
+        out_shape=[jax.ShapeDtypeStruct(out_shape, jnp.bfloat16)] * head_count,
         cost_estimate=pl.CostEstimate(
-            flops=0, bytes_accessed=4 * math.prod(out_shape), transcendentals=0
+            flops=0, bytes_accessed=4 * head_count * math.prod(out_shape), transcendentals=0
         ),
         compiler_params=pltpu.CompilerParams(vmem_limit_bytes=VMEM_LIMIT),
         name="pack_heads",
     )(*arrays)
 
 
-def unpack_kernel(packed_ref, *out_refs):
+def exchanged(chunks):
+    count = len(chunks)
+    return [chunks[0]] + [
+        lax.ppermute(chunks[step], "seq", [(source, source ^ step) for source in range(count)])
+        for step in range(1, count)
+    ]
+
+
+def unpack_kernel(*refs, count):
+    chunks, out_refs = refs[:-count], refs[-count:]
     for place, out_ref in enumerate(out_refs):
-        for head in range(packed_ref.shape[0]):
-            out_ref[0, :, head * HD : (head + 1) * HD] = packed_ref[
-                head, place * BLK : (place + 1) * BLK, :
+        for step, chunk_ref in enumerate(chunks):
+            out_ref[0, :, columns_of(partner(step))] = chunk_ref[
+                place * BLK : (place + 1) * BLK, :
             ]
 
 
-def unpacked(array_in, count):
-    head_count = array_in.shape[0]
-    out_shape = (1, BLK, head_count * HD)
+def unpacked(chunks, count):
+    out_shape = (1, BLK, len(chunks) * HD)
     return pl.pallas_call(
-        unpack_kernel,
+        functools.partial(unpack_kernel, count=count),
         out_shape=[jax.ShapeDtypeStruct(out_shape, jnp.bfloat16)] * count,
         cost_estimate=pl.CostEstimate(
             flops=0, bytes_accessed=4 * count * math.prod(out_shape), transcendentals=0
         ),
         compiler_params=pltpu.CompilerParams(vmem_limit_bytes=VMEM_LIMIT),
         name="unpack_heads",
-    )(array_in)
+    )(*chunks)
 
 
 def allowed_scores(scores, tile_key, tile_query, ids_ref, head, width):
@@ -465,24 +485,24 @@
     )
 
 
-def attention_kernel(
-    softness_ref, ids_ref, span_ref, in_ref, out_ref,
-    query, key, value, grad, key_across, score, gradient, prob_low, grad_low,
-):
+def attention_kernel(softness_ref, ids_ref, span_ref, *refs, blocks):
+    in_refs, out_refs = refs[:blocks], refs[blocks : 2 * blocks]
+    query, key, value, grad, key_across, score, gradient, prob_low, grad_low, result = refs[
+        2 * blocks :
+    ]
     head = lax.axis_index("seq")
-    blocks = in_ref.shape[0]
     tiles = blocks * BLK // TILE
     temper = softness_ref[head]
     width = span_ref[head]
     scaling = temper * (1.0 / math.sqrt(HD))
     to_log2 = scaling * math.log2(math.e)
-    for block in range(blocks):
-        rows = slice(block * BLK, (block + 1) * BLK)
-        query[rows, :] = in_ref[block, 0 * BLK : 1 * BLK, :]
-        key[rows, :] = in_ref[block, 1 * BLK : 2 * BLK, :]
-        value[rows, :] = in_ref[block, 2 * BLK : 3 * BLK, :]
-        grad[rows, :] = in_ref[block, 3 * BLK : 4 * BLK, :]
-        key_across[:, rows] = in_ref[block, 1 * BLK : 2 * BLK, :].T
+    for step, in_ref in enumerate(in_refs):
+        rows = rows_of(partner(step))
+        query[rows, :] = in_ref[0 * BLK : 1 * BLK, :]
+        key[rows, :] = in_ref[1 * BLK : 2 * BLK, :]
+        value[rows, :] = in_ref[2 * BLK : 3 * BLK, :]
+        grad[rows, :] = in_ref[3 * BLK : 4 * BLK, :]
+        key_across[:, rows] = in_ref[1 * BLK : 2 * BLK, :].T
     temper_rows = jnp.zeros((1, HD), jnp.float32)
     for tile in range(tiles):
         here = slice(tile * TILE, (tile + 1) * TILE)
@@ -518,10 +538,7 @@
             query_part * query[here, :].astype(jnp.float32), axis=0, keepdims=True
         )
         query_part = (query_part * scaling).astype(jnp.bfloat16)
-        for sub in range(TILE // BLK):
-            out_ref[tile * (TILE // BLK) + sub, 0:BLK, :] = query_part[
-                sub * BLK : (sub + 1) * BLK, :
-            ]
+        result[0, here, :] = query_part
     for tile in range(tiles):
         here = slice(tile * TILE, (tile + 1) * TILE)
         onward = slice(tile * TILE, tiles * TILE)
@@ -529,11 +546,8 @@
             jnp.bfloat16
         )
         value_part = dot_plain(prob_low[here, onward], grad[onward, :]).astype(jnp.bfloat16)
-        for sub in range(TILE // BLK):
-            block = tile * (TILE // BLK) + sub
-            part = slice(sub * BLK, (sub + 1) * BLK)
-            out_ref[block, BLK : 2 * BLK, :] = key_part[part, :]
-            out_ref[block, 2 * BLK : 3 * BLK, :] = value_part[part, :]
+        result[1, here, :] = key_part
+        result[2, here, :] = value_part
     temper_sum = jnp.sum(temper_rows, axis=1, keepdims=True) * (1.0 / math.sqrt(HD))
     spread = jnp.broadcast_to(temper_sum, (EXTRA, HD))
     high = spread.astype(jnp.bfloat16).astype(jnp.float32)
@@ -541,21 +555,24 @@
     low = spread - high - middle
     row = lax.broadcasted_iota(jnp.int32, (EXTRA, HD), 0)
     pieces = jnp.where(row == 0, high, jnp.where(row == 1, middle, low)).astype(jnp.bfloat16)
-    for block in range(blocks):
-        out_ref[block, 3 * BLK : 3 * BLK + EXTRA, :] = pieces
+    for step, out_ref in enumerate(out_refs):
+        rows = rows_of(partner(step))
+        for place in range(3):
+            out_ref[place * BLK : (place + 1) * BLK, :] = result[place, rows, :]
+        out_ref[3 * BLK : 3 * BLK + EXTRA, :] = pieces
 
 
 def attention(softness, ids, span, arrived):
-    blocks = arrived.shape[0]
+    blocks = len(arrived)
     length = blocks * BLK
-    out_shape = (blocks, 3 * BLK + EXTRA, HD)
+    out_shape = (3 * BLK + EXTRA, HD)
     smem = pl.BlockSpec(memory_space=pltpu.SMEM)
     vmem = pl.BlockSpec(memory_space=pltpu.VMEM)
     return pl.pallas_call(
-        attention_kernel,
-        out_shape=jax.ShapeDtypeStruct(out_shape, jnp.bfloat16),
-        in_specs=[smem, smem, smem, vmem],
-        out_specs=vmem,
+        functools.partial(attention_kernel, blocks=blocks),
+        out_shape=[jax.ShapeDtypeStruct(out_shape, jnp.bfloat16)] * blocks,
+        in_specs=[smem, smem, smem] + [vmem] * blocks,
+        out_specs=[vmem] * blocks,
         scratch_shapes=[
             pltpu.VMEM((length, HD), jnp.bfloat16),
             pltpu.VMEM((length, HD), jnp.bfloat16),
@@ -566,15 +583,16 @@
             pltpu.VMEM((length, TILE), jnp.float32),
             pltpu.VMEM((length, length), jnp.bfloat16),
             pltpu.VMEM((length, length), jnp.bfloat16),
+            pltpu.VMEM((3, length, HD), jnp.bfloat16),
         ],
         cost_estimate=pl.CostEstimate(
             flops=5 * length * length * HD,
-            bytes_accessed=2 * (math.prod(out_shape) + math.prod(arrived.shape)),
+            bytes_accessed=16 * length * HD,
             transcendentals=length * length // 2,
         ),
         compiler_params=pltpu.CompilerParams(vmem_limit_bytes=VMEM_LIMIT),
         name="head_attention",
-    )(softness, ids, span, arrived)
+    )(softness, ids, span, *arrived)
 
 
 def head_shards(
@@ -589,11 +607,13 @@
     ids = block_grouping[0, :, :, 0]
     dp_count = lax.axis_size("dp")
     sent = packed(probe_vectors, lookup_vectors, content_vectors, result_cotangent)
-    arrived = lax.all_to_all(sent, "seq", split_axis=0, concat_axis=0, tiled=True)
+    arrived = exchanged(sent)
     owned = attention(logit_softness, ids, neighborhood_span, arrived)
-    back = lax.all_to_all(owned, "seq", split_axis=0, concat_axis=0, tiled=True)
-    pieces = back[:, 3 * BLK : 3 * BLK + 3, 0].astype(jnp.float32)
-    temper_local = jnp.sum(pieces, axis=1)
+    back = exchanged(owned)
+    temper_local = jnp.stack(
+        [jnp.sum(chunk[3 * BLK : 3 * BLK + 3, 0].astype(jnp.float32)) for chunk in back]
+    )
+    temper_local = jnp.take(temper_local, partner(jnp.arange(len(back))))
     temper_total = temper_local
     for step in range(1, dp_count):
         pairs = [(source, (source + step) % dp_count) for source in range(dp_count)]

time: 121 us -> 140 us (1.16)
  blocking collectives: 99.7 us -> 0 us
  starting transfers between devices: 1.53 us -> 55.7 us
  waiting for transfers between devices: 0.01 us -> 42.2 us
  local copies, waits for them, and re-layouts: 0.01 us -> 11.3 us
  other arithmetic: 0.72 us -> 11.2 us
    all_to_all x2 -> x0, blocking collectives: 99.7 us -> none  [the longest x1 54.8 us: head_shards(): lax.all_to_all(sent, 'seq', split_axis=0, concat_axis=0, tiled=True)]
    ppermute x0 -> x30, starting transfers between devices: none -> 54.1 us  [exchanged(): lax.ppermute(chunks[step], 'seq', [(source, source ^ step) for source in...]
    ppermute x0 -> x30, waiting for transfers between devices: none -> 42.2 us  [exchanged(): lax.ppermute(chunks[step], 'seq', [(source, source ^ step) for source in...]
    reduce_sum x1 -> x16, other arithmetic: 0.2 us -> 10.7 us  [head_shards(): jnp.sum(chunk[3 * BLK:3 * BLK + 3, 0].astype(jnp.float32))]
    another operation x0 -> x1, local copies, waits for them, and re-layouts: none -> 10.1 us  [head_shards(): jnp.stack([jnp.sum(chunk[3 * BLK:3 * BLK + 3, 0].astype(jnp.float32)) for...]
  transfers between devices with their start and end apart: 1 -> 31, of which waited for: 0 -> 9; matrix products, arithmetic and copies ran while one was open for 0% -> 7% of each run, Pallas kernels for 2% -> 2%
where the time goes in v2:
time: 140 us
  starting transfers between devices  55.7 us (40%)
  waiting for transfers between devices  42.2 us (30%)
  Pallas kernels  18.7 us (13%)
  local copies, waits for them, and re-layouts  11.3 us (8%)
  other arithmetic  11.2 us (8%)
    ppermute x30, starting transfers between devices, exchanged(): lax.ppermute(chunks[step], 'seq', [(source, source ^ step) for source in...  54.1 us
    ppermute x30, waiting for transfers between devices, exchanged(): lax.ppermute(chunks[step], 'seq', [(source, source ^ step) for source in...  42.2 us
    pallas_call x1, Pallas kernels, attention(): pl.pallas_call(functools.partial(attention_kernel, blocks=blocks), out_sh...  12.3 us
    reduce_sum x16, other arithmetic, head_shards(): jnp.sum(chunk[3 * BLK:3 * BLK + 3, 0].astype(jnp.float32))  10.7 us
    another operation x1, local copies, waits for them, and re-layouts, head_shards(): jnp.stack([jnp.sum(chunk[3 * BLK:3 * BLK + 3, 0].astype(jnp.float32)) for...  10.1 us
    pallas_call x1, Pallas kernels, packed(): pl.pallas_call(functools.partial(pack_kernel, count=len(arrays)), out_sha...  3.37 us
    pallas_call x1, Pallas kernels, unpacked(): pl.pallas_call(functools.partial(unpack_kernel, count=count), out_shape=[...  3.05 us
  transfers between devices with their start and end apart: 31, of which 9 were waited for; matrix products, arithmetic and copies ran while one was open for 7% of the time, Pallas kernels for 2%

profile of v2, /device:TPU:0, one launch (start us, length us, event | category | flops | bytes accessed | tf_op | source)
XLA Modules:
  0.0 140.1 jit_solution(6594951717099230931)
XLA Ops:
  0.6 3.4 %pack_heads.1 = (bf16[512,128]{1,0:T(8,128)(2,1)}, bf16[512,128]{1,0:T(8,128)(2,1)}, bf16[512,128]{1,0:T(8,128)(2,1)}, bf16[512,128]{1,0:T(8,128)(2,1)}, bf16[51...) custom-call(bf16[1,128,2048]{2,1,0:T(8,128)(2,1)} %refs_0_.1, ...), custom_call_target="tpu_custom_call" | custom-call | bytes 4194304 | tf_op jit(solution)/shard_map/pack_heads/pallas_call | solution.py:406
  4.5 2.6 %collective-permute-start.1 = (bf16[512,128]{1,0:T(8,128)(2,1)}, bf16[512,128]{1,0:T(8,128)(2,1)S(1)}, u32[]{:S(2)}, u32[]{:S(2)}) collective-permute-start(bf16[512,128]{1,0:T(8,128)(2,1)} %get-tuple-element.41), channel_id=1, source_target_pairs={{0,4},{2,6},{4,0},{6,2},{8,12},{10,14},{12,8},{14,10},{16,20},{18,... | collective-permute-start | bytes 393224 | tf_op jit(solution)/shard_map/ppermute | solution.py:420
  7.1 2.3 %collective-permute-start.10 = (bf16[512,128]{1,0:T(8,128)(2,1)}, bf16[512,128]{1,0:T(8,128)(2,1)S(1)}, u32[]{:S(2)}, u32[]{:S(2)}) collective-permute-start(bf16[512,128]{1,0:T(8,128)(2,1)} %get-tuple-element.50), channel_id=1, source_target_pairs={{0,22},{2,20},{4,18},{6,16},{8,30},{10,28},{12,26},{14,24},{16,6},... | collective-permute-start | bytes 393224 | tf_op jit(solution)/shard_map/ppermute | solution.py:420
  10.7 2.1 %collective-permute-start.12 = (bf16[512,128]{1,0:T(8,128)(2,1)}, bf16[512,128]{1,0:T(8,128)(2,1)S(1)}, u32[]{:S(2)}, u32[]{:S(2)}) collective-permute-start(bf16[512,128]{1,0:T(8,128)(2,1)} %get-tuple-element.52), channel_id=1, source_target_pairs={{0,26},{2,24},{4,30},{6,28},{8,18},{10,16},{12,22},{14,20},{16,10}... | collective-permute-start | bytes 393224 | tf_op jit(solution)/shard_map/ppermute | solution.py:420
  12.9 2.3 %collective-permute-start.13 = (bf16[512,128]{1,0:T(8,128)(2,1)}, bf16[512,128]{1,0:T(8,128)(2,1)S(1)}, u32[]{:S(2)}, u32[]{:S(2)}) collective-permute-start(bf16[512,128]{1,0:T(8,128)(2,1)} %get-tuple-element.53), channel_id=1, source_target_pairs={{0,28},{2,30},{4,24},{6,26},{8,20},{10,22},{12,16},{14,18},{16,12}... | collective-permute-start | bytes 393224 | tf_op jit(solution)/shard_map/ppermute | solution.py:420
  15.2 2.2 %collective-permute-start.14 = (bf16[512,128]{1,0:T(8,128)(2,1)}, bf16[512,128]{1,0:T(8,128)(2,1)S(1)}, u32[]{:S(2)}, u32[]{:S(2)}) collective-permute-start(bf16[512,128]{1,0:T(8,128)(2,1)} %get-tuple-element.54), channel_id=1, source_target_pairs={{0,30},{2,28},{4,26},{6,24},{8,22},{10,20},{12,18},{14,16},{16,14}... | collective-permute-start | bytes 393224 | tf_op jit(solution)/shard_map/ppermute | solution.py:420
  17.4 11.3 %collective-permute-done.10.refs_11_ = bf16[512,128]{1,0:T(8,128)(2,1)S(1)} collective-permute-done((bf16[512,128]{1,0:T(8,128)(2,1)}, bf16[512,128]{1,0:T(8,128)(2,1)S(1)}, u32[]{:S(2)}, u32[]{:S(2)}) %collective-permute-start.10) | collective-permute-done | bytes 131104 | tf_op jit(solution)/shard_map/ppermute | solution.py:420
  29.1 2.5 %collective-permute-start.3 = (bf16[512,128]{1,0:T(8,128)(2,1)}, bf16[512,128]{1,0:T(8,128)(2,1)S(1)}, u32[]{:S(2)}, u32[]{:S(2)}) collective-permute-start(bf16[512,128]{1,0:T(8,128)(2,1)} %get-tuple-element.43), channel_id=1, source_target_pairs={{0,8},{2,10},{4,12},{6,14},{8,0},{10,2},{12,4},{14,6},{16,24},{18,... | collective-permute-start | bytes 393224 | tf_op jit(solution)/shard_map/ppermute | solution.py:420
  31.6 2.5 %collective-permute-start.4 = (bf16[512,128]{1,0:T(8,128)(2,1)}, bf16[512,128]{1,0:T(8,128)(2,1)S(1)}, u32[]{:S(2)}, u32[]{:S(2)}) collective-permute-start(bf16[512,128]{1,0:T(8,128)(2,1)} %get-tuple-element.44), channel_id=1, source_target_pairs={{0,10},{2,8},{4,14},{6,12},{8,2},{10,0},{12,6},{14,4},{16,26},{18,... | collective-permute-start | bytes 393224 | tf_op jit(solution)/shard_map/ppermute | solution.py:420
  34.1 4.1 %collective-permute-start.5 = (bf16[512,128]{1,0:T(8,128)(2,1)}, bf16[512,128]{1,0:T(8,128)(2,1)S(1)}, u32[]{:S(2)}, u32[]{:S(2)}) collective-permute-start(bf16[512,128]{1,0:T(8,128)(2,1)} %get-tuple-element.45), channel_id=1, source_target_pairs={{0,12},{2,14},{4,8},{6,10},{8,4},{10,6},{12,0},{14,2},{16,28},{18,... | collective-permute-start | bytes 393224 | tf_op jit(solution)/shard_map/ppermute | solution.py:420
  38.2 2.4 %collective-permute-start.6 = (bf16[512,128]{1,0:T(8,128)(2,1)}, bf16[512,128]{1,0:T(8,128)(2,1)S(1)}, u32[]{:S(2)}, u32[]{:S(2)}) collective-permute-start(bf16[512,128]{1,0:T(8,128)(2,1)} %get-tuple-element.46), channel_id=1, source_target_pairs={{0,14},{2,12},{4,10},{6,8},{8,6},{10,4},{12,2},{14,0},{16,30},{18,... | collective-permute-start | bytes 393224 | tf_op jit(solution)/shard_map/ppermute | solution.py:420
  40.6 2.2 %collective-permute-start.7 = (bf16[512,128]{1,0:T(8,128)(2,1)}, bf16[512,128]{1,0:T(8,128)(2,1)S(1)}, u32[]{:S(2)}, u32[]{:S(2)}) collective-permute-start(bf16[512,128]{1,0:T(8,128)(2,1)} %get-tuple-element.47), channel_id=1, source_target_pairs={{0,16},{2,18},{4,20},{6,22},{8,24},{10,26},{12,28},{14,30},{16,0},... | collective-permute-start | bytes 393224 | tf_op jit(solution)/shard_map/ppermute | solution.py:420
  45.3 3.1 %collective-permute-done.7.refs_8_ = bf16[512,128]{1,0:T(8,128)(2,1)S(1)} collective-permute-done((bf16[512,128]{1,0:T(8,128)(2,1)}, bf16[512,128]{1,0:T(8,128)(2,1)S(1)}, u32[]{:S(2)}, u32[]{:S(2)}) %collective-permute-start.7) | collective-permute-done | bytes 131104 | tf_op jit(solution)/shard_map/ppermute | solution.py:420
  48.4 10.0 %collective-permute-done.8.refs_9_ = bf16[512,128]{1,0:T(8,128)(2,1)S(1)} collective-permute-done((bf16[512,128]{1,0:T(8,128)(2,1)}, bf16[512,128]{1,0:T(8,128)(2,1)S(1)}, u32[]{:S(2)}, u32[]{:S(2)}) %collective-permute-start.8) | collective-permute-done | bytes 131104 | tf_op jit(solution)/shard_map/ppermute | solution.py:420
  58.4 3.7 %collective-permute-done.9.refs_10_ = bf16[512,128]{1,0:T(8,128)(2,1)S(1)} collective-permute-done((bf16[512,128]{1,0:T(8,128)(2,1)}, bf16[512,128]{1,0:T(8,128)(2,1)S(1)}, u32[]{:S(2)}, u32[]{:S(2)}) %collective-permute-start.9) | collective-permute-done | bytes 131104 | tf_op jit(solution)/shard_map/ppermute | solution.py:420
  62.7 12.3 %head_attention.1 = (bf16[400,128]{1,0:T(8,128)(2,1)}, bf16[400,128]{1,0:T(8,128)(2,1)}, bf16[400,128]{1,0:T(8,128)(2,1)}, bf16[400,128]{1,0:T(8,128)(2,1)}, bf1...) custom-call(f32[16]{0:T(128)} %softness_ref.1, ...), custom_call_target="tpu_custom_call" | custom-call | flops 2684354560 | bytes 4194304 | tf_op jit(solution)/shard_map/head_attention/pallas_call | solution.py:571
  75.1 2.7 %collective-permute-start.24 = (bf16[400,128]{1,0:T(8,128)(2,1)}, bf16[400,128]{1,0:T(8,128)(2,1)S(1)}, u32[]{:S(2)}, u32[]{:S(2)}) collective-permute-start(bf16[400,128]{1,0:T(8,128)(2,1)} %get-tuple-element.65), channel_id=1, source_target_pairs={{0,20},{2,22},{4,16},{6,18},{8,28},{10,30},{12,24},{14,26},{16,4},... | collective-permute-start | bytes 307208 | tf_op jit(solution)/shard_map/ppermute | solution.py:420
  78.3 3.6 %collective-permute-start.26 = (bf16[400,128]{1,0:T(8,128)(2,1)}, bf16[400,128]{1,0:T(8,128)(2,1)S(1)}, u32[]{:S(2)}, u32[]{:S(2)}) collective-permute-start(bf16[400,128]{1,0:T(8,128)(2,1)} %get-tuple-element.67), channel_id=1, source_target_pairs={{0,24},{2,26},{4,28},{6,30},{8,16},{10,18},{12,20},{14,22},{16,8},... | collective-permute-start | bytes 307208 | tf_op jit(solution)/shard_map/ppermute | solution.py:420
  83.7 8.6 %collective-permute-done.23.refs_9_ = bf16[400,128]{1,0:T(8,128)(2,1)S(1)} collective-permute-done((bf16[400,128]{1,0:T(8,128)(2,1)}, bf16[400,128]{1,0:T(8,128)(2,1)S(1)}, u32[]{:S(2)}, u32[]{:S(2)}) %collective-permute-start.23) | collective-permute-done | bytes 102432 | tf_op jit(solution)/shard_map/ppermute | solution.py:420
  94.7 2.1 %collective-permute-start.29 = (bf16[400,128]{1,0:T(8,128)(2,1)}, bf16[400,128]{1,0:T(8,128)(2,1)S(1)}, u32[]{:S(2)}, u32[]{:S(2)}) collective-permute-start(bf16[400,128]{1,0:T(8,128)(2,1)} %get-tuple-element.70), channel_id=1, source_target_pairs={{0,30},{2,28},{4,26},{6,24},{8,22},{10,20},{12,18},{14,16},{16,14}... | collective-permute-start | bytes 307208 | tf_op jit(solution)/shard_map/ppermute | solution.py:420
  101.7 6.8 %collective-permute-start.18 = (bf16[400,128]{1,0:T(8,128)(2,1)}, bf16[400,128]{1,0:T(8,128)(2,1)S(1)}, u32[]{:S(2)}, u32[]{:S(2)}) collective-permute-start(bf16[400,128]{1,0:T(8,128)(2,1)} %get-tuple-element.59), channel_id=1, source_target_pairs={{0,8},{2,10},{4,12},{6,14},{8,0},{10,2},{12,4},{14,6},{16,24},{18,... | collective-permute-start | bytes 307208 | tf_op jit(solution)/shard_map/ppermute | solution.py:420
  121.2 2.2 %collective-permute-done.22.refs_8_ = bf16[400,128]{1,0:T(8,128)(2,1)S(1)} collective-permute-done((bf16[400,128]{1,0:T(8,128)(2,1)}, bf16[400,128]{1,0:T(8,128)(2,1)S(1)}, u32[]{:S(2)}, u32[]{:S(2)}) %collective-permute-start.22) | collective-permute-done | bytes 102432 | tf_op jit(solution)/shard_map/ppermute | solution.py:420
  124.1 10.1 %stack.67 = f32[16]{0:T(128)S(1)} concatenate(f32[1]{0:T(128)} %bitcast.1, f32[1]{0:T(128)} %bitcast.2, f32[1]{0:T(128)} %bitcast.3, f32[1]{0:T(128)} %bitcast.4, f32[1]{0:T(128)} %bitcast.5, f32[1]{0:T(128)} %bitcast.6, f32[1]{0:T(128)} %bitcast.7, f32[1]{0:T(128)} %bitcast.8, f32[1]{0:T(128)} %bitcast.9, f32[1]{0:T(128)} %bitcast.10, f32[1]{0:T(128)} %bitcast.11, f32[1]{0:T(128)} %bitcast.12, ...), dimensions={0} | concatenate | bytes 128 | tf_op jit(solution)/shard_map/stack | solution.py:613
  136.5 3.1 %unpack_heads.1 = (bf16[1,128,2048]{2,1,0:T(8,128)(2,1)}, bf16[1,128,2048]{2,1,0:T(8,128)(2,1)}, bf16[1,128,2048]{2,1,0:T(8,128)(2,1)}) custom-call(bf16[400,128]{1,0:T(8,128)(2,1)} %get-tuple-element.55.refs_0_, bf16[400,128]{1,0:T(8,128)(2,1)} %copy-done.7, bf16[400,128]{1,0:T(8,128)(2,1)} %copy-done.8, bf16[400,128]{1,0:T(8,128)(2,1)} %copy-done.9, ...), custom_call_target="tpu_custom_call" | custom-call | bytes 3145728 | tf_op jit(solution)/shard_map/unpack_heads/pallas_call | solution.py:436
  (123 shorter events, 31.0 us)
Async XLA Ops:
  4.0 8.9 %collective-permute-start = (bf16[512,128]{1,0:T(8,128)(2,1)}, bf16[512,128]{1,0:T(8,128)(2,1)S(1)}, u32[]{:S(2)}, u32[]{:S(2)}) collective-permute-start(bf16[512,128]{1,0:T(8,128)(2,1)} %get-tuple-element.40), channel_id=1, source_target_pairs={{0,2},{2,0},{4,6},{6,4},{8,10},{10,8},{12,14},{14,12},{16,18},{18,... | collective-permute-start | bytes 393224 | tf_op jit(solution)/shard_map/ppermute | solution.py:420
  4.5 10.7 %collective-permute-start.1 = (bf16[512,128]{1,0:T(8,128)(2,1)}, bf16[512,128]{1,0:T(8,128)(2,1)S(1)}, u32[]{:S(2)}, u32[]{:S(2)}) collective-permute-start(bf16[512,128]{1,0:T(8,128)(2,1)} %get-tuple-element.41), channel_id=1, source_target_pairs={{0,4},{2,6},{4,0},{6,2},{8,12},{10,14},{12,8},{14,10},{16,20},{18,... | collective-permute-start | bytes 393224 | tf_op jit(solution)/shard_map/ppermute | solution.py:420
  7.1 21.6 %collective-permute-start.10 = (bf16[512,128]{1,0:T(8,128)(2,1)}, bf16[512,128]{1,0:T(8,128)(2,1)S(1)}, u32[]{:S(2)}, u32[]{:S(2)}) collective-permute-start(bf16[512,128]{1,0:T(8,128)(2,1)} %get-tuple-element.50), channel_id=1, source_target_pairs={{0,22},{2,20},{4,18},{6,16},{8,30},{10,28},{12,26},{14,24},{16,6},... | collective-permute-start | bytes 393224 | tf_op jit(solution)/shard_map/ppermute | solution.py:420
  9.4 19.7 %collective-permute-start.11 = (bf16[512,128]{1,0:T(8,128)(2,1)}, bf16[512,128]{1,0:T(8,128)(2,1)S(1)}, u32[]{:S(2)}, u32[]{:S(2)}) collective-permute-start(bf16[512,128]{1,0:T(8,128)(2,1)} %get-tuple-element.51), channel_id=1, source_target_pairs={{0,24},{2,26},{4,28},{6,30},{8,16},{10,18},{12,20},{14,22},{16,8},... | collective-permute-start | bytes 393224 | tf_op jit(solution)/shard_map/ppermute | solution.py:420
  10.7 20.9 %collective-permute-start.12 = (bf16[512,128]{1,0:T(8,128)(2,1)}, bf16[512,128]{1,0:T(8,128)(2,1)S(1)}, u32[]{:S(2)}, u32[]{:S(2)}) collective-permute-start(bf16[512,128]{1,0:T(8,128)(2,1)} %get-tuple-element.52), channel_id=1, source_target_pairs={{0,26},{2,24},{4,30},{6,28},{8,18},{10,16},{12,22},{14,20},{16,10}... | collective-permute-start | bytes 393224 | tf_op jit(solution)/shard_map/ppermute | solution.py:420
  12.9 21.2 %collective-permute-start.13 = (bf16[512,128]{1,0:T(8,128)(2,1)}, bf16[512,128]{1,0:T(8,128)(2,1)S(1)}, u32[]{:S(2)}, u32[]{:S(2)}) collective-permute-start(bf16[512,128]{1,0:T(8,128)(2,1)} %get-tuple-element.53), channel_id=1, source_target_pairs={{0,28},{2,30},{4,24},{6,26},{8,20},{10,22},{12,16},{14,18},{16,12}... | collective-permute-start | bytes 393224 | tf_op jit(solution)/shard_map/ppermute | solution.py:420
  15.2 23.0 %collective-permute-start.14 = (bf16[512,128]{1,0:T(8,128)(2,1)}, bf16[512,128]{1,0:T(8,128)(2,1)S(1)}, u32[]{:S(2)}, u32[]{:S(2)}) collective-permute-start(bf16[512,128]{1,0:T(8,128)(2,1)} %get-tuple-element.54), channel_id=1, source_target_pairs={{0,30},{2,28},{4,26},{6,24},{8,22},{10,20},{12,18},{14,16},{16,14}... | collective-permute-start | bytes 393224 | tf_op jit(solution)/shard_map/ppermute | solution.py:420
  28.7 12.0 %collective-permute-start.2 = (bf16[512,128]{1,0:T(8,128)(2,1)}, bf16[512,128]{1,0:T(8,128)(2,1)S(1)}, u32[]{:S(2)}, u32[]{:S(2)}) collective-permute-start(bf16[512,128]{1,0:T(8,128)(2,1)} %get-tuple-element.42), channel_id=1, source_target_pairs={{0,6},{2,4},{4,2},{6,0},{8,14},{10,12},{12,10},{14,8},{16,22},{18,... | collective-permute-start | bytes 393224 | tf_op jit(solution)/shard_map/ppermute | solution.py:420
  29.1 13.7 %collective-permute-start.3 = (bf16[512,128]{1,0:T(8,128)(2,1)}, bf16[512,128]{1,0:T(8,128)(2,1)S(1)}, u32[]{:S(2)}, u32[]{:S(2)}) collective-permute-start(bf16[512,128]{1,0:T(8,128)(2,1)} %get-tuple-element.43), channel_id=1, source_target_pairs={{0,8},{2,10},{4,12},{6,14},{8,0},{10,2},{12,4},{14,6},{16,24},{18,... | collective-permute-start | bytes 393224 | tf_op jit(solution)/shard_map/ppermute | solution.py:420
  31.6 11.7 %collective-permute-start.4 = (bf16[512,128]{1,0:T(8,128)(2,1)}, bf16[512,128]{1,0:T(8,128)(2,1)S(1)}, u32[]{:S(2)}, u32[]{:S(2)}) collective-permute-start(bf16[512,128]{1,0:T(8,128)(2,1)} %get-tuple-element.44), channel_id=1, source_target_pairs={{0,10},{2,8},{4,14},{6,12},{8,2},{10,0},{12,6},{14,4},{16,26},{18,... | collective-permute-start | bytes 393224 | tf_op jit(solution)/shard_map/ppermute | solution.py:420
  34.1 11.1 %collective-permute-start.5 = (bf16[512,128]{1,0:T(8,128)(2,1)}, bf16[512,128]{1,0:T(8,128)(2,1)S(1)}, u32[]{:S(2)}, u32[]{:S(2)}) collective-permute-start(bf16[512,128]{1,0:T(8,128)(2,1)} %get-tuple-element.45), channel_id=1, source_target_pairs={{0,12},{2,14},{4,8},{6,10},{8,4},{10,6},{12,0},{14,2},{16,28},{18,... | collective-permute-start | bytes 393224 | tf_op jit(solution)/shard_map/ppermute | solution.py:420
  42.8 15.6 %collective-permute-start.8 = (bf16[512,128]{1,0:T(8,128)(2,1)}, bf16[512,128]{1,0:T(8,128)(2,1)S(1)}, u32[]{:S(2)}, u32[]{:S(2)}) collective-permute-start(bf16[512,128]{1,0:T(8,128)(2,1)} %get-tuple-element.48), channel_id=1, source_target_pairs={{0,18},{2,16},{4,22},{6,20},{8,26},{10,24},{12,30},{14,28},{16,2},... | collective-permute-start | bytes 393224 | tf_op jit(solution)/shard_map/ppermute | solution.py:420
  43.3 18.7 %collective-permute-start.9 = (bf16[512,128]{1,0:T(8,128)(2,1)}, bf16[512,128]{1,0:T(8,128)(2,1)S(1)}, u32[]{:S(2)}, u32[]{:S(2)}) collective-permute-start(bf16[512,128]{1,0:T(8,128)(2,1)} %get-tuple-element.49), channel_id=1, source_target_pairs={{0,20},{2,22},{4,16},{6,18},{8,28},{10,30},{12,24},{14,26},{16,4},... | collective-permute-start | bytes 393224 | tf_op jit(solution)/shard_map/ppermute | solution.py:420
  75.0 17.3 %collective-permute-start.23 = (bf16[400,128]{1,0:T(8,128)(2,1)}, bf16[400,128]{1,0:T(8,128)(2,1)S(1)}, u32[]{:S(2)}, u32[]{:S(2)}) collective-permute-start(bf16[400,128]{1,0:T(8,128)(2,1)} %get-tuple-element.64), channel_id=1, source_target_pairs={{0,18},{2,16},{4,22},{6,20},{8,26},{10,24},{12,30},{14,28},{16,2},... | collective-permute-start | bytes 307208 | tf_op jit(solution)/shard_map/ppermute | solution.py:420
  75.1 19.6 %collective-permute-start.24 = (bf16[400,128]{1,0:T(8,128)(2,1)}, bf16[400,128]{1,0:T(8,128)(2,1)S(1)}, u32[]{:S(2)}, u32[]{:S(2)}) collective-permute-start(bf16[400,128]{1,0:T(8,128)(2,1)} %get-tuple-element.65), channel_id=1, source_target_pairs={{0,20},{2,22},{4,16},{6,18},{8,28},{10,30},{12,24},{14,26},{16,4},... | collective-permute-start | bytes 307208 | tf_op jit(solution)/shard_map/ppermute | solution.py:420
  77.8 19.7 %collective-permute-start.25 = (bf16[400,128]{1,0:T(8,128)(2,1)}, bf16[400,128]{1,0:T(8,128)(2,1)S(1)}, u32[]{:S(2)}, u32[]{:S(2)}) collective-permute-start(bf16[400,128]{1,0:T(8,128)(2,1)} %get-tuple-element.66), channel_id=1, source_target_pairs={{0,22},{2,20},{4,18},{6,16},{8,30},{10,28},{12,26},{14,24},{16,6},... | collective-permute-start | bytes 307208 | tf_op jit(solution)/shard_map/ppermute | solution.py:420
  78.3 20.8 %collective-permute-start.26 = (bf16[400,128]{1,0:T(8,128)(2,1)}, bf16[400,128]{1,0:T(8,128)(2,1)S(1)}, u32[]{:S(2)}, u32[]{:S(2)}) collective-permute-start(bf16[400,128]{1,0:T(8,128)(2,1)} %get-tuple-element.67), channel_id=1, source_target_pairs={{0,24},{2,26},{4,28},{6,30},{8,16},{10,18},{12,20},{14,22},{16,8},... | collective-permute-start | bytes 307208 | tf_op jit(solution)/shard_map/ppermute | solution.py:420
  81.9 18.9 %collective-permute-start.27 = (bf16[400,128]{1,0:T(8,128)(2,1)}, bf16[400,128]{1,0:T(8,128)(2,1)S(1)}, u32[]{:S(2)}, u32[]{:S(2)}) collective-permute-start(bf16[400,128]{1,0:T(8,128)(2,1)} %get-tuple-element.68), channel_id=1, source_target_pairs={{0,26},{2,24},{4,30},{6,28},{8,18},{10,16},{12,22},{14,20},{16,10}... | collective-permute-start | bytes 307208 | tf_op jit(solution)/shard_map/ppermute | solution.py:420
  92.4 9.4 %collective-permute-start.28 = (bf16[400,128]{1,0:T(8,128)(2,1)}, bf16[400,128]{1,0:T(8,128)(2,1)S(1)}, u32[]{:S(2)}, u32[]{:S(2)}) collective-permute-start(bf16[400,128]{1,0:T(8,128)(2,1)} %get-tuple-element.69), channel_id=1, source_target_pairs={{0,28},{2,30},{4,24},{6,26},{8,20},{10,22},{12,16},{14,18},{16,12}... | collective-permute-start | bytes 307208 | tf_op jit(solution)/shard_map/ppermute | solution.py:420
  94.7 14.5 %collective-permute-start.29 = (bf16[400,128]{1,0:T(8,128)(2,1)}, bf16[400,128]{1,0:T(8,128)(2,1)S(1)}, u32[]{:S(2)}, u32[]{:S(2)}) collective-permute-start(bf16[400,128]{1,0:T(8,128)(2,1)} %get-tuple-element.70), channel_id=1, source_target_pairs={{0,30},{2,28},{4,26},{6,24},{8,22},{10,20},{12,18},{14,16},{16,14}... | collective-permute-start | bytes 307208 | tf_op jit(solution)/shard_map/ppermute | solution.py:420
  97.5 13.6 %collective-permute-start.15 = (bf16[400,128]{1,0:T(8,128)(2,1)}, bf16[400,128]{1,0:T(8,128)(2,1)S(1)}, u32[]{:S(2)}, u32[]{:S(2)}) collective-permute-start(bf16[400,128]{1,0:T(8,128)(2,1)} %get-tuple-element.56), channel_id=1, source_target_pairs={{0,2},{2,0},{4,6},{6,4},{8,10},{10,8},{12,14},{14,12},{16,18},{18,... | collective-permute-start | bytes 307208 | tf_op jit(solution)/shard_map/ppermute | solution.py:420
  99.1 13.5 %collective-permute-start.16 = (bf16[400,128]{1,0:T(8,128)(2,1)}, bf16[400,128]{1,0:T(8,128)(2,1)S(1)}, u32[]{:S(2)}, u32[]{:S(2)}) collective-permute-start(bf16[400,128]{1,0:T(8,128)(2,1)} %get-tuple-element.57), channel_id=1, source_target_pairs={{0,4},{2,6},{4,0},{6,2},{8,12},{10,14},{12,8},{14,10},{16,20},{18,... | collective-permute-start | bytes 307208 | tf_op jit(solution)/shard_map/ppermute | solution.py:420
  100.8 14.4 %collective-permute-start.17 = (bf16[400,128]{1,0:T(8,128)(2,1)}, bf16[400,128]{1,0:T(8,128)(2,1)S(1)}, u32[]{:S(2)}, u32[]{:S(2)}) collective-permute-start(bf16[400,128]{1,0:T(8,128)(2,1)} %get-tuple-element.58), channel_id=1, source_target_pairs={{0,6},{2,4},{4,2},{6,0},{8,14},{10,12},{12,10},{14,8},{16,22},{18,... | collective-permute-start | bytes 307208 | tf_op jit(solution)/shard_map/ppermute | solution.py:420
  101.7 14.0 %collective-permute-start.18 = (bf16[400,128]{1,0:T(8,128)(2,1)}, bf16[400,128]{1,0:T(8,128)(2,1)S(1)}, u32[]{:S(2)}, u32[]{:S(2)}) collective-permute-start(bf16[400,128]{1,0:T(8,128)(2,1)} %get-tuple-element.59), channel_id=1, source_target_pairs={{0,8},{2,10},{4,12},{6,14},{8,0},{10,2},{12,4},{14,6},{16,24},{18,... | collective-permute-start | bytes 307208 | tf_op jit(solution)/shard_map/ppermute | solution.py:420
  (37 other events, 816.6 us)

commit v3 on v1

--- a/solution.py
+++ b/solution.py
@@ -1,3 +1,4 @@
+import functools
 import math
 
 import jax
@@ -376,7 +377,8 @@
 
 TILE = 256
 EXTRA = 16
-VMEM_LIMIT = 56 * 1024 * 1024
+PACK_VMEM = 10 * 1024 * 1024
+HEAD_VMEM = 31 * 1024 * 1024
 
 
 def pack_kernel(*refs):
@@ -397,7 +399,7 @@
         cost_estimate=pl.CostEstimate(
             flops=0, bytes_accessed=4 * math.prod(out_shape), transcendentals=0
         ),
-        compiler_params=pltpu.CompilerParams(vmem_limit_bytes=VMEM_LIMIT),
+        compiler_params=pltpu.CompilerParams(vmem_limit_bytes=PACK_VMEM),
         name="pack_heads",
     )(*arrays)
 
@@ -419,7 +421,7 @@
         cost_estimate=pl.CostEstimate(
             flops=0, bytes_accessed=4 * count * math.prod(out_shape), transcendentals=0
         ),
-        compiler_params=pltpu.CompilerParams(vmem_limit_bytes=VMEM_LIMIT),
+        compiler_params=pltpu.CompilerParams(vmem_limit_bytes=PACK_VMEM),
         name="unpack_heads",
     )(array_in)
 
@@ -447,7 +449,7 @@
                 least = jnp.where(same, -BLK, BLK - width)
                 piece = jnp.where(spread > least, piece, blocked_score)
             else:
-                piece = jnp.where(spread > jnp.where(same, -BLK, BLK), piece, blocked_score)
+                piece = piece + jnp.where(same, 0.0, blocked_score)
             pieces.append(piece)
         rows.append(jnp.concatenate(pieces, axis=1))
     return jnp.concatenate(rows, axis=0)
@@ -572,7 +574,7 @@
             bytes_accessed=2 * (math.prod(out_shape) + math.prod(arrived.shape)),
             transcendentals=length * length // 2,
         ),
-        compiler_params=pltpu.CompilerParams(vmem_limit_bytes=VMEM_LIMIT),
+        compiler_params=pltpu.CompilerParams(vmem_limit_bytes=HEAD_VMEM),
         name="head_attention",
     )(softness, ids, span, arrived)
 

time: 121 us -> 119 us (0.983)
  Pallas kernels: 18.4 us -> 11.9 us
  local copies, waits for them, and re-layouts: 0.01 us -> 4.18 us
    unnamed x2 -> x14, local copies, waits for them, and re-layouts: 0.01 us -> 4.18 us
    pallas_call x1, Pallas kernels: 3.18 us -> 0.36 us  [packed(): pl.pallas_call(pack_kernel, out_shape=jax.ShapeDtypeStruct(out_shape, jnp...]
    pallas_call x1, Pallas kernels: 12.2 us -> 9.99 us  [attention(): pl.pallas_call(attention_kernel, out_shape=jax.ShapeDtypeStruct(out_shape...]
    pallas_call x1, Pallas kernels: 2.98 us -> 1.55 us  [unpacked(): pl.pallas_call(unpack_kernel, out_shape=[jax.ShapeDtypeStruct(out_shape,...]
  transfers between devices with their start and end apart: 1 -> 1, of which waited for: 0 -> 1; matrix products, arithmetic and copies ran while one was open for 0% -> 0% of each run, Pallas kernels for 2% -> 1%
where the time goes in v3:
time: 119 us
  blocking collectives  99.3 us (83%)
  Pallas kernels  11.9 us (10%)
  local copies, waits for them, and re-layouts  4.18 us (4%)
  starting transfers between devices  1.54 us (1%)
    all_to_all x1, blocking collectives, head_shards(): lax.all_to_all(sent, 'seq', split_axis=0, concat_axis=0, tiled=True)  54.6 us
    all_to_all x1, blocking collectives, head_shards(): back = lax.all_to_all(owned, 'seq', split_axis=0, concat_axis=0, tiled=True)  44.7 us
    pallas_call x1, Pallas kernels, attention(): pl.pallas_call(attention_kernel, out_shape=jax.ShapeDtypeStruct(out_shape...  9.99 us
    unnamed x14, local copies, waits for them, and re-layouts  4.18 us
  transfers between devices with their start and end apart: 1, of which 1 were waited for; matrix products, arithmetic and copies ran while one was open for 0% of the time, Pallas kernels for 1%

profile of v3, /device:TPU:0, one launch (start us, length us, event | category | flops | bytes accessed | tf_op | source)
XLA Modules:
  0.0 118.8 jit_solution(6428229485661693088)
XLA Ops:
  0.6 0.0 copy-start
  0.6 1.0 copy-done
  1.7 0.0 copy-start.1
  1.7 1.0 copy-done.1
  2.7 0.0 copy-start.2
  2.7 1.0 copy-done.2
  3.8 0.0 copy-start.3
  3.8 1.0 copy-done.3
  4.8 0.4 pack_heads.1
  5.2 0.0 copy-start.4
  5.2 0.0 copy-start.5
  5.2 0.0 copy-start.6
  5.2 54.6 %all_to_all.10.in_ref = bf16[16,512,128]{2,1,0:T(8,128)(2,1)S(1)} all-to-all(bf16[16,512,128]{2,1,0:T(8,128)(2,1)S(1)} %pack_heads.1), channel_id=1, replica_groups=mesh['seq'=16,'dp'=2] {'seq'}, dimensions={0} | all-to-all | bytes 4194304 | tf_op jit(solution)/shard_map/all_to_all | solution.py:594
  59.8 0.0 copy-done.4
  59.8 0.0 copy-done.5
  59.8 0.0 copy-done.6
  59.8 10.0 %head_attention.1 = bf16[16,400,128]{2,1,0:T(8,128)(2,1)S(1)} custom-call(f32[16]{0:T(128)S(1)} %copy-done.5, s32[16,16]{1,0:T(8,128)S(1)} %bitcast.1, s32[16]{0:T(128)S(1)} %copy-done.6, bf16[16,512,128]{2,1,0:T(8,128)(2,1)S(1)} %all_to_all.10.in_ref), custom_call_target="tpu_custom_call" | custom-call | flops 2684354560 | bytes 3735552 | tf_op jit(solution)/shard_map/head_attention/pallas_call | solution.py:556
  69.8 44.7 %all_to_all.11.packed_ref = bf16[16,400,128]{2,1,0:T(8,128)(2,1)S(1)} all-to-all(bf16[16,400,128]{2,1,0:T(8,128)(2,1)S(1)} %head_attention.1), channel_id=1, replica_groups=mesh['seq'=16,'dp'=2] {'seq'}, dimensions={0} | all-to-all | bytes 3276800 | tf_op jit(solution)/shard_map/all_to_all | solution.py:596
  114.5 0.2 convert_reduce_fusion
  114.7 1.5 %collective-permute-start = (f32[16]{0:T(128)S(1)}, f32[16]{0:T(128)S(1)}, u32[]{:S(2)}, u32[]{:S(2)}) collective-permute-start(f32[16]{0:T(128)S(1)} %convert_reduce_fusion), channel_id=1, source_target_pairs={{0,1},{1,0},{2,3},{3,2},{4,5},{5,4},{6,7},{7,6},{8,9},{9,8},{10,11... | collective-permute-start | bytes 200 | tf_op jit(solution)/shard_map/ppermute | solution.py:602
  116.3 1.5 %unpack_heads.1 = (bf16[1,128,2048]{2,1,0:T(8,128)(2,1)}, bf16[1,128,2048]{2,1,0:T(8,128)(2,1)}, bf16[1,128,2048]{2,1,0:T(8,128)(2,1)}) custom-call(bf16[16,400,128]{2,1,0:T(8,128)(2,1)S(1)} %all_to_all.11.packed_ref), custom_call_target="tpu_custom_call" | custom-call | bytes 3145728 | tf_op jit(solution)/shard_map/unpack_heads/pallas_call | solution.py:418
  117.8 0.5 collective-permute-done
  118.3 0.5 add_multiply_fusion
Async XLA Ops:
  0.6 1.0 copy-start
  1.7 1.0 copy-start.1
  2.7 1.0 copy-start.2
  3.8 1.0 copy-start.3
  5.2 54.7 %copy-start.4 = (s32[1,16,16,1]{2,3,1,0:T(1,128)S(1)}, s32[1,16,16,1]{2,3,1,0:T(1,128)}, u32[]{:S(2)}) copy-start(s32[1,16,16,1]{2,3,1,0:T(1,128)} %param.12) | copy-start | bytes 3076
  5.2 54.7 %copy-start.5 = (f32[16]{0:T(128)S(1)}, f32[16]{0:T(128)}, u32[]{:S(2)}) copy-start(f32[16]{0:T(128)} %softness_ref.1) | copy-start | bytes 196
  5.2 54.7 %copy-start.6 = (s32[16]{0:T(128)S(1)}, s32[16]{0:T(128)}, u32[]{:S(2)}) copy-start(s32[16]{0:T(128)} %span_ref.1) | copy-start | bytes 196
  114.7 3.6 %collective-permute-start = (f32[16]{0:T(128)S(1)}, f32[16]{0:T(128)S(1)}, u32[]{:S(2)}, u32[]{:S(2)}) collective-permute-start(f32[16]{0:T(128)S(1)} %convert_reduce_fusion), channel_id=1, source_target_pairs={{0,1},{1,0},{2,3},{3,2},{4,5},{5,4},{6,7},{7,6},{8,9},{9,8},{10,11... | collective-permute-start | bytes 200 | tf_op jit(solution)/shard_map/ppermute | solution.py:602

commit v4 on v0

--- a/solution.py
+++ b/solution.py
@@ -1,8 +1,11 @@
+import functools
 import math
 
 import jax
 import jax.numpy as jnp
 from jax import lax
+from jax.experimental import pallas as pl
+from jax.experimental.pallas import tpu as pltpu
 from jax.sharding import PartitionSpec as P
 
 HD = 128
@@ -193,7 +196,7 @@
     )
 
 
-def shards(
+def clustered_shards(
     probe_vectors,
     lookup_vectors,
     content_vectors,
@@ -372,6 +375,538 @@
     return (token_major(query_out), token_major(key_out), token_major(value_out), temper_grad)
 
 
+TILE = 256
+EXTRA = 16
+MIB = 1024 * 1024
+QUERY, KEY, VALUE, GRAD = range(4)
+
+
+def columns_of(index):
+    return pl.ds(pl.multiple_of(index * HD, HD), HD)
+
+
+def rows_of(index):
+    return pl.ds(pl.multiple_of(index * BLK, BLK), BLK)
+
+
+def tile_rows(tile):
+    return slice(tile * TILE, (tile + 1) * TILE)
+
+
+def position(half_count):
+    me = lax.axis_index("seq")
+    half = jnp.where(me >= half_count, 1, 0)
+    return me, half, me - half * half_count
+
+
+def kernel_call(kernel, name, operands, in_specs, out_shape, scratch, vmem_mib, flops=0):
+    bytes_accessed = sum(
+        math.prod(item.shape) * item.dtype.itemsize for item in (*operands, *out_shape)
+    )
+    return pl.pallas_call(
+        kernel,
+        out_shape=out_shape,
+        in_specs=in_specs,
+        out_specs=[pl.BlockSpec(memory_space=pltpu.VMEM)] * len(out_shape),
+        scratch_shapes=scratch,
+        cost_estimate=pl.CostEstimate(
+            flops=flops, bytes_accessed=bytes_accessed, transcendentals=0
+        ),
+        compiler_params=pltpu.CompilerParams(vmem_limit_bytes=vmem_mib * MIB),
+        name=name,
+    )(*operands)
+
+
+def pack_kernel(*refs, half_count):
+    arrays, within_ref, across_refs = refs[:4], refs[4], refs[5 : 5 + half_count]
+    held, arrival = refs[5 + half_count :]
+    me, half, _ = position(half_count)
+    copies = [
+        pltpu.make_async_copy(array_ref.at[0], held.at[place], arrival.at[place])
+        for place, array_ref in enumerate(arrays)
+    ]
+    for copy in copies:
+        copy.start()
+    for place, copy in enumerate(copies):
+        copy.wait()
+        for peer in range(half_count):
+            for slot, base in enumerate((half * half_count, (1 - half) * half_count)):
+                start = (slot * 4 + place) * BLK
+                within_ref[peer, start : start + BLK, :] = held[
+                    place, :, columns_of(base + peer)
+                ]
+    first = jnp.where(half == 0, KEY, QUERY)
+    second = jnp.where(half == 0, VALUE, GRAD)
+    for step, across_ref in enumerate(across_refs):
+        columns = columns_of(me ^ (half_count + step))
+        across_ref[:BLK, :] = held[first, :, columns]
+        across_ref[BLK:, :] = held[second, :, columns]
+
+
+def packed(arrays, half_count):
+    width = arrays[0].shape[2]
+    return kernel_call(
+        functools.partial(pack_kernel, half_count=half_count),
+        "pack_heads",
+        arrays,
+        [pl.BlockSpec(memory_space=pltpu.HBM)] * 4,
+        [jax.ShapeDtypeStruct((half_count, 8 * BLK, HD), jnp.bfloat16)]
+        + [jax.ShapeDtypeStruct((2 * BLK, HD), jnp.bfloat16)] * half_count,
+        [pltpu.VMEM((4, BLK, width), jnp.bfloat16), pltpu.SemaphoreType.DMA((4,))],
+        10,
+    )
+
+
+def dot_rows(left, right):
+    return lax.dot_general(
+        left, right, (((1,), (1,)), ((), ())), preferred_element_type=jnp.float32
+    )
+
+
+def dot_plain(left, right):
+    return lax.dot_general(
+        left, right, (((1,), (0,)), ((), ())), preferred_element_type=jnp.float32
+    )
+
+
+class Region:
+    def __init__(self, head, settings, square, key_base, query_base, arrays, places):
+        softness_ref, self.ids_ref, span_ref = settings
+        self.head, self.square = head, square
+        self.key_base, self.query_base = key_base, query_base
+        self.arrays, self.places = arrays, places
+        self.tiles = arrays.shape[1] // TILE
+        self.width = span_ref[head]
+        self.scaling = softness_ref[head] * (1.0 / math.sqrt(HD))
+        self.to_log2 = self.scaling * math.log2(math.e)
+
+    def rows(self, which, start, stop):
+        return self.arrays[self.places[which], start * TILE : stop * TILE, :]
+
+    def keys_of(self, tile):
+        return range(self.tiles if self.square else tile + 1)
+
+    def scores(self, tile_key, tile_query):
+        per_tile = TILE // BLK
+        scores = (
+            dot_rows(
+                self.rows(KEY, tile_key, tile_key + 1), self.rows(QUERY, tile_query, tile_query + 1)
+            )
+            * self.to_log2
+        )
+        spread = lax.broadcasted_iota(jnp.int32, (BLK, BLK), 0) - lax.broadcasted_iota(
+            jnp.int32, (BLK, BLK), 1
+        )
+        rows = []
+        for sub_key in range(per_tile):
+            pieces = []
+            for sub_query in range(per_tile):
+                piece = scores[
+                    sub_key * BLK : (sub_key + 1) * BLK, sub_query * BLK : (sub_query + 1) * BLK
+                ]
+                key_block = tile_key * per_tile + sub_key
+                query_block = tile_query * per_tile + sub_query
+                apart = query_block - key_block
+                if self.square:
+                    apart += self.tiles * per_tile
+                same = (
+                    self.ids_ref[self.head, self.key_base + key_block]
+                    == self.ids_ref[self.head, self.query_base + query_block]
+                )
+                if apart < 0:
+                    piece = jnp.full_like(piece, blocked_score)
+                elif apart == 0:
+                    piece = jnp.where(spread <= 0, piece, blocked_score)
+                elif apart == 1:
+                    least = jnp.where(same, -BLK, BLK - self.width)
+                    piece = jnp.where(spread > least, piece, blocked_score)
+                else:
+                    piece = piece + jnp.where(same, 0.0, blocked_score)
+                pieces.append(piece)
+            rows.append(jnp.concatenate(pieces, axis=1))
+        return jnp.concatenate(rows, axis=0)
+
+    def statistics(self, score, out_ref, first_row):
+        for tile in range(self.tiles):
+            here = tile_rows(tile)
+            top = jnp.full((1, TILE), blocked_score, jnp.float32)
+            for other in self.keys_of(tile):
+                raw = self.scores(other, tile)
+                score[tile_rows(other), :] = raw
+                top = jnp.maximum(top, jnp.max(raw, axis=0, keepdims=True))
+            total = jnp.zeros((1, TILE), jnp.float32)
+            mass = jnp.zeros((1, TILE), jnp.float32)
+            for other in self.keys_of(tile):
+                weight = jnp.exp2(score[tile_rows(other), :] - top)
+                towards = dot_rows(
+                    self.rows(VALUE, other, other + 1), self.rows(GRAD, tile, tile + 1)
+                )
+                total += jnp.sum(weight, axis=0, keepdims=True)
+                mass += jnp.sum(weight * towards, axis=0, keepdims=True)
+            out_ref[first_row : first_row + 1, here] = top
+            out_ref[first_row + 1 : first_row + 2, here] = total
+            out_ref[first_row + 2 : first_row + 3, here] = mass
+
+    def gradients(self, log_total, delta, prob_low, grad_low, keys_flat):
+        keys_flat[...] = self.rows(KEY, 0, self.tiles).T
+        temper = jnp.zeros((1, HD), jnp.float32)
+        query_parts, key_parts, value_parts = [], [], []
+        for tile in range(self.tiles):
+            here = tile_rows(tile)
+            for other in self.keys_of(tile):
+                there = tile_rows(other)
+                probability = jnp.exp2(self.scores(other, tile) - log_total[:, here])
+                towards = dot_rows(
+                    self.rows(VALUE, other, other + 1), self.rows(GRAD, tile, tile + 1)
+                )
+                prob_low[there, here] = probability.astype(jnp.bfloat16)
+                grad_low[there, here] = (probability * (towards - delta[:, here])).astype(
+                    jnp.bfloat16
+                )
+            upto = slice(0, len(self.keys_of(tile)) * TILE)
+            query_part = dot_plain(keys_flat[:, upto], grad_low[upto, here]).T
+            temper += jnp.sum(
+                query_part * self.rows(QUERY, tile, tile + 1).astype(jnp.float32),
+                axis=0,
+                keepdims=True,
+            )
+            query_parts.append(query_part)
+        for tile in range(self.tiles):
+            first = 0 if self.square else tile
+            onward = slice(first * TILE, self.tiles * TILE)
+            here = tile_rows(tile)
+            key_parts.append(
+                dot_plain(grad_low[here, onward], self.rows(QUERY, first, self.tiles))
+            )
+            value_parts.append(
+                dot_plain(prob_low[here, onward], self.rows(GRAD, first, self.tiles))
+            )
+        return query_parts, key_parts, value_parts, temper
+
+
+def merged(first, second):
+    top = jnp.maximum(first[0], second[0])
+    left, right = jnp.exp2(first[0] - top), jnp.exp2(second[0] - top)
+    total = first[1] * left + second[1] * right
+    mass = first[2] * left + second[2] * right
+    return top + jnp.log2(total), mass / total
+
+
+def alone(rows):
+    return rows[0] + jnp.log2(rows[1]), rows[2] / rows[1]
+
+
+def three_rows(ref, first):
+    return [ref[first + row : first + row + 1, :] for row in range(3)]
+
+
+def within_kernel(softness_ref, ids_ref, span_ref, in_ref, arrays_ref, stats_ref, score, *, half_count):
+    me, half, _ = position(half_count)
+    for block in range(half_count):
+        for place in range(8):
+            arrays_ref[place, block * BLK : (block + 1) * BLK, :] = in_ref[
+                block, place * BLK : (place + 1) * BLK, :
+            ]
+    base = half * half_count
+    settings = (softness_ref, ids_ref, span_ref)
+    for slot, head in enumerate((me, me ^ half_count)):
+        places = [slot * 4 + place for place in range(4)]
+        region = Region(head, settings, False, base, base, arrays_ref, places)
+        region.statistics(score, stats_ref, slot * 3)
+
+
+def square_region(head, settings, half_count, square_ref):
+    return Region(head, settings, True, 0, half_count, square_ref, range(4))
+
+
+def square_kernel(
+    softness_ref, ids_ref, span_ref, arrays_ref, stats_ref, *refs, half_count
+):
+    across_refs = refs[:half_count]
+    square_ref, message_ref, own_ref, score, square_stats = refs[half_count:]
+    me, half, place = position(half_count)
+    first = jnp.where(half == 0, QUERY, KEY)
+    second = jnp.where(half == 0, GRAD, VALUE)
+    for step, across_ref in enumerate(across_refs):
+        rows = rows_of(place ^ step)
+        square_ref[first, rows, :] = across_ref[:BLK, :]
+        square_ref[second, rows, :] = across_ref[BLK:, :]
+    kept_first = jnp.where(half == 0, KEY, QUERY)
+    kept_second = jnp.where(half == 0, VALUE, GRAD)
+    square_ref[kept_first, :, :] = arrays_ref[kept_first, :, :]
+    square_ref[kept_second, :, :] = arrays_ref[kept_second, :, :]
+    region = square_region(me, (softness_ref, ids_ref, span_ref), half_count, square_ref)
+    region.statistics(score, square_stats, 0)
+    for row in range(3):
+        message_ref[row : row + 1, :] = jnp.where(
+            half == 0, square_stats[row : row + 1, :], stats_ref[3 + row : 4 + row, :]
+        )
+    diagonal = three_rows(stats_ref, 0)
+    whole, single = merged(diagonal, three_rows(square_stats, 0)), alone(diagonal)
+    for row in range(2):
+        own_ref[row : row + 1, :] = jnp.where(half == 0, single[row], whole[row])
+
+
+def diagonal_kernel(
+    softness_ref, ids_ref, span_ref, arrays_ref, own_ref, parts_ref, temper_ref,
+    prob_low, grad_low, keys_flat, *, half_count
+):
+    me, half, _ = position(half_count)
+    base = half * half_count
+    settings = (softness_ref, ids_ref, span_ref)
+    region = Region(me, settings, False, base, base, arrays_ref, range(4))
+    *parts, temper = region.gradients(
+        own_ref[0:1, :], own_ref[1:2, :], prob_low, grad_low, keys_flat
+    )
+    for place, tiles in enumerate(parts):
+        for tile, value in enumerate(tiles):
+            parts_ref[place, tile_rows(tile), :] = value
+    temper_ref[...] = jnp.broadcast_to(temper, temper_ref.shape)
+
+
+def temper_rows(own, other):
+    row = lax.broadcasted_iota(jnp.int32, (EXTRA, HD), 0)
+    rows = jnp.zeros((EXTRA, HD), jnp.float32)
+    for place, terms in enumerate((own, other)):
+        rest = jnp.broadcast_to(jnp.sum(terms, axis=1, keepdims=True), (EXTRA, HD)) * (
+            1.0 / math.sqrt(HD)
+        )
+        for piece in range(3):
+            high = rest.astype(jnp.bfloat16).astype(jnp.float32)
+            rows = jnp.where(row == place * 3 + piece, high, rows)
+            rest = rest - high
+    return rows.astype(jnp.bfloat16)
+
+
+def finish_kernel(
+    softness_ref, ids_ref, span_ref, arrays_ref, square_ref, message_ref, received_ref,
+    own_ref, stats_ref, parts_ref, temper_ref, within_ref, *refs, half_count
+):
+    across_refs = refs[:half_count]
+    across, prob_low, grad_low, keys_flat = refs[half_count:]
+    me, half, place = position(half_count)
+    base = half * half_count
+    settings = (softness_ref, ids_ref, span_ref)
+    per_tile = TILE // BLK
+
+    def put(array, tile, value):
+        for sub in range(per_tile):
+            within_ref[tile * per_tile + sub, array * BLK : (array + 1) * BLK, :] = value[
+                sub * BLK : (sub + 1) * BLK, :
+            ]
+
+    met = merged(three_rows(message_ref, 0), three_rows(received_ref, 0))
+    log_total = jnp.where(half == 0, met[0], own_ref[0:1, :])
+    delta = jnp.where(half == 0, met[1], own_ref[1:2, :])
+    region = square_region(me, settings, half_count, square_ref)
+    *square_parts, own_temper = region.gradients(log_total, delta, prob_low, grad_low, keys_flat)
+    scales = (region.scaling, region.scaling, 1.0)
+    for tile in range(region.tiles):
+        query_part, key_part, value_part = [
+            part[tile] * scale for part, scale in zip(square_parts, scales)
+        ]
+        here = tile_rows(tile)
+        across[0, here, :] = jnp.where(half == 0, query_part, key_part).astype(jnp.bfloat16)
+        across[1, here, :] = jnp.where(half == 0, 0.0, value_part).astype(jnp.bfloat16)
+        query_kept, key_kept, value_kept = [
+            parts_ref[array, here, :] * scale for array, scale in enumerate(scales)
+        ]
+        put(0, tile, (query_kept + jnp.where(half == 0, 0.0, query_part)).astype(jnp.bfloat16))
+        put(1, tile, (key_kept + jnp.where(half == 0, key_part, 0.0)).astype(jnp.bfloat16))
+        put(2, tile, (value_kept + jnp.where(half == 0, value_part, 0.0)).astype(jnp.bfloat16))
+    single = alone(three_rows(stats_ref, 3))
+    log_total = jnp.where(half == 0, single[0], met[0])
+    delta = jnp.where(half == 0, single[1], met[1])
+    region = Region(
+        me ^ half_count, settings, False, base, base, arrays_ref, range(4, 8)
+    )
+    *other_parts, other_temper = region.gradients(log_total, delta, prob_low, grad_low, keys_flat)
+    scales = (region.scaling, region.scaling, 1.0)
+    for tile in range(region.tiles):
+        for array, (part, scale) in enumerate(zip(other_parts, scales)):
+            put(3 + array, tile, (part[tile] * scale).astype(jnp.bfloat16))
+    pieces = temper_rows(own_temper + temper_ref[0:1, :], other_temper)
+    for block in range(half_count):
+        within_ref[block, 6 * BLK : 6 * BLK + EXTRA, :] = pieces
+    for step, across_ref in enumerate(across_refs):
+        rows = rows_of(place ^ step)
+        across_ref[:BLK, :] = across[0, rows, :]
+        across_ref[BLK : 2 * BLK, :] = across[1, rows, :]
+        across_ref[2 * BLK :, :] = pieces
+
+
+def unpack_kernel(within_ref, *refs, half_count):
+    across_refs = refs[:half_count]
+    query_ref, key_ref, value_ref, temper_ref = refs[half_count:]
+    me, half, place = position(half_count)
+
+    def sums(rows):
+        return [
+            jnp.sum(rows[3 * slot : 3 * slot + 3, :].astype(jnp.float32), axis=0, keepdims=True)
+            for slot in range(2)
+        ]
+
+    for step, across_ref in enumerate(across_refs):
+        peer = place ^ step
+        other = columns_of((1 - half) * half_count + peer)
+        own = columns_of(half * half_count + peer)
+        parts = [within_ref[peer, array * BLK : (array + 1) * BLK, :] for array in range(6)]
+        for array, out_ref in enumerate((query_ref, key_ref, value_ref)):
+            out_ref[0, :, own] = parts[array]
+        first = across_ref[:BLK, :].astype(jnp.float32)
+        second = across_ref[BLK : 2 * BLK, :].astype(jnp.float32)
+        added = (
+            jnp.where(half == 0, 0.0, first),
+            jnp.where(half == 0, first, 0.0),
+            jnp.where(half == 0, second, 0.0),
+        )
+        for array, out_ref in enumerate((query_ref, key_ref, value_ref)):
+            out_ref[0, :, other] = (parts[3 + array].astype(jnp.float32) + added[array]).astype(
+                jnp.bfloat16
+            )
+        near = sums(within_ref[peer, 6 * BLK : 6 * BLK + EXTRA, :])
+        far = sums(across_ref[2 * BLK :, :])
+        temper_ref[pl.ds(half * half_count + peer, 1), :] = near[0] + far[1]
+        temper_ref[pl.ds((1 - half) * half_count + peer, 1), :] = near[1] + far[0]
+
+
+def crossed(chunks, half_count):
+    pairs = range(2 * half_count)
+    return [
+        lax.ppermute(chunk, "seq", [(source, source ^ (half_count + step)) for source in pairs])
+        for step, chunk in enumerate(chunks)
+    ]
+
+
+def head_shards(
+    probe_vectors,
+    lookup_vectors,
+    content_vectors,
+    result_cotangent,
+    logit_softness,
+    block_grouping,
+    neighborhood_span,
+):
+    seq_count, dp_count = lax.axis_size("seq"), lax.axis_size("dp")
+    half_count = seq_count // 2
+    tokens = half_count * BLK
+    groups = [list(range(half_count)), list(range(half_count, seq_count))]
+    settings = (logit_softness, block_grouping[0, :, :, 0], neighborhood_span)
+    smem, vmem = pl.BlockSpec(memory_space=pltpu.SMEM), pl.BlockSpec(memory_space=pltpu.VMEM)
+    score = pltpu.VMEM((tokens, TILE), jnp.float32)
+    lows = [pltpu.VMEM((tokens, tokens), jnp.bfloat16)] * 2 + [
+        pltpu.VMEM((HD, tokens), jnp.bfloat16)
+    ]
+    rows_of_stats = jax.ShapeDtypeStruct((8, tokens), jnp.float32)
+    pair_flops = 2 * tokens * tokens * HD
+
+    def exchange_within(array_in):
+        return lax.all_to_all(
+            array_in, "seq", split_axis=0, concat_axis=0, axis_index_groups=groups, tiled=True
+        )
+
+    def call(kernel, name, operands, out_shape, scratch, flops):
+        return kernel_call(
+            functools.partial(kernel, half_count=half_count),
+            name,
+            (*settings, *operands),
+            [smem] * 3 + [vmem] * len(operands),
+            out_shape,
+            scratch,
+            20,
+            flops,
+        )
+
+    sent, *foreign = packed(
+        (probe_vectors, lookup_vectors, content_vectors, result_cotangent), half_count
+    )
+    arrived = exchange_within(sent)
+    foreign = crossed(foreign, half_count)
+    arrays, stats = call(
+        within_kernel,
+        "diagonal_statistics",
+        (arrived,),
+        [jax.ShapeDtypeStruct((8, tokens, HD), jnp.bfloat16), rows_of_stats],
+        [score],
+        2 * pair_flops,
+    )
+    square, message, own = call(
+        square_kernel,
+        "square_statistics",
+        (arrays, stats, *foreign),
+        [jax.ShapeDtypeStruct((4, tokens, HD), jnp.bfloat16), rows_of_stats, rows_of_stats],
+        [score, pltpu.VMEM((8, tokens), jnp.float32)],
+        2 * pair_flops,
+    )
+    swap = [(source, source ^ half_count) for source in range(seq_count)]
+    received = lax.ppermute(message, "seq", swap)
+    parts, temper = call(
+        diagonal_kernel,
+        "own_diagonal_gradients",
+        (arrays, own),
+        [
+            jax.ShapeDtypeStruct((3, tokens, HD), jnp.float32),
+            jax.ShapeDtypeStruct((8, HD), jnp.float32),
+        ],
+        lows,
+        5 * pair_flops // 2,
+    )
+    within, *across = call(
+        finish_kernel,
+        "remaining_gradients",
+        (arrays, square, message, received, own, stats, parts, temper),
+        [jax.ShapeDtypeStruct((half_count, 6 * BLK + EXTRA, HD), jnp.bfloat16)]
+        + [jax.ShapeDtypeStruct((2 * BLK + EXTRA, HD), jnp.bfloat16)] * half_count,
+        [pltpu.VMEM((2, tokens, HD), jnp.bfloat16), *lows],
+        8 * pair_flops,
+    )
+    across = crossed(across, half_count)
+    within = exchange_within(within)
+    result = jax.ShapeDtypeStruct(probe_vectors.shape, jnp.bfloat16)
+    *outs, tempers = kernel_call(
+        functools.partial(unpack_kernel, half_count=half_count),
+        "unpack_heads",
+        (within, *across),
+        [vmem] * (1 + half_count),
+        [result] * 3 + [jax.ShapeDtypeStruct((seq_count, HD), jnp.float32)],
+        [],
+        10,
+    )
+    temper_total = tempers
+    for step in range(1, dp_count):
+        pairs = [(source, (source + step) % dp_count) for source in range(dp_count)]
+        temper_total = temper_total + lax.ppermute(tempers, "dp", pairs)
+    return (*outs, temper_total[:, 0] / (dp_count * BLK * seq_count))
+
+
+def shards(
+    probe_vectors,
+    lookup_vectors,
+    content_vectors,
+    result_cotangent,
+    logit_softness,
+    block_grouping,
+    neighborhood_span,
+):
+    head_count = probe_vectors.shape[2] // HD
+    seq_count = lax.axis_size("seq")
+    one_block = probe_vectors.shape[1] == BLK
+    whole_tiles = seq_count * BLK % (2 * TILE) == 0 and seq_count & (seq_count - 1) == 0
+    if head_count == seq_count and one_block and whole_tiles:
+        plan = head_shards
+    else:
+        plan = clustered_shards
+    return plan(
+        probe_vectors,
+        lookup_vectors,
+        content_vectors,
+        result_cotangent,
+        logit_softness,
+        block_grouping,
+        neighborhood_span,
+    )
+
+
 def solution(mesh):
     in_specs = (
         P("dp", "seq", None),

time: 409 us -> 114 us (0.28)
  the two profiles are of different devices: /device:TPU:0 before, /device:TPU:8 now
where the time goes in v4:
time: 114 us
  waiting for transfers between devices  63.7 us (56%)
  starting transfers between devices  26.3 us (23%)
  Pallas kernels  16.8 us (15%)
  local copies, waits for them, and re-layouts  5.52 us (5%)
    ppermute x16, waiting for transfers between devices, crossed(): lax.ppermute(chunk, 'seq', [(source, source ^ half_count + step) for sour...  59.5 us
    ppermute x16, starting transfers between devices, crossed(): lax.ppermute(chunk, 'seq', [(source, source ^ half_count + step) for sour...  16.9 us
    pallas_call x6, Pallas kernels, kernel_call(): pl.pallas_call(kernel, out_shape=out_shape, in_specs=in_specs, out_specs=...  16.8 us
    all_to_all x2, starting transfers between devices, exchange_within(): lax.all_to_all(array_in, 'seq', split_axis=0, concat_axis=0, axis_index_g...  7.92 us
    unnamed x16, local copies, waits for them, and re-layouts  5.52 us
  transfers between devices with their start and end apart: 20, of which 15 were waited for; matrix products, arithmetic and copies ran while one was open for 0% of the time, Pallas kernels for 5%

profile of v4, /device:TPU:8, one launch (start us, length us, event | category | flops | bytes accessed | tf_op | source)
XLA Modules:
  0.0 113.8 jit_solution(16867673753608406453)
XLA Ops:
  7.0 4.4 %all-to-all-start = ((bf16[8,1024,128]{2,1,0:T(8,128)(2,1)}), bf16[8,1024,128]{2,1,0:T(8,128)(2,1)S(1)}, u32[]{:S(2)}, u32[]{:S(2)}) async-start(bf16[8,1024,128]{2,1,0:T(8,128)(2,1)} %copy-done), calls=%async_computation | async-start | bytes 4194304 | tf_op jit(solution)/shard_map/all_to_all | solution.py:804
  11.4 2.6 %collective-permute-start = (bf16[256,128]{1,0:T(8,128)(2,1)S(1)}, bf16[256,128]{1,0:T(8,128)(2,1)S(1)}, u32[]{:S(2)}, u32[]{:S(2)}) collective-permute-start(bf16[256,128]{1,0:T(8,128)(2,1)S(1)} %get-tuple-element.36), channel_id=1, source_target_pairs={{0,16},{2,18},{4,20},{6,22},{8,24},{10,26},{12,28},{14,30},{16,0},... | collective-permute-start | bytes 196616 | tf_op jit(solution)/shard_map/ppermute | solution.py:776
  14.0 3.3 %collective-permute-start.2 = (bf16[256,128]{1,0:T(8,128)(2,1)S(1)}, bf16[256,128]{1,0:T(8,128)(2,1)S(1)}, u32[]{:S(2)}, u32[]{:S(2)}) collective-permute-start(bf16[256,128]{1,0:T(8,128)(2,1)S(1)} %get-tuple-element.38), channel_id=1, source_target_pairs={{0,20},{2,22},{4,16},{6,18},{8,28},{10,30},{12,24},{14,26},{16,4},... | collective-permute-start | bytes 196616 | tf_op jit(solution)/shard_map/ppermute | solution.py:776
  18.7 20.8 %collective-permute-done.refs_0_ = bf16[256,128]{1,0:T(8,128)(2,1)S(1)} collective-permute-done((bf16[256,128]{1,0:T(8,128)(2,1)S(1)}, bf16[256,128]{1,0:T(8,128)(2,1)S(1)}, u32[]{:S(2)}, u32[]{:S(2)}) %collective-permute-start) | collective-permute-done | bytes 65568 | tf_op jit(solution)/shard_map/ppermute | solution.py:776
  41.3 2.1 %collective-permute-done.2.refs_2_ = bf16[256,128]{1,0:T(8,128)(2,1)S(1)} collective-permute-done((bf16[256,128]{1,0:T(8,128)(2,1)S(1)}, bf16[256,128]{1,0:T(8,128)(2,1)S(1)}, u32[]{:S(2)}, u32[]{:S(2)}) %collective-permute-start.2) | collective-permute-done | bytes 65568 | tf_op jit(solution)/shard_map/ppermute | solution.py:776
  43.3 2.7 %diagonal_statistics.1 = (bf16[8,1024,128]{2,1,0:T(8,128)(2,1)S(1)}, f32[8,1024]{1,0:T(8,128)S(1)}) custom-call(f32[16]{0:T(128)S(1)} %copy-done.6, s32[16,16]{1,0:T(8,128)S(1)} %bitcast.1, s32[16]{0:T(128)S(1)} %copy-done.7, bf16[8,1024,128]{2,1,0:T(8,128)(2,1)S(1)} %all-to-all-done.in_ref), custom_call_target="tpu_custom_call" | custom-call | flops 536870912 | bytes 4228224 | tf_op jit(solution)/shard_map/diagonal_statistics/pallas_call | solution.py:406
  46.0 4.3 %collective-permute-done.5.refs_5_ = bf16[256,128]{1,0:T(8,128)(2,1)S(1)} collective-permute-done((bf16[256,128]{1,0:T(8,128)(2,1)S(1)}, bf16[256,128]{1,0:T(8,128)(2,1)S(1)}, u32[]{:S(2)}, u32[]{:S(2)}) %collective-permute-start.5) | collective-permute-done | bytes 65568 | tf_op jit(solution)/shard_map/ppermute | solution.py:776
  50.4 2.2 %collective-permute-done.6.refs_6_ = bf16[256,128]{1,0:T(8,128)(2,1)S(1)} collective-permute-done((bf16[256,128]{1,0:T(8,128)(2,1)S(1)}, bf16[256,128]{1,0:T(8,128)(2,1)S(1)}, u32[]{:S(2)}, u32[]{:S(2)}) %collective-permute-start.6) | collective-permute-done | bytes 65568 | tf_op jit(solution)/shard_map/ppermute | solution.py:776
  54.0 2.3 %square_statistics.1 = (bf16[4,1024,128]{2,1,0:T(8,128)(2,1)S(1)}, f32[8,1024]{1,0:T(8,128)S(1)}, f32[8,1024]{1,0:T(8,128)S(1)}) custom-call(f32[16]{0:T(128)S(1)} %copy-done.6, s32[16,16]{1,0:T(8,128)S(1)} %bitcast.2, s32[16]{0:T(128)S(1)} %copy-done.7, bf16[8,1024,128]{2,1,0:T(8,128)(2,1)S(1)} %get-tuple-element.34.arrays_ref, ...), custom_call_target="tpu_custom_call" | custom-call | flops 536870912 | bytes 3769472 | tf_op jit(solution)/shard_map/square_statistics/pallas_call | solution.py:406
  56.4 2.8 %own_diagonal_gradients.1 = (f32[3,1024,128]{2,1,0:T(8,128)S(1)}, f32[8,128]{1,0:T(8,128)S(1)}) custom-call(f32[16]{0:T(128)S(1)} %copy-done.6, s32[16,16]{1,0:T(8,128)S(1)} %bitcast.3, s32[16]{0:T(128)S(1)} %copy-done.7, bf16[8,1024,128]{2,1,0:T(8,128)(2,1)S(1)} %get-tuple-element.34.arrays_ref, f32[8,1024]{1,0:T(8,128)S(1)} %get-tuple-element.46.own_ref), custom_call_target="tpu_custom_call" | custom-call | flops 671088640 | bytes 3708032 | tf_op jit(solution)/shard_map/own_diagonal_gradients/pallas_call | solution.py:406
  59.2 2.0 %collective-permute-done.8.received_ref = f32[8,1024]{1,0:T(8,128)S(1)} collective-permute-done((f32[8,1024]{1,0:T(8,128)S(1)}, f32[8,1024]{1,0:T(8,128)S(1)}, u32[]{:S(2)}, u32[]{:S(2)}) %collective-permute-start.8) | collective-permute-done | bytes 32800 | tf_op jit(solution)/shard_map/ppermute | solution.py:842
  61.2 6.7 %remaining_gradients.1 = (bf16[8,784,128]{2,1,0:T(8,128)(2,1)}, bf16[272,128]{1,0:T(8,128)(2,1)S(1)}, bf16[272,128]{1,0:T(8,128)(2,1)S(1)}, bf16[272,128]{1,0:T(...) custom-call(f32[16]{0:T(128)S(1)} %copy-done.6, ...), custom_call_target="tpu_custom_call" | custom-call | flops 2147483648 | bytes 7017600 | tf_op jit(solution)/shard_map/remaining_gradients/pallas_call | solution.py:406
  67.9 3.5 %all-to-all-start.1 = ((bf16[8,784,128]{2,1,0:T(8,128)(2,1)}), bf16[8,784,128]{2,1,0:T(8,128)(2,1)S(1)}, u32[]{:S(2)}, u32[]{:S(2)}) async-start(bf16[8,784,128]{2,1,0:T(8,128)(2,1)} %get-tuple-element.49), calls=%async_computation.1 | async-start | bytes 3211264 | tf_op jit(solution)/shard_map/all_to_all | solution.py:804
  73.6 1.9 %collective-permute-start.11 = (bf16[272,128]{1,0:T(8,128)(2,1)S(1)}, bf16[272,128]{1,0:T(8,128)(2,1)S(1)}, u32[]{:S(2)}, u32[]{:S(2)}) collective-permute-start(bf16[272,128]{1,0:T(8,128)(2,1)S(1)} %get-tuple-element.52), channel_id=1, source_target_pairs={{0,20},{2,22},{4,16},{6,18},{8,28},{10,30},{12,24},{14,26},{16,4},... | collective-permute-start | bytes 208904 | tf_op jit(solution)/shard_map/ppermute | solution.py:776
  75.5 2.2 %collective-permute-start.12 = (bf16[272,128]{1,0:T(8,128)(2,1)S(1)}, bf16[272,128]{1,0:T(8,128)(2,1)S(1)}, u32[]{:S(2)}, u32[]{:S(2)}) collective-permute-start(bf16[272,128]{1,0:T(8,128)(2,1)S(1)} %get-tuple-element.53), channel_id=1, source_target_pairs={{0,22},{2,20},{4,18},{6,16},{8,30},{10,28},{12,26},{14,24},{16,6},... | collective-permute-start | bytes 208904 | tf_op jit(solution)/shard_map/ppermute | solution.py:776
  77.7 15.0 %collective-permute-done.9.refs_0_ = bf16[272,128]{1,0:T(8,128)(2,1)S(1)} collective-permute-done((bf16[272,128]{1,0:T(8,128)(2,1)S(1)}, bf16[272,128]{1,0:T(8,128)(2,1)S(1)}, u32[]{:S(2)}, u32[]{:S(2)}) %collective-permute-start.9) | collective-permute-done | bytes 69664 | tf_op jit(solution)/shard_map/ppermute | solution.py:776
  93.0 2.0 %collective-permute-start.15 = (bf16[272,128]{1,0:T(8,128)(2,1)S(1)}, bf16[272,128]{1,0:T(8,128)(2,1)S(1)}, u32[]{:S(2)}, u32[]{:S(2)}) collective-permute-start(bf16[272,128]{1,0:T(8,128)(2,1)S(1)} %get-tuple-element.56), channel_id=1, source_target_pairs={{0,28},{2,30},{4,24},{6,26},{8,20},{10,22},{12,16},{14,18},{16,12}... | collective-permute-start | bytes 208904 | tf_op jit(solution)/shard_map/ppermute | solution.py:776
  95.0 1.5 %collective-permute-done.11.refs_2_ = bf16[272,128]{1,0:T(8,128)(2,1)S(1)} collective-permute-done((bf16[272,128]{1,0:T(8,128)(2,1)S(1)}, bf16[272,128]{1,0:T(8,128)(2,1)S(1)}, u32[]{:S(2)}, u32[]{:S(2)}) %collective-permute-start.11) | collective-permute-done | bytes 69664 | tf_op jit(solution)/shard_map/ppermute | solution.py:776
  97.1 7.0 %collective-permute-done.14.refs_5_ = bf16[272,128]{1,0:T(8,128)(2,1)S(1)} collective-permute-done((bf16[272,128]{1,0:T(8,128)(2,1)S(1)}, bf16[272,128]{1,0:T(8,128)(2,1)S(1)}, u32[]{:S(2)}, u32[]{:S(2)}) %collective-permute-start.14) | collective-permute-done | bytes 69664 | tf_op jit(solution)/shard_map/ppermute | solution.py:776
  104.1 2.3 %collective-permute-done.15.refs_6_ = bf16[272,128]{1,0:T(8,128)(2,1)S(1)} collective-permute-done((bf16[272,128]{1,0:T(8,128)(2,1)S(1)}, bf16[272,128]{1,0:T(8,128)(2,1)S(1)}, u32[]{:S(2)}, u32[]{:S(2)}) %collective-permute-start.15) | collective-permute-done | bytes 69664 | tf_op jit(solution)/shard_map/ppermute | solution.py:776
  106.4 1.5 %collective-permute-done.16.refs_7_ = bf16[272,128]{1,0:T(8,128)(2,1)S(1)} collective-permute-done((bf16[272,128]{1,0:T(8,128)(2,1)S(1)}, bf16[272,128]{1,0:T(8,128)(2,1)S(1)}, u32[]{:S(2)}, u32[]{:S(2)}) %collective-permute-start.16) | collective-permute-done | bytes 69664 | tf_op jit(solution)/shard_map/ppermute | solution.py:776
  107.9 1.5 %unpack_heads.1 = (bf16[1,128,2048]{2,1,0:T(8,128)(2,1)}, bf16[1,128,2048]{2,1,0:T(8,128)(2,1)}, bf16[1,128,2048]{2,1,0:T(8,128)(2,1)}, f32[16,128]{1,0:T(8,128)S(1)}) custom-call(bf16[8,784,128]{2,1,0:T(8,128)(2,1)S(1)} %all-to-all-done.1.within_ref, bf16[272,128]{1,0:T(8,128)(2,1)S(1)} %collective-permute-done.9.refs_0_, ...), custom_call_target="tpu_custom_call" | custom-call | bytes 3743744 | tf_op jit(solution)/shard_map/unpack_heads/pallas_call | solution.py:406
  109.5 1.5 %collective-permute-start.17 = (f32[16,128]{1,0:T(8,128)S(1)}, f32[16,128]{1,0:T(8,128)S(1)}, u32[]{:S(2)}, u32[]{:S(2)}) collective-permute-start(f32[16,128]{1,0:T(8,128)S(1)} %get-tuple-element.61), channel_id=1, source_target_pairs={{0,1},{1,0},{2,3},{3,2},{4,5},{5,4},{6,7},{7,6},{8,9},{9,8},{10,11... | collective-permute-start | bytes 24584 | tf_op jit(solution)/shard_map/ppermute | solution.py:878
  111.0 2.2 %collective-permute-done.17 = f32[16,128]{1,0:T(8,128)S(1)} collective-permute-done((f32[16,128]{1,0:T(8,128)S(1)}, f32[16,128]{1,0:T(8,128)S(1)}, u32[]{:S(2)}, u32[]{:S(2)}) %collective-permute-start.17) | collective-permute-done | bytes 8224 | tf_op jit(solution)/shard_map/ppermute | solution.py:878
  (39 shorter events, 14.7 us)
Async XLA Ops:
  5.7 1.4 %copy-start = (bf16[8,1024,128]{2,1,0:T(8,128)(2,1)}, bf16[8,1024,128]{2,1,0:T(8,128)(2,1)S(1)}, u32[]{:S(2)}) copy-start(bf16[8,1024,128]{2,1,0:T(8,128)(2,1)S(1)} %get-tuple-element.33) | copy-start | bytes 6291460
  7.0 36.3 %copy-start.5 = (s32[1,16,16,1]{2,3,1,0:T(1,128)S(1)}, s32[1,16,16,1]{2,3,1,0:T(1,128)}, u32[]{:S(2)}) copy-start(s32[1,16,16,1]{2,3,1,0:T(1,128)} %param.12) | copy-start | bytes 3076
  7.0 36.3 %copy-start.6 = (f32[16]{0:T(128)S(1)}, f32[16]{0:T(128)}, u32[]{:S(2)}) copy-start(f32[16]{0:T(128)} %softness_ref.7) | copy-start | bytes 196
  7.0 36.3 %copy-start.7 = (s32[16]{0:T(128)S(1)}, s32[16]{0:T(128)}, u32[]{:S(2)}) copy-start(s32[16]{0:T(128)} %span_ref.7) | copy-start | bytes 196
  7.0 36.3 %all-to-all-start = ((bf16[8,1024,128]{2,1,0:T(8,128)(2,1)}), bf16[8,1024,128]{2,1,0:T(8,128)(2,1)S(1)}, u32[]{:S(2)}, u32[]{:S(2)}) async-start(bf16[8,1024,128]{2,1,0:T(8,128)(2,1)} %copy-done), calls=%async_computation | async-start | bytes 4194304 | tf_op jit(solution)/shard_map/all_to_all | solution.py:804
  11.4 28.1 %collective-permute-start = (bf16[256,128]{1,0:T(8,128)(2,1)S(1)}, bf16[256,128]{1,0:T(8,128)(2,1)S(1)}, u32[]{:S(2)}, u32[]{:S(2)}) collective-permute-start(bf16[256,128]{1,0:T(8,128)(2,1)S(1)} %get-tuple-element.36), channel_id=1, source_target_pairs={{0,16},{2,18},{4,20},{6,22},{8,24},{10,26},{12,28},{14,30},{16,0},... | collective-permute-start | bytes 196616 | tf_op jit(solution)/shard_map/ppermute | solution.py:776
  14.0 26.0 %collective-permute-start.1 = (bf16[256,128]{1,0:T(8,128)(2,1)S(1)}, bf16[256,128]{1,0:T(8,128)(2,1)S(1)}, u32[]{:S(2)}, u32[]{:S(2)}) collective-permute-start(bf16[256,128]{1,0:T(8,128)(2,1)S(1)} %get-tuple-element.37), channel_id=1, source_target_pairs={{0,18},{2,16},{4,22},{6,20},{8,26},{10,24},{12,30},{14,28},{16,2},... | collective-permute-start | bytes 196616 | tf_op jit(solution)/shard_map/ppermute | solution.py:776
  14.0 29.3 %collective-permute-start.2 = (bf16[256,128]{1,0:T(8,128)(2,1)S(1)}, bf16[256,128]{1,0:T(8,128)(2,1)S(1)}, u32[]{:S(2)}, u32[]{:S(2)}) collective-permute-start(bf16[256,128]{1,0:T(8,128)(2,1)S(1)} %get-tuple-element.38), channel_id=1, source_target_pairs={{0,20},{2,22},{4,16},{6,18},{8,28},{10,30},{12,24},{14,26},{16,4},... | collective-permute-start | bytes 196616 | tf_op jit(solution)/shard_map/ppermute | solution.py:776
  17.3 28.7 %collective-permute-start.3 = (bf16[256,128]{1,0:T(8,128)(2,1)S(1)}, bf16[256,128]{1,0:T(8,128)(2,1)S(1)}, u32[]{:S(2)}, u32[]{:S(2)}) collective-permute-start(bf16[256,128]{1,0:T(8,128)(2,1)S(1)} %get-tuple-element.39), channel_id=1, source_target_pairs={{0,22},{2,20},{4,18},{6,16},{8,30},{10,28},{12,26},{14,24},{16,6},... | collective-permute-start | bytes 196616 | tf_op jit(solution)/shard_map/ppermute | solution.py:776
  17.6 28.4 %collective-permute-start.4 = (bf16[256,128]{1,0:T(8,128)(2,1)S(1)}, bf16[256,128]{1,0:T(8,128)(2,1)S(1)}, u32[]{:S(2)}, u32[]{:S(2)}) collective-permute-start(bf16[256,128]{1,0:T(8,128)(2,1)S(1)} %get-tuple-element.40), channel_id=1, source_target_pairs={{0,24},{2,26},{4,28},{6,30},{8,16},{10,18},{12,20},{14,22},{16,8},... | collective-permute-start | bytes 196616 | tf_op jit(solution)/shard_map/ppermute | solution.py:776
  39.6 10.8 %collective-permute-start.5 = (bf16[256,128]{1,0:T(8,128)(2,1)S(1)}, bf16[256,128]{1,0:T(8,128)(2,1)S(1)}, u32[]{:S(2)}, u32[]{:S(2)}) collective-permute-start(bf16[256,128]{1,0:T(8,128)(2,1)S(1)} %get-tuple-element.41), channel_id=1, source_target_pairs={{0,26},{2,24},{4,30},{6,28},{8,18},{10,16},{12,22},{14,20},{16,10}... | collective-permute-start | bytes 196616 | tf_op jit(solution)/shard_map/ppermute | solution.py:776
  40.0 12.6 %collective-permute-start.6 = (bf16[256,128]{1,0:T(8,128)(2,1)S(1)}, bf16[256,128]{1,0:T(8,128)(2,1)S(1)}, u32[]{:S(2)}, u32[]{:S(2)}) collective-permute-start(bf16[256,128]{1,0:T(8,128)(2,1)S(1)} %get-tuple-element.42), channel_id=1, source_target_pairs={{0,28},{2,30},{4,24},{6,26},{8,20},{10,22},{12,16},{14,18},{16,12}... | collective-permute-start | bytes 196616 | tf_op jit(solution)/shard_map/ppermute | solution.py:776
  43.3 10.7 %collective-permute-start.7 = (bf16[256,128]{1,0:T(8,128)(2,1)S(1)}, bf16[256,128]{1,0:T(8,128)(2,1)S(1)}, u32[]{:S(2)}, u32[]{:S(2)}) collective-permute-start(bf16[256,128]{1,0:T(8,128)(2,1)S(1)} %get-tuple-element.43), channel_id=1, source_target_pairs={{0,30},{2,28},{4,26},{6,24},{8,22},{10,20},{12,18},{14,16},{16,14}... | collective-permute-start | bytes 196616 | tf_op jit(solution)/shard_map/ppermute | solution.py:776
  56.3 4.9 %collective-permute-start.8 = (f32[8,1024]{1,0:T(8,128)S(1)}, f32[8,1024]{1,0:T(8,128)S(1)}, u32[]{:S(2)}, u32[]{:S(2)}) collective-permute-start(f32[8,1024]{1,0:T(8,128)S(1)} %get-tuple-element.45.message_ref), channel_id=1, source_target_pairs={{0,16},{2,18},{4,20},{6,22},{8,24},{10,26},{12,28},{14,30},{16,0},... | collective-permute-start | bytes 98312 | tf_op jit(solution)/shard_map/ppermute | solution.py:842
  67.9 40.1 %all-to-all-start.1 = ((bf16[8,784,128]{2,1,0:T(8,128)(2,1)}), bf16[8,784,128]{2,1,0:T(8,128)(2,1)S(1)}, u32[]{:S(2)}, u32[]{:S(2)}) async-start(bf16[8,784,128]{2,1,0:T(8,128)(2,1)} %get-tuple-element.49), calls=%async_computation.1 | async-start | bytes 3211264 | tf_op jit(solution)/shard_map/all_to_all | solution.py:804
  71.4 21.3 %collective-permute-start.9 = (bf16[272,128]{1,0:T(8,128)(2,1)S(1)}, bf16[272,128]{1,0:T(8,128)(2,1)S(1)}, u32[]{:S(2)}, u32[]{:S(2)}) collective-permute-start(bf16[272,128]{1,0:T(8,128)(2,1)S(1)} %get-tuple-element.50), channel_id=1, source_target_pairs={{0,16},{2,18},{4,20},{6,22},{8,24},{10,26},{12,28},{14,30},{16,0},... | collective-permute-start | bytes 208904 | tf_op jit(solution)/shard_map/ppermute | solution.py:776
  72.4 20.5 %collective-permute-start.10 = (bf16[272,128]{1,0:T(8,128)(2,1)S(1)}, bf16[272,128]{1,0:T(8,128)(2,1)S(1)}, u32[]{:S(2)}, u32[]{:S(2)}) collective-permute-start(bf16[272,128]{1,0:T(8,128)(2,1)S(1)} %get-tuple-element.51), channel_id=1, source_target_pairs={{0,18},{2,16},{4,22},{6,20},{8,26},{10,24},{12,30},{14,28},{16,2},... | collective-permute-start | bytes 208904 | tf_op jit(solution)/shard_map/ppermute | solution.py:776
  73.6 22.9 %collective-permute-start.11 = (bf16[272,128]{1,0:T(8,128)(2,1)S(1)}, bf16[272,128]{1,0:T(8,128)(2,1)S(1)}, u32[]{:S(2)}, u32[]{:S(2)}) collective-permute-start(bf16[272,128]{1,0:T(8,128)(2,1)S(1)} %get-tuple-element.52), channel_id=1, source_target_pairs={{0,20},{2,22},{4,16},{6,18},{8,28},{10,30},{12,24},{14,26},{16,4},... | collective-permute-start | bytes 208904 | tf_op jit(solution)/shard_map/ppermute | solution.py:776
  75.5 21.6 %collective-permute-start.12 = (bf16[272,128]{1,0:T(8,128)(2,1)S(1)}, bf16[272,128]{1,0:T(8,128)(2,1)S(1)}, u32[]{:S(2)}, u32[]{:S(2)}) collective-permute-start(bf16[272,128]{1,0:T(8,128)(2,1)S(1)} %get-tuple-element.53), channel_id=1, source_target_pairs={{0,22},{2,20},{4,18},{6,16},{8,30},{10,28},{12,26},{14,24},{16,6},... | collective-permute-start | bytes 208904 | tf_op jit(solution)/shard_map/ppermute | solution.py:776
  77.7 19.4 %collective-permute-start.13 = (bf16[272,128]{1,0:T(8,128)(2,1)S(1)}, bf16[272,128]{1,0:T(8,128)(2,1)S(1)}, u32[]{:S(2)}, u32[]{:S(2)}) collective-permute-start(bf16[272,128]{1,0:T(8,128)(2,1)S(1)} %get-tuple-element.54), channel_id=1, source_target_pairs={{0,24},{2,26},{4,28},{6,30},{8,16},{10,18},{12,20},{14,22},{16,8},... | collective-permute-start | bytes 208904 | tf_op jit(solution)/shard_map/ppermute | solution.py:776
  92.7 11.4 %collective-permute-start.14 = (bf16[272,128]{1,0:T(8,128)(2,1)S(1)}, bf16[272,128]{1,0:T(8,128)(2,1)S(1)}, u32[]{:S(2)}, u32[]{:S(2)}) collective-permute-start(bf16[272,128]{1,0:T(8,128)(2,1)S(1)} %get-tuple-element.55), channel_id=1, source_target_pairs={{0,26},{2,24},{4,30},{6,28},{8,18},{10,16},{12,22},{14,20},{16,10}... | collective-permute-start | bytes 208904 | tf_op jit(solution)/shard_map/ppermute | solution.py:776
  93.0 13.4 %collective-permute-start.15 = (bf16[272,128]{1,0:T(8,128)(2,1)S(1)}, bf16[272,128]{1,0:T(8,128)(2,1)S(1)}, u32[]{:S(2)}, u32[]{:S(2)}) collective-permute-start(bf16[272,128]{1,0:T(8,128)(2,1)S(1)} %get-tuple-element.56), channel_id=1, source_target_pairs={{0,28},{2,30},{4,24},{6,26},{8,20},{10,22},{12,16},{14,18},{16,12}... | collective-permute-start | bytes 208904 | tf_op jit(solution)/shard_map/ppermute | solution.py:776
  96.5 11.4 %collective-permute-start.16 = (bf16[272,128]{1,0:T(8,128)(2,1)S(1)}, bf16[272,128]{1,0:T(8,128)(2,1)S(1)}, u32[]{:S(2)}, u32[]{:S(2)}) collective-permute-start(bf16[272,128]{1,0:T(8,128)(2,1)S(1)} %get-tuple-element.57), channel_id=1, source_target_pairs={{0,30},{2,28},{4,26},{6,24},{8,22},{10,20},{12,18},{14,16},{16,14}... | collective-permute-start | bytes 208904 | tf_op jit(solution)/shard_map/ppermute | solution.py:776
  109.5 3.7 %collective-permute-start.17 = (f32[16,128]{1,0:T(8,128)S(1)}, f32[16,128]{1,0:T(8,128)S(1)}, u32[]{:S(2)}, u32[]{:S(2)}) collective-permute-start(f32[16,128]{1,0:T(8,128)S(1)} %get-tuple-element.61), channel_id=1, source_target_pairs={{0,1},{1,0},{2,3},{3,2},{4,5},{5,4},{6,7},{7,6},{8,9},{9,8},{10,11... | collective-permute-start | bytes 24584 | tf_op jit(solution)/shard_map/ppermute | solution.py:878
  (4 other events, 4.2 us)

commit v5 on v4

--- a/solution.py
+++ b/solution.py
@@ -378,6 +378,7 @@
 TILE = 256
 EXTRA = 16
 MIB = 1024 * 1024
+PIECES = 4
 QUERY, KEY, VALUE, GRAD = range(4)
 
 
@@ -399,7 +400,9 @@
     return me, half, me - half * half_count
 
 
-def kernel_call(kernel, name, operands, in_specs, out_shape, scratch, vmem_mib, flops=0):
+def kernel_call(
+    kernel, name, operands, in_specs, out_shape, scratch, vmem_mib, flops=0, out_space=pltpu.VMEM
+):
     bytes_accessed = sum(
         math.prod(item.shape) * item.dtype.itemsize for item in (*operands, *out_shape)
     )
@@ -407,7 +410,7 @@
         kernel,
         out_shape=out_shape,
         in_specs=in_specs,
-        out_specs=[pl.BlockSpec(memory_space=pltpu.VMEM)] * len(out_shape),
+        out_specs=[pl.BlockSpec(memory_space=out_space)] * len(out_shape),
         scratch_shapes=scratch,
         cost_estimate=pl.CostEstimate(
             flops=flops, bytes_accessed=bytes_accessed, transcendentals=0
@@ -419,41 +422,71 @@
 
 def pack_kernel(*refs, half_count):
     arrays, within_ref, across_refs = refs[:4], refs[4], refs[5 : 5 + half_count]
-    held, arrival = refs[5 + half_count :]
+    held, within, across, arrival, left_within, left_across = refs[5 + half_count :]
     me, half, _ = position(half_count)
-    copies = [
-        pltpu.make_async_copy(array_ref.at[0], held.at[place], arrival.at[place])
+    piece = BLK // PIECES
+    arrivals = [
+        [
+            pltpu.make_async_copy(
+                array_ref.at[0, part * piece : (part + 1) * piece, :],
+                held.at[place, part * piece : (part + 1) * piece, :],
+                arrival.at[place, part],
+            )
+            for part in range(PIECES)
+        ]
         for place, array_ref in enumerate(arrays)
     ]
-    for copy in copies:
-        copy.start()
-    for place, copy in enumerate(copies):
-        copy.wait()
-        for peer in range(half_count):
-            for slot, base in enumerate((half * half_count, (1 - half) * half_count)):
-                start = (slot * 4 + place) * BLK
-                within_ref[peer, start : start + BLK, :] = held[
-                    place, :, columns_of(base + peer)
-                ]
+    for copies in arrivals:
+        for copy in copies:
+            copy.start()
+    leaving = []
+    for place, copies in enumerate(arrivals):
+        for copy in copies:
+            copy.wait()
+        for slot, base in enumerate((half * half_count, (1 - half) * half_count)):
+            rows = slice((slot * 4 + place) * BLK, (slot * 4 + place + 1) * BLK)
+            for peer in range(half_count):
+                within[peer, rows, :] = held[place, :, columns_of(base + peer)]
+            leaving.append(
+                pltpu.make_async_copy(
+                    within.at[:, rows, :], within_ref.at[:, rows, :], left_within.at[place, slot]
+                )
+            )
+            leaving[-1].start()
     first = jnp.where(half == 0, KEY, QUERY)
     second = jnp.where(half == 0, VALUE, GRAD)
     for step, across_ref in enumerate(across_refs):
         columns = columns_of(me ^ (half_count + step))
-        across_ref[:BLK, :] = held[first, :, columns]
-        across_ref[BLK:, :] = held[second, :, columns]
+        across[step, :BLK, :] = held[first, :, columns]
+        across[step, BLK:, :] = held[second, :, columns]
+        leaving.append(
+            pltpu.make_async_copy(across.at[step], across_ref, left_across.at[step])
+        )
+        leaving[-1].start()
+    for copy in leaving:
+        copy.wait()
 
 
 def packed(arrays, half_count):
     width = arrays[0].shape[2]
+    within_shape, across_shape = (half_count, 8 * BLK, HD), (2 * BLK, HD)
     return kernel_call(
         functools.partial(pack_kernel, half_count=half_count),
         "pack_heads",
         arrays,
-        [pl.BlockSpec(memory_space=pltpu.HBM)] * 4,
-        [jax.ShapeDtypeStruct((half_count, 8 * BLK, HD), jnp.bfloat16)]
-        + [jax.ShapeDtypeStruct((2 * BLK, HD), jnp.bfloat16)] * half_count,
-        [pltpu.VMEM((4, BLK, width), jnp.bfloat16), pltpu.SemaphoreType.DMA((4,))],
-        10,
+        [pl.BlockSpec(memory_space=pl.ANY)] * 4,
+        [jax.ShapeDtypeStruct(within_shape, jnp.bfloat16)]
+        + [jax.ShapeDtypeStruct(across_shape, jnp.bfloat16)] * half_count,
+        [
+            pltpu.VMEM((4, BLK, width), jnp.bfloat16),
+            pltpu.VMEM(within_shape, jnp.bfloat16),
+            pltpu.VMEM((half_count, *across_shape), jnp.bfloat16),
+            pltpu.SemaphoreType.DMA((4, PIECES)),
+            pltpu.SemaphoreType.DMA((4, 2)),
+            pltpu.SemaphoreType.DMA((half_count,)),
+        ],
+        60,
+        out_space=pl.ANY,
     )
 
 
@@ -526,43 +559,44 @@
             rows.append(jnp.concatenate(pieces, axis=1))
         return jnp.concatenate(rows, axis=0)
 
-    def statistics(self, score, out_ref, first_row):
+    def statistics(self, weight_ref, towards_ref, out_ref, first_row):
         for tile in range(self.tiles):
             here = tile_rows(tile)
             top = jnp.full((1, TILE), blocked_score, jnp.float32)
             for other in self.keys_of(tile):
                 raw = self.scores(other, tile)
-                score[tile_rows(other), :] = raw
+                weight_ref[tile_rows(other), here] = raw
                 top = jnp.maximum(top, jnp.max(raw, axis=0, keepdims=True))
             total = jnp.zeros((1, TILE), jnp.float32)
             mass = jnp.zeros((1, TILE), jnp.float32)
             for other in self.keys_of(tile):
-                weight = jnp.exp2(score[tile_rows(other), :] - top)
+                there = tile_rows(other)
+                weight = jnp.exp2(weight_ref[there, here] - top)
                 towards = dot_rows(
                     self.rows(VALUE, other, other + 1), self.rows(GRAD, tile, tile + 1)
                 )
+                weight_ref[there, here] = weight
+                towards_ref[there, here] = towards
                 total += jnp.sum(weight, axis=0, keepdims=True)
                 mass += jnp.sum(weight * towards, axis=0, keepdims=True)
             out_ref[first_row : first_row + 1, here] = top
             out_ref[first_row + 1 : first_row + 2, here] = total
             out_ref[first_row + 2 : first_row + 3, here] = mass
 
-    def gradients(self, log_total, delta, prob_low, grad_low, keys_flat):
+    def gradients(self, weight_ref, towards_ref, top, log_total, delta, prob_low, grad_low, keys_flat):
         keys_flat[...] = self.rows(KEY, 0, self.tiles).T
+        share = jnp.exp2(top - log_total)
         temper = jnp.zeros((1, HD), jnp.float32)
         query_parts, key_parts, value_parts = [], [], []
         for tile in range(self.tiles):
             here = tile_rows(tile)
             for other in self.keys_of(tile):
                 there = tile_rows(other)
-                probability = jnp.exp2(self.scores(other, tile) - log_total[:, here])
-                towards = dot_rows(
-                    self.rows(VALUE, other, other + 1), self.rows(GRAD, tile, tile + 1)
-                )
+                probability = weight_ref[there, here] * share[:, here]
                 prob_low[there, here] = probability.astype(jnp.bfloat16)
-                grad_low[there, here] = (probability * (towards - delta[:, here])).astype(
-                    jnp.bfloat16
-                )
+                grad_low[there, here] = (
+                    probability * (towards_ref[there, here] - delta[:, here])
+                ).astype(jnp.bfloat16)
             upto = slice(0, len(self.keys_of(tile)) * TILE)
             query_part = dot_plain(keys_flat[:, upto], grad_low[upto, here]).T
             temper += jnp.sum(
@@ -600,7 +634,10 @@
     return [ref[first + row : first + row + 1, :] for row in range(3)]
 
 
-def within_kernel(softness_ref, ids_ref, span_ref, in_ref, arrays_ref, stats_ref, score, *, half_count):
+def within_kernel(
+    softness_ref, ids_ref, span_ref, in_ref, arrays_ref, stats_ref,
+    own_weight, own_towards, other_weight, other_towards, *, half_count
+):
     me, half, _ = position(half_count)
     for block in range(half_count):
         for place in range(8):
@@ -612,7 +649,8 @@
     for slot, head in enumerate((me, me ^ half_count)):
         places = [slot * 4 + place for place in range(4)]
         region = Region(head, settings, False, base, base, arrays_ref, places)
-        region.statistics(score, stats_ref, slot * 3)
+        kept = ((own_weight, own_towards), (other_weight, other_towards))[slot]
+        region.statistics(*kept, stats_ref, slot * 3)
 
 
 def square_region(head, settings, half_count, square_ref):
@@ -623,7 +661,7 @@
     softness_ref, ids_ref, span_ref, arrays_ref, stats_ref, *refs, half_count
 ):
     across_refs = refs[:half_count]
-    square_ref, message_ref, own_ref, score, square_stats = refs[half_count:]
+    square_ref, message_ref, own_ref, square_stats, weight, towards = refs[half_count:]
     me, half, place = position(half_count)
     first = jnp.where(half == 0, QUERY, KEY)
     second = jnp.where(half == 0, GRAD, VALUE)
@@ -636,7 +674,7 @@
     square_ref[kept_first, :, :] = arrays_ref[kept_first, :, :]
     square_ref[kept_second, :, :] = arrays_ref[kept_second, :, :]
     region = square_region(me, (softness_ref, ids_ref, span_ref), half_count, square_ref)
-    region.statistics(score, square_stats, 0)
+    region.statistics(weight, towards, square_stats, 0)
     for row in range(3):
         message_ref[row : row + 1, :] = jnp.where(
             half == 0, square_stats[row : row + 1, :], stats_ref[3 + row : 4 + row, :]
@@ -648,15 +686,16 @@
 
 
 def diagonal_kernel(
-    softness_ref, ids_ref, span_ref, arrays_ref, own_ref, parts_ref, temper_ref,
-    prob_low, grad_low, keys_flat, *, half_count
+    softness_ref, ids_ref, span_ref, arrays_ref, own_ref, stats_ref, weight, towards,
+    parts_ref, temper_ref, prob_low, grad_low, keys_flat, *, half_count
 ):
     me, half, _ = position(half_count)
     base = half * half_count
     settings = (softness_ref, ids_ref, span_ref)
     region = Region(me, settings, False, base, base, arrays_ref, range(4))
     *parts, temper = region.gradients(
-        own_ref[0:1, :], own_ref[1:2, :], prob_low, grad_low, keys_flat
+        weight, towards, stats_ref[0:1, :], own_ref[0:1, :], own_ref[1:2, :],
+        prob_low, grad_low, keys_flat,
     )
     for place, tiles in enumerate(parts):
         for tile, value in enumerate(tiles):
@@ -680,7 +719,8 @@
 
 def finish_kernel(
     softness_ref, ids_ref, span_ref, arrays_ref, square_ref, message_ref, received_ref,
-    own_ref, stats_ref, parts_ref, temper_ref, within_ref, *refs, half_count
+    own_ref, stats_ref, square_stats, parts_ref, temper_ref,
+    square_weight, square_towards, other_weight, other_towards, within_ref, *refs, half_count
 ):
     across_refs = refs[:half_count]
     across, prob_low, grad_low, keys_flat = refs[half_count:]
@@ -699,7 +739,10 @@
     log_total = jnp.where(half == 0, met[0], own_ref[0:1, :])
     delta = jnp.where(half == 0, met[1], own_ref[1:2, :])
     region = square_region(me, settings, half_count, square_ref)
-    *square_parts, own_temper = region.gradients(log_total, delta, prob_low, grad_low, keys_flat)
+    *square_parts, own_temper = region.gradients(
+        square_weight, square_towards, square_stats[0:1, :], log_total, delta,
+        prob_low, grad_low, keys_flat,
+    )
     scales = (region.scaling, region.scaling, 1.0)
     for tile in range(region.tiles):
         query_part, key_part, value_part = [
@@ -720,7 +763,10 @@
     region = Region(
         me ^ half_count, settings, False, base, base, arrays_ref, range(4, 8)
     )
-    *other_parts, other_temper = region.gradients(log_total, delta, prob_low, grad_low, keys_flat)
+    *other_parts, other_temper = region.gradients(
+        other_weight, other_towards, stats_ref[3:4, :], log_total, delta,
+        prob_low, grad_low, keys_flat,
+    )
     scales = (region.scaling, region.scaling, 1.0)
     for tile in range(region.tiles):
         for array, (part, scale) in enumerate(zip(other_parts, scales)):
@@ -735,10 +781,9 @@
         across_ref[2 * BLK :, :] = pieces
 
 
-def unpack_kernel(within_ref, *refs, half_count):
-    across_refs = refs[:half_count]
-    query_ref, key_ref, value_ref, temper_ref = refs[half_count:]
-    me, half, place = position(half_count)
+def temper_kernel(within_ref, *refs, half_count):
+    across_refs, temper_ref = refs[:half_count], refs[half_count]
+    _, half, place = position(half_count)
 
     def sums(rows):
         return [
@@ -746,6 +791,31 @@
             for slot in range(2)
         ]
 
+    for step, across_ref in enumerate(across_refs):
+        peer = place ^ step
+        near, far = sums(within_ref[peer]), sums(across_ref[...])
+        temper_ref[pl.ds(half * half_count + peer, 1), :] = near[0] + far[1]
+        temper_ref[pl.ds((1 - half) * half_count + peer, 1), :] = near[1] + far[0]
+
+
+def temper_sums(within, across, half_count):
+    last = (6 * BLK // EXTRA, 2 * BLK // EXTRA)
+    return pl.pallas_call(
+        functools.partial(temper_kernel, half_count=half_count),
+        grid=(1,),
+        out_shape=jax.ShapeDtypeStruct((2 * half_count, HD), jnp.float32),
+        in_specs=[pl.BlockSpec((half_count, EXTRA, HD), lambda step: (0, last[0], 0))]
+        + [pl.BlockSpec((EXTRA, HD), lambda step: (last[1], 0))] * half_count,
+        out_specs=pl.BlockSpec((2 * half_count, HD), lambda step: (0, 0)),
+        compiler_params=pltpu.CompilerParams(vmem_limit_bytes=4 * MIB),
+        name="temper_sums",
+    )(within, *across)
+
+
+def unpack_kernel(within_ref, *refs, half_count):
+    across_refs = refs[:half_count]
+    query_ref, key_ref, value_ref = refs[half_count:]
+    _, half, place = position(half_count)
     for step, across_ref in enumerate(across_refs):
         peer = place ^ step
         other = columns_of((1 - half) * half_count + peer)
@@ -764,10 +834,6 @@
             out_ref[0, :, other] = (parts[3 + array].astype(jnp.float32) + added[array]).astype(
                 jnp.bfloat16
             )
-        near = sums(within_ref[peer, 6 * BLK : 6 * BLK + EXTRA, :])
-        far = sums(across_ref[2 * BLK :, :])
-        temper_ref[pl.ds(half * half_count + peer, 1), :] = near[0] + far[1]
-        temper_ref[pl.ds((1 - half) * half_count + peer, 1), :] = near[1] + far[0]
 
 
 def crossed(chunks, half_count):
@@ -793,11 +859,11 @@
     groups = [list(range(half_count)), list(range(half_count, seq_count))]
     settings = (logit_softness, block_grouping[0, :, :, 0], neighborhood_span)
     smem, vmem = pl.BlockSpec(memory_space=pltpu.SMEM), pl.BlockSpec(memory_space=pltpu.VMEM)
-    score = pltpu.VMEM((tokens, TILE), jnp.float32)
     lows = [pltpu.VMEM((tokens, tokens), jnp.bfloat16)] * 2 + [
         pltpu.VMEM((HD, tokens), jnp.bfloat16)
     ]
     rows_of_stats = jax.ShapeDtypeStruct((8, tokens), jnp.float32)
+    pairs = jax.ShapeDtypeStruct((tokens, tokens), jnp.float32)
     pair_flops = 2 * tokens * tokens * HD
 
     def exchange_within(array_in):
@@ -805,7 +871,7 @@
             array_in, "seq", split_axis=0, concat_axis=0, axis_index_groups=groups, tiled=True
         )
 
-    def call(kernel, name, operands, out_shape, scratch, flops):
+    def call(kernel, name, operands, out_shape, scratch, flops, vmem_mib):
         return kernel_call(
             functools.partial(kernel, half_count=half_count),
             name,
@@ -813,7 +879,7 @@
             [smem] * 3 + [vmem] * len(operands),
             out_shape,
             scratch,
-            20,
+            vmem_mib,
             flops,
         )
 
@@ -822,60 +888,67 @@
     )
     arrived = exchange_within(sent)
     foreign = crossed(foreign, half_count)
-    arrays, stats = call(
+    arrays, stats, own_weight, own_towards, other_weight, other_towards = call(
         within_kernel,
         "diagonal_statistics",
         (arrived,),
-        [jax.ShapeDtypeStruct((8, tokens, HD), jnp.bfloat16), rows_of_stats],
-        [score],
+        [jax.ShapeDtypeStruct((8, tokens, HD), jnp.bfloat16), rows_of_stats] + [pairs] * 4,
+        [],
         2 * pair_flops,
-    )
-    square, message, own = call(
+        20,
+    )
+    square, message, own, square_stats, square_weight, square_towards = call(
         square_kernel,
         "square_statistics",
         (arrays, stats, *foreign),
-        [jax.ShapeDtypeStruct((4, tokens, HD), jnp.bfloat16), rows_of_stats, rows_of_stats],
-        [score, pltpu.VMEM((8, tokens), jnp.float32)],
+        [jax.ShapeDtypeStruct((4, tokens, HD), jnp.bfloat16)] + [rows_of_stats] * 3 + [pairs] * 2,
+        [],
         2 * pair_flops,
+        12,
     )
     swap = [(source, source ^ half_count) for source in range(seq_count)]
     received = lax.ppermute(message, "seq", swap)
     parts, temper = call(
         diagonal_kernel,
         "own_diagonal_gradients",
-        (arrays, own),
+        (arrays, own, stats, own_weight, own_towards),
         [
             jax.ShapeDtypeStruct((3, tokens, HD), jnp.float32),
             jax.ShapeDtypeStruct((8, HD), jnp.float32),
         ],
         lows,
-        5 * pair_flops // 2,
+        3 * pair_flops // 2,
+        14,
     )
     within, *across = call(
         finish_kernel,
         "remaining_gradients",
-        (arrays, square, message, received, own, stats, parts, temper),
+        (
+            arrays, square, message, received, own, stats, square_stats, parts, temper,
+            square_weight, square_towards, other_weight, other_towards,
+        ),
         [jax.ShapeDtypeStruct((half_count, 6 * BLK + EXTRA, HD), jnp.bfloat16)]
         + [jax.ShapeDtypeStruct((2 * BLK + EXTRA, HD), jnp.bfloat16)] * half_count,
         [pltpu.VMEM((2, tokens, HD), jnp.bfloat16), *lows],
-        8 * pair_flops,
+        5 * pair_flops,
+        20,
     )
     across = crossed(across, half_count)
     within = exchange_within(within)
-    result = jax.ShapeDtypeStruct(probe_vectors.shape, jnp.bfloat16)
-    *outs, tempers = kernel_call(
+    tempers = temper_sums(within, across, half_count)
+    temper_total = tempers
+    for step in range(1, dp_count):
+        swap = [(source, (source + step) % dp_count) for source in range(dp_count)]
+        temper_total = temper_total + lax.ppermute(tempers, "dp", swap)
+    outs = kernel_call(
         functools.partial(unpack_kernel, half_count=half_count),
         "unpack_heads",
         (within, *across),
         [vmem] * (1 + half_count),
-        [result] * 3 + [jax.ShapeDtypeStruct((seq_count, HD), jnp.float32)],
+        [jax.ShapeDtypeStruct(probe_vectors.shape, jnp.bfloat16)] * 3,
         [],
         10,
     )
-    temper_total = tempers
-    for step in range(1, dp_count):
-        pairs = [(source, (source + step) % dp_count) for source in range(dp_count)]
-        temper_total = temper_total + lax.ppermute(tempers, "dp", pairs)
     return (*outs, temper_total[:, 0] / (dp_count * BLK * seq_count))
 
 

time: 114 us -> 108 us (0.947)
  local copies, waits for them, and re-layouts: 5.52 us -> 0.05 us
  waiting for transfers between devices: 63.7 us -> 62.5 us
    unnamed x16 -> x22, local copies, waits for them, and re-layouts: 5.52 us -> 0.05 us
    ppermute x1, waiting for transfers between devices: 2.18 us -> 0.63 us  [head_shards(): temper_total = temper_total + lax.ppermute(tempers, 'dp', swap)]
  transfers between devices with their start and end apart: 20 -> 20, of which waited for: 15 -> 15; matrix products, arithmetic and copies ran while one was open for 0% -> 0% of each run, Pallas kernels for 5% -> 6%
where the time goes in v5:
time: 108 us
  waiting for transfers between devices  62.5 us (58%)
  starting transfers between devices  26.4 us (24%)
  Pallas kernels  17.3 us (16%)
    ppermute x16, waiting for transfers between devices, crossed(): lax.ppermute(chunk, 'seq', [(source, source ^ half_count + step) for sour...  59 us
    pallas_call x6, Pallas kernels, kernel_call(): pl.pallas_call(kernel, out_shape=out_shape, in_specs=in_specs, out_specs=...  17.3 us
    ppermute x16, starting transfers between devices, crossed(): lax.ppermute(chunk, 'seq', [(source, source ^ half_count + step) for sour...  16.8 us
    all_to_all x2, starting transfers between devices, exchange_within(): lax.all_to_all(array_in, 'seq', split_axis=0, concat_axis=0, axis_index_g...  7.93 us
    ppermute x1, waiting for transfers between devices, head_shards(): received = lax.ppermute(message, 'seq', swap)  2.88 us
  transfers between devices with their start and end apart: 20, of which 15 were waited for; matrix products, arithmetic and copies ran while one was open for 0% of the time, Pallas kernels for 6%

profile of v5, /device:TPU:8, one launch (start us, length us, event | category | flops | bytes accessed | tf_op | source)
XLA Modules:
  0.0 107.7 jit_solution(12375921867675348438)
XLA Ops:
  0.7 2.9 %pack_heads.1 = (bf16[8,1024,128]{2,1,0:T(8,128)(2,1)}, bf16[256,128]{1,0:T(8,128)(2,1)}, bf16[256,128]{1,0:T(8,128)(2,1)}, bf16[256,128]{1,0:T(8,128)(2,1)}, bf...) custom-call(bf16[1,128,2048]{2,1,0:T(8,128)(2,1)} %refs_0_.1, ...), custom_call_target="tpu_custom_call" | custom-call | bytes 4718592 | tf_op jit(solution)/shard_map/pack_heads/pallas_call | solution.py:409
  3.7 4.4 %all-to-all-start = ((bf16[8,1024,128]{2,1,0:T(8,128)(2,1)}), bf16[8,1024,128]{2,1,0:T(8,128)(2,1)S(1)}, u32[]{:S(2)}, u32[]{:S(2)}) async-start(bf16[8,1024,128]{2,1,0:T(8,128)(2,1)} %get-tuple-element.39), calls=%async_computation | async-start | bytes 4194304 | tf_op jit(solution)/shard_map/all_to_all | solution.py:870
  8.1 2.6 %collective-permute-start = (bf16[256,128]{1,0:T(8,128)(2,1)S(1)}, bf16[256,128]{1,0:T(8,128)(2,1)S(1)}, u32[]{:S(2)}, u32[]{:S(2)}) collective-permute-start(bf16[256,128]{1,0:T(8,128)(2,1)S(1)} %copy-done.10), channel_id=1, source_target_pairs={{0,16},{2,18},{4,20},{6,22},{8,24},{10,26},{12,28},{14,30},{16,0},... | collective-permute-start | bytes 196616 | tf_op jit(solution)/shard_map/ppermute | solution.py:842
  10.7 3.3 %collective-permute-start.2 = (bf16[256,128]{1,0:T(8,128)(2,1)S(1)}, bf16[256,128]{1,0:T(8,128)(2,1)S(1)}, u32[]{:S(2)}, u32[]{:S(2)}) collective-permute-start(bf16[256,128]{1,0:T(8,128)(2,1)S(1)} %copy-done.8), channel_id=1, source_target_pairs={{0,20},{2,22},{4,16},{6,18},{8,28},{10,30},{12,24},{14,26},{16,4},... | collective-permute-start | bytes 196616 | tf_op jit(solution)/shard_map/ppermute | solution.py:842
  15.5 20.7 %collective-permute-done.refs_0_ = bf16[256,128]{1,0:T(8,128)(2,1)S(1)} collective-permute-done((bf16[256,128]{1,0:T(8,128)(2,1)S(1)}, bf16[256,128]{1,0:T(8,128)(2,1)S(1)}, u32[]{:S(2)}, u32[]{:S(2)}) %collective-permute-start) | collective-permute-done | bytes 65568 | tf_op jit(solution)/shard_map/ppermute | solution.py:842
  37.9 2.0 %collective-permute-done.2.refs_2_ = bf16[256,128]{1,0:T(8,128)(2,1)S(1)} collective-permute-done((bf16[256,128]{1,0:T(8,128)(2,1)S(1)}, bf16[256,128]{1,0:T(8,128)(2,1)S(1)}, u32[]{:S(2)}, u32[]{:S(2)}) %collective-permute-start.2) | collective-permute-done | bytes 65568 | tf_op jit(solution)/shard_map/ppermute | solution.py:842
  40.0 3.2 %diagonal_statistics.1 = (bf16[8,1024,128]{2,1,0:T(8,128)(2,1)S(1)}, f32[8,1024]{1,0:T(8,128)S(1)}, f32[1024,1024]{1,0:T(8,128)S(1)}, f32[1024,1024]{1,0:T(8,128...) custom-call(f32[16]{0:T(128)S(1)} %copy-done.1, s32[16,16]{1,0:T(8,128)S(1)} %bitcast.1, s32[16]{0:T(128)S(1)} %copy-done.2, ...), custom_call_target="tpu_custom_call" | custom-call | flops 536870912 | bytes 21005440 | tf_op jit(solution)/shard_map/diagonal_statistics/pallas_call | solution.py:409
  43.2 3.8 %collective-permute-done.5.refs_5_ = bf16[256,128]{1,0:T(8,128)(2,1)S(1)} collective-permute-done((bf16[256,128]{1,0:T(8,128)(2,1)S(1)}, bf16[256,128]{1,0:T(8,128)(2,1)S(1)}, u32[]{:S(2)}, u32[]{:S(2)}) %collective-permute-start.5) | collective-permute-done | bytes 65568 | tf_op jit(solution)/shard_map/ppermute | solution.py:842
  47.1 2.2 %collective-permute-done.6.refs_6_ = bf16[256,128]{1,0:T(8,128)(2,1)S(1)} collective-permute-done((bf16[256,128]{1,0:T(8,128)(2,1)S(1)}, bf16[256,128]{1,0:T(8,128)(2,1)S(1)}, u32[]{:S(2)}, u32[]{:S(2)}) %collective-permute-start.6) | collective-permute-done | bytes 65568 | tf_op jit(solution)/shard_map/ppermute | solution.py:842
  50.7 2.6 %square_statistics.1 = (bf16[4,1024,128]{2,1,0:T(8,128)(2,1)S(1)}, f32[8,1024]{1,0:T(8,128)S(1)}, f32[8,1024]{1,0:T(8,128)S(1)}, f32[8,1024]{1,0:T(8,128)S(1)}, ...) custom-call(f32[16]{0:T(128)S(1)} %copy-done.1, s32[16,16]{1,0:T(8,128)S(1)} %bitcast.2, s32[16]{0:T(128)S(1)} %copy-done.2, ...), custom_call_target="tpu_custom_call" | custom-call | flops 536870912 | bytes 12190848 | tf_op jit(solution)/shard_map/square_statistics/pallas_call | solution.py:409
  53.4 1.9 %own_diagonal_gradients.1 = (f32[3,1024,128]{2,1,0:T(8,128)S(1)}, f32[8,128]{1,0:T(8,128)S(1)}) custom-call(f32[16]{0:T(128)S(1)} %copy-done.1, s32[16,16]{1,0:T(8,128)S(1)} %bitcast.3, s32[16]{0:T(128)S(1)} %copy-done.2, bf16[8,1024,128]{2,1,0:T(8,128)(2,1)S(1)} %get-tuple-element.40.arrays_ref, f32[8,1024]{1,0:T(8,128)S(1)} %get-tuple-element.52.own_ref, ...), custom_call_target="tpu_custom_call" | custom-call | flops 402653184 | bytes 12129408 | tf_op jit(solution)/shard_map/own_diagonal_gradients/pallas_call | solution.py:409
  55.4 2.9 %collective-permute-done.8.received_ref = f32[8,1024]{1,0:T(8,128)S(1)} collective-permute-done((f32[8,1024]{1,0:T(8,128)S(1)}, f32[8,1024]{1,0:T(8,128)S(1)}, u32[]{:S(2)}, u32[]{:S(2)}) %collective-permute-start.8) | collective-permute-done | bytes 32800 | tf_op jit(solution)/shard_map/ppermute | solution.py:910
  58.2 5.1 %remaining_gradients.1 = (bf16[8,784,128]{2,1,0:T(8,128)(2,1)}, bf16[272,128]{1,0:T(8,128)(2,1)S(1)}, bf16[272,128]{1,0:T(8,128)(2,1)S(1)}, bf16[272,128]{1,0:T(...) custom-call(f32[16]{0:T(128)S(1)} %copy-done.1, ...), custom_call_target="tpu_custom_call" | custom-call | flops 1342177280 | bytes 23827584 | tf_op jit(solution)/shard_map/remaining_gradients/pallas_call | solution.py:409
  63.3 3.5 %all-to-all-start.1 = ((bf16[8,784,128]{2,1,0:T(8,128)(2,1)}), bf16[8,784,128]{2,1,0:T(8,128)(2,1)S(1)}, u32[]{:S(2)}, u32[]{:S(2)}) async-start(bf16[8,784,128]{2,1,0:T(8,128)(2,1)} %get-tuple-element.62), calls=%async_computation.1 | async-start | bytes 3211264 | tf_op jit(solution)/shard_map/all_to_all | solution.py:870
  69.0 1.9 %collective-permute-start.11 = (bf16[272,128]{1,0:T(8,128)(2,1)S(1)}, bf16[272,128]{1,0:T(8,128)(2,1)S(1)}, u32[]{:S(2)}, u32[]{:S(2)}) collective-permute-start(bf16[272,128]{1,0:T(8,128)(2,1)S(1)} %get-tuple-element.65), channel_id=1, source_target_pairs={{0,20},{2,22},{4,16},{6,18},{8,28},{10,30},{12,24},{14,26},{16,4},... | collective-permute-start | bytes 208904 | tf_op jit(solution)/shard_map/ppermute | solution.py:842
  70.9 2.2 %collective-permute-start.12 = (bf16[272,128]{1,0:T(8,128)(2,1)S(1)}, bf16[272,128]{1,0:T(8,128)(2,1)S(1)}, u32[]{:S(2)}, u32[]{:S(2)}) collective-permute-start(bf16[272,128]{1,0:T(8,128)(2,1)S(1)} %get-tuple-element.66), channel_id=1, source_target_pairs={{0,22},{2,20},{4,18},{6,16},{8,30},{10,28},{12,26},{14,24},{16,6},... | collective-permute-start | bytes 208904 | tf_op jit(solution)/shard_map/ppermute | solution.py:842
  73.1 14.9 %collective-permute-done.9.refs_0_ = bf16[272,128]{1,0:T(8,128)(2,1)S(1)} collective-permute-done((bf16[272,128]{1,0:T(8,128)(2,1)S(1)}, bf16[272,128]{1,0:T(8,128)(2,1)S(1)}, u32[]{:S(2)}, u32[]{:S(2)}) %collective-permute-start.9) | collective-permute-done | bytes 69664 | tf_op jit(solution)/shard_map/ppermute | solution.py:842
  88.5 1.9 %collective-permute-start.15 = (bf16[272,128]{1,0:T(8,128)(2,1)S(1)}, bf16[272,128]{1,0:T(8,128)(2,1)S(1)}, u32[]{:S(2)}, u32[]{:S(2)}) collective-permute-start(bf16[272,128]{1,0:T(8,128)(2,1)S(1)} %get-tuple-element.69), channel_id=1, source_target_pairs={{0,28},{2,30},{4,24},{6,26},{8,20},{10,22},{12,16},{14,18},{16,12}... | collective-permute-start | bytes 208904 | tf_op jit(solution)/shard_map/ppermute | solution.py:842
  90.4 1.5 %collective-permute-done.11.refs_2_ = bf16[272,128]{1,0:T(8,128)(2,1)S(1)} collective-permute-done((bf16[272,128]{1,0:T(8,128)(2,1)S(1)}, bf16[272,128]{1,0:T(8,128)(2,1)S(1)}, u32[]{:S(2)}, u32[]{:S(2)}) %collective-permute-start.11) | collective-permute-done | bytes 69664 | tf_op jit(solution)/shard_map/ppermute | solution.py:842
  92.5 7.0 %collective-permute-done.14.refs_5_ = bf16[272,128]{1,0:T(8,128)(2,1)S(1)} collective-permute-done((bf16[272,128]{1,0:T(8,128)(2,1)S(1)}, bf16[272,128]{1,0:T(8,128)(2,1)S(1)}, u32[]{:S(2)}, u32[]{:S(2)}) %collective-permute-start.14) | collective-permute-done | bytes 69664 | tf_op jit(solution)/shard_map/ppermute | solution.py:842
  99.5 2.3 %collective-permute-done.15.refs_6_ = bf16[272,128]{1,0:T(8,128)(2,1)S(1)} collective-permute-done((bf16[272,128]{1,0:T(8,128)(2,1)S(1)}, bf16[272,128]{1,0:T(8,128)(2,1)S(1)}, u32[]{:S(2)}, u32[]{:S(2)}) %collective-permute-start.15) | collective-permute-done | bytes 69664 | tf_op jit(solution)/shard_map/ppermute | solution.py:842
  101.8 1.5 %collective-permute-done.16.refs_7_ = bf16[272,128]{1,0:T(8,128)(2,1)S(1)} collective-permute-done((bf16[272,128]{1,0:T(8,128)(2,1)S(1)}, bf16[272,128]{1,0:T(8,128)(2,1)S(1)}, u32[]{:S(2)}, u32[]{:S(2)}) %collective-permute-start.16) | collective-permute-done | bytes 69664 | tf_op jit(solution)/shard_map/ppermute | solution.py:842
  103.4 1.6 %collective-permute-start.17 = (f32[16,128]{1,0:T(8,128)S(1)}, f32[16,128]{1,0:T(8,128)S(1)}, u32[]{:S(2)}, u32[]{:S(2)}) collective-permute-start(f32[16,128]{1,0:T(8,128)S(1)} %temper_sums.1), channel_id=1, source_target_pairs={{0,1},{1,0},{2,3},{3,2},{4,5},{5,4},{6,7},{7,6},{8,9},{9,8},{10,11... | collective-permute-start | bytes 24584 | tf_op jit(solution)/shard_map/ppermute | solution.py:942
  104.9 1.5 %unpack_heads.1 = (bf16[1,128,2048]{2,1,0:T(8,128)(2,1)}, bf16[1,128,2048]{2,1,0:T(8,128)(2,1)}, bf16[1,128,2048]{2,1,0:T(8,128)(2,1)}) custom-call(bf16[8,784,128]{2,1,0:T(8,128)(2,1)S(1)} %all-to-all-done.1.within_ref, bf16[272,128]{1,0:T(8,128)(2,1)S(1)} %collective-permute-done.9.refs_0_, bf16[272,128]{1,0:T(8,128)(2,1)S(1)} %collective-permute-done.10.refs_1_, ...), custom_call_target="tpu_custom_call" | custom-call | bytes 3735552 | tf_op jit(solution)/shard_map/unpack_heads/pallas_call | solution.py:409
  (46 shorter events, 9.4 us)
Async XLA Ops:
  0.6 39.4 %copy-start.2 = (s32[16]{0:T(128)S(1)}, s32[16]{0:T(128)}, u32[]{:S(2)}) copy-start(s32[16]{0:T(128)} %span_ref.7) | copy-start | bytes 196
  0.6 39.4 %copy-start.1 = (f32[16]{0:T(128)S(1)}, f32[16]{0:T(128)}, u32[]{:S(2)}) copy-start(f32[16]{0:T(128)} %softness_ref.7) | copy-start | bytes 196
  0.7 39.4 %copy-start = (s32[1,16,16,1]{2,3,1,0:T(1,128)S(1)}, s32[1,16,16,1]{2,3,1,0:T(1,128)}, u32[]{:S(2)}) copy-start(s32[1,16,16,1]{2,3,1,0:T(1,128)} %param.12) | copy-start | bytes 3076
  3.7 36.3 %copy-start.3 = (bf16[256,128]{1,0:T(8,128)(2,1)S(1)}, bf16[256,128]{1,0:T(8,128)(2,1)}, u32[]{:S(2)}) copy-start(bf16[256,128]{1,0:T(8,128)(2,1)} %get-tuple-element.49) | copy-start | bytes 196612
  3.7 36.3 %all-to-all-start = ((bf16[8,1024,128]{2,1,0:T(8,128)(2,1)}), bf16[8,1024,128]{2,1,0:T(8,128)(2,1)S(1)}, u32[]{:S(2)}, u32[]{:S(2)}) async-start(bf16[8,1024,128]{2,1,0:T(8,128)(2,1)} %get-tuple-element.39), calls=%async_computation | async-start | bytes 4194304 | tf_op jit(solution)/shard_map/all_to_all | solution.py:870
  8.1 28.1 %collective-permute-start = (bf16[256,128]{1,0:T(8,128)(2,1)S(1)}, bf16[256,128]{1,0:T(8,128)(2,1)S(1)}, u32[]{:S(2)}, u32[]{:S(2)}) collective-permute-start(bf16[256,128]{1,0:T(8,128)(2,1)S(1)} %copy-done.10), channel_id=1, source_target_pairs={{0,16},{2,18},{4,20},{6,22},{8,24},{10,26},{12,28},{14,30},{16,0},... | collective-permute-start | bytes 196616 | tf_op jit(solution)/shard_map/ppermute | solution.py:842
  10.7 26.0 %collective-permute-start.1 = (bf16[256,128]{1,0:T(8,128)(2,1)S(1)}, bf16[256,128]{1,0:T(8,128)(2,1)S(1)}, u32[]{:S(2)}, u32[]{:S(2)}) collective-permute-start(bf16[256,128]{1,0:T(8,128)(2,1)S(1)} %copy-done.9), channel_id=1, source_target_pairs={{0,18},{2,16},{4,22},{6,20},{8,26},{10,24},{12,30},{14,28},{16,2},... | collective-permute-start | bytes 196616 | tf_op jit(solution)/shard_map/ppermute | solution.py:842
  10.7 29.3 %collective-permute-start.2 = (bf16[256,128]{1,0:T(8,128)(2,1)S(1)}, bf16[256,128]{1,0:T(8,128)(2,1)S(1)}, u32[]{:S(2)}, u32[]{:S(2)}) collective-permute-start(bf16[256,128]{1,0:T(8,128)(2,1)S(1)} %copy-done.8), channel_id=1, source_target_pairs={{0,20},{2,22},{4,16},{6,18},{8,28},{10,30},{12,24},{14,26},{16,4},... | collective-permute-start | bytes 196616 | tf_op jit(solution)/shard_map/ppermute | solution.py:842
  14.0 29.2 %collective-permute-start.3 = (bf16[256,128]{1,0:T(8,128)(2,1)S(1)}, bf16[256,128]{1,0:T(8,128)(2,1)S(1)}, u32[]{:S(2)}, u32[]{:S(2)}) collective-permute-start(bf16[256,128]{1,0:T(8,128)(2,1)S(1)} %copy-done.7), channel_id=1, source_target_pairs={{0,22},{2,20},{4,18},{6,16},{8,30},{10,28},{12,26},{14,24},{16,6},... | collective-permute-start | bytes 196616 | tf_op jit(solution)/shard_map/ppermute | solution.py:842
  14.3 28.9 %collective-permute-start.4 = (bf16[256,128]{1,0:T(8,128)(2,1)S(1)}, bf16[256,128]{1,0:T(8,128)(2,1)S(1)}, u32[]{:S(2)}, u32[]{:S(2)}) collective-permute-start(bf16[256,128]{1,0:T(8,128)(2,1)S(1)} %copy-done.6), channel_id=1, source_target_pairs={{0,24},{2,26},{4,28},{6,30},{8,16},{10,18},{12,20},{14,22},{16,8},... | collective-permute-start | bytes 196616 | tf_op jit(solution)/shard_map/ppermute | solution.py:842
  36.2 10.8 %collective-permute-start.5 = (bf16[256,128]{1,0:T(8,128)(2,1)S(1)}, bf16[256,128]{1,0:T(8,128)(2,1)S(1)}, u32[]{:S(2)}, u32[]{:S(2)}) collective-permute-start(bf16[256,128]{1,0:T(8,128)(2,1)S(1)} %copy-done.5), channel_id=1, source_target_pairs={{0,26},{2,24},{4,30},{6,28},{8,18},{10,16},{12,22},{14,20},{16,10}... | collective-permute-start | bytes 196616 | tf_op jit(solution)/shard_map/ppermute | solution.py:842
  36.7 12.5 %collective-permute-start.6 = (bf16[256,128]{1,0:T(8,128)(2,1)S(1)}, bf16[256,128]{1,0:T(8,128)(2,1)S(1)}, u32[]{:S(2)}, u32[]{:S(2)}) collective-permute-start(bf16[256,128]{1,0:T(8,128)(2,1)S(1)} %copy-done.4), channel_id=1, source_target_pairs={{0,28},{2,30},{4,24},{6,26},{8,20},{10,22},{12,16},{14,18},{16,12}... | collective-permute-start | bytes 196616 | tf_op jit(solution)/shard_map/ppermute | solution.py:842
  40.0 10.7 %collective-permute-start.7 = (bf16[256,128]{1,0:T(8,128)(2,1)S(1)}, bf16[256,128]{1,0:T(8,128)(2,1)S(1)}, u32[]{:S(2)}, u32[]{:S(2)}) collective-permute-start(bf16[256,128]{1,0:T(8,128)(2,1)S(1)} %copy-done.3), channel_id=1, source_target_pairs={{0,30},{2,28},{4,26},{6,24},{8,22},{10,20},{12,18},{14,16},{16,14}... | collective-permute-start | bytes 196616 | tf_op jit(solution)/shard_map/ppermute | solution.py:842
  53.4 4.9 %collective-permute-start.8 = (f32[8,1024]{1,0:T(8,128)S(1)}, f32[8,1024]{1,0:T(8,128)S(1)}, u32[]{:S(2)}, u32[]{:S(2)}) collective-permute-start(f32[8,1024]{1,0:T(8,128)S(1)} %get-tuple-element.51.message_ref), channel_id=1, source_target_pairs={{0,16},{2,18},{4,20},{6,22},{8,24},{10,26},{12,28},{14,30},{16,0},... | collective-permute-start | bytes 98312 | tf_op jit(solution)/shard_map/ppermute | solution.py:910
  63.3 40.0 %all-to-all-start.1 = ((bf16[8,784,128]{2,1,0:T(8,128)(2,1)}), bf16[8,784,128]{2,1,0:T(8,128)(2,1)S(1)}, u32[]{:S(2)}, u32[]{:S(2)}) async-start(bf16[8,784,128]{2,1,0:T(8,128)(2,1)} %get-tuple-element.62), calls=%async_computation.1 | async-start | bytes 3211264 | tf_op jit(solution)/shard_map/all_to_all | solution.py:870
  66.8 21.1 %collective-permute-start.9 = (bf16[272,128]{1,0:T(8,128)(2,1)S(1)}, bf16[272,128]{1,0:T(8,128)(2,1)S(1)}, u32[]{:S(2)}, u32[]{:S(2)}) collective-permute-start(bf16[272,128]{1,0:T(8,128)(2,1)S(1)} %get-tuple-element.63), channel_id=1, source_target_pairs={{0,16},{2,18},{4,20},{6,22},{8,24},{10,26},{12,28},{14,30},{16,0},... | collective-permute-start | bytes 208904 | tf_op jit(solution)/shard_map/ppermute | solution.py:842
  67.6 20.9 %collective-permute-start.10 = (bf16[272,128]{1,0:T(8,128)(2,1)S(1)}, bf16[272,128]{1,0:T(8,128)(2,1)S(1)}, u32[]{:S(2)}, u32[]{:S(2)}) collective-permute-start(bf16[272,128]{1,0:T(8,128)(2,1)S(1)} %get-tuple-element.64), channel_id=1, source_target_pairs={{0,18},{2,16},{4,22},{6,20},{8,26},{10,24},{12,30},{14,28},{16,2},... | collective-permute-start | bytes 208904 | tf_op jit(solution)/shard_map/ppermute | solution.py:842
  69.0 22.9 %collective-permute-start.11 = (bf16[272,128]{1,0:T(8,128)(2,1)S(1)}, bf16[272,128]{1,0:T(8,128)(2,1)S(1)}, u32[]{:S(2)}, u32[]{:S(2)}) collective-permute-start(bf16[272,128]{1,0:T(8,128)(2,1)S(1)} %get-tuple-element.65), channel_id=1, source_target_pairs={{0,20},{2,22},{4,16},{6,18},{8,28},{10,30},{12,24},{14,26},{16,4},... | collective-permute-start | bytes 208904 | tf_op jit(solution)/shard_map/ppermute | solution.py:842
  70.9 21.6 %collective-permute-start.12 = (bf16[272,128]{1,0:T(8,128)(2,1)S(1)}, bf16[272,128]{1,0:T(8,128)(2,1)S(1)}, u32[]{:S(2)}, u32[]{:S(2)}) collective-permute-start(bf16[272,128]{1,0:T(8,128)(2,1)S(1)} %get-tuple-element.66), channel_id=1, source_target_pairs={{0,22},{2,20},{4,18},{6,16},{8,30},{10,28},{12,26},{14,24},{16,6},... | collective-permute-start | bytes 208904 | tf_op jit(solution)/shard_map/ppermute | solution.py:842
  73.1 19.4 %collective-permute-start.13 = (bf16[272,128]{1,0:T(8,128)(2,1)S(1)}, bf16[272,128]{1,0:T(8,128)(2,1)S(1)}, u32[]{:S(2)}, u32[]{:S(2)}) collective-permute-start(bf16[272,128]{1,0:T(8,128)(2,1)S(1)} %get-tuple-element.67), channel_id=1, source_target_pairs={{0,24},{2,26},{4,28},{6,30},{8,16},{10,18},{12,20},{14,22},{16,8},... | collective-permute-start | bytes 208904 | tf_op jit(solution)/shard_map/ppermute | solution.py:842
  88.0 11.5 %collective-permute-start.14 = (bf16[272,128]{1,0:T(8,128)(2,1)S(1)}, bf16[272,128]{1,0:T(8,128)(2,1)S(1)}, u32[]{:S(2)}, u32[]{:S(2)}) collective-permute-start(bf16[272,128]{1,0:T(8,128)(2,1)S(1)} %get-tuple-element.68), channel_id=1, source_target_pairs={{0,26},{2,24},{4,30},{6,28},{8,18},{10,16},{12,22},{14,20},{16,10}... | collective-permute-start | bytes 208904 | tf_op jit(solution)/shard_map/ppermute | solution.py:842
  88.5 13.3 %collective-permute-start.15 = (bf16[272,128]{1,0:T(8,128)(2,1)S(1)}, bf16[272,128]{1,0:T(8,128)(2,1)S(1)}, u32[]{:S(2)}, u32[]{:S(2)}) collective-permute-start(bf16[272,128]{1,0:T(8,128)(2,1)S(1)} %get-tuple-element.69), channel_id=1, source_target_pairs={{0,28},{2,30},{4,24},{6,26},{8,20},{10,22},{12,16},{14,18},{16,12}... | collective-permute-start | bytes 208904 | tf_op jit(solution)/shard_map/ppermute | solution.py:842
  91.9 11.4 %collective-permute-start.16 = (bf16[272,128]{1,0:T(8,128)(2,1)S(1)}, bf16[272,128]{1,0:T(8,128)(2,1)S(1)}, u32[]{:S(2)}, u32[]{:S(2)}) collective-permute-start(bf16[272,128]{1,0:T(8,128)(2,1)S(1)} %get-tuple-element.70), channel_id=1, source_target_pairs={{0,30},{2,28},{4,26},{6,24},{8,22},{10,20},{12,18},{14,16},{16,14}... | collective-permute-start | bytes 208904 | tf_op jit(solution)/shard_map/ppermute | solution.py:842
  103.4 3.7 %collective-permute-start.17 = (f32[16,128]{1,0:T(8,128)S(1)}, f32[16,128]{1,0:T(8,128)S(1)}, u32[]{:S(2)}, u32[]{:S(2)}) collective-permute-start(f32[16,128]{1,0:T(8,128)S(1)} %temper_sums.1), channel_id=1, source_target_pairs={{0,1},{1,0},{2,3},{3,2},{4,5},{5,4},{6,7},{7,6},{8,9},{9,8},{10,11... | collective-permute-start | bytes 24584 | tf_op jit(solution)/shard_map/ppermute | solution.py:942
  (7 other events, 105.2 us)

commit v6 on v5

--- a/solution.py
+++ b/solution.py
@@ -634,35 +634,60 @@
     return [ref[first + row : first + row + 1, :] for row in range(3)]
 
 
+def put(within_ref, array, tile, value):
+    per_tile = TILE // BLK
+    for sub in range(per_tile):
+        within_ref[tile * per_tile + sub, array * BLK : (array + 1) * BLK, :] = value[
+            sub * BLK : (sub + 1) * BLK, :
+        ].astype(jnp.bfloat16)
+
+
+def diagonal_region(slot, settings, half_count, arrays_ref):
+    me, half, _ = position(half_count)
+    head = me ^ (slot * half_count)
+    places = [slot * 4 + place for place in range(4)]
+    base = half * half_count
+    return Region(head, settings, False, base, base, arrays_ref, places)
+
+
+def square_region(settings, half_count, square_ref):
+    me = lax.axis_index("seq")
+    return Region(me, settings, True, 0, half_count, square_ref, range(4))
+
+
 def within_kernel(
-    softness_ref, ids_ref, span_ref, in_ref, arrays_ref, stats_ref,
-    own_weight, own_towards, other_weight, other_towards, *, half_count
+    softness_ref, ids_ref, span_ref, in_ref, arrays_ref, stats_ref, parts_ref, temper_ref,
+    own_weight, own_towards, other_weight, other_towards, *scratch, half_count
 ):
-    me, half, _ = position(half_count)
+    _, half, _ = position(half_count)
     for block in range(half_count):
         for place in range(8):
             arrays_ref[place, block * BLK : (block + 1) * BLK, :] = in_ref[
                 block, place * BLK : (place + 1) * BLK, :
             ]
-    base = half * half_count
     settings = (softness_ref, ids_ref, span_ref)
-    for slot, head in enumerate((me, me ^ half_count)):
-        places = [slot * 4 + place for place in range(4)]
-        region = Region(head, settings, False, base, base, arrays_ref, places)
-        kept = ((own_weight, own_towards), (other_weight, other_towards))[slot]
-        region.statistics(*kept, stats_ref, slot * 3)
-
-
-def square_region(head, settings, half_count, square_ref):
-    return Region(head, settings, True, 0, half_count, square_ref, range(4))
+    kept = ((own_weight, own_towards), (other_weight, other_towards))
+    regions = [diagonal_region(slot, settings, half_count, arrays_ref) for slot in range(2)]
+    for slot, region in enumerate(regions):
+        region.statistics(*kept[slot], stats_ref, slot * 3)
+    temper_ref[...] = jnp.zeros_like(temper_ref)
+
+    @pl.when(half == 0)
+    def _():
+        single = alone(three_rows(stats_ref, 0))
+        *parts, temper = regions[0].gradients(*kept[0], stats_ref[0:1, :], *single, *scratch)
+        for place, tiles in enumerate(parts):
+            for tile, value in enumerate(tiles):
+                parts_ref[place, tile_rows(tile), :] = value
+        temper_ref[0:1, :] = temper
 
 
 def square_kernel(
     softness_ref, ids_ref, span_ref, arrays_ref, stats_ref, *refs, half_count
 ):
     across_refs = refs[:half_count]
-    square_ref, message_ref, own_ref, square_stats, weight, towards = refs[half_count:]
-    me, half, place = position(half_count)
+    square_ref, message_ref, square_stats, weight, towards = refs[half_count:]
+    _, half, place = position(half_count)
     first = jnp.where(half == 0, QUERY, KEY)
     second = jnp.where(half == 0, GRAD, VALUE)
     for step, across_ref in enumerate(across_refs):
@@ -673,34 +698,62 @@
     kept_second = jnp.where(half == 0, VALUE, GRAD)
     square_ref[kept_first, :, :] = arrays_ref[kept_first, :, :]
     square_ref[kept_second, :, :] = arrays_ref[kept_second, :, :]
-    region = square_region(me, (softness_ref, ids_ref, span_ref), half_count, square_ref)
+    region = square_region((softness_ref, ids_ref, span_ref), half_count, square_ref)
     region.statistics(weight, towards, square_stats, 0)
     for row in range(3):
         message_ref[row : row + 1, :] = jnp.where(
             half == 0, square_stats[row : row + 1, :], stats_ref[3 + row : 4 + row, :]
         )
-    diagonal = three_rows(stats_ref, 0)
-    whole, single = merged(diagonal, three_rows(square_stats, 0)), alone(diagonal)
-    for row in range(2):
-        own_ref[row : row + 1, :] = jnp.where(half == 0, single[row], whole[row])
-
-
-def diagonal_kernel(
-    softness_ref, ids_ref, span_ref, arrays_ref, own_ref, stats_ref, weight, towards,
-    parts_ref, temper_ref, prob_low, grad_low, keys_flat, *, half_count
+
+
+def other_diagonal(region, kept, stats_ref, totals, scratch, within_ref):
+    *parts, temper = region.gradients(*kept, stats_ref[3:4, :], *totals, *scratch)
+    scales = (region.scaling, region.scaling, 1.0)
+    for array, (part, scale) in enumerate(zip(parts, scales)):
+        for tile in range(region.tiles):
+            put(within_ref, 3 + array, tile, part[tile] * scale)
+    return temper
+
+
+def first_kernel(
+    softness_ref, ids_ref, span_ref, arrays_ref, square_ref, stats_ref, square_stats, temper_in,
+    own_weight, own_towards, other_weight, other_towards, square_weight, square_towards,
+    within_ref, across_ref, temper_ref, *scratch, half_count
 ):
-    me, half, _ = position(half_count)
-    base = half * half_count
+    _, half, _ = position(half_count)
     settings = (softness_ref, ids_ref, span_ref)
-    region = Region(me, settings, False, base, base, arrays_ref, range(4))
-    *parts, temper = region.gradients(
-        weight, towards, stats_ref[0:1, :], own_ref[0:1, :], own_ref[1:2, :],
-        prob_low, grad_low, keys_flat,
-    )
-    for place, tiles in enumerate(parts):
-        for tile, value in enumerate(tiles):
-            parts_ref[place, tile_rows(tile), :] = value
-    temper_ref[...] = jnp.broadcast_to(temper, temper_ref.shape)
+    temper_ref[...] = temper_in[...]
+
+    @pl.when(half == 0)
+    def _():
+        region = diagonal_region(1, settings, half_count, arrays_ref)
+        totals = alone(three_rows(stats_ref, 3))
+        temper_ref[1:2, :] = other_diagonal(
+            region, (other_weight, other_towards), stats_ref, totals, scratch, within_ref
+        )
+
+    @pl.when(half == 1)
+    def _():
+        totals = merged(three_rows(stats_ref, 0), three_rows(square_stats, 0))
+        square = square_region(settings, half_count, square_ref)
+        scales = (square.scaling, square.scaling, 1.0)
+        across_query, *foreign, square_temper = square.gradients(
+            square_weight, square_towards, square_stats[0:1, :], *totals, *scratch
+        )
+        for array, part in enumerate(foreign):
+            for tile in range(square.tiles):
+                across_ref[array, tile_rows(tile), :] = (part[tile] * scales[1 + array]).astype(
+                    jnp.bfloat16
+                )
+        diagonal = diagonal_region(0, settings, half_count, arrays_ref)
+        *parts, temper = diagonal.gradients(
+            own_weight, own_towards, stats_ref[0:1, :], *totals, *scratch
+        )
+        for tile in range(square.tiles):
+            put(within_ref, 0, tile, (parts[0][tile] + across_query[tile]) * scales[0])
+            put(within_ref, 1, tile, parts[1][tile] * scales[1])
+            put(within_ref, 2, tile, parts[2][tile])
+        temper_ref[0:1, :] = temper + square_temper
 
 
 def temper_rows(own, other):
@@ -719,59 +772,44 @@
 
 def finish_kernel(
     softness_ref, ids_ref, span_ref, arrays_ref, square_ref, message_ref, received_ref,
-    own_ref, stats_ref, square_stats, parts_ref, temper_ref,
-    square_weight, square_towards, other_weight, other_towards, within_ref, *refs, half_count
+    stats_ref, square_stats, parts_ref, temper_ref,
+    square_weight, square_towards, other_weight, other_towards, across_in, begun_ref,
+    within_ref, *refs, half_count
 ):
     across_refs = refs[:half_count]
-    across, prob_low, grad_low, keys_flat = refs[half_count:]
-    me, half, place = position(half_count)
-    base = half * half_count
+    across, temper, *scratch = refs[half_count:]
+    _, half, place = position(half_count)
     settings = (softness_ref, ids_ref, span_ref)
-    per_tile = TILE // BLK
-
-    def put(array, tile, value):
-        for sub in range(per_tile):
-            within_ref[tile * per_tile + sub, array * BLK : (array + 1) * BLK, :] = value[
-                sub * BLK : (sub + 1) * BLK, :
-            ]
-
-    met = merged(three_rows(message_ref, 0), three_rows(received_ref, 0))
-    log_total = jnp.where(half == 0, met[0], own_ref[0:1, :])
-    delta = jnp.where(half == 0, met[1], own_ref[1:2, :])
-    region = square_region(me, settings, half_count, square_ref)
-    *square_parts, own_temper = region.gradients(
-        square_weight, square_towards, square_stats[0:1, :], log_total, delta,
-        prob_low, grad_low, keys_flat,
-    )
-    scales = (region.scaling, region.scaling, 1.0)
-    for tile in range(region.tiles):
-        query_part, key_part, value_part = [
-            part[tile] * scale for part, scale in zip(square_parts, scales)
-        ]
-        here = tile_rows(tile)
-        across[0, here, :] = jnp.where(half == 0, query_part, key_part).astype(jnp.bfloat16)
-        across[1, here, :] = jnp.where(half == 0, 0.0, value_part).astype(jnp.bfloat16)
-        query_kept, key_kept, value_kept = [
-            parts_ref[array, here, :] * scale for array, scale in enumerate(scales)
-        ]
-        put(0, tile, (query_kept + jnp.where(half == 0, 0.0, query_part)).astype(jnp.bfloat16))
-        put(1, tile, (key_kept + jnp.where(half == 0, key_part, 0.0)).astype(jnp.bfloat16))
-        put(2, tile, (value_kept + jnp.where(half == 0, value_part, 0.0)).astype(jnp.bfloat16))
-    single = alone(three_rows(stats_ref, 3))
-    log_total = jnp.where(half == 0, single[0], met[0])
-    delta = jnp.where(half == 0, single[1], met[1])
-    region = Region(
-        me ^ half_count, settings, False, base, base, arrays_ref, range(4, 8)
-    )
-    *other_parts, other_temper = region.gradients(
-        other_weight, other_towards, stats_ref[3:4, :], log_total, delta,
-        prob_low, grad_low, keys_flat,
-    )
-    scales = (region.scaling, region.scaling, 1.0)
-    for tile in range(region.tiles):
-        for array, (part, scale) in enumerate(zip(other_parts, scales)):
-            put(3 + array, tile, (part[tile] * scale).astype(jnp.bfloat16))
-    pieces = temper_rows(own_temper + temper_ref[0:1, :], other_temper)
+    temper[...] = temper_ref[...]
+
+    @pl.when(half == 0)
+    def _():
+        totals = merged(three_rows(message_ref, 0), three_rows(received_ref, 0))
+        region = square_region(settings, half_count, square_ref)
+        query_parts, key_parts, value_parts, square_temper = region.gradients(
+            square_weight, square_towards, square_stats[0:1, :], *totals, *scratch
+        )
+        for tile in range(region.tiles):
+            here = tile_rows(tile)
+            across[0, here, :] = (query_parts[tile] * region.scaling).astype(jnp.bfloat16)
+            put(within_ref, 0, tile, parts_ref[0, here, :] * region.scaling)
+            put(within_ref, 1, tile, (parts_ref[1, here, :] + key_parts[tile]) * region.scaling)
+            put(within_ref, 2, tile, parts_ref[2, here, :] + value_parts[tile])
+        across[1] = jnp.zeros(across.shape[1:], jnp.bfloat16)
+        within_ref[:, 3 * BLK : 6 * BLK, :] = begun_ref[:, 3 * BLK : 6 * BLK, :]
+        temper[0:1, :] = temper_ref[0:1, :] + square_temper
+
+    @pl.when(half == 1)
+    def _():
+        totals = merged(three_rows(message_ref, 0), three_rows(received_ref, 0))
+        region = diagonal_region(1, settings, half_count, arrays_ref)
+        temper[1:2, :] = other_diagonal(
+            region, (other_weight, other_towards), stats_ref, totals, scratch, within_ref
+        )
+        across[...] = across_in[...]
+        within_ref[:, : 3 * BLK, :] = begun_ref[:, : 3 * BLK, :]
+
+    pieces = temper_rows(temper[0:1, :], temper[1:2, :])
     for block in range(half_count):
         within_ref[block, 6 * BLK : 6 * BLK + EXTRA, :] = pieces
     for step, across_ref in enumerate(across_refs):
@@ -888,49 +926,56 @@
     )
     arrived = exchange_within(sent)
     foreign = crossed(foreign, half_count)
-    arrays, stats, own_weight, own_towards, other_weight, other_towards = call(
+    kept_parts = jax.ShapeDtypeStruct((3, tokens, HD), jnp.float32)
+    tempers = jax.ShapeDtypeStruct((8, HD), jnp.float32)
+    arrays, stats, parts, temper, own_weight, own_towards, other_weight, other_towards = call(
         within_kernel,
         "diagonal_statistics",
         (arrived,),
-        [jax.ShapeDtypeStruct((8, tokens, HD), jnp.bfloat16), rows_of_stats] + [pairs] * 4,
-        [],
+        [jax.ShapeDtypeStruct((8, tokens, HD), jnp.bfloat16), rows_of_stats, kept_parts, tempers]
+        + [pairs] * 4,
+        lows,
         2 * pair_flops,
         20,
     )
-    square, message, own, square_stats, square_weight, square_towards = call(
+    square, message, square_stats, square_weight, square_towards = call(
         square_kernel,
         "square_statistics",
         (arrays, stats, *foreign),
-        [jax.ShapeDtypeStruct((4, tokens, HD), jnp.bfloat16)] + [rows_of_stats] * 3 + [pairs] * 2,
+        [jax.ShapeDtypeStruct((4, tokens, HD), jnp.bfloat16)] + [rows_of_stats] * 2 + [pairs] * 2,
         [],
         2 * pair_flops,
         12,
     )
     swap = [(source, source ^ half_count) for source in range(seq_count)]
     received = lax.ppermute(message, "seq", swap)
-    parts, temper = call(
-        diagonal_kernel,
-        "own_diagonal_gradients",
-        (arrays, own, stats, own_weight, own_towards),
+    begun, across, temper = call(
+        first_kernel,
+        "gradients_before_totals",
+        (
+            arrays, square, stats, square_stats, temper, own_weight, own_towards,
+            other_weight, other_towards, square_weight, square_towards,
+        ),
         [
-            jax.ShapeDtypeStruct((3, tokens, HD), jnp.float32),
-            jax.ShapeDtypeStruct((8, HD), jnp.float32),
+            jax.ShapeDtypeStruct((half_count, 6 * BLK, HD), jnp.bfloat16),
+            jax.ShapeDtypeStruct((2, tokens, HD), jnp.bfloat16),
+            tempers,
         ],
         lows,
-        3 * pair_flops // 2,
+        4 * pair_flops,
         14,
     )
     within, *across = call(
         finish_kernel,
-        "remaining_gradients",
+        "gradients_after_totals",
         (
-            arrays, square, message, received, own, stats, square_stats, parts, temper,
-            square_weight, square_towards, other_weight, other_towards,
+            arrays, square, message, received, stats, square_stats, parts, temper,
+            square_weight, square_towards, other_weight, other_towards, across, begun,
         ),
         [jax.ShapeDtypeStruct((half_count, 6 * BLK + EXTRA, HD), jnp.bfloat16)]
         + [jax.ShapeDtypeStruct((2 * BLK + EXTRA, HD), jnp.bfloat16)] * half_count,
-        [pltpu.VMEM((2, tokens, HD), jnp.bfloat16), *lows],
-        5 * pair_flops,
+        [pltpu.VMEM((2, tokens, HD), jnp.bfloat16), pltpu.VMEM((8, HD), jnp.float32), *lows],
+        2 * pair_flops,
         20,
     )
     across = crossed(across, half_count)

time: 108 us -> 108 us (level)
  the two profiles are of different devices: /device:TPU:8 before, /device:TPU:10 now
where the time goes in v6:
time: 108 us; the launch traced here: 107 us
  waiting for transfers between devices  62.4 us (58%)
  starting transfers between devices  25.4 us (24%)
  Pallas kernels  17.9 us (17%)
    ppermute x16, waiting for transfers between devices, crossed(): lax.ppermute(chunk, 'seq', [(source, source ^ half_count + step) for sour...  58.1 us
    pallas_call x6, Pallas kernels, kernel_call(): pl.pallas_call(kernel, out_shape=out_shape, in_specs=in_specs, out_specs=...  17.9 us
    ppermute x16, starting transfers between devices, crossed(): lax.ppermute(chunk, 'seq', [(source, source ^ half_count + step) for sour...  16.8 us
    all_to_all x2, starting transfers between devices, exchange_within(): lax.all_to_all(array_in, 'seq', split_axis=0, concat_axis=0, axis_index_g...  7.93 us
    ppermute x1, waiting for transfers between devices, head_shards(): received = lax.ppermute(message, 'seq', swap)  2.75 us
  transfers between devices with their start and end apart: 20, of which 15 were waited for; matrix products, arithmetic and copies ran while one was open for 0% of the time, Pallas kernels for 7%

profile of v6, /device:TPU:10, one launch (start us, length us, event | category | flops | bytes accessed | tf_op | source)
XLA Modules:
  0.0 107.2 jit_solution(149645215598622569)
XLA Ops:
  0.6 2.9 %pack_heads.1 = (bf16[8,1024,128]{2,1,0:T(8,128)(2,1)}, bf16[256,128]{1,0:T(8,128)(2,1)}, bf16[256,128]{1,0:T(8,128)(2,1)}, bf16[256,128]{1,0:T(8,128)(2,1)}, bf...) custom-call(bf16[1,128,2048]{2,1,0:T(8,128)(2,1)} %refs_0_.1, ...), custom_call_target="tpu_custom_call" | custom-call | bytes 4718592 | tf_op jit(solution)/shard_map/pack_heads/pallas_call | solution.py:409
  3.7 4.4 %all-to-all-start = ((bf16[8,1024,128]{2,1,0:T(8,128)(2,1)}), bf16[8,1024,128]{2,1,0:T(8,128)(2,1)S(1)}, u32[]{:S(2)}, u32[]{:S(2)}) async-start(bf16[8,1024,128]{2,1,0:T(8,128)(2,1)} %get-tuple-element.41), calls=%async_computation | async-start | bytes 4194304 | tf_op jit(solution)/shard_map/all_to_all | solution.py:908
  8.1 2.6 %collective-permute-start = (bf16[256,128]{1,0:T(8,128)(2,1)S(1)}, bf16[256,128]{1,0:T(8,128)(2,1)S(1)}, u32[]{:S(2)}, u32[]{:S(2)}) collective-permute-start(bf16[256,128]{1,0:T(8,128)(2,1)S(1)} %copy-done.10), channel_id=1, source_target_pairs={{0,16},{2,18},{4,20},{6,22},{8,24},{10,26},{12,28},{14,30},{16,0},... | collective-permute-start | bytes 196616 | tf_op jit(solution)/shard_map/ppermute | solution.py:880
  10.7 3.3 %collective-permute-start.2 = (bf16[256,128]{1,0:T(8,128)(2,1)S(1)}, bf16[256,128]{1,0:T(8,128)(2,1)S(1)}, u32[]{:S(2)}, u32[]{:S(2)}) collective-permute-start(bf16[256,128]{1,0:T(8,128)(2,1)S(1)} %copy-done.8), channel_id=1, source_target_pairs={{0,20},{2,22},{4,16},{6,18},{8,28},{10,30},{12,24},{14,26},{16,4},... | collective-permute-start | bytes 196616 | tf_op jit(solution)/shard_map/ppermute | solution.py:880
  15.5 20.7 %collective-permute-done.refs_0_ = bf16[256,128]{1,0:T(8,128)(2,1)S(1)} collective-permute-done((bf16[256,128]{1,0:T(8,128)(2,1)S(1)}, bf16[256,128]{1,0:T(8,128)(2,1)S(1)}, u32[]{:S(2)}, u32[]{:S(2)}) %collective-permute-start) | collective-permute-done | bytes 65568 | tf_op jit(solution)/shard_map/ppermute | solution.py:880
  37.9 2.0 %collective-permute-done.2.refs_2_ = bf16[256,128]{1,0:T(8,128)(2,1)S(1)} collective-permute-done((bf16[256,128]{1,0:T(8,128)(2,1)S(1)}, bf16[256,128]{1,0:T(8,128)(2,1)S(1)}, u32[]{:S(2)}, u32[]{:S(2)}) %collective-permute-start.2) | collective-permute-done | bytes 65568 | tf_op jit(solution)/shard_map/ppermute | solution.py:880
  40.0 4.4 %diagonal_statistics.1 = (bf16[8,1024,128]{2,1,0:T(8,128)(2,1)S(1)}, f32[8,1024]{1,0:T(8,128)S(1)}, f32[3,1024,128]{2,1,0:T(8,128)S(1)}, f32[8,128]{1,0:T(8,128)...) custom-call(f32[16]{0:T(128)S(1)} %copy-done.1, ...), custom_call_target="tpu_custom_call" | custom-call | flops 536870912 | bytes 22582400 | tf_op jit(solution)/shard_map/diagonal_statistics/pallas_call | solution.py:409
  44.5 2.6 %collective-permute-done.5.refs_5_ = bf16[256,128]{1,0:T(8,128)(2,1)S(1)} collective-permute-done((bf16[256,128]{1,0:T(8,128)(2,1)S(1)}, bf16[256,128]{1,0:T(8,128)(2,1)S(1)}, u32[]{:S(2)}, u32[]{:S(2)}) %collective-permute-start.5) | collective-permute-done | bytes 65568 | tf_op jit(solution)/shard_map/ppermute | solution.py:880
  47.0 2.2 %collective-permute-done.6.refs_6_ = bf16[256,128]{1,0:T(8,128)(2,1)S(1)} collective-permute-done((bf16[256,128]{1,0:T(8,128)(2,1)S(1)}, bf16[256,128]{1,0:T(8,128)(2,1)S(1)}, u32[]{:S(2)}, u32[]{:S(2)}) %collective-permute-start.6) | collective-permute-done | bytes 65568 | tf_op jit(solution)/shard_map/ppermute | solution.py:880
  50.7 2.6 %square_statistics.1 = (bf16[4,1024,128]{2,1,0:T(8,128)(2,1)S(1)}, f32[8,1024]{1,0:T(8,128)S(1)}, f32[8,1024]{1,0:T(8,128)S(1)}, f32[1024,1024]{1,0:T(8,128)S(1)}, f32[1024,1024]{1,0:T(8,128)S(1)}) custom-call(f32[16]{0:T(128)S(1)} %copy-done.1, s32[16,16]{1,0:T(8,128)S(1)} %bitcast.2, s32[16]{0:T(128)S(1)} %copy-done.2, ...), custom_call_target="tpu_custom_call" | custom-call | flops 536870912 | bytes 12158080 | tf_op jit(solution)/shard_map/square_statistics/pallas_call | solution.py:409
  53.4 2.0 %gradients_before_totals.1 = (bf16[8,768,128]{2,1,0:T(8,128)(2,1)S(1)}, bf16[2,1024,128]{2,1,0:T(8,128)(2,1)S(1)}, f32[8,128]{1,0:T(8,128)S(1)}) custom-call(f32[16]{0:T(128)S(1)} %copy-done.1, s32[16,16]{1,0:T(8,128)S(1)} %bitcast.3, s32[16]{0:T(128)S(1)} %copy-done.2, bf16[8,1024,128]{2,1,0:T(8,128)(2,1)S(1)} %get-tuple-element.42.arrays_ref, ...), custom_call_target="tpu_custom_call" | custom-call | flops 1073741824 | bytes 30483584 | tf_op jit(solution)/shard_map/gradients_before_totals/pallas_call | solution.py:409
  55.5 2.8 %collective-permute-done.8.received_ref = f32[8,1024]{1,0:T(8,128)S(1)} collective-permute-done((f32[8,1024]{1,0:T(8,128)S(1)}, f32[8,1024]{1,0:T(8,128)S(1)}, u32[]{:S(2)}, u32[]{:S(2)}) %collective-permute-start.8) | collective-permute-done | bytes 32800 | tf_op jit(solution)/shard_map/ppermute | solution.py:951
  58.2 4.3 %gradients_after_totals.1 = (bf16[8,784,128]{2,1,0:T(8,128)(2,1)}, bf16[272,128]{1,0:T(8,128)(2,1)S(1)}, bf16[272,128]{1,0:T(8,128)(2,1)S(1)}, bf16[272,128]{1,0...) custom-call(f32[16]{0:T(128)S(1)} %copy-done.1, ...), custom_call_target="tpu_custom_call" | custom-call | flops 536870912 | bytes 25891968 | tf_op jit(solution)/shard_map/gradients_after_totals/pallas_call | solution.py:409
  62.5 3.5 %all-to-all-start.1 = ((bf16[8,784,128]{2,1,0:T(8,128)(2,1)}), bf16[8,784,128]{2,1,0:T(8,128)(2,1)S(1)}, u32[]{:S(2)}, u32[]{:S(2)}) async-start(bf16[8,784,128]{2,1,0:T(8,128)(2,1)} %get-tuple-element.66), calls=%async_computation.1 | async-start | bytes 3211264 | tf_op jit(solution)/shard_map/all_to_all | solution.py:908
  68.2 2.2 %collective-permute-start.11 = (bf16[272,128]{1,0:T(8,128)(2,1)S(1)}, bf16[272,128]{1,0:T(8,128)(2,1)S(1)}, u32[]{:S(2)}, u32[]{:S(2)}) collective-permute-start(bf16[272,128]{1,0:T(8,128)(2,1)S(1)} %get-tuple-element.69), channel_id=1, source_target_pairs={{0,20},{2,22},{4,16},{6,18},{8,28},{10,30},{12,24},{14,26},{16,4},... | collective-permute-start | bytes 208904 | tf_op jit(solution)/shard_map/ppermute | solution.py:880
  70.4 1.9 %collective-permute-start.12 = (bf16[272,128]{1,0:T(8,128)(2,1)S(1)}, bf16[272,128]{1,0:T(8,128)(2,1)S(1)}, u32[]{:S(2)}, u32[]{:S(2)}) collective-permute-start(bf16[272,128]{1,0:T(8,128)(2,1)S(1)} %get-tuple-element.70), channel_id=1, source_target_pairs={{0,22},{2,20},{4,18},{6,16},{8,30},{10,28},{12,26},{14,24},{16,6},... | collective-permute-start | bytes 208904 | tf_op jit(solution)/shard_map/ppermute | solution.py:880
  72.3 15.4 %collective-permute-done.9.refs_0_ = bf16[272,128]{1,0:T(8,128)(2,1)S(1)} collective-permute-done((bf16[272,128]{1,0:T(8,128)(2,1)S(1)}, bf16[272,128]{1,0:T(8,128)(2,1)S(1)}, u32[]{:S(2)}, u32[]{:S(2)}) %collective-permute-start.9) | collective-permute-done | bytes 69664 | tf_op jit(solution)/shard_map/ppermute | solution.py:880
  87.8 1.9 %collective-permute-start.15 = (bf16[272,128]{1,0:T(8,128)(2,1)S(1)}, bf16[272,128]{1,0:T(8,128)(2,1)S(1)}, u32[]{:S(2)}, u32[]{:S(2)}) collective-permute-start(bf16[272,128]{1,0:T(8,128)(2,1)S(1)} %get-tuple-element.73), channel_id=1, source_target_pairs={{0,28},{2,30},{4,24},{6,26},{8,20},{10,22},{12,16},{14,18},{16,12}... | collective-permute-start | bytes 208904 | tf_op jit(solution)/shard_map/ppermute | solution.py:880
  89.7 1.7 %collective-permute-done.11.refs_2_ = bf16[272,128]{1,0:T(8,128)(2,1)S(1)} collective-permute-done((bf16[272,128]{1,0:T(8,128)(2,1)S(1)}, bf16[272,128]{1,0:T(8,128)(2,1)S(1)}, u32[]{:S(2)}, u32[]{:S(2)}) %collective-permute-start.11) | collective-permute-done | bytes 69664 | tf_op jit(solution)/shard_map/ppermute | solution.py:880
  92.0 7.0 %collective-permute-done.14.refs_5_ = bf16[272,128]{1,0:T(8,128)(2,1)S(1)} collective-permute-done((bf16[272,128]{1,0:T(8,128)(2,1)S(1)}, bf16[272,128]{1,0:T(8,128)(2,1)S(1)}, u32[]{:S(2)}, u32[]{:S(2)}) %collective-permute-start.14) | collective-permute-done | bytes 69664 | tf_op jit(solution)/shard_map/ppermute | solution.py:880
  99.0 2.2 %collective-permute-done.15.refs_6_ = bf16[272,128]{1,0:T(8,128)(2,1)S(1)} collective-permute-done((bf16[272,128]{1,0:T(8,128)(2,1)S(1)}, bf16[272,128]{1,0:T(8,128)(2,1)S(1)}, u32[]{:S(2)}, u32[]{:S(2)}) %collective-permute-start.15) | collective-permute-done | bytes 69664 | tf_op jit(solution)/shard_map/ppermute | solution.py:880
  101.3 1.6 %collective-permute-done.16.refs_7_ = bf16[272,128]{1,0:T(8,128)(2,1)S(1)} collective-permute-done((bf16[272,128]{1,0:T(8,128)(2,1)S(1)}, bf16[272,128]{1,0:T(8,128)(2,1)S(1)}, u32[]{:S(2)}, u32[]{:S(2)}) %collective-permute-start.16) | collective-permute-done | bytes 69664 | tf_op jit(solution)/shard_map/ppermute | solution.py:880
  103.5 1.5 %unpack_heads.1 = (bf16[1,128,2048]{2,1,0:T(8,128)(2,1)}, bf16[1,128,2048]{2,1,0:T(8,128)(2,1)}, bf16[1,128,2048]{2,1,0:T(8,128)(2,1)}) custom-call(bf16[8,784,128]{2,1,0:T(8,128)(2,1)S(1)} %all-to-all-done.1.within_ref, bf16[272,128]{1,0:T(8,128)(2,1)S(1)} %collective-permute-done.9.refs_0_, bf16[272,128]{1,0:T(8,128)(2,1)S(1)} %collective-permute-done.10.refs_1_, ...), custom_call_target="tpu_custom_call" | custom-call | bytes 3735552 | tf_op jit(solution)/shard_map/unpack_heads/pallas_call | solution.py:409
  105.0 1.6 %collective-permute-done.17 = f32[16,128]{1,0:T(8,128)S(1)} collective-permute-done((f32[16,128]{1,0:T(8,128)S(1)}, f32[16,128]{1,0:T(8,128)S(1)}, u32[]{:S(2)}, u32[]{:S(2)}) %collective-permute-start.17) | collective-permute-done | bytes 8224 | tf_op jit(solution)/shard_map/ppermute | solution.py:987
  (46 shorter events, 8.9 us)
Async XLA Ops:
  3.6 36.3 %copy-start.3 = (bf16[256,128]{1,0:T(8,128)(2,1)S(1)}, bf16[256,128]{1,0:T(8,128)(2,1)}, u32[]{:S(2)}) copy-start(bf16[256,128]{1,0:T(8,128)(2,1)} %get-tuple-element.51) | copy-start | bytes 196612
  3.7 36.3 %copy-start = (s32[1,16,16,1]{2,3,1,0:T(1,128)S(1)}, s32[1,16,16,1]{2,3,1,0:T(1,128)}, u32[]{:S(2)}) copy-start(s32[1,16,16,1]{2,3,1,0:T(1,128)} %param.12) | copy-start | bytes 3076
  3.7 36.3 %copy-start.1 = (f32[16]{0:T(128)S(1)}, f32[16]{0:T(128)}, u32[]{:S(2)}) copy-start(f32[16]{0:T(128)} %softness_ref.7) | copy-start | bytes 196
  3.7 36.3 %copy-start.2 = (s32[16]{0:T(128)S(1)}, s32[16]{0:T(128)}, u32[]{:S(2)}) copy-start(s32[16]{0:T(128)} %span_ref.7) | copy-start | bytes 196
  3.7 36.3 %all-to-all-start = ((bf16[8,1024,128]{2,1,0:T(8,128)(2,1)}), bf16[8,1024,128]{2,1,0:T(8,128)(2,1)S(1)}, u32[]{:S(2)}, u32[]{:S(2)}) async-start(bf16[8,1024,128]{2,1,0:T(8,128)(2,1)} %get-tuple-element.41), calls=%async_computation | async-start | bytes 4194304 | tf_op jit(solution)/shard_map/all_to_all | solution.py:908
  8.1 28.1 %collective-permute-start = (bf16[256,128]{1,0:T(8,128)(2,1)S(1)}, bf16[256,128]{1,0:T(8,128)(2,1)S(1)}, u32[]{:S(2)}, u32[]{:S(2)}) collective-permute-start(bf16[256,128]{1,0:T(8,128)(2,1)S(1)} %copy-done.10), channel_id=1, source_target_pairs={{0,16},{2,18},{4,20},{6,22},{8,24},{10,26},{12,28},{14,30},{16,0},... | collective-permute-start | bytes 196616 | tf_op jit(solution)/shard_map/ppermute | solution.py:880
  10.7 26.0 %collective-permute-start.1 = (bf16[256,128]{1,0:T(8,128)(2,1)S(1)}, bf16[256,128]{1,0:T(8,128)(2,1)S(1)}, u32[]{:S(2)}, u32[]{:S(2)}) collective-permute-start(bf16[256,128]{1,0:T(8,128)(2,1)S(1)} %copy-done.9), channel_id=1, source_target_pairs={{0,18},{2,16},{4,22},{6,20},{8,26},{10,24},{12,30},{14,28},{16,2},... | collective-permute-start | bytes 196616 | tf_op jit(solution)/shard_map/ppermute | solution.py:880
  10.7 29.3 %collective-permute-start.2 = (bf16[256,128]{1,0:T(8,128)(2,1)S(1)}, bf16[256,128]{1,0:T(8,128)(2,1)S(1)}, u32[]{:S(2)}, u32[]{:S(2)}) collective-permute-start(bf16[256,128]{1,0:T(8,128)(2,1)S(1)} %copy-done.8), channel_id=1, source_target_pairs={{0,20},{2,22},{4,16},{6,18},{8,28},{10,30},{12,24},{14,26},{16,4},... | collective-permute-start | bytes 196616 | tf_op jit(solution)/shard_map/ppermute | solution.py:880
  14.0 30.5 %collective-permute-start.3 = (bf16[256,128]{1,0:T(8,128)(2,1)S(1)}, bf16[256,128]{1,0:T(8,128)(2,1)S(1)}, u32[]{:S(2)}, u32[]{:S(2)}) collective-permute-start(bf16[256,128]{1,0:T(8,128)(2,1)S(1)} %copy-done.7), channel_id=1, source_target_pairs={{0,22},{2,20},{4,18},{6,16},{8,30},{10,28},{12,26},{14,24},{16,6},... | collective-permute-start | bytes 196616 | tf_op jit(solution)/shard_map/ppermute | solution.py:880
  14.3 30.2 %collective-permute-start.4 = (bf16[256,128]{1,0:T(8,128)(2,1)S(1)}, bf16[256,128]{1,0:T(8,128)(2,1)S(1)}, u32[]{:S(2)}, u32[]{:S(2)}) collective-permute-start(bf16[256,128]{1,0:T(8,128)(2,1)S(1)} %copy-done.6), channel_id=1, source_target_pairs={{0,24},{2,26},{4,28},{6,30},{8,16},{10,18},{12,20},{14,22},{16,8},... | collective-permute-start | bytes 196616 | tf_op jit(solution)/shard_map/ppermute | solution.py:880
  36.2 10.8 %collective-permute-start.5 = (bf16[256,128]{1,0:T(8,128)(2,1)S(1)}, bf16[256,128]{1,0:T(8,128)(2,1)S(1)}, u32[]{:S(2)}, u32[]{:S(2)}) collective-permute-start(bf16[256,128]{1,0:T(8,128)(2,1)S(1)} %copy-done.5), channel_id=1, source_target_pairs={{0,26},{2,24},{4,30},{6,28},{8,18},{10,16},{12,22},{14,20},{16,10}... | collective-permute-start | bytes 196616 | tf_op jit(solution)/shard_map/ppermute | solution.py:880
  36.7 12.5 %collective-permute-start.6 = (bf16[256,128]{1,0:T(8,128)(2,1)S(1)}, bf16[256,128]{1,0:T(8,128)(2,1)S(1)}, u32[]{:S(2)}, u32[]{:S(2)}) collective-permute-start(bf16[256,128]{1,0:T(8,128)(2,1)S(1)} %copy-done.4), channel_id=1, source_target_pairs={{0,28},{2,30},{4,24},{6,26},{8,20},{10,22},{12,16},{14,18},{16,12}... | collective-permute-start | bytes 196616 | tf_op jit(solution)/shard_map/ppermute | solution.py:880
  40.0 10.7 %collective-permute-start.7 = (bf16[256,128]{1,0:T(8,128)(2,1)S(1)}, bf16[256,128]{1,0:T(8,128)(2,1)S(1)}, u32[]{:S(2)}, u32[]{:S(2)}) collective-permute-start(bf16[256,128]{1,0:T(8,128)(2,1)S(1)} %copy-done.3), channel_id=1, source_target_pairs={{0,30},{2,28},{4,26},{6,24},{8,22},{10,20},{12,18},{14,16},{16,14}... | collective-permute-start | bytes 196616 | tf_op jit(solution)/shard_map/ppermute | solution.py:880
  53.3 4.9 %collective-permute-start.8 = (f32[8,1024]{1,0:T(8,128)S(1)}, f32[8,1024]{1,0:T(8,128)S(1)}, u32[]{:S(2)}, u32[]{:S(2)}) collective-permute-start(f32[8,1024]{1,0:T(8,128)S(1)} %get-tuple-element.53.message_ref), channel_id=1, source_target_pairs={{0,16},{2,18},{4,20},{6,22},{8,24},{10,26},{12,28},{14,30},{16,0},... | collective-permute-start | bytes 98312 | tf_op jit(solution)/shard_map/ppermute | solution.py:951
  62.5 40.3 %all-to-all-start.1 = ((bf16[8,784,128]{2,1,0:T(8,128)(2,1)}), bf16[8,784,128]{2,1,0:T(8,128)(2,1)S(1)}, u32[]{:S(2)}, u32[]{:S(2)}) async-start(bf16[8,784,128]{2,1,0:T(8,128)(2,1)} %get-tuple-element.66), calls=%async_computation.1 | async-start | bytes 3211264 | tf_op jit(solution)/shard_map/all_to_all | solution.py:908
  66.1 21.6 %collective-permute-start.9 = (bf16[272,128]{1,0:T(8,128)(2,1)S(1)}, bf16[272,128]{1,0:T(8,128)(2,1)S(1)}, u32[]{:S(2)}, u32[]{:S(2)}) collective-permute-start(bf16[272,128]{1,0:T(8,128)(2,1)S(1)} %get-tuple-element.67), channel_id=1, source_target_pairs={{0,16},{2,18},{4,20},{6,22},{8,24},{10,26},{12,28},{14,30},{16,0},... | collective-permute-start | bytes 208904 | tf_op jit(solution)/shard_map/ppermute | solution.py:880
  67.4 20.4 %collective-permute-start.10 = (bf16[272,128]{1,0:T(8,128)(2,1)S(1)}, bf16[272,128]{1,0:T(8,128)(2,1)S(1)}, u32[]{:S(2)}, u32[]{:S(2)}) collective-permute-start(bf16[272,128]{1,0:T(8,128)(2,1)S(1)} %get-tuple-element.68), channel_id=1, source_target_pairs={{0,18},{2,16},{4,22},{6,20},{8,26},{10,24},{12,30},{14,28},{16,2},... | collective-permute-start | bytes 208904 | tf_op jit(solution)/shard_map/ppermute | solution.py:880
  68.2 23.2 %collective-permute-start.11 = (bf16[272,128]{1,0:T(8,128)(2,1)S(1)}, bf16[272,128]{1,0:T(8,128)(2,1)S(1)}, u32[]{:S(2)}, u32[]{:S(2)}) collective-permute-start(bf16[272,128]{1,0:T(8,128)(2,1)S(1)} %get-tuple-element.69), channel_id=1, source_target_pairs={{0,20},{2,22},{4,16},{6,18},{8,28},{10,30},{12,24},{14,26},{16,4},... | collective-permute-start | bytes 208904 | tf_op jit(solution)/shard_map/ppermute | solution.py:880
  70.4 21.6 %collective-permute-start.12 = (bf16[272,128]{1,0:T(8,128)(2,1)S(1)}, bf16[272,128]{1,0:T(8,128)(2,1)S(1)}, u32[]{:S(2)}, u32[]{:S(2)}) collective-permute-start(bf16[272,128]{1,0:T(8,128)(2,1)S(1)} %get-tuple-element.70), channel_id=1, source_target_pairs={{0,22},{2,20},{4,18},{6,16},{8,30},{10,28},{12,26},{14,24},{16,6},... | collective-permute-start | bytes 208904 | tf_op jit(solution)/shard_map/ppermute | solution.py:880
  72.3 19.7 %collective-permute-start.13 = (bf16[272,128]{1,0:T(8,128)(2,1)S(1)}, bf16[272,128]{1,0:T(8,128)(2,1)S(1)}, u32[]{:S(2)}, u32[]{:S(2)}) collective-permute-start(bf16[272,128]{1,0:T(8,128)(2,1)S(1)} %get-tuple-element.71), channel_id=1, source_target_pairs={{0,24},{2,26},{4,28},{6,30},{8,16},{10,18},{12,20},{14,22},{16,8},... | collective-permute-start | bytes 208904 | tf_op jit(solution)/shard_map/ppermute | solution.py:880
  87.7 11.3 %collective-permute-start.14 = (bf16[272,128]{1,0:T(8,128)(2,1)S(1)}, bf16[272,128]{1,0:T(8,128)(2,1)S(1)}, u32[]{:S(2)}, u32[]{:S(2)}) collective-permute-start(bf16[272,128]{1,0:T(8,128)(2,1)S(1)} %get-tuple-element.72), channel_id=1, source_target_pairs={{0,26},{2,24},{4,30},{6,28},{8,18},{10,16},{12,22},{14,20},{16,10}... | collective-permute-start | bytes 208904 | tf_op jit(solution)/shard_map/ppermute | solution.py:880
  87.8 13.5 %collective-permute-start.15 = (bf16[272,128]{1,0:T(8,128)(2,1)S(1)}, bf16[272,128]{1,0:T(8,128)(2,1)S(1)}, u32[]{:S(2)}, u32[]{:S(2)}) collective-permute-start(bf16[272,128]{1,0:T(8,128)(2,1)S(1)} %get-tuple-element.73), channel_id=1, source_target_pairs={{0,28},{2,30},{4,24},{6,26},{8,20},{10,22},{12,16},{14,18},{16,12}... | collective-permute-start | bytes 208904 | tf_op jit(solution)/shard_map/ppermute | solution.py:880
  91.4 11.4 %collective-permute-start.16 = (bf16[272,128]{1,0:T(8,128)(2,1)S(1)}, bf16[272,128]{1,0:T(8,128)(2,1)S(1)}, u32[]{:S(2)}, u32[]{:S(2)}) collective-permute-start(bf16[272,128]{1,0:T(8,128)(2,1)S(1)} %get-tuple-element.74), channel_id=1, source_target_pairs={{0,30},{2,28},{4,26},{6,24},{8,22},{10,20},{12,18},{14,16},{16,14}... | collective-permute-start | bytes 208904 | tf_op jit(solution)/shard_map/ppermute | solution.py:880
  102.9 3.7 %collective-permute-start.17 = (f32[16,128]{1,0:T(8,128)S(1)}, f32[16,128]{1,0:T(8,128)S(1)}, u32[]{:S(2)}, u32[]{:S(2)}) collective-permute-start(f32[16,128]{1,0:T(8,128)S(1)} %temper_sums.1), channel_id=1, source_target_pairs={{0,1},{1,0},{2,3},{3,2},{4,5},{5,4},{6,7},{7,6},{8,9},{9,8},{10,11... | collective-permute-start | bytes 24584 | tf_op jit(solution)/shard_map/ppermute | solution.py:987
  (7 other events, 105.5 us)

commit v7 on v6

--- a/solution.py
+++ b/solution.py
@@ -421,8 +421,8 @@
 
 
 def pack_kernel(*refs, half_count):
-    arrays, within_ref, across_refs = refs[:4], refs[4], refs[5 : 5 + half_count]
-    held, within, across, arrival, left_within, left_across = refs[5 + half_count :]
+    arrays, within_ref, foreign_refs = refs[:4], refs[4], refs[5:7]
+    held, within, across, arrival, left_within, left_across = refs[7:]
     me, half, _ = position(half_count)
     piece = BLK // PIECES
     arrivals = [
@@ -455,13 +455,12 @@
             leaving[-1].start()
     first = jnp.where(half == 0, KEY, QUERY)
     second = jnp.where(half == 0, VALUE, GRAD)
-    for step, across_ref in enumerate(across_refs):
-        columns = columns_of(me ^ (half_count + step))
-        across[step, :BLK, :] = held[first, :, columns]
-        across[step, BLK:, :] = held[second, :, columns]
-        leaving.append(
-            pltpu.make_async_copy(across.at[step], across_ref, left_across.at[step])
-        )
+    for core, foreign_ref in enumerate(foreign_refs):
+        for step in range(half_count // 2):
+            columns = columns_of(me ^ core ^ (half_count + 2 * step))
+            across[core, step, :BLK, :] = held[first, :, columns]
+            across[core, step, BLK:, :] = held[second, :, columns]
+        leaving.append(pltpu.make_async_copy(across.at[core], foreign_ref, left_across.at[core]))
         leaving[-1].start()
     for copy in leaving:
         copy.wait()
@@ -469,21 +468,21 @@
 
 def packed(arrays, half_count):
     width = arrays[0].shape[2]
-    within_shape, across_shape = (half_count, 8 * BLK, HD), (2 * BLK, HD)
+    within_shape, across_shape = (half_count, 8 * BLK, HD), (half_count // 2, 2 * BLK, HD)
     return kernel_call(
         functools.partial(pack_kernel, half_count=half_count),
         "pack_heads",
         arrays,
         [pl.BlockSpec(memory_space=pl.ANY)] * 4,
         [jax.ShapeDtypeStruct(within_shape, jnp.bfloat16)]
-        + [jax.ShapeDtypeStruct(across_shape, jnp.bfloat16)] * half_count,
+        + [jax.ShapeDtypeStruct(across_shape, jnp.bfloat16)] * 2,
         [
             pltpu.VMEM((4, BLK, width), jnp.bfloat16),
             pltpu.VMEM(within_shape, jnp.bfloat16),
-            pltpu.VMEM((half_count, *across_shape), jnp.bfloat16),
+            pltpu.VMEM((2, *across_shape), jnp.bfloat16),
             pltpu.SemaphoreType.DMA((4, PIECES)),
             pltpu.SemaphoreType.DMA((4, 2)),
-            pltpu.SemaphoreType.DMA((half_count,)),
+            pltpu.SemaphoreType.DMA((2,)),
         ],
         60,
         out_space=pl.ANY,
@@ -685,15 +684,16 @@
 def square_kernel(
     softness_ref, ids_ref, span_ref, arrays_ref, stats_ref, *refs, half_count
 ):
-    across_refs = refs[:half_count]
-    square_ref, message_ref, square_stats, weight, towards = refs[half_count:]
+    across_refs = refs[: half_count // 2]
+    square_ref, message_ref, square_stats, weight, towards = refs[half_count // 2 :]
     _, half, place = position(half_count)
     first = jnp.where(half == 0, QUERY, KEY)
     second = jnp.where(half == 0, GRAD, VALUE)
     for step, across_ref in enumerate(across_refs):
-        rows = rows_of(place ^ step)
-        square_ref[first, rows, :] = across_ref[:BLK, :]
-        square_ref[second, rows, :] = across_ref[BLK:, :]
+        for core in range(2):
+            rows = rows_of(place ^ core ^ (2 * step))
+            square_ref[first, rows, :] = across_ref[core, :BLK, :]
+            square_ref[second, rows, :] = across_ref[core, BLK:, :]
     kept_first = jnp.where(half == 0, KEY, QUERY)
     kept_second = jnp.where(half == 0, VALUE, GRAD)
     square_ref[kept_first, :, :] = arrays_ref[kept_first, :, :]
@@ -776,8 +776,8 @@
     square_weight, square_towards, other_weight, other_towards, across_in, begun_ref,
     within_ref, *refs, half_count
 ):
-    across_refs = refs[:half_count]
-    across, temper, *scratch = refs[half_count:]
+    foreign_refs = refs[:2]
+    across, temper, *scratch = refs[2:]
     _, half, place = position(half_count)
     settings = (softness_ref, ids_ref, span_ref)
     temper[...] = temper_ref[...]
@@ -812,15 +812,16 @@
     pieces = temper_rows(temper[0:1, :], temper[1:2, :])
     for block in range(half_count):
         within_ref[block, 6 * BLK : 6 * BLK + EXTRA, :] = pieces
-    for step, across_ref in enumerate(across_refs):
-        rows = rows_of(place ^ step)
-        across_ref[:BLK, :] = across[0, rows, :]
-        across_ref[BLK : 2 * BLK, :] = across[1, rows, :]
-        across_ref[2 * BLK :, :] = pieces
+    for core, foreign_ref in enumerate(foreign_refs):
+        for step in range(half_count // 2):
+            rows = rows_of(place ^ core ^ (2 * step))
+            foreign_ref[step, :BLK, :] = across[0, rows, :]
+            foreign_ref[step, BLK : 2 * BLK, :] = across[1, rows, :]
+            foreign_ref[step, 2 * BLK :, :] = pieces
 
 
 def temper_kernel(within_ref, *refs, half_count):
-    across_refs, temper_ref = refs[:half_count], refs[half_count]
+    across_refs, temper_ref = refs[: half_count // 2], refs[half_count // 2]
     _, half, place = position(half_count)
 
     def sums(rows):
@@ -830,10 +831,11 @@
         ]
 
     for step, across_ref in enumerate(across_refs):
-        peer = place ^ step
-        near, far = sums(within_ref[peer]), sums(across_ref[...])
-        temper_ref[pl.ds(half * half_count + peer, 1), :] = near[0] + far[1]
-        temper_ref[pl.ds((1 - half) * half_count + peer, 1), :] = near[1] + far[0]
+        for core in range(2):
+            peer = place ^ core ^ (2 * step)
+            near, far = sums(within_ref[peer]), sums(across_ref[core])
+            temper_ref[pl.ds(half * half_count + peer, 1), :] = near[0] + far[1]
+            temper_ref[pl.ds((1 - half) * half_count + peer, 1), :] = near[1] + far[0]
 
 
 def temper_sums(within, across, half_count):
@@ -843,7 +845,7 @@
         grid=(1,),
         out_shape=jax.ShapeDtypeStruct((2 * half_count, HD), jnp.float32),
         in_specs=[pl.BlockSpec((half_count, EXTRA, HD), lambda step: (0, last[0], 0))]
-        + [pl.BlockSpec((EXTRA, HD), lambda step: (last[1], 0))] * half_count,
+        + [pl.BlockSpec((2, EXTRA, HD), lambda step: (0, last[1], 0))] * (half_count // 2),
         out_specs=pl.BlockSpec((2 * half_count, HD), lambda step: (0, 0)),
         compiler_params=pltpu.CompilerParams(vmem_limit_bytes=4 * MIB),
         name="temper_sums",
@@ -851,34 +853,53 @@
 
 
 def unpack_kernel(within_ref, *refs, half_count):
-    across_refs = refs[:half_count]
-    query_ref, key_ref, value_ref = refs[half_count:]
+    across_refs = refs[: half_count // 2]
+    out_refs = refs[half_count // 2 :]
     _, half, place = position(half_count)
     for step, across_ref in enumerate(across_refs):
-        peer = place ^ step
-        other = columns_of((1 - half) * half_count + peer)
-        own = columns_of(half * half_count + peer)
-        parts = [within_ref[peer, array * BLK : (array + 1) * BLK, :] for array in range(6)]
-        for array, out_ref in enumerate((query_ref, key_ref, value_ref)):
-            out_ref[0, :, own] = parts[array]
-        first = across_ref[:BLK, :].astype(jnp.float32)
-        second = across_ref[BLK : 2 * BLK, :].astype(jnp.float32)
-        added = (
-            jnp.where(half == 0, 0.0, first),
-            jnp.where(half == 0, first, 0.0),
-            jnp.where(half == 0, second, 0.0),
-        )
-        for array, out_ref in enumerate((query_ref, key_ref, value_ref)):
-            out_ref[0, :, other] = (parts[3 + array].astype(jnp.float32) + added[array]).astype(
-                jnp.bfloat16
+        for core in range(2):
+            peer = place ^ core ^ (2 * step)
+            other = columns_of((1 - half) * half_count + peer)
+            own = columns_of(half * half_count + peer)
+            first = across_ref[core, :BLK, :].astype(jnp.float32)
+            second = across_ref[core, BLK : 2 * BLK, :].astype(jnp.float32)
+            added = (
+                jnp.where(half == 0, 0.0, first),
+                jnp.where(half == 0, first, 0.0),
+                jnp.where(half == 0, second, 0.0),
             )
-
-
-def crossed(chunks, half_count):
-    pairs = range(2 * half_count)
+            for array, out_ref in enumerate(out_refs):
+                out_ref[0, :, own] = within_ref[peer, array * BLK : (array + 1) * BLK, :]
+                kept = within_ref[peer, (3 + array) * BLK : (4 + array) * BLK, :]
+                out_ref[0, :, other] = (kept.astype(jnp.float32) + added[array]).astype(
+                    jnp.bfloat16
+                )
+
+
+def join_kernel(kept_ref, taken_ref, *out_refs):
+    for step, out_ref in enumerate(out_refs):
+        out_ref[0] = kept_ref[step]
+        out_ref[1] = taken_ref[step]
+
+
+def crossed(kept, given, half_count):
+    devices = range(2 * half_count)
+    steps, *shape = kept.shape
+    taken = lax.ppermute(given, "seq", [(source, source ^ 1) for source in devices])
+    messages = kernel_call(
+        join_kernel,
+        "join_chunks",
+        (kept, taken),
+        [pl.BlockSpec(memory_space=pltpu.VMEM)] * 2,
+        [jax.ShapeDtypeStruct((2, *shape), jnp.bfloat16)] * steps,
+        [],
+        4,
+    )
     return [
-        lax.ppermute(chunk, "seq", [(source, source ^ (half_count + step)) for source in pairs])
-        for step, chunk in enumerate(chunks)
+        lax.ppermute(
+            message, "seq", [(source, source ^ (half_count + 2 * step)) for source in devices]
+        )
+        for step, message in enumerate(messages)
     ]
 
 
@@ -925,7 +946,7 @@
         (probe_vectors, lookup_vectors, content_vectors, result_cotangent), half_count
     )
     arrived = exchange_within(sent)
-    foreign = crossed(foreign, half_count)
+    foreign = crossed(*foreign, half_count)
     kept_parts = jax.ShapeDtypeStruct((3, tokens, HD), jnp.float32)
     tempers = jax.ShapeDtypeStruct((8, HD), jnp.float32)
     arrays, stats, parts, temper, own_weight, own_towards, other_weight, other_towards = call(
@@ -965,7 +986,7 @@
         4 * pair_flops,
         14,
     )
-    within, *across = call(
+    within, *foreign = call(
         finish_kernel,
         "gradients_after_totals",
         (
@@ -973,12 +994,12 @@
             square_weight, square_towards, other_weight, other_towards, across, begun,
         ),
         [jax.ShapeDtypeStruct((half_count, 6 * BLK + EXTRA, HD), jnp.bfloat16)]
-        + [jax.ShapeDtypeStruct((2 * BLK + EXTRA, HD), jnp.bfloat16)] * half_count,
+        + [jax.ShapeDtypeStruct((half_count // 2, 2 * BLK + EXTRA, HD), jnp.bfloat16)] * 2,
         [pltpu.VMEM((2, tokens, HD), jnp.bfloat16), pltpu.VMEM((8, HD), jnp.float32), *lows],
         2 * pair_flops,
         20,
     )
-    across = crossed(across, half_count)
+    across = crossed(*foreign, half_count)
     within = exchange_within(within)
     tempers = temper_sums(within, across, half_count)
     temper_total = tempers
@@ -989,7 +1010,7 @@
         functools.partial(unpack_kernel, half_count=half_count),
         "unpack_heads",
         (within, *across),
-        [vmem] * (1 + half_count),
+        [vmem] * (1 + len(across)),
         [jax.ShapeDtypeStruct(probe_vectors.shape, jnp.bfloat16)] * 3,
         [],
         10,

time: 108 us -> 103 us (0.954)
  the two profiles are of different devices: /device:TPU:10 before, /device:TPU:0 now
where the time goes in v7:
time: 103 us
  waiting for transfers between devices  56.3 us (55%)
  starting transfers between devices  26.9 us (26%)
  Pallas kernels  18 us (17%)
    ppermute x8, waiting for transfers between devices, crossed(): lax.ppermute(message, 'seq', [(source, source ^ half_count + 2 * step) fo...  28.4 us
    all_to_all x2, waiting for transfers between devices, exchange_within(): lax.all_to_all(array_in, 'seq', split_axis=0, concat_axis=0, axis_index_g...  21.7 us
    pallas_call x8, Pallas kernels, kernel_call(): pl.pallas_call(kernel, out_shape=out_shape, in_specs=in_specs, out_specs=...  17.9 us
    ppermute x8, starting transfers between devices, crossed(): lax.ppermute(message, 'seq', [(source, source ^ half_count + 2 * step) fo...  15.4 us
    all_to_all x2, starting transfers between devices, exchange_within(): lax.all_to_all(array_in, 'seq', split_axis=0, concat_axis=0, axis_index_g...  8.98 us
    ppermute x1, waiting for transfers between devices, head_shards(): received = lax.ppermute(message, 'seq', swap)  2.86 us
    ppermute x2, waiting for transfers between devices, crossed(): lax.ppermute(given, 'seq', [(source, source ^ 1) for source in devices])  2.73 us
  transfers between devices with their start and end apart: 14, of which 11 were waited for; matrix products, arithmetic and copies ran while one was open for 0% of the time, Pallas kernels for 8%

profile of v7, /device:TPU:0, one launch (start us, length us, event | category | flops | bytes accessed | tf_op | source)
XLA Modules:
  0.0 102.6 jit_solution(10167757766032185299)
XLA Ops:
  0.6 2.9 %pack_heads.1 = (bf16[8,1024,128]{2,1,0:T(8,128)(2,1)}, bf16[4,256,128]{2,1,0:T(8,128)(2,1)}, bf16[4,256,128]{2,1,0:T(8,128)(2,1)}) custom-call(bf16[1,128,2048]{2,1,0:T(8,128)(2,1)} %refs_0_.1, bf16[1,128,2048]{2,1,0:T(8,128)(2,1)} %refs_1_.1, bf16[1,128,2048]{2,1,0:T(8,128)(2,1)} %refs_2_.1, bf16[1,128,2048]{2,1,0:T(8,128)(2,1)} %refs_3_.1), custom_call_target="tpu_custom_call" | custom-call | bytes 4718592 | tf_op jit(solution)/shard_map/pack_heads/pallas_call | solution.py:409
  3.6 5.4 %all-to-all-start = ((bf16[8,1024,128]{2,1,0:T(8,128)(2,1)}), bf16[8,1024,128]{2,1,0:T(8,128)(2,1)S(1)}, u32[]{:S(2)}, u32[]{:S(2)}) async-start(bf16[8,1024,128]{2,1,0:T(8,128)(2,1)} %get-tuple-element.37), calls=%async_computation | async-start | bytes 4194304 | tf_op jit(solution)/shard_map/all_to_all | solution.py:929
  9.5 1.4 %collective-permute-done.taken_ref = bf16[4,256,128]{2,1,0:T(8,128)(2,1)S(1)} collective-permute-done((bf16[4,256,128]{2,1,0:T(8,128)(2,1)S(1)}, bf16[4,256,128]{2,1,0:T(8,128)(2,1)S(1)}, u32[]{:S(2)}, u32[]{:S(2)}) %collective-permute-start) | collective-permute-done | bytes 262176 | tf_op jit(solution)/shard_map/ppermute | solution.py:888
  11.0 2.7 %collective-permute-start.1 = (bf16[2,256,128]{2,1,0:T(8,128)(2,1)S(1)}, bf16[2,256,128]{2,1,0:T(8,128)(2,1)S(1)}, u32[]{:S(2)}, u32[]{:S(2)}) collective-permute-start(bf16[2,256,128]{2,1,0:T(8,128)(2,1)S(1)} %get-tuple-element.42), channel_id=1, source_target_pairs={{0,16},{2,18},{4,20},{6,22},{8,24},{10,26},{12,28},{14,30},{16,0},... | collective-permute-start | bytes 393224 | tf_op jit(solution)/shard_map/ppermute | solution.py:899
  13.6 1.5 %collective-permute-start.2 = (bf16[2,256,128]{2,1,0:T(8,128)(2,1)S(1)}, bf16[2,256,128]{2,1,0:T(8,128)(2,1)S(1)}, u32[]{:S(2)}, u32[]{:S(2)}) collective-permute-start(bf16[2,256,128]{2,1,0:T(8,128)(2,1)S(1)} %get-tuple-element.43), channel_id=1, source_target_pairs={{0,20},{2,22},{4,16},{6,18},{8,28},{10,30},{12,24},{14,26},{16,4},... | collective-permute-start | bytes 393224 | tf_op jit(solution)/shard_map/ppermute | solution.py:899
  15.1 3.5 %collective-permute-start.3 = (bf16[2,256,128]{2,1,0:T(8,128)(2,1)S(1)}, bf16[2,256,128]{2,1,0:T(8,128)(2,1)S(1)}, u32[]{:S(2)}, u32[]{:S(2)}) collective-permute-start(bf16[2,256,128]{2,1,0:T(8,128)(2,1)S(1)} %get-tuple-element.44), channel_id=1, source_target_pairs={{0,24},{2,26},{4,28},{6,30},{8,16},{10,18},{12,20},{14,22},{16,8},... | collective-permute-start | bytes 393224 | tf_op jit(solution)/shard_map/ppermute | solution.py:899
  18.7 21.7 %all-to-all-done.in_ref = bf16[8,1024,128]{2,1,0:T(8,128)(2,1)S(1)} async-done(((bf16[8,1024,128]{2,1,0:T(8,128)(2,1)}), bf16[8,1024,128]{2,1,0:T(8,128)(2,1)S(1)}, u32[]{:S(2)}, u32[]{:S(2)}) %all-to-all-start) | async-done | bytes 2097184 | tf_op jit(solution)/shard_map/all_to_all | solution.py:929
  40.4 4.4 %diagonal_statistics.1 = (bf16[8,1024,128]{2,1,0:T(8,128)(2,1)S(1)}, f32[8,1024]{1,0:T(8,128)S(1)}, f32[3,1024,128]{2,1,0:T(8,128)S(1)}, f32[8,128]{1,0:T(8,128)...) custom-call(f32[16]{0:T(128)S(1)} %copy-done.2, ...), custom_call_target="tpu_custom_call" | custom-call | flops 536870912 | bytes 22582400 | tf_op jit(solution)/shard_map/diagonal_statistics/pallas_call | solution.py:409
  45.7 3.2 %collective-permute-done.4.refs_3_ = bf16[2,256,128]{2,1,0:T(8,128)(2,1)S(1)} collective-permute-done((bf16[2,256,128]{2,1,0:T(8,128)(2,1)S(1)}, bf16[2,256,128]{2,1,0:T(8,128)(2,1)S(1)}, u32[]{:S(2)}, u32[]{:S(2)}) %collective-permute-start.4) | collective-permute-done | bytes 131104 | tf_op jit(solution)/shard_map/ppermute | solution.py:899
  48.9 2.6 %square_statistics.1 = (bf16[4,1024,128]{2,1,0:T(8,128)(2,1)S(1)}, f32[8,1024]{1,0:T(8,128)S(1)}, f32[8,1024]{1,0:T(8,128)S(1)}, f32[1024,1024]{1,0:T(8,128)S(1)}, f32[1024,1024]{1,0:T(8,128)S(1)}) custom-call(f32[16]{0:T(128)S(1)} %copy-done.2, s32[16,16]{1,0:T(8,128)S(1)} %bitcast.2, s32[16]{0:T(128)S(1)} %copy-done.3, ...), custom_call_target="tpu_custom_call" | custom-call | flops 536870912 | bytes 12158080 | tf_op jit(solution)/shard_map/square_statistics/pallas_call | solution.py:409
  51.6 2.0 %gradients_before_totals.1 = (bf16[8,768,128]{2,1,0:T(8,128)(2,1)S(1)}, bf16[2,1024,128]{2,1,0:T(8,128)(2,1)S(1)}, f32[8,128]{1,0:T(8,128)S(1)}) custom-call(f32[16]{0:T(128)S(1)} %copy-done.2, s32[16,16]{1,0:T(8,128)S(1)} %bitcast.3, s32[16]{0:T(128)S(1)} %copy-done.3, bf16[8,1024,128]{2,1,0:T(8,128)(2,1)S(1)} %get-tuple-element.38.arrays_ref, ...), custom_call_target="tpu_custom_call" | custom-call | flops 1073741824 | bytes 30483584 | tf_op jit(solution)/shard_map/gradients_before_totals/pallas_call | solution.py:409
  53.7 2.9 %collective-permute-done.5.received_ref = f32[8,1024]{1,0:T(8,128)S(1)} collective-permute-done((f32[8,1024]{1,0:T(8,128)S(1)}, f32[8,1024]{1,0:T(8,128)S(1)}, u32[]{:S(2)}, u32[]{:S(2)}) %collective-permute-start.5) | collective-permute-done | bytes 32800 | tf_op jit(solution)/shard_map/ppermute | solution.py:972
  56.5 4.3 %gradients_after_totals.1 = (bf16[8,784,128]{2,1,0:T(8,128)(2,1)}, bf16[4,272,128]{2,1,0:T(8,128)(2,1)S(1)}, bf16[4,272,128]{2,1,0:T(8,128)(2,1)S(1)}) custom-call(f32[16]{0:T(128)S(1)} %copy-done.2, s32[16,16]{1,0:T(8,128)S(1)} %bitcast.4, s32[16]{0:T(128)S(1)} %copy-done.3, bf16[8,1024,128]{2,1,0:T(8,128)(2,1)S(1)} %get-tuple-element.38.arrays_ref, ...), custom_call_target="tpu_custom_call" | custom-call | flops 536870912 | bytes 25891968 | tf_op jit(solution)/shard_map/gradients_after_totals/pallas_call | solution.py:409
  60.8 3.6 %all-to-all-start.1 = ((bf16[8,784,128]{2,1,0:T(8,128)(2,1)}), bf16[8,784,128]{2,1,0:T(8,128)(2,1)S(1)}, u32[]{:S(2)}, u32[]{:S(2)}) async-start(bf16[8,784,128]{2,1,0:T(8,128)(2,1)} %get-tuple-element.60), calls=%async_computation.1 | async-start | bytes 3211264 | tf_op jit(solution)/shard_map/all_to_all | solution.py:929
  64.8 1.3 %collective-permute-done.6.taken_ref = bf16[4,272,128]{2,1,0:T(8,128)(2,1)S(1)} collective-permute-done((bf16[4,272,128]{2,1,0:T(8,128)(2,1)S(1)}, bf16[4,272,128]{2,1,0:T(8,128)(2,1)S(1)}, u32[]{:S(2)}, u32[]{:S(2)}) %collective-permute-start.6) | collective-permute-done | bytes 278560 | tf_op jit(solution)/shard_map/ppermute | solution.py:888
  67.5 2.9 %collective-permute-start.8 = (bf16[2,272,128]{2,1,0:T(8,128)(2,1)S(1)}, bf16[2,272,128]{2,1,0:T(8,128)(2,1)S(1)}, u32[]{:S(2)}, u32[]{:S(2)}) collective-permute-start(bf16[2,272,128]{2,1,0:T(8,128)(2,1)S(1)} %get-tuple-element.64), channel_id=1, source_target_pairs={{0,20},{2,22},{4,16},{6,18},{8,28},{10,30},{12,24},{14,26},{16,4},... | collective-permute-start | bytes 417800 | tf_op jit(solution)/shard_map/ppermute | solution.py:899
  70.4 2.1 %collective-permute-start.9 = (bf16[2,272,128]{2,1,0:T(8,128)(2,1)S(1)}, bf16[2,272,128]{2,1,0:T(8,128)(2,1)S(1)}, u32[]{:S(2)}, u32[]{:S(2)}) collective-permute-start(bf16[2,272,128]{2,1,0:T(8,128)(2,1)S(1)} %get-tuple-element.65), channel_id=1, source_target_pairs={{0,24},{2,26},{4,28},{6,30},{8,16},{10,18},{12,20},{14,22},{16,8},... | collective-permute-start | bytes 417800 | tf_op jit(solution)/shard_map/ppermute | solution.py:899
  72.5 1.4 %collective-permute-start.10 = (bf16[2,272,128]{2,1,0:T(8,128)(2,1)S(1)}, bf16[2,272,128]{2,1,0:T(8,128)(2,1)S(1)}, u32[]{:S(2)}, u32[]{:S(2)}) collective-permute-start(bf16[2,272,128]{2,1,0:T(8,128)(2,1)S(1)} %get-tuple-element.66), channel_id=1, source_target_pairs={{0,28},{2,30},{4,24},{6,26},{8,20},{10,22},{12,16},{14,18},{16,12}... | collective-permute-start | bytes 417800 | tf_op jit(solution)/shard_map/ppermute | solution.py:899
  73.9 12.0 %collective-permute-done.7.refs_0_ = bf16[2,272,128]{2,1,0:T(8,128)(2,1)S(1)} collective-permute-done((bf16[2,272,128]{2,1,0:T(8,128)(2,1)S(1)}, bf16[2,272,128]{2,1,0:T(8,128)(2,1)S(1)}, u32[]{:S(2)}, u32[]{:S(2)}) %collective-permute-start.7) | collective-permute-done | bytes 139296 | tf_op jit(solution)/shard_map/ppermute | solution.py:899
  85.9 3.0 %collective-permute-done.8.refs_1_ = bf16[2,272,128]{2,1,0:T(8,128)(2,1)S(1)} collective-permute-done((bf16[2,272,128]{2,1,0:T(8,128)(2,1)S(1)}, bf16[2,272,128]{2,1,0:T(8,128)(2,1)S(1)}, u32[]{:S(2)}, u32[]{:S(2)}) %collective-permute-start.8) | collective-permute-done | bytes 139296 | tf_op jit(solution)/shard_map/ppermute | solution.py:899
  88.9 6.0 %collective-permute-done.9.refs_2_ = bf16[2,272,128]{2,1,0:T(8,128)(2,1)S(1)} collective-permute-done((bf16[2,272,128]{2,1,0:T(8,128)(2,1)S(1)}, bf16[2,272,128]{2,1,0:T(8,128)(2,1)S(1)}, u32[]{:S(2)}, u32[]{:S(2)}) %collective-permute-start.9) | collective-permute-done | bytes 139296 | tf_op jit(solution)/shard_map/ppermute | solution.py:899
  94.8 3.4 %collective-permute-done.10.refs_3_ = bf16[2,272,128]{2,1,0:T(8,128)(2,1)S(1)} collective-permute-done((bf16[2,272,128]{2,1,0:T(8,128)(2,1)S(1)}, bf16[2,272,128]{2,1,0:T(8,128)(2,1)S(1)}, u32[]{:S(2)}, u32[]{:S(2)}) %collective-permute-start.10) | collective-permute-done | bytes 139296 | tf_op jit(solution)/shard_map/ppermute | solution.py:899
  98.3 1.6 %collective-permute-start.11 = (f32[16,128]{1,0:T(8,128)S(1)}, f32[16,128]{1,0:T(8,128)S(1)}, u32[]{:S(2)}, u32[]{:S(2)}) collective-permute-start(f32[16,128]{1,0:T(8,128)S(1)} %temper_sums.1), channel_id=1, source_target_pairs={{0,1},{1,0},{2,3},{3,2},{4,5},{5,4},{6,7},{7,6},{8,9},{9,8},{10,11... | collective-permute-start | bytes 24584 | tf_op jit(solution)/shard_map/ppermute | solution.py:1008
  99.8 1.5 %unpack_heads.1 = (bf16[1,128,2048]{2,1,0:T(8,128)(2,1)}, bf16[1,128,2048]{2,1,0:T(8,128)(2,1)}, bf16[1,128,2048]{2,1,0:T(8,128)(2,1)}) custom-call(bf16[8,784,128]{2,1,0:T(8,128)(2,1)S(1)} %all-to-all-done.1.within_ref, bf16[2,272,128]{2,1,0:T(8,128)(2,1)S(1)} %collective-permute-done.7.refs_0_, bf16[2,272,128]{2,1,0:T(8,128)(2,1)S(1)} %collective-permute-done.8.refs_1_, ...), custom_call_target="tpu_custom_call" | custom-call | bytes 3735552 | tf_op jit(solution)/shard_map/unpack_heads/pallas_call | solution.py:409
  (24 shorter events, 4.6 us)
Async XLA Ops:
  3.6 5.5 %copy-start.4 = (bf16[4,256,128]{2,1,0:T(8,128)(2,1)S(1)}, bf16[4,256,128]{2,1,0:T(8,128)(2,1)}, u32[]{:S(2)}) copy-start(bf16[4,256,128]{2,1,0:T(8,128)(2,1)} %get-tuple-element.41) | copy-start | bytes 786436
  3.6 7.4 %copy-start = (bf16[4,256,128]{2,1,0:T(8,128)(2,1)S(1)}, bf16[4,256,128]{2,1,0:T(8,128)(2,1)}, u32[]{:S(2)}) copy-start(bf16[4,256,128]{2,1,0:T(8,128)(2,1)} %get-tuple-element.40.kept_ref) | copy-start | bytes 786436
  3.6 36.8 %copy-start.1 = (s32[1,16,16,1]{2,3,1,0:T(1,128)S(1)}, s32[1,16,16,1]{2,3,1,0:T(1,128)}, u32[]{:S(2)}) copy-start(s32[1,16,16,1]{2,3,1,0:T(1,128)} %param.12) | copy-start | bytes 3076
  3.6 36.7 %copy-start.2 = (f32[16]{0:T(128)S(1)}, f32[16]{0:T(128)}, u32[]{:S(2)}) copy-start(f32[16]{0:T(128)} %softness_ref.7) | copy-start | bytes 196
  3.6 36.7 %copy-start.3 = (s32[16]{0:T(128)S(1)}, s32[16]{0:T(128)}, u32[]{:S(2)}) copy-start(s32[16]{0:T(128)} %span_ref.7) | copy-start | bytes 196
  3.6 36.7 %all-to-all-start = ((bf16[8,1024,128]{2,1,0:T(8,128)(2,1)}), bf16[8,1024,128]{2,1,0:T(8,128)(2,1)S(1)}, u32[]{:S(2)}, u32[]{:S(2)}) async-start(bf16[8,1024,128]{2,1,0:T(8,128)(2,1)} %get-tuple-element.37), calls=%async_computation | async-start | bytes 4194304 | tf_op jit(solution)/shard_map/all_to_all | solution.py:929
  9.0 1.9 %collective-permute-start = (bf16[4,256,128]{2,1,0:T(8,128)(2,1)S(1)}, bf16[4,256,128]{2,1,0:T(8,128)(2,1)S(1)}, u32[]{:S(2)}, u32[]{:S(2)}) collective-permute-start(bf16[4,256,128]{2,1,0:T(8,128)(2,1)S(1)} %copy-done.4), channel_id=1, source_target_pairs={{0,2},{2,0},{4,6},{6,4},{8,10},{10,8},{12,14},{14,12},{16,18},{18,... | collective-permute-start | bytes 786440 | tf_op jit(solution)/shard_map/ppermute | solution.py:888
  11.0 33.8 %collective-permute-start.1 = (bf16[2,256,128]{2,1,0:T(8,128)(2,1)S(1)}, bf16[2,256,128]{2,1,0:T(8,128)(2,1)S(1)}, u32[]{:S(2)}, u32[]{:S(2)}) collective-permute-start(bf16[2,256,128]{2,1,0:T(8,128)(2,1)S(1)} %get-tuple-element.42), channel_id=1, source_target_pairs={{0,16},{2,18},{4,20},{6,22},{8,24},{10,26},{12,28},{14,30},{16,0},... | collective-permute-start | bytes 393224 | tf_op jit(solution)/shard_map/ppermute | solution.py:899
  13.6 31.2 %collective-permute-start.2 = (bf16[2,256,128]{2,1,0:T(8,128)(2,1)S(1)}, bf16[2,256,128]{2,1,0:T(8,128)(2,1)S(1)}, u32[]{:S(2)}, u32[]{:S(2)}) collective-permute-start(bf16[2,256,128]{2,1,0:T(8,128)(2,1)S(1)} %get-tuple-element.43), channel_id=1, source_target_pairs={{0,20},{2,22},{4,16},{6,18},{8,28},{10,30},{12,24},{14,26},{16,4},... | collective-permute-start | bytes 393224 | tf_op jit(solution)/shard_map/ppermute | solution.py:899
  15.1 30.6 %collective-permute-start.3 = (bf16[2,256,128]{2,1,0:T(8,128)(2,1)S(1)}, bf16[2,256,128]{2,1,0:T(8,128)(2,1)S(1)}, u32[]{:S(2)}, u32[]{:S(2)}) collective-permute-start(bf16[2,256,128]{2,1,0:T(8,128)(2,1)S(1)} %get-tuple-element.44), channel_id=1, source_target_pairs={{0,24},{2,26},{4,28},{6,30},{8,16},{10,18},{12,20},{14,22},{16,8},... | collective-permute-start | bytes 393224 | tf_op jit(solution)/shard_map/ppermute | solution.py:899
  18.6 30.3 %collective-permute-start.4 = (bf16[2,256,128]{2,1,0:T(8,128)(2,1)S(1)}, bf16[2,256,128]{2,1,0:T(8,128)(2,1)S(1)}, u32[]{:S(2)}, u32[]{:S(2)}) collective-permute-start(bf16[2,256,128]{2,1,0:T(8,128)(2,1)S(1)} %get-tuple-element.45), channel_id=1, source_target_pairs={{0,28},{2,30},{4,24},{6,26},{8,20},{10,22},{12,16},{14,18},{16,12}... | collective-permute-start | bytes 393224 | tf_op jit(solution)/shard_map/ppermute | solution.py:899
  51.5 5.0 %collective-permute-start.5 = (f32[8,1024]{1,0:T(8,128)S(1)}, f32[8,1024]{1,0:T(8,128)S(1)}, u32[]{:S(2)}, u32[]{:S(2)}) collective-permute-start(f32[8,1024]{1,0:T(8,128)S(1)} %get-tuple-element.47.message_ref), channel_id=1, source_target_pairs={{0,16},{2,18},{4,20},{6,22},{8,24},{10,26},{12,28},{14,30},{16,0},... | collective-permute-start | bytes 98312 | tf_op jit(solution)/shard_map/ppermute | solution.py:972
  60.8 37.4 %all-to-all-start.1 = ((bf16[8,784,128]{2,1,0:T(8,128)(2,1)}), bf16[8,784,128]{2,1,0:T(8,128)(2,1)S(1)}, u32[]{:S(2)}, u32[]{:S(2)}) async-start(bf16[8,784,128]{2,1,0:T(8,128)(2,1)} %get-tuple-element.60), calls=%async_computation.1 | async-start | bytes 3211264 | tf_op jit(solution)/shard_map/all_to_all | solution.py:929
  64.4 1.7 %collective-permute-start.6 = (bf16[4,272,128]{2,1,0:T(8,128)(2,1)S(1)}, bf16[4,272,128]{2,1,0:T(8,128)(2,1)S(1)}, u32[]{:S(2)}, u32[]{:S(2)}) collective-permute-start(bf16[4,272,128]{2,1,0:T(8,128)(2,1)S(1)} %get-tuple-element.62), channel_id=1, source_target_pairs={{0,2},{2,0},{4,6},{6,4},{8,10},{10,8},{12,14},{14,12},{16,18},{18,... | collective-permute-start | bytes 835592 | tf_op jit(solution)/shard_map/ppermute | solution.py:888
  66.2 19.7 %collective-permute-start.7 = (bf16[2,272,128]{2,1,0:T(8,128)(2,1)S(1)}, bf16[2,272,128]{2,1,0:T(8,128)(2,1)S(1)}, u32[]{:S(2)}, u32[]{:S(2)}) collective-permute-start(bf16[2,272,128]{2,1,0:T(8,128)(2,1)S(1)} %get-tuple-element.63), channel_id=1, source_target_pairs={{0,16},{2,18},{4,20},{6,22},{8,24},{10,26},{12,28},{14,30},{16,0},... | collective-permute-start | bytes 417800 | tf_op jit(solution)/shard_map/ppermute | solution.py:899
  67.5 21.4 %collective-permute-start.8 = (bf16[2,272,128]{2,1,0:T(8,128)(2,1)S(1)}, bf16[2,272,128]{2,1,0:T(8,128)(2,1)S(1)}, u32[]{:S(2)}, u32[]{:S(2)}) collective-permute-start(bf16[2,272,128]{2,1,0:T(8,128)(2,1)S(1)} %get-tuple-element.64), channel_id=1, source_target_pairs={{0,20},{2,22},{4,16},{6,18},{8,28},{10,30},{12,24},{14,26},{16,4},... | collective-permute-start | bytes 417800 | tf_op jit(solution)/shard_map/ppermute | solution.py:899
  70.4 24.5 %collective-permute-start.9 = (bf16[2,272,128]{2,1,0:T(8,128)(2,1)S(1)}, bf16[2,272,128]{2,1,0:T(8,128)(2,1)S(1)}, u32[]{:S(2)}, u32[]{:S(2)}) collective-permute-start(bf16[2,272,128]{2,1,0:T(8,128)(2,1)S(1)} %get-tuple-element.65), channel_id=1, source_target_pairs={{0,24},{2,26},{4,28},{6,30},{8,16},{10,18},{12,20},{14,22},{16,8},... | collective-permute-start | bytes 417800 | tf_op jit(solution)/shard_map/ppermute | solution.py:899
  72.5 25.8 %collective-permute-start.10 = (bf16[2,272,128]{2,1,0:T(8,128)(2,1)S(1)}, bf16[2,272,128]{2,1,0:T(8,128)(2,1)S(1)}, u32[]{:S(2)}, u32[]{:S(2)}) collective-permute-start(bf16[2,272,128]{2,1,0:T(8,128)(2,1)S(1)} %get-tuple-element.66), channel_id=1, source_target_pairs={{0,28},{2,30},{4,24},{6,26},{8,20},{10,22},{12,16},{14,18},{16,12}... | collective-permute-start | bytes 417800 | tf_op jit(solution)/shard_map/ppermute | solution.py:899
  98.3 3.7 %collective-permute-start.11 = (f32[16,128]{1,0:T(8,128)S(1)}, f32[16,128]{1,0:T(8,128)S(1)}, u32[]{:S(2)}, u32[]{:S(2)}) collective-permute-start(f32[16,128]{1,0:T(8,128)S(1)} %temper_sums.1), channel_id=1, source_target_pairs={{0,1},{1,0},{2,3},{3,2},{4,5},{5,4},{6,7},{7,6},{8,9},{9,8},{10,11... | collective-permute-start | bytes 24584 | tf_op jit(solution)/shard_map/ppermute | solution.py:1008

commit v8 on v7

--- a/solution.py
+++ b/solution.py
@@ -376,7 +376,6 @@
 
 
 TILE = 256
-EXTRA = 16
 MIB = 1024 * 1024
 PIECES = 4
 QUERY, KEY, VALUE, GRAD = range(4)
@@ -655,8 +654,8 @@
 
 
 def within_kernel(
-    softness_ref, ids_ref, span_ref, in_ref, arrays_ref, stats_ref, parts_ref, temper_ref,
-    own_weight, own_towards, other_weight, other_towards, *scratch, half_count
+    softness_ref, ids_ref, span_ref, in_ref, arrays_ref, stats_ref, message_ref, parts_ref,
+    other_ref, temper_ref, own_weight, own_towards, other_weight, other_towards, *scratch, half_count
 ):
     _, half, _ = position(half_count)
     for block in range(half_count):
@@ -670,6 +669,8 @@
     for slot, region in enumerate(regions):
         region.statistics(*kept[slot], stats_ref, slot * 3)
     temper_ref[...] = jnp.zeros_like(temper_ref)
+    for row in range(3):
+        message_ref[row : row + 1, :] = stats_ref[3 + row : 4 + row, :]
 
     @pl.when(half == 0)
     def _():
@@ -679,13 +680,17 @@
             for tile, value in enumerate(tiles):
                 parts_ref[place, tile_rows(tile), :] = value
         temper_ref[0:1, :] = temper
+        single = alone(three_rows(stats_ref, 3))
+        temper_ref[1:2, :] = other_diagonal(
+            regions[1], kept[1], stats_ref, single, scratch, other_ref, 0
+        )
 
 
 def square_kernel(
     softness_ref, ids_ref, span_ref, arrays_ref, stats_ref, *refs, half_count
 ):
     across_refs = refs[: half_count // 2]
-    square_ref, message_ref, square_stats, weight, towards = refs[half_count // 2 :]
+    square_ref, square_stats, weight, towards = refs[half_count // 2 :]
     _, half, place = position(half_count)
     first = jnp.where(half == 0, QUERY, KEY)
     second = jnp.where(half == 0, GRAD, VALUE)
@@ -700,25 +705,21 @@
     square_ref[kept_second, :, :] = arrays_ref[kept_second, :, :]
     region = square_region((softness_ref, ids_ref, span_ref), half_count, square_ref)
     region.statistics(weight, towards, square_stats, 0)
-    for row in range(3):
-        message_ref[row : row + 1, :] = jnp.where(
-            half == 0, square_stats[row : row + 1, :], stats_ref[3 + row : 4 + row, :]
-        )
-
-
-def other_diagonal(region, kept, stats_ref, totals, scratch, within_ref):
+
+
+def other_diagonal(region, kept, stats_ref, totals, scratch, out_ref, first):
     *parts, temper = region.gradients(*kept, stats_ref[3:4, :], *totals, *scratch)
     scales = (region.scaling, region.scaling, 1.0)
     for array, (part, scale) in enumerate(zip(parts, scales)):
         for tile in range(region.tiles):
-            put(within_ref, 3 + array, tile, part[tile] * scale)
+            put(out_ref, first + array, tile, part[tile] * scale)
     return temper
 
 
-def first_kernel(
-    softness_ref, ids_ref, span_ref, arrays_ref, square_ref, stats_ref, square_stats, temper_in,
-    own_weight, own_towards, other_weight, other_towards, square_weight, square_towards,
-    within_ref, across_ref, temper_ref, *scratch, half_count
+def own_kernel(
+    softness_ref, ids_ref, span_ref, arrays_ref, square_ref, stats_ref, square_stats, received_ref,
+    parts_ref, temper_in, own_weight, own_towards, square_weight, square_towards,
+    own_ref, across_ref, temper_ref, *scratch, half_count
 ):
     _, half, _ = position(half_count)
     settings = (softness_ref, ids_ref, span_ref)
@@ -726,11 +727,19 @@
 
     @pl.when(half == 0)
     def _():
-        region = diagonal_region(1, settings, half_count, arrays_ref)
-        totals = alone(three_rows(stats_ref, 3))
-        temper_ref[1:2, :] = other_diagonal(
-            region, (other_weight, other_towards), stats_ref, totals, scratch, within_ref
-        )
+        totals = merged(three_rows(square_stats, 0), three_rows(received_ref, 0))
+        square = square_region(settings, half_count, square_ref)
+        query_parts, key_parts, value_parts, square_temper = square.gradients(
+            square_weight, square_towards, square_stats[0:1, :], *totals, *scratch
+        )
+        for tile in range(square.tiles):
+            here = tile_rows(tile)
+            across_ref[0, here, :] = (query_parts[tile] * square.scaling).astype(jnp.bfloat16)
+            put(own_ref, 0, tile, parts_ref[0, here, :] * square.scaling)
+            put(own_ref, 1, tile, (parts_ref[1, here, :] + key_parts[tile]) * square.scaling)
+            put(own_ref, 2, tile, parts_ref[2, here, :] + value_parts[tile])
+        across_ref[1] = jnp.zeros(across_ref.shape[1:], jnp.bfloat16)
+        temper_ref[0:1, :] = temper_in[0:1, :] + square_temper
 
     @pl.when(half == 1)
     def _():
@@ -750,112 +759,54 @@
             own_weight, own_towards, stats_ref[0:1, :], *totals, *scratch
         )
         for tile in range(square.tiles):
-            put(within_ref, 0, tile, (parts[0][tile] + across_query[tile]) * scales[0])
-            put(within_ref, 1, tile, parts[1][tile] * scales[1])
-            put(within_ref, 2, tile, parts[2][tile])
+            put(own_ref, 0, tile, (parts[0][tile] + across_query[tile]) * scales[0])
+            put(own_ref, 1, tile, parts[1][tile] * scales[1])
+            put(own_ref, 2, tile, parts[2][tile])
         temper_ref[0:1, :] = temper + square_temper
 
 
-def temper_rows(own, other):
-    row = lax.broadcasted_iota(jnp.int32, (EXTRA, HD), 0)
-    rows = jnp.zeros((EXTRA, HD), jnp.float32)
-    for place, terms in enumerate((own, other)):
-        rest = jnp.broadcast_to(jnp.sum(terms, axis=1, keepdims=True), (EXTRA, HD)) * (
-            1.0 / math.sqrt(HD)
-        )
-        for piece in range(3):
-            high = rest.astype(jnp.bfloat16).astype(jnp.float32)
-            rows = jnp.where(row == place * 3 + piece, high, rows)
-            rest = rest - high
-    return rows.astype(jnp.bfloat16)
-
-
 def finish_kernel(
-    softness_ref, ids_ref, span_ref, arrays_ref, square_ref, message_ref, received_ref,
-    stats_ref, square_stats, parts_ref, temper_ref,
-    square_weight, square_towards, other_weight, other_towards, across_in, begun_ref,
-    within_ref, *refs, half_count
+    softness_ref, ids_ref, span_ref, arrays_ref, stats_ref, received_ref, own_ref, other_ref,
+    temper_ref, other_weight, other_towards, across_ref, within_ref, *refs, half_count
 ):
-    foreign_refs = refs[:2]
-    across, temper, *scratch = refs[2:]
-    _, half, place = position(half_count)
+    foreign_refs, (out_temper, temper, *scratch) = refs[:2], refs[2:]
+    me, half, place = position(half_count)
     settings = (softness_ref, ids_ref, span_ref)
     temper[...] = temper_ref[...]
-
-    @pl.when(half == 0)
-    def _():
-        totals = merged(three_rows(message_ref, 0), three_rows(received_ref, 0))
-        region = square_region(settings, half_count, square_ref)
-        query_parts, key_parts, value_parts, square_temper = region.gradients(
-            square_weight, square_towards, square_stats[0:1, :], *totals, *scratch
-        )
-        for tile in range(region.tiles):
-            here = tile_rows(tile)
-            across[0, here, :] = (query_parts[tile] * region.scaling).astype(jnp.bfloat16)
-            put(within_ref, 0, tile, parts_ref[0, here, :] * region.scaling)
-            put(within_ref, 1, tile, (parts_ref[1, here, :] + key_parts[tile]) * region.scaling)
-            put(within_ref, 2, tile, parts_ref[2, here, :] + value_parts[tile])
-        across[1] = jnp.zeros(across.shape[1:], jnp.bfloat16)
-        within_ref[:, 3 * BLK : 6 * BLK, :] = begun_ref[:, 3 * BLK : 6 * BLK, :]
-        temper[0:1, :] = temper_ref[0:1, :] + square_temper
-
-    @pl.when(half == 1)
-    def _():
-        totals = merged(three_rows(message_ref, 0), three_rows(received_ref, 0))
-        region = diagonal_region(1, settings, half_count, arrays_ref)
-        temper[1:2, :] = other_diagonal(
-            region, (other_weight, other_towards), stats_ref, totals, scratch, within_ref
-        )
-        across[...] = across_in[...]
-        within_ref[:, : 3 * BLK, :] = begun_ref[:, : 3 * BLK, :]
-
-    pieces = temper_rows(temper[0:1, :], temper[1:2, :])
-    for block in range(half_count):
-        within_ref[block, 6 * BLK : 6 * BLK + EXTRA, :] = pieces
+    within_ref[:, : 3 * BLK, :] = own_ref[...]
     for core, foreign_ref in enumerate(foreign_refs):
         for step in range(half_count // 2):
             rows = rows_of(place ^ core ^ (2 * step))
-            foreign_ref[step, :BLK, :] = across[0, rows, :]
-            foreign_ref[step, BLK : 2 * BLK, :] = across[1, rows, :]
-            foreign_ref[step, 2 * BLK :, :] = pieces
-
-
-def temper_kernel(within_ref, *refs, half_count):
-    across_refs, temper_ref = refs[: half_count // 2], refs[half_count // 2]
+            foreign_ref[step, :BLK, :] = across_ref[0, rows, :]
+            foreign_ref[step, BLK:, :] = across_ref[1, rows, :]
+
+    @pl.when(half == 0)
+    def _():
+        within_ref[:, 3 * BLK :, :] = other_ref[...]
+
+    @pl.when(half == 1)
+    def _():
+        totals = merged(three_rows(stats_ref, 3), three_rows(received_ref, 0))
+        region = diagonal_region(1, settings, half_count, arrays_ref)
+        temper[1:2, :] = other_diagonal(
+            region, (other_weight, other_towards), stats_ref, totals, scratch, within_ref, 3
+        )
+
+    lane = lax.broadcasted_iota(jnp.int32, (1, HD), 1)
+    own_sum = jnp.sum(temper[0:1, :], axis=1, keepdims=True)
+    other_sum = jnp.sum(temper[1:2, :], axis=1, keepdims=True)
+    terms = jnp.where(lane == me, own_sum, 0.0) + jnp.where(
+        lane == me ^ half_count, other_sum, 0.0
+    )
+    out_temper[...] = terms * (1.0 / math.sqrt(HD))
+
+
+def unpack_kernel(tempers_ref, within_ref, *refs, half_count):
+    across_refs = refs[: half_count // 2]
+    *out_refs, temper_ref = refs[half_count // 2 :]
     _, half, place = position(half_count)
-
-    def sums(rows):
-        return [
-            jnp.sum(rows[3 * slot : 3 * slot + 3, :].astype(jnp.float32), axis=0, keepdims=True)
-            for slot in range(2)
-        ]
-
-    for step, across_ref in enumerate(across_refs):
-        for core in range(2):
-            peer = place ^ core ^ (2 * step)
-            near, far = sums(within_ref[peer]), sums(across_ref[core])
-            temper_ref[pl.ds(half * half_count + peer, 1), :] = near[0] + far[1]
-            temper_ref[pl.ds((1 - half) * half_count + peer, 1), :] = near[1] + far[0]
-
-
-def temper_sums(within, across, half_count):
-    last = (6 * BLK // EXTRA, 2 * BLK // EXTRA)
-    return pl.pallas_call(
-        functools.partial(temper_kernel, half_count=half_count),
-        grid=(1,),
-        out_shape=jax.ShapeDtypeStruct((2 * half_count, HD), jnp.float32),
-        in_specs=[pl.BlockSpec((half_count, EXTRA, HD), lambda step: (0, last[0], 0))]
-        + [pl.BlockSpec((2, EXTRA, HD), lambda step: (0, last[1], 0))] * (half_count // 2),
-        out_specs=pl.BlockSpec((2 * half_count, HD), lambda step: (0, 0)),
-        compiler_params=pltpu.CompilerParams(vmem_limit_bytes=4 * MIB),
-        name="temper_sums",
-    )(within, *across)
-
-
-def unpack_kernel(within_ref, *refs, half_count):
-    across_refs = refs[: half_count // 2]
-    out_refs = refs[half_count // 2 :]
-    _, half, place = position(half_count)
+    every = jnp.sum(tempers_ref[...], axis=0, keepdims=True)
+    temper_ref[...] = every[:, : temper_ref.shape[1]] * (1.0 / (tempers_ref.shape[0] * BLK))
     for step, across_ref in enumerate(across_refs):
         for core in range(2):
             peer = place ^ core ^ (2 * step)
@@ -912,7 +863,7 @@
     block_grouping,
     neighborhood_span,
 ):
-    seq_count, dp_count = lax.axis_size("seq"), lax.axis_size("dp")
+    seq_count = lax.axis_size("seq")
     half_count = seq_count // 2
     tokens = half_count * BLK
     groups = [list(range(half_count)), list(range(half_count, seq_count))]
@@ -948,74 +899,78 @@
     arrived = exchange_within(sent)
     foreign = crossed(*foreign, half_count)
     kept_parts = jax.ShapeDtypeStruct((3, tokens, HD), jnp.float32)
+    three_arrays = jax.ShapeDtypeStruct((half_count, 3 * BLK, HD), jnp.bfloat16)
     tempers = jax.ShapeDtypeStruct((8, HD), jnp.float32)
-    arrays, stats, parts, temper, own_weight, own_towards, other_weight, other_towards = call(
+    first_half = range(half_count)
+    (
+        arrays, stats, message, parts, other_done, temper,
+        own_weight, own_towards, other_weight, other_towards,
+    ) = call(
         within_kernel,
         "diagonal_statistics",
         (arrived,),
-        [jax.ShapeDtypeStruct((8, tokens, HD), jnp.bfloat16), rows_of_stats, kept_parts, tempers]
+        [jax.ShapeDtypeStruct((8, tokens, HD), jnp.bfloat16), rows_of_stats, rows_of_stats]
+        + [kept_parts, three_arrays, tempers]
         + [pairs] * 4,
         lows,
-        2 * pair_flops,
+        3 * pair_flops,
         20,
     )
-    square, message, square_stats, square_weight, square_towards = call(
+    from_second = lax.ppermute(
+        message, "seq", [(source + half_count, source) for source in first_half]
+    )
+    square, square_stats, square_weight, square_towards = call(
         square_kernel,
         "square_statistics",
         (arrays, stats, *foreign),
-        [jax.ShapeDtypeStruct((4, tokens, HD), jnp.bfloat16)] + [rows_of_stats] * 2 + [pairs] * 2,
+        [jax.ShapeDtypeStruct((4, tokens, HD), jnp.bfloat16), rows_of_stats] + [pairs] * 2,
         [],
         2 * pair_flops,
         12,
     )
-    swap = [(source, source ^ half_count) for source in range(seq_count)]
-    received = lax.ppermute(message, "seq", swap)
-    begun, across, temper = call(
-        first_kernel,
-        "gradients_before_totals",
+    from_first = lax.ppermute(
+        square_stats, "seq", [(source, source + half_count) for source in first_half]
+    )
+    own_done, across, temper = call(
+        own_kernel,
+        "own_gradients",
         (
-            arrays, square, stats, square_stats, temper, own_weight, own_towards,
-            other_weight, other_towards, square_weight, square_towards,
+            arrays, square, stats, square_stats, from_second, parts, temper,
+            own_weight, own_towards, square_weight, square_towards,
         ),
-        [
-            jax.ShapeDtypeStruct((half_count, 6 * BLK, HD), jnp.bfloat16),
-            jax.ShapeDtypeStruct((2, tokens, HD), jnp.bfloat16),
-            tempers,
-        ],
+        [three_arrays, jax.ShapeDtypeStruct((2, tokens, HD), jnp.bfloat16), tempers],
         lows,
         4 * pair_flops,
         14,
     )
-    within, *foreign = call(
+    within, *foreign, temper = call(
         finish_kernel,
-        "gradients_after_totals",
+        "other_gradients",
         (
-            arrays, square, message, received, stats, square_stats, parts, temper,
-            square_weight, square_towards, other_weight, other_towards, across, begun,
+            arrays, stats, from_first, own_done, other_done, temper,
+            other_weight, other_towards, across,
         ),
-        [jax.ShapeDtypeStruct((half_count, 6 * BLK + EXTRA, HD), jnp.bfloat16)]
-        + [jax.ShapeDtypeStruct((half_count // 2, 2 * BLK + EXTRA, HD), jnp.bfloat16)] * 2,
-        [pltpu.VMEM((2, tokens, HD), jnp.bfloat16), pltpu.VMEM((8, HD), jnp.float32), *lows],
-        2 * pair_flops,
-        20,
-    )
+        [jax.ShapeDtypeStruct((half_count, 6 * BLK, HD), jnp.bfloat16)]
+        + [jax.ShapeDtypeStruct((half_count // 2, 2 * BLK, HD), jnp.bfloat16)] * 2
+        + [jax.ShapeDtypeStruct((1, HD), jnp.float32)],
+        [pltpu.VMEM((8, HD), jnp.float32), *lows],
+        pair_flops,
+        16,
+    )
+    tempers = lax.all_gather(temper, ("dp", "seq"), tiled=True)
     across = crossed(*foreign, half_count)
     within = exchange_within(within)
-    tempers = temper_sums(within, across, half_count)
-    temper_total = tempers
-    for step in range(1, dp_count):
-        swap = [(source, (source + step) % dp_count) for source in range(dp_count)]
-        temper_total = temper_total + lax.ppermute(tempers, "dp", swap)
-    outs = kernel_call(
+    *outs, temper = kernel_call(
         functools.partial(unpack_kernel, half_count=half_count),
         "unpack_heads",
-        (within, *across),
-        [vmem] * (1 + len(across)),
-        [jax.ShapeDtypeStruct(probe_vectors.shape, jnp.bfloat16)] * 3,
+        (tempers, within, *across),
+        [vmem] * (2 + len(across)),
+        [jax.ShapeDtypeStruct(probe_vectors.shape, jnp.bfloat16)] * 3
+        + [jax.ShapeDtypeStruct((1, seq_count), jnp.float32)],
         [],
         10,
     )
-    return (*outs, temper_total[:, 0] / (dp_count * BLK * seq_count))
+    return (*outs, temper.reshape(seq_count))
 
 
 def shards(

time: 103 us -> 131 us (1.27)
  blocking collectives: 0 us -> 53.9 us
  waiting for transfers between devices: 56.3 us -> 26.2 us
  starting transfers between devices: 26.9 us -> 32.3 us
    all_gather x0 -> x1, blocking collectives: none -> 53.9 us  [head_shards(): tempers = lax.all_gather(temper, ('dp', 'seq'), tiled=True)]
    ppermute x8, waiting for transfers between devices: 28.4 us -> 1.81 us  [crossed(): lax.ppermute(message, 'seq', [(source, source ^ half_count + 2 * step) fo...]
    ppermute x2, waiting for transfers between devices: 3.48 us -> 0.01 us  [the longest x1 0.01 us: head_shards(): lax.ppermute(message, 'seq', [(source + half_count, source) for source in...]
    ppermute x2, starting transfers between devices: 1.63 us -> 4.97 us  [the longest x1 3.67 us: head_shards(): lax.ppermute(square_stats, 'seq', [(source, source + half_count) for sour...]
    all_to_all x2, starting transfers between devices: 8.98 us -> 10.6 us  [exchange_within(): lax.all_to_all(array_in, 'seq', split_axis=0, concat_axis=0, axis_index_g...]
  transfers between devices with their start and end apart: 14 -> 14, of which waited for: 11 -> 4; matrix products, arithmetic and copies ran while one was open for 0% -> 0% of each run, Pallas kernels for 8% -> 8%
where the time goes in v8:
time: 131 us
  blocking collectives  53.9 us (41%)
  starting transfers between devices  32.3 us (25%)
  waiting for transfers between devices  26.2 us (20%)
  Pallas kernels  17.6 us (13%)
    all_gather x1, blocking collectives, head_shards(): tempers = lax.all_gather(temper, ('dp', 'seq'), tiled=True)  53.9 us
    all_to_all x2, waiting for transfers between devices, exchange_within(): lax.all_to_all(array_in, 'seq', split_axis=0, concat_axis=0, axis_index_g...  21.7 us
    pallas_call x8, Pallas kernels, kernel_call(): pl.pallas_call(kernel, out_shape=out_shape, in_specs=in_specs, out_specs=...  17.6 us
    ppermute x8, starting transfers between devices, crossed(): lax.ppermute(message, 'seq', [(source, source ^ half_count + 2 * step) fo...  15.7 us
    all_to_all x2, starting transfers between devices, exchange_within(): lax.all_to_all(array_in, 'seq', split_axis=0, concat_axis=0, axis_index_g...  10.6 us
    ppermute x1, starting transfers between devices, head_shards(): lax.ppermute(square_stats, 'seq', [(source, source + half_count) for sour...  3.67 us
    ppermute x2, waiting for transfers between devices, crossed(): lax.ppermute(given, 'seq', [(source, source ^ 1) for source in devices])  2.7 us
  transfers between devices with their start and end apart: 14, of which 4 were waited for; matrix products, arithmetic and copies ran while one was open for 0% of the time, Pallas kernels for 8%

profile of v8, /device:TPU:0, one launch (start us, length us, event | category | flops | bytes accessed | tf_op | source)
XLA Modules:
  0.0 130.7 jit_solution(8430196092419382524)
XLA Ops:
  0.7 2.9 %pack_heads.1 = (bf16[8,1024,128]{2,1,0:T(8,128)(2,1)}, bf16[4,256,128]{2,1,0:T(8,128)(2,1)}, bf16[4,256,128]{2,1,0:T(8,128)(2,1)}) custom-call(bf16[1,128,2048]{2,1,0:T(8,128)(2,1)} %refs_0_.1, bf16[1,128,2048]{2,1,0:T(8,128)(2,1)} %refs_1_.1, bf16[1,128,2048]{2,1,0:T(8,128)(2,1)} %refs_2_.1, bf16[1,128,2048]{2,1,0:T(8,128)(2,1)} %refs_3_.1), custom_call_target="tpu_custom_call" | custom-call | bytes 4718592 | tf_op jit(solution)/shard_map/pack_heads/pallas_call | solution.py:408
  3.6 5.4 %all-to-all-start = ((bf16[8,1024,128]{2,1,0:T(8,128)(2,1)}), bf16[8,1024,128]{2,1,0:T(8,128)(2,1)S(1)}, u32[]{:S(2)}, u32[]{:S(2)}) async-start(bf16[8,1024,128]{2,1,0:T(8,128)(2,1)} %get-tuple-element.40), calls=%async_computation | async-start | bytes 4194304 | tf_op jit(solution)/shard_map/all_to_all | solution.py:880
  9.0 0.5 collective-permute-start
  9.5 1.4 %collective-permute-done.taken_ref = bf16[4,256,128]{2,1,0:T(8,128)(2,1)S(1)} collective-permute-done((bf16[4,256,128]{2,1,0:T(8,128)(2,1)S(1)}, bf16[4,256,128]{2,1,0:T(8,128)(2,1)S(1)}, u32[]{:S(2)}, u32[]{:S(2)}) %collective-permute-start) | collective-permute-done | bytes 262176 | tf_op jit(solution)/shard_map/ppermute | solution.py:839
  11.0 2.7 %collective-permute-start.1 = (bf16[2,256,128]{2,1,0:T(8,128)(2,1)S(1)}, bf16[2,256,128]{2,1,0:T(8,128)(2,1)S(1)}, u32[]{:S(2)}, u32[]{:S(2)}) collective-permute-start(bf16[2,256,128]{2,1,0:T(8,128)(2,1)S(1)} %get-tuple-element.45), channel_id=1, source_target_pairs={{0,16},{2,18},{4,20},{6,22},{8,24},{10,26},{12,28},{14,30},{16,0},... | collective-permute-start | bytes 393224 | tf_op jit(solution)/shard_map/ppermute | solution.py:850
  13.6 1.5 %collective-permute-start.2 = (bf16[2,256,128]{2,1,0:T(8,128)(2,1)S(1)}, bf16[2,256,128]{2,1,0:T(8,128)(2,1)S(1)}, u32[]{:S(2)}, u32[]{:S(2)}) collective-permute-start(bf16[2,256,128]{2,1,0:T(8,128)(2,1)S(1)} %get-tuple-element.46), channel_id=1, source_target_pairs={{0,20},{2,22},{4,16},{6,18},{8,28},{10,30},{12,24},{14,26},{16,4},... | collective-permute-start | bytes 393224 | tf_op jit(solution)/shard_map/ppermute | solution.py:850
  15.1 3.5 %collective-permute-start.3 = (bf16[2,256,128]{2,1,0:T(8,128)(2,1)S(1)}, bf16[2,256,128]{2,1,0:T(8,128)(2,1)S(1)}, u32[]{:S(2)}, u32[]{:S(2)}) collective-permute-start(bf16[2,256,128]{2,1,0:T(8,128)(2,1)S(1)} %get-tuple-element.47), channel_id=1, source_target_pairs={{0,24},{2,26},{4,28},{6,30},{8,16},{10,18},{12,20},{14,22},{16,8},... | collective-permute-start | bytes 393224 | tf_op jit(solution)/shard_map/ppermute | solution.py:850
  18.6 0.1 collective-permute-start.4
  18.7 21.7 %all-to-all-done.in_ref = bf16[8,1024,128]{2,1,0:T(8,128)(2,1)S(1)} async-done(((bf16[8,1024,128]{2,1,0:T(8,128)(2,1)}), bf16[8,1024,128]{2,1,0:T(8,128)(2,1)S(1)}, u32[]{:S(2)}, u32[]{:S(2)}) %all-to-all-start) | async-done | bytes 2097184 | tf_op jit(solution)/shard_map/all_to_all | solution.py:880
  40.4 5.4 %diagonal_statistics.1 = (bf16[8,1024,128]{2,1,0:T(8,128)(2,1)S(1)}, f32[8,1024]{1,0:T(8,128)S(1)}, f32[8,1024]{1,0:T(8,128)S(1)}, f32[3,1024,128]{2,1,0:T(8,128...) custom-call(f32[16]{0:T(128)S(1)} %copy-done.2, ...), custom_call_target="tpu_custom_call" | custom-call | flops 805306368 | bytes 23401600 | tf_op jit(solution)/shard_map/diagonal_statistics/pallas_call | solution.py:408
  45.8 1.3 collective-permute-start.6
  47.1 1.8 %collective-permute-done.4.refs_3_ = bf16[2,256,128]{2,1,0:T(8,128)(2,1)S(1)} collective-permute-done((bf16[2,256,128]{2,1,0:T(8,128)(2,1)S(1)}, bf16[2,256,128]{2,1,0:T(8,128)(2,1)S(1)}, u32[]{:S(2)}, u32[]{:S(2)}) %collective-permute-start.4) | collective-permute-done | bytes 131104 | tf_op jit(solution)/shard_map/ppermute | solution.py:850
  48.9 2.6 %square_statistics.1 = (bf16[4,1024,128]{2,1,0:T(8,128)(2,1)S(1)}, f32[8,1024]{1,0:T(8,128)S(1)}, f32[1024,1024]{1,0:T(8,128)S(1)}, f32[1024,1024]{1,0:T(8,128)S(1)}) custom-call(f32[16]{0:T(128)S(1)} %copy-done.2, s32[16,16]{1,0:T(8,128)S(1)} %bitcast.5, s32[16]{0:T(128)S(1)} %copy-done.3, bf16[8,1024,128]{2,1,0:T(8,128)(2,1)S(1)} %get-tuple-element.41.arrays_ref, ...), custom_call_target="tpu_custom_call" | custom-call | flops 536870912 | bytes 12125312 | tf_op jit(solution)/shard_map/square_statistics/pallas_call | solution.py:408
  51.5 3.7 %collective-permute-start.5 = (f32[8,1024]{1,0:T(8,128)S(1)}, f32[8,1024]{1,0:T(8,128)S(1)}, u32[]{:S(2)}, u32[]{:S(2)}) collective-permute-start(f32[8,1024]{1,0:T(8,128)S(1)} %get-tuple-element.49.square_stats), channel_id=1, source_target_pairs={{0,16},{2,18},{4,20},{6,22},{8,24},{10,26},{12,28},{14,30},{1,17},... | collective-permute-start | bytes 98312 | tf_op jit(solution)/shard_map/ppermute | solution.py:931
  55.2 3.0 %own_gradients.1 = (bf16[8,384,128]{2,1,0:T(8,128)(2,1)S(1)}, bf16[2,1024,128]{2,1,0:T(8,128)(2,1)S(1)}, f32[8,128]{1,0:T(8,128)S(1)}) custom-call(f32[16]{0:T(128)S(1)} %copy-done.2, s32[16,16]{1,0:T(8,128)S(1)} %bitcast.6, s32[16]{0:T(128)S(1)} %copy-done.3, bf16[8,1024,128]{2,1,0:T(8,128)(2,1)S(1)} %get-tuple-element.41.arrays_ref, ...), custom_call_target="tpu_custom_call" | custom-call | flops 1073741824 | bytes 22914176 | tf_op jit(solution)/shard_map/own_gradients/pallas_call | solution.py:408
  58.2 2.0 %other_gradients.1 = (bf16[8,768,128]{2,1,0:T(8,128)(2,1)}, bf16[4,256,128]{2,1,0:T(8,128)(2,1)S(1)}, bf16[4,256,128]{2,1,0:T(8,128)(2,1)S(1)}, f32[1,128]{1,0:T(1,128)S(1)}) custom-call(f32[16]{0:T(128)S(1)} %copy-done.2, s32[16,16]{1,0:T(8,128)S(1)} %bitcast.7, s32[16]{0:T(128)S(1)} %copy-done.3, bf16[8,1024,128]{2,1,0:T(8,128)(2,1)S(1)} %get-tuple-element.41.arrays_ref, ...), custom_call_target="tpu_custom_call" | custom-call | flops 268435456 | bytes 14751360 | tf_op jit(solution)/shard_map/other_gradients/pallas_call | solution.py:408
  60.2 5.2 %all-to-all-start.1 = ((bf16[8,768,128]{2,1,0:T(8,128)(2,1)}), bf16[8,768,128]{2,1,0:T(8,128)(2,1)S(1)}, u32[]{:S(2)}, u32[]{:S(2)}) async-start(bf16[8,768,128]{2,1,0:T(8,128)(2,1)} %get-tuple-element.65), calls=%async_computation.1 | async-start | bytes 3145728 | tf_op jit(solution)/shard_map/all_to_all | solution.py:880
  65.4 0.5 collective-permute-start.7
  65.9 1.3 collective-permute-done.7.taken_ref
  67.2 3.0 %collective-permute-start.8 = (bf16[2,256,128]{2,1,0:T(8,128)(2,1)S(1)}, bf16[2,256,128]{2,1,0:T(8,128)(2,1)S(1)}, u32[]{:S(2)}, u32[]{:S(2)}) collective-permute-start(bf16[2,256,128]{2,1,0:T(8,128)(2,1)S(1)} %get-tuple-element.68), channel_id=1, source_target_pairs={{0,16},{2,18},{4,20},{6,22},{8,24},{10,26},{12,28},{14,30},{16,0},... | collective-permute-start | bytes 393224 | tf_op jit(solution)/shard_map/ppermute | solution.py:850
  70.2 1.3 collective-permute-start.9
  71.5 3.7 %collective-permute-start.10 = (bf16[2,256,128]{2,1,0:T(8,128)(2,1)S(1)}, bf16[2,256,128]{2,1,0:T(8,128)(2,1)S(1)}, u32[]{:S(2)}, u32[]{:S(2)}) collective-permute-start(bf16[2,256,128]{2,1,0:T(8,128)(2,1)S(1)} %get-tuple-element.70), channel_id=1, source_target_pairs={{0,24},{2,26},{4,28},{6,30},{8,16},{10,18},{12,20},{14,22},{16,8},... | collective-permute-start | bytes 393224 | tf_op jit(solution)/shard_map/ppermute | solution.py:850
  75.3 53.9 %all-gather = f32[32,1,128]{2,1,0:T(1,128)S(1)} all-gather(f32[1,1,128]{2,1,0:T(1,128)S(1)} %bitcast.9), channel_id=1, replica_groups=mesh['seq'=16,'dp'=2] {'dp','seq'}, dimensions={0}, use_global_device_ids=true | all-gather | bytes 16896 | tf_op jit(solution)/shard_map/all_gather | solution.py:960
  129.2 1.5 %unpack_heads.1 = (bf16[1,128,2048]{2,1,0:T(8,128)(2,1)}, bf16[1,128,2048]{2,1,0:T(8,128)(2,1)}, bf16[1,128,2048]{2,1,0:T(8,128)(2,1)}, f32[1,16]{1,0:T(1,128)}) custom-call(f32[32,128]{1,0:T(8,128)S(1)} %bitcast.8, bf16[8,768,128]{2,1,0:T(8,128)(2,1)S(1)} %all-to-all-done.1.within_ref, bf16[2,256,128]{2,1,0:T(8,128)(2,1)S(1)} %collective-permute-done.8.refs_0_, ...), custom_call_target="tpu_custom_call" | custom-call | bytes 3686464 | tf_op jit(solution)/shard_map/unpack_heads/pallas_call | solution.py:408
  (23 shorter events, 0.1 us)
Async XLA Ops:
  0.6 39.7 %copy-start.3 = (s32[16]{0:T(128)S(1)}, s32[16]{0:T(128)}, u32[]{:S(2)}) copy-start(s32[16]{0:T(128)} %span_ref.7) | copy-start | bytes 196
  0.6 39.7 %copy-start.2 = (f32[16]{0:T(128)S(1)}, f32[16]{0:T(128)}, u32[]{:S(2)}) copy-start(f32[16]{0:T(128)} %softness_ref.7) | copy-start | bytes 196
  0.7 39.7 %copy-start.1 = (s32[1,16,16,1]{2,3,1,0:T(1,128)S(1)}, s32[1,16,16,1]{2,3,1,0:T(1,128)}, u32[]{:S(2)}) copy-start(s32[1,16,16,1]{2,3,1,0:T(1,128)} %param.12) | copy-start | bytes 3076
  3.6 5.4 %copy-start.4 = (bf16[4,256,128]{2,1,0:T(8,128)(2,1)S(1)}, bf16[4,256,128]{2,1,0:T(8,128)(2,1)}, u32[]{:S(2)}) copy-start(bf16[4,256,128]{2,1,0:T(8,128)(2,1)} %get-tuple-element.44) | copy-start | bytes 786436
  3.6 7.3 %copy-start = (bf16[4,256,128]{2,1,0:T(8,128)(2,1)S(1)}, bf16[4,256,128]{2,1,0:T(8,128)(2,1)}, u32[]{:S(2)}) copy-start(bf16[4,256,128]{2,1,0:T(8,128)(2,1)} %get-tuple-element.43.kept_ref) | copy-start | bytes 786436
  3.6 36.7 %all-to-all-start = ((bf16[8,1024,128]{2,1,0:T(8,128)(2,1)}), bf16[8,1024,128]{2,1,0:T(8,128)(2,1)S(1)}, u32[]{:S(2)}, u32[]{:S(2)}) async-start(bf16[8,1024,128]{2,1,0:T(8,128)(2,1)} %get-tuple-element.40), calls=%async_computation | async-start | bytes 4194304 | tf_op jit(solution)/shard_map/all_to_all | solution.py:880
  9.0 1.9 %collective-permute-start = (bf16[4,256,128]{2,1,0:T(8,128)(2,1)S(1)}, bf16[4,256,128]{2,1,0:T(8,128)(2,1)S(1)}, u32[]{:S(2)}, u32[]{:S(2)}) collective-permute-start(bf16[4,256,128]{2,1,0:T(8,128)(2,1)S(1)} %copy-done.4), channel_id=1, source_target_pairs={{0,2},{2,0},{4,6},{6,4},{8,10},{10,8},{12,14},{14,12},{16,18},{18,... | collective-permute-start | bytes 786440 | tf_op jit(solution)/shard_map/ppermute | solution.py:839
  11.0 36.1 %collective-permute-start.1 = (bf16[2,256,128]{2,1,0:T(8,128)(2,1)S(1)}, bf16[2,256,128]{2,1,0:T(8,128)(2,1)S(1)}, u32[]{:S(2)}, u32[]{:S(2)}) collective-permute-start(bf16[2,256,128]{2,1,0:T(8,128)(2,1)S(1)} %get-tuple-element.45), channel_id=1, source_target_pairs={{0,16},{2,18},{4,20},{6,22},{8,24},{10,26},{12,28},{14,30},{16,0},... | collective-permute-start | bytes 393224 | tf_op jit(solution)/shard_map/ppermute | solution.py:850
  13.6 33.5 %collective-permute-start.2 = (bf16[2,256,128]{2,1,0:T(8,128)(2,1)S(1)}, bf16[2,256,128]{2,1,0:T(8,128)(2,1)S(1)}, u32[]{:S(2)}, u32[]{:S(2)}) collective-permute-start(bf16[2,256,128]{2,1,0:T(8,128)(2,1)S(1)} %get-tuple-element.46), channel_id=1, source_target_pairs={{0,20},{2,22},{4,16},{6,18},{8,28},{10,30},{12,24},{14,26},{16,4},... | collective-permute-start | bytes 393224 | tf_op jit(solution)/shard_map/ppermute | solution.py:850
  15.1 32.0 %collective-permute-start.3 = (bf16[2,256,128]{2,1,0:T(8,128)(2,1)S(1)}, bf16[2,256,128]{2,1,0:T(8,128)(2,1)S(1)}, u32[]{:S(2)}, u32[]{:S(2)}) collective-permute-start(bf16[2,256,128]{2,1,0:T(8,128)(2,1)S(1)} %get-tuple-element.47), channel_id=1, source_target_pairs={{0,24},{2,26},{4,28},{6,30},{8,16},{10,18},{12,20},{14,22},{16,8},... | collective-permute-start | bytes 393224 | tf_op jit(solution)/shard_map/ppermute | solution.py:850
  18.6 30.3 %collective-permute-start.4 = (bf16[2,256,128]{2,1,0:T(8,128)(2,1)S(1)}, bf16[2,256,128]{2,1,0:T(8,128)(2,1)S(1)}, u32[]{:S(2)}, u32[]{:S(2)}) collective-permute-start(bf16[2,256,128]{2,1,0:T(8,128)(2,1)S(1)} %get-tuple-element.48), channel_id=1, source_target_pairs={{0,28},{2,30},{4,24},{6,26},{8,20},{10,22},{12,16},{14,18},{16,12}... | collective-permute-start | bytes 393224 | tf_op jit(solution)/shard_map/ppermute | solution.py:850
  45.8 9.4 %collective-permute-start.6 = (f32[8,1024]{1,0:T(8,128)S(1)}, f32[8,1024]{1,0:T(8,128)S(1)}, u32[]{:S(2)}, u32[]{:S(2)}) collective-permute-start(f32[8,1024]{1,0:T(8,128)S(1)} %get-tuple-element.51), channel_id=1, source_target_pairs={{16,0},{18,2},{20,4},{22,6},{24,8},{26,10},{28,12},{30,14},{17,1},... | collective-permute-start | bytes 98312 | tf_op jit(solution)/shard_map/ppermute | solution.py:919
  51.5 6.7 %collective-permute-start.5 = (f32[8,1024]{1,0:T(8,128)S(1)}, f32[8,1024]{1,0:T(8,128)S(1)}, u32[]{:S(2)}, u32[]{:S(2)}) collective-permute-start(f32[8,1024]{1,0:T(8,128)S(1)} %get-tuple-element.49.square_stats), channel_id=1, source_target_pairs={{0,16},{2,18},{4,20},{6,22},{8,24},{10,26},{12,28},{14,30},{1,17},... | collective-permute-start | bytes 98312 | tf_op jit(solution)/shard_map/ppermute | solution.py:931
  60.2 69.0 %all-to-all-start.1 = ((bf16[8,768,128]{2,1,0:T(8,128)(2,1)}), bf16[8,768,128]{2,1,0:T(8,128)(2,1)S(1)}, u32[]{:S(2)}, u32[]{:S(2)}) async-start(bf16[8,768,128]{2,1,0:T(8,128)(2,1)} %get-tuple-element.65), calls=%async_computation.1 | async-start | bytes 3145728 | tf_op jit(solution)/shard_map/all_to_all | solution.py:880
  65.4 1.8 %collective-permute-start.7 = (bf16[4,256,128]{2,1,0:T(8,128)(2,1)S(1)}, bf16[4,256,128]{2,1,0:T(8,128)(2,1)S(1)}, u32[]{:S(2)}, u32[]{:S(2)}) collective-permute-start(bf16[4,256,128]{2,1,0:T(8,128)(2,1)S(1)} %get-tuple-element.67), channel_id=1, source_target_pairs={{0,2},{2,0},{4,6},{6,4},{8,10},{10,8},{12,14},{14,12},{16,18},{18,... | collective-permute-start | bytes 786440 | tf_op jit(solution)/shard_map/ppermute | solution.py:839
  67.2 61.9 %collective-permute-start.8 = (bf16[2,256,128]{2,1,0:T(8,128)(2,1)S(1)}, bf16[2,256,128]{2,1,0:T(8,128)(2,1)S(1)}, u32[]{:S(2)}, u32[]{:S(2)}) collective-permute-start(bf16[2,256,128]{2,1,0:T(8,128)(2,1)S(1)} %get-tuple-element.68), channel_id=1, source_target_pairs={{0,16},{2,18},{4,20},{6,22},{8,24},{10,26},{12,28},{14,30},{16,0},... | collective-permute-start | bytes 393224 | tf_op jit(solution)/shard_map/ppermute | solution.py:850
  70.2 58.9 %collective-permute-start.9 = (bf16[2,256,128]{2,1,0:T(8,128)(2,1)S(1)}, bf16[2,256,128]{2,1,0:T(8,128)(2,1)S(1)}, u32[]{:S(2)}, u32[]{:S(2)}) collective-permute-start(bf16[2,256,128]{2,1,0:T(8,128)(2,1)S(1)} %get-tuple-element.69), channel_id=1, source_target_pairs={{0,20},{2,22},{4,16},{6,18},{8,28},{10,30},{12,24},{14,26},{16,4},... | collective-permute-start | bytes 393224 | tf_op jit(solution)/shard_map/ppermute | solution.py:850
  71.5 57.6 %collective-permute-start.10 = (bf16[2,256,128]{2,1,0:T(8,128)(2,1)S(1)}, bf16[2,256,128]{2,1,0:T(8,128)(2,1)S(1)}, u32[]{:S(2)}, u32[]{:S(2)}) collective-permute-start(bf16[2,256,128]{2,1,0:T(8,128)(2,1)S(1)} %get-tuple-element.70), channel_id=1, source_target_pairs={{0,24},{2,26},{4,28},{6,30},{8,16},{10,18},{12,20},{14,22},{16,8},... | collective-permute-start | bytes 393224 | tf_op jit(solution)/shard_map/ppermute | solution.py:850
  75.3 53.9 %collective-permute-start.11 = (bf16[2,256,128]{2,1,0:T(8,128)(2,1)S(1)}, bf16[2,256,128]{2,1,0:T(8,128)(2,1)S(1)}, u32[]{:S(2)}, u32[]{:S(2)}) collective-permute-start(bf16[2,256,128]{2,1,0:T(8,128)(2,1)S(1)} %get-tuple-element.71), channel_id=1, source_target_pairs={{0,28},{2,30},{4,24},{6,26},{8,20},{10,22},{12,16},{14,18},{16,12}... | collective-permute-start | bytes 393224 | tf_op jit(solution)/shard_map/ppermute | solution.py:850

commit v9 on v7

--- a/solution.py
+++ b/solution.py
@@ -502,15 +502,9 @@
 
 
 class Region:
-    def __init__(self, head, settings, square, key_base, query_base, arrays, places):
-        softness_ref, self.ids_ref, span_ref = settings
-        self.head, self.square = head, square
-        self.key_base, self.query_base = key_base, query_base
-        self.arrays, self.places = arrays, places
+    def __init__(self, square, arrays, places, scaling):
+        self.square, self.arrays, self.places, self.scaling = square, arrays, places, scaling
         self.tiles = arrays.shape[1] // TILE
-        self.width = span_ref[head]
-        self.scaling = softness_ref[head] * (1.0 / math.sqrt(HD))
-        self.to_log2 = self.scaling * math.log2(math.e)
 
     def rows(self, which, start, stop):
         return self.arrays[self.places[which], start * TILE : stop * TILE, :]
@@ -518,17 +512,25 @@
     def keys_of(self, tile):
         return range(self.tiles if self.square else tile + 1)
 
+    def products(self, tile_key, tile_query):
+        return dot_rows(
+            self.rows(KEY, tile_key, tile_key + 1), self.rows(QUERY, tile_query, tile_query + 1)
+        ) * (self.scaling * math.log2(math.e))
+
+
+class Diagonal(Region):
+    def __init__(self, arrays, places, scaling, ids_ref=None, head=None, base=None, width=None):
+        super().__init__(False, arrays, places, scaling)
+        self.ids_ref, self.head, self.base, self.width = ids_ref, head, base, width
+
+    def same(self, key_block, query_block):
+        ids_ref, head, base = self.ids_ref, self.head, self.base
+        return ids_ref[head, base + key_block] == ids_ref[head, base + query_block]
+
     def scores(self, tile_key, tile_query):
         per_tile = TILE // BLK
-        scores = (
-            dot_rows(
-                self.rows(KEY, tile_key, tile_key + 1), self.rows(QUERY, tile_query, tile_query + 1)
-            )
-            * self.to_log2
-        )
-        spread = lax.broadcasted_iota(jnp.int32, (BLK, BLK), 0) - lax.broadcasted_iota(
-            jnp.int32, (BLK, BLK), 1
-        )
+        scores = self.products(tile_key, tile_query)
+        spread = key_minus_query()
         rows = []
         for sub_key in range(per_tile):
             pieces = []
@@ -538,83 +540,111 @@
                 ]
                 key_block = tile_key * per_tile + sub_key
                 query_block = tile_query * per_tile + sub_query
-                apart = query_block - key_block
-                if self.square:
-                    apart += self.tiles * per_tile
-                same = (
-                    self.ids_ref[self.head, self.key_base + key_block]
-                    == self.ids_ref[self.head, self.query_base + query_block]
-                )
-                if apart < 0:
+                if key_block > query_block:
                     piece = jnp.full_like(piece, blocked_score)
-                elif apart == 0:
+                elif key_block == query_block:
                     piece = jnp.where(spread <= 0, piece, blocked_score)
-                elif apart == 1:
-                    least = jnp.where(same, -BLK, BLK - self.width)
+                elif key_block == query_block - 1:
+                    least = jnp.where(self.same(key_block, query_block), -BLK, BLK - self.width)
                     piece = jnp.where(spread > least, piece, blocked_score)
                 else:
-                    piece = piece + jnp.where(same, 0.0, blocked_score)
+                    piece = piece + jnp.where(
+                        self.same(key_block, query_block), 0.0, blocked_score
+                    )
                 pieces.append(piece)
             rows.append(jnp.concatenate(pieces, axis=1))
         return jnp.concatenate(rows, axis=0)
 
-    def statistics(self, weight_ref, towards_ref, out_ref, first_row):
-        for tile in range(self.tiles):
-            here = tile_rows(tile)
-            top = jnp.full((1, TILE), blocked_score, jnp.float32)
-            for other in self.keys_of(tile):
-                raw = self.scores(other, tile)
-                weight_ref[tile_rows(other), here] = raw
-                top = jnp.maximum(top, jnp.max(raw, axis=0, keepdims=True))
-            total = jnp.zeros((1, TILE), jnp.float32)
-            mass = jnp.zeros((1, TILE), jnp.float32)
-            for other in self.keys_of(tile):
-                there = tile_rows(other)
-                weight = jnp.exp2(weight_ref[there, here] - top)
-                towards = dot_rows(
-                    self.rows(VALUE, other, other + 1), self.rows(GRAD, tile, tile + 1)
+
+class Square(Region):
+    def __init__(self, arrays, scaling, bias_ref=None, corner_ref=None):
+        super().__init__(True, arrays, range(4), scaling)
+        self.bias_ref, self.corner_ref = bias_ref, corner_ref
+
+    def scores(self, tile_key, tile_query):
+        per_tile = TILE // BLK
+        scores = self.products(tile_key, tile_query)
+        rows = []
+        for sub_key in range(per_tile):
+            block = tile_key * per_tile + sub_key
+            row = scores[sub_key * BLK : (sub_key + 1) * BLK, :]
+            bias = self.bias_ref[block : block + 1, tile_rows(tile_query)]
+            if block == self.tiles * per_tile - 1 and tile_query == 0:
+                rows.append(
+                    jnp.concatenate(
+                        [row[:, :BLK] + self.corner_ref[...], row[:, BLK:] + bias[:, BLK:]], axis=1
+                    )
                 )
-                weight_ref[there, here] = weight
-                towards_ref[there, here] = towards
-                total += jnp.sum(weight, axis=0, keepdims=True)
-                mass += jnp.sum(weight * towards, axis=0, keepdims=True)
-            out_ref[first_row : first_row + 1, here] = top
-            out_ref[first_row + 1 : first_row + 2, here] = total
-            out_ref[first_row + 2 : first_row + 3, here] = mass
-
-    def gradients(self, weight_ref, towards_ref, top, log_total, delta, prob_low, grad_low, keys_flat):
-        keys_flat[...] = self.rows(KEY, 0, self.tiles).T
-        share = jnp.exp2(top - log_total)
-        temper = jnp.zeros((1, HD), jnp.float32)
-        query_parts, key_parts, value_parts = [], [], []
-        for tile in range(self.tiles):
-            here = tile_rows(tile)
-            for other in self.keys_of(tile):
-                there = tile_rows(other)
-                probability = weight_ref[there, here] * share[:, here]
-                prob_low[there, here] = probability.astype(jnp.bfloat16)
-                grad_low[there, here] = (
-                    probability * (towards_ref[there, here] - delta[:, here])
-                ).astype(jnp.bfloat16)
-            upto = slice(0, len(self.keys_of(tile)) * TILE)
-            query_part = dot_plain(keys_flat[:, upto], grad_low[upto, here]).T
-            temper += jnp.sum(
-                query_part * self.rows(QUERY, tile, tile + 1).astype(jnp.float32),
-                axis=0,
-                keepdims=True,
+            else:
+                rows.append(row + bias)
+        return jnp.concatenate(rows, axis=0)
+
+
+def key_minus_query():
+    shape = (BLK, BLK)
+    return lax.broadcasted_iota(jnp.int32, shape, 0) - lax.broadcasted_iota(jnp.int32, shape, 1)
+
+
+def statistics(region, weight_ref, towards_ref, out_ref, first_row):
+    for tile in range(region.tiles):
+        here = tile_rows(tile)
+        top = jnp.full((1, TILE), blocked_score, jnp.float32)
+        for other in region.keys_of(tile):
+            raw = region.scores(other, tile)
+            weight_ref[tile_rows(other), here] = raw
+            top = jnp.maximum(top, jnp.max(raw, axis=0, keepdims=True))
+        total = jnp.zeros((1, TILE), jnp.float32)
+        mass = jnp.zeros((1, TILE), jnp.float32)
+        for other in region.keys_of(tile):
+            there = tile_rows(other)
+            weight = jnp.exp2(weight_ref[there, here] - top)
+            towards = dot_rows(
+                region.rows(VALUE, other, other + 1), region.rows(GRAD, tile, tile + 1)
             )
-            query_parts.append(query_part)
-        for tile in range(self.tiles):
-            first = 0 if self.square else tile
-            onward = slice(first * TILE, self.tiles * TILE)
-            here = tile_rows(tile)
-            key_parts.append(
-                dot_plain(grad_low[here, onward], self.rows(QUERY, first, self.tiles))
-            )
-            value_parts.append(
-                dot_plain(prob_low[here, onward], self.rows(GRAD, first, self.tiles))
-            )
-        return query_parts, key_parts, value_parts, temper
+            weight_ref[there, here] = weight
+            towards_ref[there, here] = towards
+            total += jnp.sum(weight, axis=0, keepdims=True)
+            mass += jnp.sum(weight * towards, axis=0, keepdims=True)
+        out_ref[first_row : first_row + 1, here] = top
+        out_ref[first_row + 1 : first_row + 2, here] = total
+        out_ref[first_row + 2 : first_row + 3, here] = mass
+
+
+def gradients(
+    region, weight_ref, towards_ref, top, log_total, delta, prob_low, grad_low, keys_flat
+):
+    keys_flat[...] = region.rows(KEY, 0, region.tiles).T
+    share = jnp.exp2(top - log_total)
+    temper = jnp.zeros((1, HD), jnp.float32)
+    query_parts, key_parts, value_parts = [], [], []
+    for tile in range(region.tiles):
+        here = tile_rows(tile)
+        for other in region.keys_of(tile):
+            there = tile_rows(other)
+            probability = weight_ref[there, here] * share[:, here]
+            prob_low[there, here] = probability.astype(jnp.bfloat16)
+            grad_low[there, here] = (
+                probability * (towards_ref[there, here] - delta[:, here])
+            ).astype(jnp.bfloat16)
+        upto = slice(0, len(region.keys_of(tile)) * TILE)
+        query_part = dot_plain(keys_flat[:, upto], grad_low[upto, here]).T
+        temper += jnp.sum(
+            query_part * region.rows(QUERY, tile, tile + 1).astype(jnp.float32),
+            axis=0,
+            keepdims=True,
+        )
+        query_parts.append(query_part)
+    for tile in range(region.tiles):
+        first = 0 if region.square else tile
+        onward = slice(first * TILE, region.tiles * TILE)
+        here = tile_rows(tile)
+        key_parts.append(
+            dot_plain(grad_low[here, onward], region.rows(QUERY, first, region.tiles))
+        )
+        value_parts.append(
+            dot_plain(prob_low[here, onward], region.rows(GRAD, first, region.tiles))
+        )
+    return query_parts, key_parts, value_parts, temper
 
 
 def merged(first, second):
@@ -641,49 +671,61 @@
         ].astype(jnp.bfloat16)
 
 
-def diagonal_region(slot, settings, half_count, arrays_ref):
+def scale_row(stats_ref, slot):
+    return stats_ref[6 + slot : 7 + slot, :HD]
+
+
+def scaled(region, parts):
+    return [
+        [value * scale for value in part]
+        for part, scale in zip(parts, (region.scaling, region.scaling, 1.0))
+    ]
+
+
+def within_kernel(
+    softness_ref, ids_ref, span_ref, in_ref, arrays_ref, stats_ref, bias_ref, corner_ref,
+    parts_ref, temper_ref, own_weight, own_towards, other_weight, other_towards, *scratch,
+    half_count
+):
     me, half, _ = position(half_count)
-    head = me ^ (slot * half_count)
-    places = [slot * 4 + place for place in range(4)]
-    base = half * half_count
-    return Region(head, settings, False, base, base, arrays_ref, places)
-
-
-def square_region(settings, half_count, square_ref):
-    me = lax.axis_index("seq")
-    return Region(me, settings, True, 0, half_count, square_ref, range(4))
-
-
-def within_kernel(
-    softness_ref, ids_ref, span_ref, in_ref, arrays_ref, stats_ref, parts_ref, temper_ref,
-    own_weight, own_towards, other_weight, other_towards, *scratch, half_count
-):
-    _, half, _ = position(half_count)
     for block in range(half_count):
         for place in range(8):
             arrays_ref[place, block * BLK : (block + 1) * BLK, :] = in_ref[
                 block, place * BLK : (place + 1) * BLK, :
             ]
-    settings = (softness_ref, ids_ref, span_ref)
     kept = ((own_weight, own_towards), (other_weight, other_towards))
-    regions = [diagonal_region(slot, settings, half_count, arrays_ref) for slot in range(2)]
-    for slot, region in enumerate(regions):
-        region.statistics(*kept[slot], stats_ref, slot * 3)
+    for slot in range(2):
+        head = me ^ (slot * half_count)
+        scaling = softness_ref[head] * (1.0 / math.sqrt(HD))
+        places = [slot * 4 + place for place in range(4)]
+        region = Diagonal(
+            arrays_ref, places, scaling, ids_ref, head, half * half_count, span_ref[head]
+        )
+        statistics(region, *kept[slot], stats_ref, slot * 3)
+        stats_ref[6 + slot : 7 + slot, :] = jnp.full((1, stats_ref.shape[1]), scaling, jnp.float32)
+    for key_block in range(half_count):
+        for query_block in range(half_count):
+            same = ids_ref[me, key_block] == ids_ref[me, half_count + query_block]
+            bias_ref[key_block : key_block + 1, query_block * BLK : (query_block + 1) * BLK] = (
+                jnp.full((1, BLK), jnp.where(same, 0.0, blocked_score), jnp.float32)
+            )
+    same = ids_ref[me, half_count - 1] == ids_ref[me, half_count]
+    least = jnp.where(same, -BLK, BLK - span_ref[me])
+    corner_ref[...] = jnp.where(key_minus_query() > least, 0.0, blocked_score)
     temper_ref[...] = jnp.zeros_like(temper_ref)
 
     @pl.when(half == 0)
     def _():
+        region = Diagonal(arrays_ref, range(4), scale_row(stats_ref, 0))
         single = alone(three_rows(stats_ref, 0))
-        *parts, temper = regions[0].gradients(*kept[0], stats_ref[0:1, :], *single, *scratch)
-        for place, tiles in enumerate(parts):
+        *parts, temper = gradients(region, *kept[0], stats_ref[0:1, :], *single, *scratch)
+        for place, tiles in enumerate(scaled(region, parts)):
             for tile, value in enumerate(tiles):
                 parts_ref[place, tile_rows(tile), :] = value
         temper_ref[0:1, :] = temper
 
 
-def square_kernel(
-    softness_ref, ids_ref, span_ref, arrays_ref, stats_ref, *refs, half_count
-):
+def square_kernel(arrays_ref, stats_ref, bias_ref, corner_ref, *refs, half_count):
     across_refs = refs[: half_count // 2]
     square_ref, message_ref, square_stats, weight, towards = refs[half_count // 2 :]
     _, half, place = position(half_count)
@@ -698,61 +740,58 @@
     kept_second = jnp.where(half == 0, VALUE, GRAD)
     square_ref[kept_first, :, :] = arrays_ref[kept_first, :, :]
     square_ref[kept_second, :, :] = arrays_ref[kept_second, :, :]
-    region = square_region((softness_ref, ids_ref, span_ref), half_count, square_ref)
-    region.statistics(weight, towards, square_stats, 0)
+    region = Square(square_ref, stats_ref[6:7, :TILE], bias_ref, corner_ref)
+    statistics(region, weight, towards, square_stats, 0)
     for row in range(3):
         message_ref[row : row + 1, :] = jnp.where(
             half == 0, square_stats[row : row + 1, :], stats_ref[3 + row : 4 + row, :]
         )
 
 
-def other_diagonal(region, kept, stats_ref, totals, scratch, within_ref):
-    *parts, temper = region.gradients(*kept, stats_ref[3:4, :], *totals, *scratch)
-    scales = (region.scaling, region.scaling, 1.0)
-    for array, (part, scale) in enumerate(zip(parts, scales)):
-        for tile in range(region.tiles):
-            put(within_ref, 3 + array, tile, part[tile] * scale)
+def other_diagonal(arrays_ref, kept, stats_ref, totals, scratch, within_ref):
+    region = Diagonal(arrays_ref, range(4, 8), scale_row(stats_ref, 1))
+    *parts, temper = gradients(region, *kept, stats_ref[3:4, :], *totals, *scratch)
+    for array, tiles in enumerate(scaled(region, parts)):
+        for tile, value in enumerate(tiles):
+            put(within_ref, 3 + array, tile, value)
     return temper
 
 
 def first_kernel(
-    softness_ref, ids_ref, span_ref, arrays_ref, square_ref, stats_ref, square_stats, temper_in,
+    arrays_ref, square_ref, stats_ref, square_stats, temper_in,
     own_weight, own_towards, other_weight, other_towards, square_weight, square_towards,
     within_ref, across_ref, temper_ref, *scratch, half_count
 ):
     _, half, _ = position(half_count)
-    settings = (softness_ref, ids_ref, span_ref)
     temper_ref[...] = temper_in[...]
 
     @pl.when(half == 0)
     def _():
-        region = diagonal_region(1, settings, half_count, arrays_ref)
         totals = alone(three_rows(stats_ref, 3))
         temper_ref[1:2, :] = other_diagonal(
-            region, (other_weight, other_towards), stats_ref, totals, scratch, within_ref
+            arrays_ref, (other_weight, other_towards), stats_ref, totals, scratch, within_ref
         )
 
     @pl.when(half == 1)
     def _():
         totals = merged(three_rows(stats_ref, 0), three_rows(square_stats, 0))
-        square = square_region(settings, half_count, square_ref)
-        scales = (square.scaling, square.scaling, 1.0)
-        across_query, *foreign, square_temper = square.gradients(
-            square_weight, square_towards, square_stats[0:1, :], *totals, *scratch
-        )
-        for array, part in enumerate(foreign):
-            for tile in range(square.tiles):
-                across_ref[array, tile_rows(tile), :] = (part[tile] * scales[1 + array]).astype(
-                    jnp.bfloat16
-                )
-        diagonal = diagonal_region(0, settings, half_count, arrays_ref)
-        *parts, temper = diagonal.gradients(
-            own_weight, own_towards, stats_ref[0:1, :], *totals, *scratch
-        )
+        square = Square(square_ref, scale_row(stats_ref, 0))
+        *parts, square_temper = gradients(
+            square, square_weight, square_towards, square_stats[0:1, :], *totals, *scratch
+        )
+        across_query, *foreign = scaled(square, parts)
+        for array, tiles in enumerate(foreign):
+            for tile, value in enumerate(tiles):
+                across_ref[array, tile_rows(tile), :] = value.astype(jnp.bfloat16)
+        diagonal = Diagonal(arrays_ref, range(4), scale_row(stats_ref, 0))
+        *parts, temper = gradients(
+            diagonal, own_weight, own_towards, stats_ref[0:1, :], *totals, *scratch
+        )
+        query_parts, key_parts, value_parts = scaled(diagonal, parts)
         for tile in range(square.tiles):
-            put(within_ref, 0, tile, (parts[0][tile] + across_query[tile]) * scales[0])
-            put(within_ref, 1, tile, parts[1][tile] * scales[1])
-            put(within_ref, 2, tile, parts[2][tile])
+            put(within_ref, 0, tile, query_parts[tile] + across_query[tile])
+            put(within_ref, 1, tile, key_parts[tile])
+            put(within_ref, 2, tile, value_parts[tile])
         temper_ref[0:1, :] = temper + square_temper
 
 
@@ -771,29 +810,28 @@
 
 
 def finish_kernel(
-    softness_ref, ids_ref, span_ref, arrays_ref, square_ref, message_ref, received_ref,
-    stats_ref, square_stats, parts_ref, temper_ref,
-    square_weight, square_towards, other_weight, other_towards, across_in, begun_ref,
+    arrays_ref, square_ref, message_ref, received_ref, stats_ref, square_stats, parts_ref,
+    temper_ref, square_weight, square_towards, other_weight, other_towards, across_in, begun_ref,
     within_ref, *refs, half_count
 ):
     foreign_refs = refs[:2]
     across, temper, *scratch = refs[2:]
     _, half, place = position(half_count)
-    settings = (softness_ref, ids_ref, span_ref)
     temper[...] = temper_ref[...]
 
     @pl.when(half == 0)
     def _():
         totals = merged(three_rows(message_ref, 0), three_rows(received_ref, 0))
-        region = square_region(settings, half_count, square_ref)
-        query_parts, key_parts, value_parts, square_temper = region.gradients(
-            square_weight, square_towards, square_stats[0:1, :], *totals, *scratch
-        )
+        region = Square(square_ref, scale_row(stats_ref, 0))
+        *parts, square_temper = gradients(
+            region, square_weight, square_towards, square_stats[0:1, :], *totals, *scratch
+        )
+        query_parts, key_parts, value_parts = scaled(region, parts)
         for tile in range(region.tiles):
             here = tile_rows(tile)
-            across[0, here, :] = (query_parts[tile] * region.scaling).astype(jnp.bfloat16)
-            put(within_ref, 0, tile, parts_ref[0, here, :] * region.scaling)
-            put(within_ref, 1, tile, (parts_ref[1, here, :] + key_parts[tile]) * region.scaling)
+            across[0, here, :] = query_parts[tile].astype(jnp.bfloat16)
+            put(within_ref, 0, tile, parts_ref[0, here, :])
+            put(within_ref, 1, tile, parts_ref[1, here, :] + key_parts[tile])
             put(within_ref, 2, tile, parts_ref[2, here, :] + value_parts[tile])
         across[1] = jnp.zeros(across.shape[1:], jnp.bfloat16)
         within_ref[:, 3 * BLK : 6 * BLK, :] = begun_ref[:, 3 * BLK : 6 * BLK, :]
@@ -802,9 +840,8 @@
     @pl.when(half == 1)
     def _():
         totals = merged(three_rows(message_ref, 0), three_rows(received_ref, 0))
-        region = diagonal_region(1, settings, half_count, arrays_ref)
         temper[1:2, :] = other_diagonal(
-            region, (other_weight, other_towards), stats_ref, totals, scratch, within_ref
+            arrays_ref, (other_weight, other_towards), stats_ref, totals, scratch, within_ref
         )
         across[...] = across_in[...]
         within_ref[:, : 3 * BLK, :] = begun_ref[:, : 3 * BLK, :]
@@ -930,12 +967,12 @@
             array_in, "seq", split_axis=0, concat_axis=0, axis_index_groups=groups, tiled=True
         )
 
-    def call(kernel, name, operands, out_shape, scratch, flops, vmem_mib):
+    def call(kernel, name, operands, out_shape, scratch, flops, vmem_mib, scalars=()):
         return kernel_call(
             functools.partial(kernel, half_count=half_count),
             name,
-            (*settings, *operands),
-            [smem] * 3 + [vmem] * len(operands),
+            (*scalars, *operands),
+            [smem] * len(scalars) + [vmem] * len(operands),
             out_shape,
             scratch,
             vmem_mib,
@@ -949,20 +986,28 @@
     foreign = crossed(*foreign, half_count)
     kept_parts = jax.ShapeDtypeStruct((3, tokens, HD), jnp.float32)
     tempers = jax.ShapeDtypeStruct((8, HD), jnp.float32)
-    arrays, stats, parts, temper, own_weight, own_towards, other_weight, other_towards = call(
+    (
+        arrays, stats, bias, corner, parts, temper,
+        own_weight, own_towards, other_weight, other_towards,
+    ) = call(
         within_kernel,
         "diagonal_statistics",
         (arrived,),
-        [jax.ShapeDtypeStruct((8, tokens, HD), jnp.bfloat16), rows_of_stats, kept_parts, tempers]
+        [
+            jax.ShapeDtypeStruct((8, tokens, HD), jnp.bfloat16), rows_of_stats,
+            jax.ShapeDtypeStruct((half_count, tokens), jnp.float32),
+            jax.ShapeDtypeStruct((BLK, BLK), jnp.float32), kept_parts, tempers,
+        ]
         + [pairs] * 4,
         lows,
         2 * pair_flops,
         20,
+        settings,
     )
     square, message, square_stats, square_weight, square_towards = call(
         square_kernel,
         "square_statistics",
-        (arrays, stats, *foreign),
+        (arrays, stats, bias, corner, *foreign),
         [jax.ShapeDtypeStruct((4, tokens, HD), jnp.bfloat16)] + [rows_of_stats] * 2 + [pairs] * 2,
         [],
         2 * pair_flops,

time: 103 us -> 101 us (0.981)
  Pallas kernels: 18 us -> 15.8 us
    pallas_call x8, Pallas kernels: 17.9 us -> 15.8 us  [kernel_call(): pl.pallas_call(kernel, out_shape=out_shape, in_specs=in_specs, out_specs=...]
  transfers between devices with their start and end apart: 14 -> 14, of which waited for: 11 -> 11; matrix products, arithmetic and copies ran while one was open for 0% -> 0% of each run, Pallas kernels for 8% -> 7%
where the time goes in v9:
time: 101 us
  waiting for transfers between devices  56.9 us (56%)
  starting transfers between devices  26.9 us (27%)
  Pallas kernels  15.8 us (16%)
    ppermute x8, waiting for transfers between devices, crossed(): lax.ppermute(message, 'seq', [(source, source ^ half_count + 2 * step) fo...  28.3 us
    all_to_all x2, waiting for transfers between devices, exchange_within(): lax.all_to_all(array_in, 'seq', split_axis=0, concat_axis=0, axis_index_g...  21.7 us
    pallas_call x8, Pallas kernels, kernel_call(): pl.pallas_call(kernel, out_shape=out_shape, in_specs=in_specs, out_specs=...  15.8 us
    ppermute x8, starting transfers between devices, crossed(): lax.ppermute(message, 'seq', [(source, source ^ half_count + 2 * step) fo...  15.4 us
    all_to_all x2, starting transfers between devices, exchange_within(): lax.all_to_all(array_in, 'seq', split_axis=0, concat_axis=0, axis_index_g...  8.98 us
    ppermute x1, waiting for transfers between devices, head_shards(): received = lax.ppermute(message, 'seq', swap)  3.59 us
    ppermute x2, waiting for transfers between devices, crossed(): lax.ppermute(given, 'seq', [(source, source ^ 1) for source in devices])  2.73 us
  transfers between devices with their start and end apart: 14, of which 11 were waited for; matrix products, arithmetic and copies ran while one was open for 0% of the time, Pallas kernels for 7%

profile of v9, /device:TPU:0, one launch (start us, length us, event | category | flops | bytes accessed | tf_op | source)
XLA Modules:
  0.0 101.1 jit_solution(6600002235937182956)
XLA Ops:
  0.6 2.9 %pack_heads.1 = (bf16[8,1024,128]{2,1,0:T(8,128)(2,1)}, bf16[4,256,128]{2,1,0:T(8,128)(2,1)}, bf16[4,256,128]{2,1,0:T(8,128)(2,1)}) custom-call(bf16[1,128,2048]{2,1,0:T(8,128)(2,1)} %refs_0_.1, bf16[1,128,2048]{2,1,0:T(8,128)(2,1)} %refs_1_.1, bf16[1,128,2048]{2,1,0:T(8,128)(2,1)} %refs_2_.1, bf16[1,128,2048]{2,1,0:T(8,128)(2,1)} %refs_3_.1), custom_call_target="tpu_custom_call" | custom-call | bytes 4718592 | tf_op jit(solution)/shard_map/pack_heads/pallas_call | solution.py:409
  3.6 5.4 %all-to-all-start = ((bf16[8,1024,128]{2,1,0:T(8,128)(2,1)}), bf16[8,1024,128]{2,1,0:T(8,128)(2,1)S(1)}, u32[]{:S(2)}, u32[]{:S(2)}) async-start(bf16[8,1024,128]{2,1,0:T(8,128)(2,1)} %get-tuple-element.39), calls=%async_computation | async-start | bytes 4194304 | tf_op jit(solution)/shard_map/all_to_all | solution.py:966
  9.5 1.4 %collective-permute-done.taken_ref = bf16[4,256,128]{2,1,0:T(8,128)(2,1)S(1)} collective-permute-done((bf16[4,256,128]{2,1,0:T(8,128)(2,1)S(1)}, bf16[4,256,128]{2,1,0:T(8,128)(2,1)S(1)}, u32[]{:S(2)}, u32[]{:S(2)}) %collective-permute-start) | collective-permute-done | bytes 262176 | tf_op jit(solution)/shard_map/ppermute | solution.py:925
  11.0 2.7 %collective-permute-start.1 = (bf16[2,256,128]{2,1,0:T(8,128)(2,1)S(1)}, bf16[2,256,128]{2,1,0:T(8,128)(2,1)S(1)}, u32[]{:S(2)}, u32[]{:S(2)}) collective-permute-start(bf16[2,256,128]{2,1,0:T(8,128)(2,1)S(1)} %get-tuple-element.46), channel_id=1, source_target_pairs={{0,16},{2,18},{4,20},{6,22},{8,24},{10,26},{12,28},{14,30},{16,0},... | collective-permute-start | bytes 393224 | tf_op jit(solution)/shard_map/ppermute | solution.py:936
  13.6 1.5 %collective-permute-start.2 = (bf16[2,256,128]{2,1,0:T(8,128)(2,1)S(1)}, bf16[2,256,128]{2,1,0:T(8,128)(2,1)S(1)}, u32[]{:S(2)}, u32[]{:S(2)}) collective-permute-start(bf16[2,256,128]{2,1,0:T(8,128)(2,1)S(1)} %get-tuple-element.47), channel_id=1, source_target_pairs={{0,20},{2,22},{4,16},{6,18},{8,28},{10,30},{12,24},{14,26},{16,4},... | collective-permute-start | bytes 393224 | tf_op jit(solution)/shard_map/ppermute | solution.py:936
  15.1 3.5 %collective-permute-start.3 = (bf16[2,256,128]{2,1,0:T(8,128)(2,1)S(1)}, bf16[2,256,128]{2,1,0:T(8,128)(2,1)S(1)}, u32[]{:S(2)}, u32[]{:S(2)}) collective-permute-start(bf16[2,256,128]{2,1,0:T(8,128)(2,1)S(1)} %get-tuple-element.48), channel_id=1, source_target_pairs={{0,24},{2,26},{4,28},{6,30},{8,16},{10,18},{12,20},{14,22},{16,8},... | collective-permute-start | bytes 393224 | tf_op jit(solution)/shard_map/ppermute | solution.py:936
  18.7 21.7 %all-to-all-done.in_ref = bf16[8,1024,128]{2,1,0:T(8,128)(2,1)S(1)} async-done(((bf16[8,1024,128]{2,1,0:T(8,128)(2,1)}), bf16[8,1024,128]{2,1,0:T(8,128)(2,1)S(1)}, u32[]{:S(2)}, u32[]{:S(2)}) %all-to-all-start) | async-done | bytes 2097184 | tf_op jit(solution)/shard_map/all_to_all | solution.py:966
  40.4 4.5 %diagonal_statistics.1 = (bf16[8,1024,128]{2,1,0:T(8,128)(2,1)S(1)}, f32[8,1024]{1,0:T(8,128)S(1)}, f32[8,1024]{1,0:T(8,128)S(1)}, f32[128,128]{1,0:T(8,128)S(1)...) custom-call(f32[16]{0:T(128)S(1)} %copy-done.2, ...), custom_call_target="tpu_custom_call" | custom-call | flops 536870912 | bytes 22680704 | tf_op jit(solution)/shard_map/diagonal_statistics/pallas_call | solution.py:409
  45.7 3.2 %collective-permute-done.4.refs_3_ = bf16[2,256,128]{2,1,0:T(8,128)(2,1)S(1)} collective-permute-done((bf16[2,256,128]{2,1,0:T(8,128)(2,1)S(1)}, bf16[2,256,128]{2,1,0:T(8,128)(2,1)S(1)}, u32[]{:S(2)}, u32[]{:S(2)}) %collective-permute-start.4) | collective-permute-done | bytes 131104 | tf_op jit(solution)/shard_map/ppermute | solution.py:936
  48.9 2.0 %square_statistics.1 = (bf16[4,1024,128]{2,1,0:T(8,128)(2,1)S(1)}, f32[8,1024]{1,0:T(8,128)S(1)}, f32[8,1024]{1,0:T(8,128)S(1)}, f32[1024,1024]{1,0:T(8,128)S(1)}, f32[1024,1024]{1,0:T(8,128)S(1)}) custom-call(bf16[8,1024,128]{2,1,0:T(8,128)(2,1)S(1)} %get-tuple-element.40.arrays_ref, f32[8,1024]{1,0:T(8,128)S(1)} %get-tuple-element.41.stats_ref, ...), custom_call_target="tpu_custom_call" | custom-call | flops 536870912 | bytes 12255232 | tf_op jit(solution)/shard_map/square_statistics/pallas_call | solution.py:409
  50.9 1.4 %gradients_before_totals.1 = (bf16[8,768,128]{2,1,0:T(8,128)(2,1)S(1)}, bf16[2,1024,128]{2,1,0:T(8,128)(2,1)S(1)}, f32[8,128]{1,0:T(8,128)S(1)}) custom-call(bf16[8,1024,128]{2,1,0:T(8,128)(2,1)S(1)} %get-tuple-element.40.arrays_ref, bf16[4,1024,128]{2,1,0:T(8,128)(2,1)S(1)} %get-tuple-element.50.square_ref, f32[8,1024]{1,0:T(8,128)S(1)} %get-tuple-element.41.stats_ref, ...), custom_call_target="tpu_custom_call" | custom-call | flops 1073741824 | bytes 30482432 | tf_op jit(solution)/shard_map/gradients_before_totals/pallas_call | solution.py:409
  52.3 3.6 %collective-permute-done.5.received_ref = f32[8,1024]{1,0:T(8,128)S(1)} collective-permute-done((f32[8,1024]{1,0:T(8,128)S(1)}, f32[8,1024]{1,0:T(8,128)S(1)}, u32[]{:S(2)}, u32[]{:S(2)}) %collective-permute-start.5) | collective-permute-done | bytes 32800 | tf_op jit(solution)/shard_map/ppermute | solution.py:1017
  55.9 3.4 %gradients_after_totals.1 = (bf16[8,784,128]{2,1,0:T(8,128)(2,1)}, bf16[4,272,128]{2,1,0:T(8,128)(2,1)S(1)}, bf16[4,272,128]{2,1,0:T(8,128)(2,1)S(1)}) custom-call(bf16[8,1024,128]{2,1,0:T(8,128)(2,1)S(1)} %get-tuple-element.40.arrays_ref, bf16[4,1024,128]{2,1,0:T(8,128)(2,1)S(1)} %get-tuple-element.50.square_ref, ...), custom_call_target="tpu_custom_call" | custom-call | flops 536870912 | bytes 25890816 | tf_op jit(solution)/shard_map/gradients_after_totals/pallas_call | solution.py:409
  59.3 3.6 %all-to-all-start.1 = ((bf16[8,784,128]{2,1,0:T(8,128)(2,1)}), bf16[8,784,128]{2,1,0:T(8,128)(2,1)S(1)}, u32[]{:S(2)}, u32[]{:S(2)}) async-start(bf16[8,784,128]{2,1,0:T(8,128)(2,1)} %get-tuple-element.64), calls=%async_computation.1 | async-start | bytes 3211264 | tf_op jit(solution)/shard_map/all_to_all | solution.py:966
  63.3 1.3 %collective-permute-done.6.taken_ref = bf16[4,272,128]{2,1,0:T(8,128)(2,1)S(1)} collective-permute-done((bf16[4,272,128]{2,1,0:T(8,128)(2,1)S(1)}, bf16[4,272,128]{2,1,0:T(8,128)(2,1)S(1)}, u32[]{:S(2)}, u32[]{:S(2)}) %collective-permute-start.6) | collective-permute-done | bytes 278560 | tf_op jit(solution)/shard_map/ppermute | solution.py:925
  66.0 2.9 %collective-permute-start.8 = (bf16[2,272,128]{2,1,0:T(8,128)(2,1)S(1)}, bf16[2,272,128]{2,1,0:T(8,128)(2,1)S(1)}, u32[]{:S(2)}, u32[]{:S(2)}) collective-permute-start(bf16[2,272,128]{2,1,0:T(8,128)(2,1)S(1)} %get-tuple-element.68), channel_id=1, source_target_pairs={{0,20},{2,22},{4,16},{6,18},{8,28},{10,30},{12,24},{14,26},{16,4},... | collective-permute-start | bytes 417800 | tf_op jit(solution)/shard_map/ppermute | solution.py:936
  68.9 2.1 %collective-permute-start.9 = (bf16[2,272,128]{2,1,0:T(8,128)(2,1)S(1)}, bf16[2,272,128]{2,1,0:T(8,128)(2,1)S(1)}, u32[]{:S(2)}, u32[]{:S(2)}) collective-permute-start(bf16[2,272,128]{2,1,0:T(8,128)(2,1)S(1)} %get-tuple-element.69), channel_id=1, source_target_pairs={{0,24},{2,26},{4,28},{6,30},{8,16},{10,18},{12,20},{14,22},{16,8},... | collective-permute-start | bytes 417800 | tf_op jit(solution)/shard_map/ppermute | solution.py:936
  71.0 1.4 %collective-permute-start.10 = (bf16[2,272,128]{2,1,0:T(8,128)(2,1)S(1)}, bf16[2,272,128]{2,1,0:T(8,128)(2,1)S(1)}, u32[]{:S(2)}, u32[]{:S(2)}) collective-permute-start(bf16[2,272,128]{2,1,0:T(8,128)(2,1)S(1)} %get-tuple-element.70), channel_id=1, source_target_pairs={{0,28},{2,30},{4,24},{6,26},{8,20},{10,22},{12,16},{14,18},{16,12}... | collective-permute-start | bytes 417800 | tf_op jit(solution)/shard_map/ppermute | solution.py:936
  72.4 12.0 %collective-permute-done.7.refs_0_ = bf16[2,272,128]{2,1,0:T(8,128)(2,1)S(1)} collective-permute-done((bf16[2,272,128]{2,1,0:T(8,128)(2,1)S(1)}, bf16[2,272,128]{2,1,0:T(8,128)(2,1)S(1)}, u32[]{:S(2)}, u32[]{:S(2)}) %collective-permute-start.7) | collective-permute-done | bytes 139296 | tf_op jit(solution)/shard_map/ppermute | solution.py:936
  84.4 3.0 %collective-permute-done.8.refs_1_ = bf16[2,272,128]{2,1,0:T(8,128)(2,1)S(1)} collective-permute-done((bf16[2,272,128]{2,1,0:T(8,128)(2,1)S(1)}, bf16[2,272,128]{2,1,0:T(8,128)(2,1)S(1)}, u32[]{:S(2)}, u32[]{:S(2)}) %collective-permute-start.8) | collective-permute-done | bytes 139296 | tf_op jit(solution)/shard_map/ppermute | solution.py:936
  87.4 6.0 %collective-permute-done.9.refs_2_ = bf16[2,272,128]{2,1,0:T(8,128)(2,1)S(1)} collective-permute-done((bf16[2,272,128]{2,1,0:T(8,128)(2,1)S(1)}, bf16[2,272,128]{2,1,0:T(8,128)(2,1)S(1)}, u32[]{:S(2)}, u32[]{:S(2)}) %collective-permute-start.9) | collective-permute-done | bytes 139296 | tf_op jit(solution)/shard_map/ppermute | solution.py:936
  93.3 3.4 %collective-permute-done.10.refs_3_ = bf16[2,272,128]{2,1,0:T(8,128)(2,1)S(1)} collective-permute-done((bf16[2,272,128]{2,1,0:T(8,128)(2,1)S(1)}, bf16[2,272,128]{2,1,0:T(8,128)(2,1)S(1)}, u32[]{:S(2)}, u32[]{:S(2)}) %collective-permute-start.10) | collective-permute-done | bytes 139296 | tf_op jit(solution)/shard_map/ppermute | solution.py:936
  96.8 1.5 %collective-permute-start.11 = (f32[16,128]{1,0:T(8,128)S(1)}, f32[16,128]{1,0:T(8,128)S(1)}, u32[]{:S(2)}, u32[]{:S(2)}) collective-permute-start(f32[16,128]{1,0:T(8,128)S(1)} %temper_sums.1), channel_id=1, source_target_pairs={{0,1},{1,0},{2,3},{3,2},{4,5},{5,4},{6,7},{7,6},{8,9},{9,8},{10,11... | collective-permute-start | bytes 24584 | tf_op jit(solution)/shard_map/ppermute | solution.py:1053
  98.3 1.5 %unpack_heads.1 = (bf16[1,128,2048]{2,1,0:T(8,128)(2,1)}, bf16[1,128,2048]{2,1,0:T(8,128)(2,1)}, bf16[1,128,2048]{2,1,0:T(8,128)(2,1)}) custom-call(bf16[8,784,128]{2,1,0:T(8,128)(2,1)S(1)} %all-to-all-done.1.within_ref, bf16[2,272,128]{2,1,0:T(8,128)(2,1)S(1)} %collective-permute-done.7.refs_0_, bf16[2,272,128]{2,1,0:T(8,128)(2,1)S(1)} %collective-permute-done.8.refs_1_, ...), custom_call_target="tpu_custom_call" | custom-call | bytes 3735552 | tf_op jit(solution)/shard_map/unpack_heads/pallas_call | solution.py:409
  (24 shorter events, 4.6 us)
Async XLA Ops:
  3.6 5.5 %copy-start.4 = (bf16[4,256,128]{2,1,0:T(8,128)(2,1)S(1)}, bf16[4,256,128]{2,1,0:T(8,128)(2,1)}, u32[]{:S(2)}) copy-start(bf16[4,256,128]{2,1,0:T(8,128)(2,1)} %get-tuple-element.45) | copy-start | bytes 786436
  3.6 7.4 %copy-start = (bf16[4,256,128]{2,1,0:T(8,128)(2,1)S(1)}, bf16[4,256,128]{2,1,0:T(8,128)(2,1)}, u32[]{:S(2)}) copy-start(bf16[4,256,128]{2,1,0:T(8,128)(2,1)} %get-tuple-element.44.kept_ref) | copy-start | bytes 786436
  3.6 36.8 %copy-start.1 = (s32[1,16,16,1]{2,3,1,0:T(1,128)S(1)}, s32[1,16,16,1]{2,3,1,0:T(1,128)}, u32[]{:S(2)}) copy-start(s32[1,16,16,1]{2,3,1,0:T(1,128)} %param.12) | copy-start | bytes 3076
  3.6 36.7 %copy-start.2 = (f32[16]{0:T(128)S(1)}, f32[16]{0:T(128)}, u32[]{:S(2)}) copy-start(f32[16]{0:T(128)} %softness_ref.1) | copy-start | bytes 196
  3.6 36.7 %copy-start.3 = (s32[16]{0:T(128)S(1)}, s32[16]{0:T(128)}, u32[]{:S(2)}) copy-start(s32[16]{0:T(128)} %span_ref.1) | copy-start | bytes 196
  3.6 36.7 %all-to-all-start = ((bf16[8,1024,128]{2,1,0:T(8,128)(2,1)}), bf16[8,1024,128]{2,1,0:T(8,128)(2,1)S(1)}, u32[]{:S(2)}, u32[]{:S(2)}) async-start(bf16[8,1024,128]{2,1,0:T(8,128)(2,1)} %get-tuple-element.39), calls=%async_computation | async-start | bytes 4194304 | tf_op jit(solution)/shard_map/all_to_all | solution.py:966
  9.0 1.9 %collective-permute-start = (bf16[4,256,128]{2,1,0:T(8,128)(2,1)S(1)}, bf16[4,256,128]{2,1,0:T(8,128)(2,1)S(1)}, u32[]{:S(2)}, u32[]{:S(2)}) collective-permute-start(bf16[4,256,128]{2,1,0:T(8,128)(2,1)S(1)} %copy-done.4), channel_id=1, source_target_pairs={{0,2},{2,0},{4,6},{6,4},{8,10},{10,8},{12,14},{14,12},{16,18},{18,... | collective-permute-start | bytes 786440 | tf_op jit(solution)/shard_map/ppermute | solution.py:925
  11.0 33.9 %collective-permute-start.1 = (bf16[2,256,128]{2,1,0:T(8,128)(2,1)S(1)}, bf16[2,256,128]{2,1,0:T(8,128)(2,1)S(1)}, u32[]{:S(2)}, u32[]{:S(2)}) collective-permute-start(bf16[2,256,128]{2,1,0:T(8,128)(2,1)S(1)} %get-tuple-element.46), channel_id=1, source_target_pairs={{0,16},{2,18},{4,20},{6,22},{8,24},{10,26},{12,28},{14,30},{16,0},... | collective-permute-start | bytes 393224 | tf_op jit(solution)/shard_map/ppermute | solution.py:936
  13.6 31.3 %collective-permute-start.2 = (bf16[2,256,128]{2,1,0:T(8,128)(2,1)S(1)}, bf16[2,256,128]{2,1,0:T(8,128)(2,1)S(1)}, u32[]{:S(2)}, u32[]{:S(2)}) collective-permute-start(bf16[2,256,128]{2,1,0:T(8,128)(2,1)S(1)} %get-tuple-element.47), channel_id=1, source_target_pairs={{0,20},{2,22},{4,16},{6,18},{8,28},{10,30},{12,24},{14,26},{16,4},... | collective-permute-start | bytes 393224 | tf_op jit(solution)/shard_map/ppermute | solution.py:936
  15.1 30.6 %collective-permute-start.3 = (bf16[2,256,128]{2,1,0:T(8,128)(2,1)S(1)}, bf16[2,256,128]{2,1,0:T(8,128)(2,1)S(1)}, u32[]{:S(2)}, u32[]{:S(2)}) collective-permute-start(bf16[2,256,128]{2,1,0:T(8,128)(2,1)S(1)} %get-tuple-element.48), channel_id=1, source_target_pairs={{0,24},{2,26},{4,28},{6,30},{8,16},{10,18},{12,20},{14,22},{16,8},... | collective-permute-start | bytes 393224 | tf_op jit(solution)/shard_map/ppermute | solution.py:936
  18.6 30.3 %collective-permute-start.4 = (bf16[2,256,128]{2,1,0:T(8,128)(2,1)S(1)}, bf16[2,256,128]{2,1,0:T(8,128)(2,1)S(1)}, u32[]{:S(2)}, u32[]{:S(2)}) collective-permute-start(bf16[2,256,128]{2,1,0:T(8,128)(2,1)S(1)} %get-tuple-element.49), channel_id=1, source_target_pairs={{0,28},{2,30},{4,24},{6,26},{8,20},{10,22},{12,16},{14,18},{16,12}... | collective-permute-start | bytes 393224 | tf_op jit(solution)/shard_map/ppermute | solution.py:936
  50.9 5.0 %collective-permute-start.5 = (f32[8,1024]{1,0:T(8,128)S(1)}, f32[8,1024]{1,0:T(8,128)S(1)}, u32[]{:S(2)}, u32[]{:S(2)}) collective-permute-start(f32[8,1024]{1,0:T(8,128)S(1)} %get-tuple-element.51.message_ref), channel_id=1, source_target_pairs={{0,16},{2,18},{4,20},{6,22},{8,24},{10,26},{12,28},{14,30},{16,0},... | collective-permute-start | bytes 98312 | tf_op jit(solution)/shard_map/ppermute | solution.py:1017
  59.3 37.4 %all-to-all-start.1 = ((bf16[8,784,128]{2,1,0:T(8,128)(2,1)}), bf16[8,784,128]{2,1,0:T(8,128)(2,1)S(1)}, u32[]{:S(2)}, u32[]{:S(2)}) async-start(bf16[8,784,128]{2,1,0:T(8,128)(2,1)} %get-tuple-element.64), calls=%async_computation.1 | async-start | bytes 3211264 | tf_op jit(solution)/shard_map/all_to_all | solution.py:966
  62.9 1.7 %collective-permute-start.6 = (bf16[4,272,128]{2,1,0:T(8,128)(2,1)S(1)}, bf16[4,272,128]{2,1,0:T(8,128)(2,1)S(1)}, u32[]{:S(2)}, u32[]{:S(2)}) collective-permute-start(bf16[4,272,128]{2,1,0:T(8,128)(2,1)S(1)} %get-tuple-element.66), channel_id=1, source_target_pairs={{0,2},{2,0},{4,6},{6,4},{8,10},{10,8},{12,14},{14,12},{16,18},{18,... | collective-permute-start | bytes 835592 | tf_op jit(solution)/shard_map/ppermute | solution.py:925
  64.7 19.7 %collective-permute-start.7 = (bf16[2,272,128]{2,1,0:T(8,128)(2,1)S(1)}, bf16[2,272,128]{2,1,0:T(8,128)(2,1)S(1)}, u32[]{:S(2)}, u32[]{:S(2)}) collective-permute-start(bf16[2,272,128]{2,1,0:T(8,128)(2,1)S(1)} %get-tuple-element.67), channel_id=1, source_target_pairs={{0,16},{2,18},{4,20},{6,22},{8,24},{10,26},{12,28},{14,30},{16,0},... | collective-permute-start | bytes 417800 | tf_op jit(solution)/shard_map/ppermute | solution.py:936
  66.0 21.4 %collective-permute-start.8 = (bf16[2,272,128]{2,1,0:T(8,128)(2,1)S(1)}, bf16[2,272,128]{2,1,0:T(8,128)(2,1)S(1)}, u32[]{:S(2)}, u32[]{:S(2)}) collective-permute-start(bf16[2,272,128]{2,1,0:T(8,128)(2,1)S(1)} %get-tuple-element.68), channel_id=1, source_target_pairs={{0,20},{2,22},{4,16},{6,18},{8,28},{10,30},{12,24},{14,26},{16,4},... | collective-permute-start | bytes 417800 | tf_op jit(solution)/shard_map/ppermute | solution.py:936
  68.9 24.5 %collective-permute-start.9 = (bf16[2,272,128]{2,1,0:T(8,128)(2,1)S(1)}, bf16[2,272,128]{2,1,0:T(8,128)(2,1)S(1)}, u32[]{:S(2)}, u32[]{:S(2)}) collective-permute-start(bf16[2,272,128]{2,1,0:T(8,128)(2,1)S(1)} %get-tuple-element.69), channel_id=1, source_target_pairs={{0,24},{2,26},{4,28},{6,30},{8,16},{10,18},{12,20},{14,22},{16,8},... | collective-permute-start | bytes 417800 | tf_op jit(solution)/shard_map/ppermute | solution.py:936
  71.0 25.8 %collective-permute-start.10 = (bf16[2,272,128]{2,1,0:T(8,128)(2,1)S(1)}, bf16[2,272,128]{2,1,0:T(8,128)(2,1)S(1)}, u32[]{:S(2)}, u32[]{:S(2)}) collective-permute-start(bf16[2,272,128]{2,1,0:T(8,128)(2,1)S(1)} %get-tuple-element.70), channel_id=1, source_target_pairs={{0,28},{2,30},{4,24},{6,26},{8,20},{10,22},{12,16},{14,18},{16,12}... | collective-permute-start | bytes 417800 | tf_op jit(solution)/shard_map/ppermute | solution.py:936
  96.8 3.7 %collective-permute-start.11 = (f32[16,128]{1,0:T(8,128)S(1)}, f32[16,128]{1,0:T(8,128)S(1)}, u32[]{:S(2)}, u32[]{:S(2)}) collective-permute-start(f32[16,128]{1,0:T(8,128)S(1)} %temper_sums.1), channel_id=1, source_target_pairs={{0,1},{1,0},{2,3},{3,2},{4,5},{5,4},{6,7},{7,6},{8,9},{9,8},{10,11... | collective-permute-start | bytes 24584 | tf_op jit(solution)/shard_map/ppermute | solution.py:1053

commit v10 on v9

--- a/solution.py
+++ b/solution.py
@@ -585,7 +585,7 @@
     return lax.broadcasted_iota(jnp.int32, shape, 0) - lax.broadcasted_iota(jnp.int32, shape, 1)
 
 
-def statistics(region, weight_ref, towards_ref, out_ref, first_row):
+def statistics(region, weight_ref, towards_ref, out_ref, first_row, temper_ref=None):
     for tile in range(region.tiles):
         here = tile_rows(tile)
         top = jnp.full((1, TILE), blocked_score, jnp.float32)
@@ -595,9 +595,12 @@
             top = jnp.maximum(top, jnp.max(raw, axis=0, keepdims=True))
         total = jnp.zeros((1, TILE), jnp.float32)
         mass = jnp.zeros((1, TILE), jnp.float32)
+        moment = jnp.zeros((1, TILE), jnp.float32)
+        spread = jnp.zeros((1, TILE), jnp.float32)
         for other in region.keys_of(tile):
             there = tile_rows(other)
-            weight = jnp.exp2(weight_ref[there, here] - top)
+            raw = weight_ref[there, here]
+            weight = jnp.exp2(raw - top)
             towards = dot_rows(
                 region.rows(VALUE, other, other + 1), region.rows(GRAD, tile, tile + 1)
             )
@@ -605,6 +608,13 @@
             towards_ref[there, here] = towards
             total += jnp.sum(weight, axis=0, keepdims=True)
             mass += jnp.sum(weight * towards, axis=0, keepdims=True)
+            if temper_ref is not None:
+                weighted = weight * raw
+                moment += jnp.sum(weighted * towards, axis=0, keepdims=True)
+                spread += jnp.sum(weighted, axis=0, keepdims=True)
+        if temper_ref is not None:
+            temper_ref[0:1, here] = moment
+            temper_ref[1:2, here] = spread
         out_ref[first_row : first_row + 1, here] = top
         out_ref[first_row + 1 : first_row + 2, here] = total
         out_ref[first_row + 2 : first_row + 3, here] = mass
@@ -683,8 +693,8 @@
 
 
 def within_kernel(
-    softness_ref, ids_ref, span_ref, in_ref, arrays_ref, stats_ref, bias_ref, corner_ref,
-    parts_ref, temper_ref, own_weight, own_towards, other_weight, other_towards, *scratch,
+    softness_ref, ids_ref, span_ref, in_ref, arrays_ref, stats_ref, message_ref, bias_ref,
+    corner_ref, parts_ref, other_ref, temper_ref, own_weight, own_towards, other_weight, other_towards, *scratch,
     half_count
 ):
     me, half, _ = position(half_count)
@@ -701,7 +711,9 @@
         region = Diagonal(
             arrays_ref, places, scaling, ids_ref, head, half * half_count, span_ref[head]
         )
-        statistics(region, *kept[slot], stats_ref, slot * 3)
+        statistics(
+            region, *kept[slot], stats_ref, slot * 3, None if slot == 0 else message_ref.at[3:5]
+        )
         stats_ref[6 + slot : 7 + slot, :] = jnp.full((1, stats_ref.shape[1]), scaling, jnp.float32)
     for key_block in range(half_count):
         for query_block in range(half_count):
@@ -713,9 +725,13 @@
     least = jnp.where(same, -BLK, BLK - span_ref[me])
     corner_ref[...] = jnp.where(key_minus_query() > least, 0.0, blocked_score)
     temper_ref[...] = jnp.zeros_like(temper_ref)
+    message_ref[0:3, :] = stats_ref[3:6, :]
 
     @pl.when(half == 0)
     def _():
+        temper_ref[1:2, :] = other_diagonal(
+            arrays_ref, kept[1], stats_ref, alone(three_rows(stats_ref, 3)), scratch, other_ref, 0
+        )
         region = Diagonal(arrays_ref, range(4), scale_row(stats_ref, 0))
         single = alone(three_rows(stats_ref, 0))
         *parts, temper = gradients(region, *kept[0], stats_ref[0:1, :], *single, *scratch)
@@ -727,7 +743,7 @@
 
 def square_kernel(arrays_ref, stats_ref, bias_ref, corner_ref, *refs, half_count):
     across_refs = refs[: half_count // 2]
-    square_ref, message_ref, square_stats, weight, towards = refs[half_count // 2 :]
+    square_ref, square_stats, weight, towards = refs[half_count // 2 :]
     _, half, place = position(half_count)
     first = jnp.where(half == 0, QUERY, KEY)
     second = jnp.where(half == 0, GRAD, VALUE)
@@ -740,59 +756,111 @@
     kept_second = jnp.where(half == 0, VALUE, GRAD)
     square_ref[kept_first, :, :] = arrays_ref[kept_first, :, :]
     square_ref[kept_second, :, :] = arrays_ref[kept_second, :, :]
-    region = Square(square_ref, stats_ref[6:7, :TILE], bias_ref, corner_ref)
-    statistics(region, weight, towards, square_stats, 0)
-    for row in range(3):
-        message_ref[row : row + 1, :] = jnp.where(
-            half == 0, square_stats[row : row + 1, :], stats_ref[3 + row : 4 + row, :]
-        )
-
-
-def other_diagonal(arrays_ref, kept, stats_ref, totals, scratch, within_ref):
+
+    @pl.when(half == 0)
+    def _():
+        region = Square(square_ref, stats_ref[6:7, :TILE], bias_ref, corner_ref)
+        statistics(region, weight, towards, square_stats, 0)
+
+
+def other_diagonal(arrays_ref, kept, stats_ref, totals, scratch, out_ref, first):
     region = Diagonal(arrays_ref, range(4, 8), scale_row(stats_ref, 1))
     *parts, temper = gradients(region, *kept, stats_ref[3:4, :], *totals, *scratch)
     for array, tiles in enumerate(scaled(region, parts)):
         for tile, value in enumerate(tiles):
-            put(within_ref, 3 + array, tile, value)
+            put(out_ref, first + array, tile, value)
     return temper
 
 
-def first_kernel(
-    arrays_ref, square_ref, stats_ref, square_stats, temper_in,
-    own_weight, own_towards, other_weight, other_towards, square_weight, square_towards,
-    within_ref, across_ref, temper_ref, *scratch, half_count
+def temper_terms(message_ref, totals, scaling):
+    log_total, delta = totals
+    share = jnp.exp2(message_ref[0:1, :] - log_total)
+    terms = (message_ref[3:4, :] - delta * message_ref[4:5, :]) * share
+    folded = sum(terms[:, start : start + HD] for start in range(0, terms.shape[1], HD))
+    return folded / (scaling * math.log2(math.e))
+
+
+def own_kernel(
+    arrays_ref, square_ref, stats_ref, bias_ref, corner_ref, square_stats, received_ref, parts_ref,
+    temper_in, own_weight, own_towards, square_weight, square_towards,
+    own_ref, kept_ref, given_ref, temper_ref, across, late_stats, weight, towards, *scratch,
+    half_count
 ):
-    _, half, _ = position(half_count)
+    _, half, place = position(half_count)
     temper_ref[...] = temper_in[...]
+    square = Square(square_ref, scale_row(stats_ref, 0))
 
     @pl.when(half == 0)
     def _():
-        totals = alone(three_rows(stats_ref, 3))
-        temper_ref[1:2, :] = other_diagonal(
-            arrays_ref, (other_weight, other_towards), stats_ref, totals, scratch, within_ref
+        totals = merged(three_rows(square_stats, 0), three_rows(received_ref, 0))
+        *parts, temper = gradients(
+            square, square_weight, square_towards, square_stats[0:1, :], *totals, *scratch
+        )
+        query_parts, key_parts, value_parts = scaled(square, parts)
+        for tile in range(square.tiles):
+            here = tile_rows(tile)
+            across[0, here, :] = query_parts[tile].astype(jnp.bfloat16)
+            put(own_ref, 0, tile, parts_ref[0, here, :])
+            put(own_ref, 1, tile, parts_ref[1, here, :] + key_parts[tile])
+            put(own_ref, 2, tile, parts_ref[2, here, :] + value_parts[tile])
+        across[1] = jnp.zeros(across.shape[1:], jnp.bfloat16)
+        temper_ref[0:1, :] = (
+            temper_in[0:1, :] + temper + temper_terms(received_ref, totals, square.scaling)
         )
 
     @pl.when(half == 1)
     def _():
-        totals = merged(three_rows(stats_ref, 0), three_rows(square_stats, 0))
-        square = Square(square_ref, scale_row(stats_ref, 0))
+        masked = Square(square_ref, stats_ref[6:7, :TILE], bias_ref, corner_ref)
+        statistics(masked, weight, towards, late_stats, 0)
+        totals = merged(three_rows(stats_ref, 0), three_rows(late_stats, 0))
         *parts, square_temper = gradients(
-            square, square_weight, square_towards, square_stats[0:1, :], *totals, *scratch
+            square, weight, towards, late_stats[0:1, :], *totals, *scratch
         )
         across_query, *foreign = scaled(square, parts)
         for array, tiles in enumerate(foreign):
             for tile, value in enumerate(tiles):
-                across_ref[array, tile_rows(tile), :] = value.astype(jnp.bfloat16)
+                across[array, tile_rows(tile), :] = value.astype(jnp.bfloat16)
         diagonal = Diagonal(arrays_ref, range(4), scale_row(stats_ref, 0))
         *parts, temper = gradients(
             diagonal, own_weight, own_towards, stats_ref[0:1, :], *totals, *scratch
         )
         query_parts, key_parts, value_parts = scaled(diagonal, parts)
         for tile in range(square.tiles):
-            put(within_ref, 0, tile, query_parts[tile] + across_query[tile])
-            put(within_ref, 1, tile, key_parts[tile])
-            put(within_ref, 2, tile, value_parts[tile])
+            put(own_ref, 0, tile, query_parts[tile] + across_query[tile])
+            put(own_ref, 1, tile, key_parts[tile])
+            put(own_ref, 2, tile, value_parts[tile])
         temper_ref[0:1, :] = temper + square_temper
+
+    pieces = temper_rows(temper_ref[0:1, :], temper_ref[1:2, :])
+    for core, foreign_ref in enumerate((kept_ref, given_ref)):
+        for step in range(half_count // 2):
+            rows = rows_of(place ^ core ^ (2 * step))
+            foreign_ref[step, :BLK, :] = across[0, rows, :]
+            foreign_ref[step, BLK : 2 * BLK, :] = across[1, rows, :]
+            foreign_ref[step, 2 * BLK :, :] = pieces
+
+
+def finish_kernel(
+    arrays_ref, stats_ref, received_ref, own_ref, other_ref, temper_ref, other_weight,
+    other_towards, within_ref, *scratch, half_count
+):
+    _, half, _ = position(half_count)
+    pieces = temper_rows(temper_ref[0:1, :], temper_ref[1:2, :])
+    for block in range(half_count):
+        within_ref[block, : 3 * BLK, :] = own_ref[block]
+        within_ref[block, 6 * BLK :, :] = pieces
+
+    @pl.when(half == 0)
+    def _():
+        for block in range(half_count):
+            within_ref[block, 3 * BLK : 6 * BLK, :] = other_ref[block]
+
+    @pl.when(half == 1)
+    def _():
+        totals = merged(three_rows(stats_ref, 3), three_rows(received_ref, 0))
+        other_diagonal(
+            arrays_ref, (other_weight, other_towards), stats_ref, totals, scratch, within_ref, 3
+        )
 
 
 def temper_rows(own, other):
@@ -807,54 +875,6 @@
             rows = jnp.where(row == place * 3 + piece, high, rows)
             rest = rest - high
     return rows.astype(jnp.bfloat16)
-
-
-def finish_kernel(
-    arrays_ref, square_ref, message_ref, received_ref, stats_ref, square_stats, parts_ref,
-    temper_ref, square_weight, square_towards, other_weight, other_towards, across_in, begun_ref,
-    within_ref, *refs, half_count
-):
-    foreign_refs = refs[:2]
-    across, temper, *scratch = refs[2:]
-    _, half, place = position(half_count)
-    temper[...] = temper_ref[...]
-
-    @pl.when(half == 0)
-    def _():
-        totals = merged(three_rows(message_ref, 0), three_rows(received_ref, 0))
-        region = Square(square_ref, scale_row(stats_ref, 0))
-        *parts, square_temper = gradients(
-            region, square_weight, square_towards, square_stats[0:1, :], *totals, *scratch
-        )
-        query_parts, key_parts, value_parts = scaled(region, parts)
-        for tile in range(region.tiles):
-            here = tile_rows(tile)
-            across[0, here, :] = query_parts[tile].astype(jnp.bfloat16)
-            put(within_ref, 0, tile, parts_ref[0, here, :])
-            put(within_ref, 1, tile, parts_ref[1, here, :] + key_parts[tile])
-            put(within_ref, 2, tile, parts_ref[2, here, :] + value_parts[tile])
-        across[1] = jnp.zeros(across.shape[1:], jnp.bfloat16)
-        within_ref[:, 3 * BLK : 6 * BLK, :] = begun_ref[:, 3 * BLK : 6 * BLK, :]
-        temper[0:1, :] = temper_ref[0:1, :] + square_temper
-
-    @pl.when(half == 1)
-    def _():
-        totals = merged(three_rows(message_ref, 0), three_rows(received_ref, 0))
-        temper[1:2, :] = other_diagonal(
-            arrays_ref, (other_weight, other_towards), stats_ref, totals, scratch, within_ref
-        )
-        across[...] = across_in[...]
-        within_ref[:, : 3 * BLK, :] = begun_ref[:, : 3 * BLK, :]
-
-    pieces = temper_rows(temper[0:1, :], temper[1:2, :])
-    for block in range(half_count):
-        within_ref[block, 6 * BLK : 6 * BLK + EXTRA, :] = pieces
-    for core, foreign_ref in enumerate(foreign_refs):
-        for step in range(half_count // 2):
-            rows = rows_of(place ^ core ^ (2 * step))
-            foreign_ref[step, :BLK, :] = across[0, rows, :]
-            foreign_ref[step, BLK : 2 * BLK, :] = across[1, rows, :]
-            foreign_ref[step, 2 * BLK :, :] = pieces
 
 
 def temper_kernel(within_ref, *refs, half_count):
@@ -985,18 +1005,21 @@
     arrived = exchange_within(sent)
     foreign = crossed(*foreign, half_count)
     kept_parts = jax.ShapeDtypeStruct((3, tokens, HD), jnp.float32)
+    three_arrays = jax.ShapeDtypeStruct((half_count, 3 * BLK, HD), jnp.bfloat16)
     tempers = jax.ShapeDtypeStruct((8, HD), jnp.float32)
+    chunks = jax.ShapeDtypeStruct((half_count // 2, 2 * BLK + EXTRA, HD), jnp.bfloat16)
+    first_half = range(half_count)
     (
-        arrays, stats, bias, corner, parts, temper,
+        arrays, stats, message, bias, corner, parts, other_done, temper,
         own_weight, own_towards, other_weight, other_towards,
     ) = call(
         within_kernel,
         "diagonal_statistics",
         (arrived,),
         [
-            jax.ShapeDtypeStruct((8, tokens, HD), jnp.bfloat16), rows_of_stats,
+            jax.ShapeDtypeStruct((8, tokens, HD), jnp.bfloat16), rows_of_stats, rows_of_stats,
             jax.ShapeDtypeStruct((half_count, tokens), jnp.float32),
-            jax.ShapeDtypeStruct((BLK, BLK), jnp.float32), kept_parts, tempers,
+            jax.ShapeDtypeStruct((BLK, BLK), jnp.float32), kept_parts, three_arrays, tempers,
         ]
         + [pairs] * 4,
         lows,
@@ -1004,46 +1027,47 @@
         20,
         settings,
     )
-    square, message, square_stats, square_weight, square_towards = call(
+    from_second = lax.ppermute(
+        message, "seq", [(source + half_count, source) for source in first_half]
+    )
+    square, square_stats, square_weight, square_towards = call(
         square_kernel,
         "square_statistics",
         (arrays, stats, bias, corner, *foreign),
-        [jax.ShapeDtypeStruct((4, tokens, HD), jnp.bfloat16)] + [rows_of_stats] * 2 + [pairs] * 2,
+        [jax.ShapeDtypeStruct((4, tokens, HD), jnp.bfloat16), rows_of_stats] + [pairs] * 2,
         [],
         2 * pair_flops,
         12,
     )
-    swap = [(source, source ^ half_count) for source in range(seq_count)]
-    received = lax.ppermute(message, "seq", swap)
-    begun, across, temper = call(
-        first_kernel,
-        "gradients_before_totals",
+    from_first = lax.ppermute(
+        square_stats, "seq", [(source, source + half_count) for source in first_half]
+    )
+    own_done, *foreign, temper = call(
+        own_kernel,
+        "own_gradients",
         (
-            arrays, square, stats, square_stats, temper, own_weight, own_towards,
-            other_weight, other_towards, square_weight, square_towards,
+            arrays, square, stats, bias, corner, square_stats, from_second, parts, temper,
+            own_weight, own_towards, square_weight, square_towards,
         ),
+        [three_arrays, chunks, chunks, tempers],
         [
-            jax.ShapeDtypeStruct((half_count, 6 * BLK, HD), jnp.bfloat16),
-            jax.ShapeDtypeStruct((2, tokens, HD), jnp.bfloat16),
-            tempers,
+            pltpu.VMEM((2, tokens, HD), jnp.bfloat16), pltpu.VMEM((8, tokens), jnp.float32),
+            pltpu.VMEM((tokens, tokens), jnp.float32), pltpu.VMEM((tokens, tokens), jnp.float32),
+            *lows,
         ],
+        6 * pair_flops,
+        20,
+    )
+    (within,) = call(
+        finish_kernel,
+        "other_gradients",
+        (arrays, stats, from_first, own_done, other_done, temper, other_weight, other_towards),
+        [jax.ShapeDtypeStruct((half_count, 6 * BLK + EXTRA, HD), jnp.bfloat16)],
         lows,
-        4 * pair_flops,
+        2 * pair_flops,
         14,
     )
-    within, *foreign = call(
-        finish_kernel,
-        "gradients_after_totals",
-        (
-            arrays, square, message, received, stats, square_stats, parts, temper,
-            square_weight, square_towards, other_weight, other_towards, across, begun,
-        ),
-        [jax.ShapeDtypeStruct((half_count, 6 * BLK + EXTRA, HD), jnp.bfloat16)]
-        + [jax.ShapeDtypeStruct((half_count // 2, 2 * BLK + EXTRA, HD), jnp.bfloat16)] * 2,
-        [pltpu.VMEM((2, tokens, HD), jnp.bfloat16), pltpu.VMEM((8, HD), jnp.float32), *lows],
-        2 * pair_flops,
-        20,
-    )
+    within, *foreign = lax.optimization_barrier((within, *foreign))
     across = crossed(*foreign, half_count)
     within = exchange_within(within)
     tempers = temper_sums(within, across, half_count)

time: 101 us -> 104 us (1.030)
  starting transfers between devices: 26.9 us -> 33.7 us
  waiting for transfers between devices: 56.9 us -> 52.1 us
    ppermute x1 -> x2, waiting for transfers between devices: 3.59 us -> 0.01 us  [the longest x1 0.01 us: head_shards(): lax.ppermute(message, 'seq', [(source + half_count, source) for source in...]
    ppermute x1 -> x2, starting transfers between devices: 0.07 us -> 3.62 us  [the longest x1 2.33 us: head_shards(): lax.ppermute(square_stats, 'seq', [(source, source + half_count) for sour...]
    all_to_all x2, starting transfers between devices: 8.98 us -> 10.5 us  [exchange_within(): lax.all_to_all(array_in, 'seq', split_axis=0, concat_axis=0, axis_index_g...]
    ppermute x8, starting transfers between devices: 15.4 us -> 16.9 us  [crossed(): lax.ppermute(message, 'seq', [(source, source ^ half_count + 2 * step) fo...]
    ppermute x8, waiting for transfers between devices: 28.3 us -> 27.1 us  [crossed(): lax.ppermute(message, 'seq', [(source, source ^ half_count + 2 * step) fo...]
  transfers between devices with their start and end apart: 14 -> 15, of which waited for: 11 -> 9; matrix products, arithmetic and copies ran while one was open for 0% -> 0% of each run, Pallas kernels for 7% -> 11%
where the time goes in v10:
time: 104 us; the launch traced here: 103 us
  waiting for transfers between devices  52.1 us (50%)
  starting transfers between devices  33.7 us (32%)
  Pallas kernels  16.1 us (15%)
    ppermute x8, waiting for transfers between devices, crossed(): lax.ppermute(message, 'seq', [(source, source ^ half_count + 2 * step) fo...  27.1 us
    all_to_all x2, waiting for transfers between devices, exchange_within(): lax.all_to_all(array_in, 'seq', split_axis=0, concat_axis=0, axis_index_g...  21.7 us
    ppermute x8, starting transfers between devices, crossed(): lax.ppermute(message, 'seq', [(source, source ^ half_count + 2 * step) fo...  16.9 us
    pallas_call x8, Pallas kernels, kernel_call(): pl.pallas_call(kernel, out_shape=out_shape, in_specs=in_specs, out_specs=...  16 us
    all_to_all x2, starting transfers between devices, exchange_within(): lax.all_to_all(array_in, 'seq', split_axis=0, concat_axis=0, axis_index_g...  10.5 us
    ppermute x2, waiting for transfers between devices, crossed(): lax.ppermute(given, 'seq', [(source, source ^ 1) for source in devices])  2.73 us
    ppermute x1, starting transfers between devices, head_shards(): lax.ppermute(square_stats, 'seq', [(source, source + half_count) for sour...  2.33 us
  transfers between devices with their start and end apart: 15, of which 9 were waited for; matrix products, arithmetic and copies ran while one was open for 0% of the time, Pallas kernels for 11%

profile of v10, /device:TPU:0, one launch (start us, length us, event | category | flops | bytes accessed | tf_op | source)
XLA Modules:
  0.0 103.2 jit_solution(6474607004541922457)
XLA Ops:
  0.7 2.9 %pack_heads.1 = (bf16[8,1024,128]{2,1,0:T(8,128)(2,1)}, bf16[4,256,128]{2,1,0:T(8,128)(2,1)}, bf16[4,256,128]{2,1,0:T(8,128)(2,1)}) custom-call(bf16[1,128,2048]{2,1,0:T(8,128)(2,1)} %refs_0_.1, bf16[1,128,2048]{2,1,0:T(8,128)(2,1)} %refs_1_.1, bf16[1,128,2048]{2,1,0:T(8,128)(2,1)} %refs_2_.1, bf16[1,128,2048]{2,1,0:T(8,128)(2,1)} %refs_3_.1), custom_call_target="tpu_custom_call" | custom-call | bytes 4718592 | tf_op jit(solution)/shard_map/pack_heads/pallas_call | solution.py:409
  3.6 5.4 %all-to-all-start = ((bf16[8,1024,128]{2,1,0:T(8,128)(2,1)}), bf16[8,1024,128]{2,1,0:T(8,128)(2,1)S(1)}, u32[]{:S(2)}, u32[]{:S(2)}) async-start(bf16[8,1024,128]{2,1,0:T(8,128)(2,1)} %get-tuple-element.41), calls=%async_computation | async-start | bytes 4194304 | tf_op jit(solution)/shard_map/all_to_all | solution.py:986
  9.5 1.4 %collective-permute-done.taken_ref = bf16[4,256,128]{2,1,0:T(8,128)(2,1)S(1)} collective-permute-done((bf16[4,256,128]{2,1,0:T(8,128)(2,1)S(1)}, bf16[4,256,128]{2,1,0:T(8,128)(2,1)S(1)}, u32[]{:S(2)}, u32[]{:S(2)}) %collective-permute-start) | collective-permute-done | bytes 262176 | tf_op jit(solution)/shard_map/ppermute | solution.py:945
  11.0 2.7 %collective-permute-start.1 = (bf16[2,256,128]{2,1,0:T(8,128)(2,1)S(1)}, bf16[2,256,128]{2,1,0:T(8,128)(2,1)S(1)}, u32[]{:S(2)}, u32[]{:S(2)}) collective-permute-start(bf16[2,256,128]{2,1,0:T(8,128)(2,1)S(1)} %get-tuple-element.48), channel_id=1, source_target_pairs={{0,16},{2,18},{4,20},{6,22},{8,24},{10,26},{12,28},{14,30},{16,0},... | collective-permute-start | bytes 393224 | tf_op jit(solution)/shard_map/ppermute | solution.py:956
  13.6 1.5 %collective-permute-start.2 = (bf16[2,256,128]{2,1,0:T(8,128)(2,1)S(1)}, bf16[2,256,128]{2,1,0:T(8,128)(2,1)S(1)}, u32[]{:S(2)}, u32[]{:S(2)}) collective-permute-start(bf16[2,256,128]{2,1,0:T(8,128)(2,1)S(1)} %get-tuple-element.49), channel_id=1, source_target_pairs={{0,20},{2,22},{4,16},{6,18},{8,28},{10,30},{12,24},{14,26},{16,4},... | collective-permute-start | bytes 393224 | tf_op jit(solution)/shard_map/ppermute | solution.py:956
  15.1 3.5 %collective-permute-start.3 = (bf16[2,256,128]{2,1,0:T(8,128)(2,1)S(1)}, bf16[2,256,128]{2,1,0:T(8,128)(2,1)S(1)}, u32[]{:S(2)}, u32[]{:S(2)}) collective-permute-start(bf16[2,256,128]{2,1,0:T(8,128)(2,1)S(1)} %get-tuple-element.50), channel_id=1, source_target_pairs={{0,24},{2,26},{4,28},{6,30},{8,16},{10,18},{12,20},{14,22},{16,8},... | collective-permute-start | bytes 393224 | tf_op jit(solution)/shard_map/ppermute | solution.py:956
  18.7 21.7 %all-to-all-done.in_ref = bf16[8,1024,128]{2,1,0:T(8,128)(2,1)S(1)} async-done(((bf16[8,1024,128]{2,1,0:T(8,128)(2,1)}), bf16[8,1024,128]{2,1,0:T(8,128)(2,1)S(1)}, u32[]{:S(2)}, u32[]{:S(2)}) %all-to-all-start) | async-done | bytes 2097184 | tf_op jit(solution)/shard_map/all_to_all | solution.py:986
  40.4 5.9 %diagonal_statistics.1 = (bf16[8,1024,128]{2,1,0:T(8,128)(2,1)S(1)}, f32[8,1024]{1,0:T(8,128)S(1)}, f32[8,1024]{1,0:T(8,128)S(1)}, f32[8,1024]{1,0:T(8,128)S(1)}...) custom-call(f32[16]{0:T(128)S(1)} %copy-done.2, ...), custom_call_target="tpu_custom_call" | custom-call | flops 536870912 | bytes 23499904 | tf_op jit(solution)/shard_map/diagonal_statistics/pallas_call | solution.py:409
  46.3 1.3 %collective-permute-start.6 = (f32[8,1024]{1,0:T(8,128)S(1)}, f32[8,1024]{1,0:T(8,128)S(1)}, u32[]{:S(2)}, u32[]{:S(2)}) collective-permute-start(f32[8,1024]{1,0:T(8,128)S(1)} %get-tuple-element.54), channel_id=1, source_target_pairs={{16,0},{18,2},{20,4},{22,6},{24,8},{26,10},{28,12},{30,14},{17,1},... | collective-permute-start | bytes 98312 | tf_op jit(solution)/shard_map/ppermute | solution.py:1030
  47.6 1.3 %collective-permute-done.4.refs_3_ = bf16[2,256,128]{2,1,0:T(8,128)(2,1)S(1)} collective-permute-done((bf16[2,256,128]{2,1,0:T(8,128)(2,1)S(1)}, bf16[2,256,128]{2,1,0:T(8,128)(2,1)S(1)}, u32[]{:S(2)}, u32[]{:S(2)}) %collective-permute-start.4) | collective-permute-done | bytes 131104 | tf_op jit(solution)/shard_map/ppermute | solution.py:956
  48.9 1.9 %square_statistics.1 = (bf16[4,1024,128]{2,1,0:T(8,128)(2,1)S(1)}, f32[8,1024]{1,0:T(8,128)S(1)}, f32[1024,1024]{1,0:T(8,128)S(1)}, f32[1024,1024]{1,0:T(8,128)S(1)}) custom-call(bf16[8,1024,128]{2,1,0:T(8,128)(2,1)S(1)} %get-tuple-element.42.arrays_ref, f32[8,1024]{1,0:T(8,128)S(1)} %get-tuple-element.43.stats_ref, ...), custom_call_target="tpu_custom_call" | custom-call | flops 536870912 | bytes 12222464 | tf_op jit(solution)/shard_map/square_statistics/pallas_call | solution.py:409
  50.8 2.3 %collective-permute-start.5 = (f32[8,1024]{1,0:T(8,128)S(1)}, f32[8,1024]{1,0:T(8,128)S(1)}, u32[]{:S(2)}, u32[]{:S(2)}) collective-permute-start(f32[8,1024]{1,0:T(8,128)S(1)} %get-tuple-element.52.square_stats), channel_id=1, source_target_pairs={{0,16},{2,18},{4,20},{6,22},{8,24},{10,26},{12,28},{14,30},{1,17},... | collective-permute-start | bytes 98312 | tf_op jit(solution)/shard_map/ppermute | solution.py:1042
  53.2 2.3 %own_gradients.1 = (bf16[8,384,128]{2,1,0:T(8,128)(2,1)S(1)}, bf16[4,272,128]{2,1,0:T(8,128)(2,1)S(1)}, bf16[4,272,128]{2,1,0:T(8,128)(2,1)S(1)}, f32[8,128]{1,0:T(8,128)S(1)}) custom-call(bf16[8,1024,128]{2,1,0:T(8,128)(2,1)S(1)} %get-tuple-element.42.arrays_ref, bf16[4,1024,128]{2,1,0:T(8,128)(2,1)S(1)} %get-tuple-element.53.square_ref, ...), custom_call_target="tpu_custom_call" | custom-call | flops 1610612736 | bytes 23044096 | tf_op jit(solution)/shard_map/own_gradients/pallas_call | solution.py:409
  55.5 1.3 %other_gradients.1 = bf16[8,784,128]{2,1,0:T(8,128)(2,1)} custom-call(bf16[8,1024,128]{2,1,0:T(8,128)(2,1)S(1)} %get-tuple-element.42.arrays_ref, f32[8,1024]{1,0:T(8,128)S(1)} %get-tuple-element.43.stats_ref, f32[8,1024]{1,0:T(8,128)S(1)} %collective-permute-done.5.received_ref, bf16[8,384,128]{2,1,0:T(8,128)(2,1)S(1)} %get-tuple-element.61.own_ref, ...), custom_call_target="tpu_custom_call" | custom-call | flops 536870912 | bytes 13733888 | tf_op jit(solution)/shard_map/other_gradients/pallas_call | solution.py:409
  56.8 5.1 %all-to-all-start.1 = ((bf16[8,784,128]{2,1,0:T(8,128)(2,1)}), bf16[8,784,128]{2,1,0:T(8,128)(2,1)S(1)}, u32[]{:S(2)}, u32[]{:S(2)}) async-start(bf16[8,784,128]{2,1,0:T(8,128)(2,1)} %other_gradients.1), calls=%async_computation.1 | async-start | bytes 3211264 | tf_op jit(solution)/shard_map/all_to_all | solution.py:986
  62.4 1.3 %collective-permute-done.7.taken_ref = bf16[4,272,128]{2,1,0:T(8,128)(2,1)S(1)} collective-permute-done((bf16[4,272,128]{2,1,0:T(8,128)(2,1)S(1)}, bf16[4,272,128]{2,1,0:T(8,128)(2,1)S(1)}, u32[]{:S(2)}, u32[]{:S(2)}) %collective-permute-start.7) | collective-permute-done | bytes 278560 | tf_op jit(solution)/shard_map/ppermute | solution.py:945
  63.8 4.2 %collective-permute-start.8 = (bf16[2,272,128]{2,1,0:T(8,128)(2,1)S(1)}, bf16[2,272,128]{2,1,0:T(8,128)(2,1)S(1)}, u32[]{:S(2)}, u32[]{:S(2)}) collective-permute-start(bf16[2,272,128]{2,1,0:T(8,128)(2,1)S(1)} %get-tuple-element.71), channel_id=1, source_target_pairs={{0,16},{2,18},{4,20},{6,22},{8,24},{10,26},{12,28},{14,30},{16,0},... | collective-permute-start | bytes 417800 | tf_op jit(solution)/shard_map/ppermute | solution.py:956
  69.3 3.7 %collective-permute-start.10 = (bf16[2,272,128]{2,1,0:T(8,128)(2,1)S(1)}, bf16[2,272,128]{2,1,0:T(8,128)(2,1)S(1)}, u32[]{:S(2)}, u32[]{:S(2)}) collective-permute-start(bf16[2,272,128]{2,1,0:T(8,128)(2,1)S(1)} %get-tuple-element.73), channel_id=1, source_target_pairs={{0,24},{2,26},{4,28},{6,30},{8,16},{10,18},{12,20},{14,22},{16,8},... | collective-permute-start | bytes 417800 | tf_op jit(solution)/shard_map/ppermute | solution.py:956
  73.1 10.4 %collective-permute-done.8.refs_0_ = bf16[2,272,128]{2,1,0:T(8,128)(2,1)S(1)} collective-permute-done((bf16[2,272,128]{2,1,0:T(8,128)(2,1)S(1)}, bf16[2,272,128]{2,1,0:T(8,128)(2,1)S(1)}, u32[]{:S(2)}, u32[]{:S(2)}) %collective-permute-start.8) | collective-permute-done | bytes 139296 | tf_op jit(solution)/shard_map/ppermute | solution.py:956
  83.5 3.0 %collective-permute-done.9.refs_1_ = bf16[2,272,128]{2,1,0:T(8,128)(2,1)S(1)} collective-permute-done((bf16[2,272,128]{2,1,0:T(8,128)(2,1)S(1)}, bf16[2,272,128]{2,1,0:T(8,128)(2,1)S(1)}, u32[]{:S(2)}, u32[]{:S(2)}) %collective-permute-start.9) | collective-permute-done | bytes 139296 | tf_op jit(solution)/shard_map/ppermute | solution.py:956
  86.5 8.9 %collective-permute-done.10.refs_2_ = bf16[2,272,128]{2,1,0:T(8,128)(2,1)S(1)} collective-permute-done((bf16[2,272,128]{2,1,0:T(8,128)(2,1)S(1)}, bf16[2,272,128]{2,1,0:T(8,128)(2,1)S(1)}, u32[]{:S(2)}, u32[]{:S(2)}) %collective-permute-start.10) | collective-permute-done | bytes 139296 | tf_op jit(solution)/shard_map/ppermute | solution.py:956
  95.4 3.4 %collective-permute-done.11.refs_3_ = bf16[2,272,128]{2,1,0:T(8,128)(2,1)S(1)} collective-permute-done((bf16[2,272,128]{2,1,0:T(8,128)(2,1)S(1)}, bf16[2,272,128]{2,1,0:T(8,128)(2,1)S(1)}, u32[]{:S(2)}, u32[]{:S(2)}) %collective-permute-start.11) | collective-permute-done | bytes 139296 | tf_op jit(solution)/shard_map/ppermute | solution.py:956
  98.9 1.6 %collective-permute-start.12 = (f32[16,128]{1,0:T(8,128)S(1)}, f32[16,128]{1,0:T(8,128)S(1)}, u32[]{:S(2)}, u32[]{:S(2)}) collective-permute-start(f32[16,128]{1,0:T(8,128)S(1)} %temper_sums.1), channel_id=1, source_target_pairs={{0,1},{1,0},{2,3},{3,2},{4,5},{5,4},{6,7},{7,6},{8,9},{9,8},{10,11... | collective-permute-start | bytes 24584 | tf_op jit(solution)/shard_map/ppermute | solution.py:1077
  100.4 1.5 %unpack_heads.1 = (bf16[1,128,2048]{2,1,0:T(8,128)(2,1)}, bf16[1,128,2048]{2,1,0:T(8,128)(2,1)}, bf16[1,128,2048]{2,1,0:T(8,128)(2,1)}) custom-call(bf16[8,784,128]{2,1,0:T(8,128)(2,1)S(1)} %all-to-all-done.1.within_ref, bf16[2,272,128]{2,1,0:T(8,128)(2,1)S(1)} %collective-permute-done.8.refs_0_, bf16[2,272,128]{2,1,0:T(8,128)(2,1)S(1)} %collective-permute-done.9.refs_1_, ...), custom_call_target="tpu_custom_call" | custom-call | bytes 3735552 | tf_op jit(solution)/shard_map/unpack_heads/pallas_call | solution.py:409
  (26 shorter events, 3.8 us)
Async XLA Ops:
  0.6 39.7 %copy-start.3 = (s32[16]{0:T(128)S(1)}, s32[16]{0:T(128)}, u32[]{:S(2)}) copy-start(s32[16]{0:T(128)} %span_ref.1) | copy-start | bytes 196
  0.6 39.7 %copy-start.1 = (s32[1,16,16,1]{2,3,1,0:T(1,128)S(1)}, s32[1,16,16,1]{2,3,1,0:T(1,128)}, u32[]{:S(2)}) copy-start(s32[1,16,16,1]{2,3,1,0:T(1,128)} %param.12) | copy-start | bytes 3076
  0.7 39.7 %copy-start.2 = (f32[16]{0:T(128)S(1)}, f32[16]{0:T(128)}, u32[]{:S(2)}) copy-start(f32[16]{0:T(128)} %softness_ref.1) | copy-start | bytes 196
  3.6 5.4 %copy-start.4 = (bf16[4,256,128]{2,1,0:T(8,128)(2,1)S(1)}, bf16[4,256,128]{2,1,0:T(8,128)(2,1)}, u32[]{:S(2)}) copy-start(bf16[4,256,128]{2,1,0:T(8,128)(2,1)} %get-tuple-element.47) | copy-start | bytes 786436
  3.6 7.3 %copy-start = (bf16[4,256,128]{2,1,0:T(8,128)(2,1)S(1)}, bf16[4,256,128]{2,1,0:T(8,128)(2,1)}, u32[]{:S(2)}) copy-start(bf16[4,256,128]{2,1,0:T(8,128)(2,1)} %get-tuple-element.46.kept_ref) | copy-start | bytes 786436
  3.6 36.7 %all-to-all-start = ((bf16[8,1024,128]{2,1,0:T(8,128)(2,1)}), bf16[8,1024,128]{2,1,0:T(8,128)(2,1)S(1)}, u32[]{:S(2)}, u32[]{:S(2)}) async-start(bf16[8,1024,128]{2,1,0:T(8,128)(2,1)} %get-tuple-element.41), calls=%async_computation | async-start | bytes 4194304 | tf_op jit(solution)/shard_map/all_to_all | solution.py:986
  9.0 1.9 %collective-permute-start = (bf16[4,256,128]{2,1,0:T(8,128)(2,1)S(1)}, bf16[4,256,128]{2,1,0:T(8,128)(2,1)S(1)}, u32[]{:S(2)}, u32[]{:S(2)}) collective-permute-start(bf16[4,256,128]{2,1,0:T(8,128)(2,1)S(1)} %copy-done.4), channel_id=1, source_target_pairs={{0,2},{2,0},{4,6},{6,4},{8,10},{10,8},{12,14},{14,12},{16,18},{18,... | collective-permute-start | bytes 786440 | tf_op jit(solution)/shard_map/ppermute | solution.py:945
  11.0 36.6 %collective-permute-start.1 = (bf16[2,256,128]{2,1,0:T(8,128)(2,1)S(1)}, bf16[2,256,128]{2,1,0:T(8,128)(2,1)S(1)}, u32[]{:S(2)}, u32[]{:S(2)}) collective-permute-start(bf16[2,256,128]{2,1,0:T(8,128)(2,1)S(1)} %get-tuple-element.48), channel_id=1, source_target_pairs={{0,16},{2,18},{4,20},{6,22},{8,24},{10,26},{12,28},{14,30},{16,0},... | collective-permute-start | bytes 393224 | tf_op jit(solution)/shard_map/ppermute | solution.py:956
  13.6 34.0 %collective-permute-start.2 = (bf16[2,256,128]{2,1,0:T(8,128)(2,1)S(1)}, bf16[2,256,128]{2,1,0:T(8,128)(2,1)S(1)}, u32[]{:S(2)}, u32[]{:S(2)}) collective-permute-start(bf16[2,256,128]{2,1,0:T(8,128)(2,1)S(1)} %get-tuple-element.49), channel_id=1, source_target_pairs={{0,20},{2,22},{4,16},{6,18},{8,28},{10,30},{12,24},{14,26},{16,4},... | collective-permute-start | bytes 393224 | tf_op jit(solution)/shard_map/ppermute | solution.py:956
  15.1 32.5 %collective-permute-start.3 = (bf16[2,256,128]{2,1,0:T(8,128)(2,1)S(1)}, bf16[2,256,128]{2,1,0:T(8,128)(2,1)S(1)}, u32[]{:S(2)}, u32[]{:S(2)}) collective-permute-start(bf16[2,256,128]{2,1,0:T(8,128)(2,1)S(1)} %get-tuple-element.50), channel_id=1, source_target_pairs={{0,24},{2,26},{4,28},{6,30},{8,16},{10,18},{12,20},{14,22},{16,8},... | collective-permute-start | bytes 393224 | tf_op jit(solution)/shard_map/ppermute | solution.py:956
  18.6 30.3 %collective-permute-start.4 = (bf16[2,256,128]{2,1,0:T(8,128)(2,1)S(1)}, bf16[2,256,128]{2,1,0:T(8,128)(2,1)S(1)}, u32[]{:S(2)}, u32[]{:S(2)}) collective-permute-start(bf16[2,256,128]{2,1,0:T(8,128)(2,1)S(1)} %get-tuple-element.51), channel_id=1, source_target_pairs={{0,28},{2,30},{4,24},{6,26},{8,20},{10,22},{12,16},{14,18},{16,12}... | collective-permute-start | bytes 393224 | tf_op jit(solution)/shard_map/ppermute | solution.py:956
  46.3 6.9 %collective-permute-start.6 = (f32[8,1024]{1,0:T(8,128)S(1)}, f32[8,1024]{1,0:T(8,128)S(1)}, u32[]{:S(2)}, u32[]{:S(2)}) collective-permute-start(f32[8,1024]{1,0:T(8,128)S(1)} %get-tuple-element.54), channel_id=1, source_target_pairs={{16,0},{18,2},{20,4},{22,6},{24,8},{26,10},{28,12},{30,14},{17,1},... | collective-permute-start | bytes 98312 | tf_op jit(solution)/shard_map/ppermute | solution.py:1030
  50.8 4.7 %collective-permute-start.5 = (f32[8,1024]{1,0:T(8,128)S(1)}, f32[8,1024]{1,0:T(8,128)S(1)}, u32[]{:S(2)}, u32[]{:S(2)}) collective-permute-start(f32[8,1024]{1,0:T(8,128)S(1)} %get-tuple-element.52.square_stats), channel_id=1, source_target_pairs={{0,16},{2,18},{4,20},{6,22},{8,24},{10,26},{12,28},{14,30},{1,17},... | collective-permute-start | bytes 98312 | tf_op jit(solution)/shard_map/ppermute | solution.py:1042
  56.8 42.0 %all-to-all-start.1 = ((bf16[8,784,128]{2,1,0:T(8,128)(2,1)}), bf16[8,784,128]{2,1,0:T(8,128)(2,1)S(1)}, u32[]{:S(2)}, u32[]{:S(2)}) async-start(bf16[8,784,128]{2,1,0:T(8,128)(2,1)} %other_gradients.1), calls=%async_computation.1 | async-start | bytes 3211264 | tf_op jit(solution)/shard_map/all_to_all | solution.py:986
  61.9 1.8 %collective-permute-start.7 = (bf16[4,272,128]{2,1,0:T(8,128)(2,1)S(1)}, bf16[4,272,128]{2,1,0:T(8,128)(2,1)S(1)}, u32[]{:S(2)}, u32[]{:S(2)}) collective-permute-start(bf16[4,272,128]{2,1,0:T(8,128)(2,1)S(1)} %get-tuple-element.70), channel_id=1, source_target_pairs={{0,2},{2,0},{4,6},{6,4},{8,10},{10,8},{12,14},{14,12},{16,18},{18,... | collective-permute-start | bytes 835592 | tf_op jit(solution)/shard_map/ppermute | solution.py:945
  63.8 19.7 %collective-permute-start.8 = (bf16[2,272,128]{2,1,0:T(8,128)(2,1)S(1)}, bf16[2,272,128]{2,1,0:T(8,128)(2,1)S(1)}, u32[]{:S(2)}, u32[]{:S(2)}) collective-permute-start(bf16[2,272,128]{2,1,0:T(8,128)(2,1)S(1)} %get-tuple-element.71), channel_id=1, source_target_pairs={{0,16},{2,18},{4,20},{6,22},{8,24},{10,26},{12,28},{14,30},{16,0},... | collective-permute-start | bytes 417800 | tf_op jit(solution)/shard_map/ppermute | solution.py:956
  68.0 18.5 %collective-permute-start.9 = (bf16[2,272,128]{2,1,0:T(8,128)(2,1)S(1)}, bf16[2,272,128]{2,1,0:T(8,128)(2,1)S(1)}, u32[]{:S(2)}, u32[]{:S(2)}) collective-permute-start(bf16[2,272,128]{2,1,0:T(8,128)(2,1)S(1)} %get-tuple-element.72), channel_id=1, source_target_pairs={{0,20},{2,22},{4,16},{6,18},{8,28},{10,30},{12,24},{14,26},{16,4},... | collective-permute-start | bytes 417800 | tf_op jit(solution)/shard_map/ppermute | solution.py:956
  69.3 26.1 %collective-permute-start.10 = (bf16[2,272,128]{2,1,0:T(8,128)(2,1)S(1)}, bf16[2,272,128]{2,1,0:T(8,128)(2,1)S(1)}, u32[]{:S(2)}, u32[]{:S(2)}) collective-permute-start(bf16[2,272,128]{2,1,0:T(8,128)(2,1)S(1)} %get-tuple-element.73), channel_id=1, source_target_pairs={{0,24},{2,26},{4,28},{6,30},{8,16},{10,18},{12,20},{14,22},{16,8},... | collective-permute-start | bytes 417800 | tf_op jit(solution)/shard_map/ppermute | solution.py:956
  73.1 25.8 %collective-permute-start.11 = (bf16[2,272,128]{2,1,0:T(8,128)(2,1)S(1)}, bf16[2,272,128]{2,1,0:T(8,128)(2,1)S(1)}, u32[]{:S(2)}, u32[]{:S(2)}) collective-permute-start(bf16[2,272,128]{2,1,0:T(8,128)(2,1)S(1)} %get-tuple-element.74), channel_id=1, source_target_pairs={{0,28},{2,30},{4,24},{6,26},{8,20},{10,22},{12,16},{14,18},{16,12}... | collective-permute-start | bytes 417800 | tf_op jit(solution)/shard_map/ppermute | solution.py:956
  98.9 3.7 %collective-permute-start.12 = (f32[16,128]{1,0:T(8,128)S(1)}, f32[16,128]{1,0:T(8,128)S(1)}, u32[]{:S(2)}, u32[]{:S(2)}) collective-permute-start(f32[16,128]{1,0:T(8,128)S(1)} %temper_sums.1), channel_id=1, source_target_pairs={{0,1},{1,0},{2,3},{3,2},{4,5},{5,4},{6,7},{7,6},{8,9},{9,8},{10,11... | collective-permute-start | bytes 24584 | tf_op jit(solution)/shard_map/ppermute | solution.py:1077

commit v11 on v9

--- a/solution.py
+++ b/solution.py
@@ -501,83 +501,85 @@
     )
 
 
+def from_blocks(ref, place):
+    def rows(start, stop):
+        per_tile = TILE // BLK
+        return jnp.concatenate(
+            [
+                ref[block, place * BLK : (place + 1) * BLK, :]
+                for block in range(start * per_tile, stop * per_tile)
+            ],
+            axis=0,
+        )
+
+    return rows
+
+
+def from_array(ref, place):
+    return lambda start, stop: ref[place, start * TILE : stop * TILE, :]
+
+
 class Region:
-    def __init__(self, square, arrays, places, scaling):
-        self.square, self.arrays, self.places, self.scaling = square, arrays, places, scaling
-        self.tiles = arrays.shape[1] // TILE
+    def __init__(self, square, sources, tiles, scaling, bias_ref=None, corner_ref=None, first=0):
+        self.square, self.sources, self.tiles, self.scaling = square, sources, tiles, scaling
+        self.bias_ref, self.corner_ref, self.first = bias_ref, corner_ref, first
 
     def rows(self, which, start, stop):
-        return self.arrays[self.places[which], start * TILE : stop * TILE, :]
+        return self.sources[which](start, stop)
 
     def keys_of(self, tile):
         return range(self.tiles if self.square else tile + 1)
 
-    def products(self, tile_key, tile_query):
-        return dot_rows(
-            self.rows(KEY, tile_key, tile_key + 1), self.rows(QUERY, tile_query, tile_query + 1)
-        ) * (self.scaling * math.log2(math.e))
-
-
-class Diagonal(Region):
-    def __init__(self, arrays, places, scaling, ids_ref=None, head=None, base=None, width=None):
-        super().__init__(False, arrays, places, scaling)
-        self.ids_ref, self.head, self.base, self.width = ids_ref, head, base, width
-
-    def same(self, key_block, query_block):
-        ids_ref, head, base = self.ids_ref, self.head, self.base
-        return ids_ref[head, base + key_block] == ids_ref[head, base + query_block]
-
     def scores(self, tile_key, tile_query):
         per_tile = TILE // BLK
-        scores = self.products(tile_key, tile_query)
-        spread = key_minus_query()
+        scores = dot_rows(
+            self.rows(KEY, tile_key, tile_key + 1), self.rows(QUERY, tile_query, tile_query + 1)
+        ) * (self.scaling[:, :1] * math.log2(math.e))
+        before = self.tiles * per_tile if self.square else 0
         rows = []
         for sub_key in range(per_tile):
+            key_block = tile_key * per_tile + sub_key
             pieces = []
             for sub_query in range(per_tile):
-                piece = scores[
-                    sub_key * BLK : (sub_key + 1) * BLK, sub_query * BLK : (sub_query + 1) * BLK
-                ]
-                key_block = tile_key * per_tile + sub_key
                 query_block = tile_query * per_tile + sub_query
-                if key_block > query_block:
+                lanes = slice(sub_query * BLK, (sub_query + 1) * BLK)
+                piece = scores[sub_key * BLK : (sub_key + 1) * BLK, lanes]
+                apart = before + query_block - key_block
+                if apart < 0:
                     piece = jnp.full_like(piece, blocked_score)
-                elif key_block == query_block:
-                    piece = jnp.where(spread <= 0, piece, blocked_score)
-                elif key_block == query_block - 1:
-                    least = jnp.where(self.same(key_block, query_block), -BLK, BLK - self.width)
-                    piece = jnp.where(spread > least, piece, blocked_score)
+                elif apart == 0:
+                    piece = jnp.where(key_minus_query() <= 0, piece, blocked_score)
+                elif apart == 1:
+                    piece = piece + self.corner_ref[self.first + (0 if self.square else key_block)]
                 else:
-                    piece = piece + jnp.where(
-                        self.same(key_block, query_block), 0.0, blocked_score
-                    )
+                    at = slice(query_block * BLK, (query_block + 1) * BLK)
+                    piece = piece + self.bias_ref[key_block : key_block + 1, at]
                 pieces.append(piece)
             rows.append(jnp.concatenate(pieces, axis=1))
         return jnp.concatenate(rows, axis=0)
 
 
-class Square(Region):
-    def __init__(self, arrays, scaling, bias_ref=None, corner_ref=None):
-        super().__init__(True, arrays, range(4), scaling)
-        self.bias_ref, self.corner_ref = bias_ref, corner_ref
-
-    def scores(self, tile_key, tile_query):
-        per_tile = TILE // BLK
-        scores = self.products(tile_key, tile_query)
-        rows = []
-        for sub_key in range(per_tile):
-            block = tile_key * per_tile + sub_key
-            row = scores[sub_key * BLK : (sub_key + 1) * BLK, :]
-            bias = self.bias_ref[block : block + 1, tile_rows(tile_query)]
-            if block == self.tiles * per_tile - 1 and tile_query == 0:
-                rows.append(
-                    jnp.concatenate(
-                        [row[:, :BLK] + self.corner_ref[...], row[:, BLK:] + bias[:, BLK:]], axis=1
-                    )
-                )
-            else:
-                rows.append(row + bias)
-        return jnp.concatenate(rows, axis=0)
+def diagonal(slot, arrived_ref, scales_ref, bias_ref=None, corner_ref=None):
+    blocks = arrived_ref.shape[0]
+    sources = [from_blocks(arrived_ref, slot * 4 + place) for place in range(4)]
+    bias = None if bias_ref is None else bias_ref.at[slot]
+    first = slot * (blocks - 1)
+    scaling = scales_ref[slot : slot + 1, :]
+    return Region(False, sources, blocks * BLK // TILE, scaling, bias, corner_ref, first)
+
+
+def square(half, arrived_ref, foreign_ref, scales_ref, bias_ref=None, corner_ref=None):
+    blocks = arrived_ref.shape[0]
+    near = [from_blocks(arrived_ref, place) for place in range(4)]
+    far = [from_array(foreign_ref, place) for place in range(2)]
+    if half == 0:
+        sources = [far[0], near[KEY], near[VALUE], far[1]]
+    else:
+        sources = [near[QUERY], far[0], far[1], near[GRAD]]
+    bias = None if bias_ref is None else bias_ref.at[2]
+    first = 2 * (blocks - 1)
+    scaling = scales_ref[0:1, :]
+    return Region(True, sources, blocks * BLK // TILE, scaling, bias, corner_ref, first)
 
 
 def key_minus_query():
@@ -671,10 +673,6 @@
         ].astype(jnp.bfloat16)
 
 
-def scale_row(stats_ref, slot):
-    return stats_ref[6 + slot : 7 + slot, :HD]
-
-
 def scaled(region, parts):
     return [
         [value * scale for value in part]
@@ -682,41 +680,56 @@
     ]
 
 
+def masks_kernel(softness_ref, ids_ref, span_ref, scales_ref, bias_ref, corner_ref, *, half_count):
+    me, half, _ = position(half_count)
+    base = half * half_count
+    regions = (
+        (me, base, base),
+        (me ^ half_count, base, base),
+        (me, 0, half_count),
+    )
+    for slot, (head, key_base, query_base) in enumerate(regions):
+        if slot < 2:
+            scales_ref[slot : slot + 1, :] = jnp.full(
+                (1, HD), softness_ref[head] * (1.0 / math.sqrt(HD)), jnp.float32
+            )
+
+        def same(key_block, query_block):
+            return ids_ref[head, key_base + key_block] == ids_ref[head, query_base + query_block]
+
+        def bias(key_block, query_block):
+            return jnp.full(
+                (1, BLK), jnp.where(same(key_block, query_block), 0.0, blocked_score), jnp.float32
+            )
+
+        for key_block in range(half_count):
+            bias_ref[slot, key_block : key_block + 1, :] = jnp.concatenate(
+                [bias(key_block, query_block) for query_block in range(half_count)], axis=1
+            )
+        pairs = [(block, block + 1) for block in range(half_count - 1)]
+        if slot == 2:
+            pairs = [(half_count - 1, 0)]
+        for place, pair in enumerate(pairs):
+            least = jnp.where(same(*pair), -BLK, BLK - span_ref[head])
+            corner_ref[slot * (half_count - 1) + place] = jnp.where(
+                key_minus_query() > least, 0.0, blocked_score
+            )
+
+
 def within_kernel(
-    softness_ref, ids_ref, span_ref, in_ref, arrays_ref, stats_ref, bias_ref, corner_ref,
-    parts_ref, temper_ref, own_weight, own_towards, other_weight, other_towards, *scratch,
-    half_count
+    arrived_ref, scales_ref, bias_ref, corner_ref, stats_ref, parts_ref, temper_ref,
+    own_weight, own_towards, other_weight, other_towards, *scratch, half_count
 ):
-    me, half, _ = position(half_count)
-    for block in range(half_count):
-        for place in range(8):
-            arrays_ref[place, block * BLK : (block + 1) * BLK, :] = in_ref[
-                block, place * BLK : (place + 1) * BLK, :
-            ]
+    _, half, _ = position(half_count)
     kept = ((own_weight, own_towards), (other_weight, other_towards))
     for slot in range(2):
-        head = me ^ (slot * half_count)
-        scaling = softness_ref[head] * (1.0 / math.sqrt(HD))
-        places = [slot * 4 + place for place in range(4)]
-        region = Diagonal(
-            arrays_ref, places, scaling, ids_ref, head, half * half_count, span_ref[head]
-        )
+        region = diagonal(slot, arrived_ref, scales_ref, bias_ref, corner_ref)
         statistics(region, *kept[slot], stats_ref, slot * 3)
-        stats_ref[6 + slot : 7 + slot, :] = jnp.full((1, stats_ref.shape[1]), scaling, jnp.float32)
-    for key_block in range(half_count):
-        for query_block in range(half_count):
-            same = ids_ref[me, key_block] == ids_ref[me, half_count + query_block]
-            bias_ref[key_block : key_block + 1, query_block * BLK : (query_block + 1) * BLK] = (
-                jnp.full((1, BLK), jnp.where(same, 0.0, blocked_score), jnp.float32)
-            )
-    same = ids_ref[me, half_count - 1] == ids_ref[me, half_count]
-    least = jnp.where(same, -BLK, BLK - span_ref[me])
-    corner_ref[...] = jnp.where(key_minus_query() > least, 0.0, blocked_score)
     temper_ref[...] = jnp.zeros_like(temper_ref)
 
     @pl.when(half == 0)
     def _():
-        region = Diagonal(arrays_ref, range(4), scale_row(stats_ref, 0))
+        region = diagonal(0, arrived_ref, scales_ref)
         single = alone(three_rows(stats_ref, 0))
         *parts, temper = gradients(region, *kept[0], stats_ref[0:1, :], *single, *scratch)
         for place, tiles in enumerate(scaled(region, parts)):
@@ -725,31 +738,28 @@
         temper_ref[0:1, :] = temper
 
 
-def square_kernel(arrays_ref, stats_ref, bias_ref, corner_ref, *refs, half_count):
+def square_kernel(arrived_ref, scales_ref, bias_ref, corner_ref, stats_ref, *refs, half_count):
     across_refs = refs[: half_count // 2]
-    square_ref, message_ref, square_stats, weight, towards = refs[half_count // 2 :]
+    foreign_ref, message_ref, square_stats, weight, towards = refs[half_count // 2 :]
     _, half, place = position(half_count)
-    first = jnp.where(half == 0, QUERY, KEY)
-    second = jnp.where(half == 0, GRAD, VALUE)
     for step, across_ref in enumerate(across_refs):
         for core in range(2):
             rows = rows_of(place ^ core ^ (2 * step))
-            square_ref[first, rows, :] = across_ref[core, :BLK, :]
-            square_ref[second, rows, :] = across_ref[core, BLK:, :]
-    kept_first = jnp.where(half == 0, KEY, QUERY)
-    kept_second = jnp.where(half == 0, VALUE, GRAD)
-    square_ref[kept_first, :, :] = arrays_ref[kept_first, :, :]
-    square_ref[kept_second, :, :] = arrays_ref[kept_second, :, :]
-    region = Square(square_ref, stats_ref[6:7, :TILE], bias_ref, corner_ref)
-    statistics(region, weight, towards, square_stats, 0)
-    for row in range(3):
-        message_ref[row : row + 1, :] = jnp.where(
-            half == 0, square_stats[row : row + 1, :], stats_ref[3 + row : 4 + row, :]
-        )
-
-
-def other_diagonal(arrays_ref, kept, stats_ref, totals, scratch, within_ref):
-    region = Diagonal(arrays_ref, range(4, 8), scale_row(stats_ref, 1))
+            foreign_ref[0, rows, :] = across_ref[core, :BLK, :]
+            foreign_ref[1, rows, :] = across_ref[core, BLK:, :]
+
+    for role in range(2):
+
+        @pl.when(half == role)
+        def _():
+            region = square(role, arrived_ref, foreign_ref, scales_ref, bias_ref, corner_ref)
+            statistics(region, weight, towards, square_stats, 0)
+            source, first = ((square_stats, 0), (stats_ref, 3))[role]
+            message_ref[0:3, :] = source[first : first + 3, :]
+
+
+def other_diagonal(arrived_ref, scales_ref, kept, stats_ref, totals, scratch, within_ref):
+    region = diagonal(1, arrived_ref, scales_ref)
     *parts, temper = gradients(region, *kept, stats_ref[3:4, :], *totals, *scratch)
     for array, tiles in enumerate(scaled(region, parts)):
         for tile, value in enumerate(tiles):
@@ -758,7 +768,7 @@
 
 
 def first_kernel(
-    arrays_ref, square_ref, stats_ref, square_stats, temper_in,
+    arrived_ref, scales_ref, foreign_ref, stats_ref, square_stats, temper_in,
     own_weight, own_towards, other_weight, other_towards, square_weight, square_towards,
     within_ref, across_ref, temper_ref, *scratch, half_count
 ):
@@ -768,27 +778,28 @@
     @pl.when(half == 0)
     def _():
         totals = alone(three_rows(stats_ref, 3))
+        kept = (other_weight, other_towards)
         temper_ref[1:2, :] = other_diagonal(
-            arrays_ref, (other_weight, other_towards), stats_ref, totals, scratch, within_ref
+            arrived_ref, scales_ref, kept, stats_ref, totals, scratch, within_ref
         )
 
     @pl.when(half == 1)
     def _():
         totals = merged(three_rows(stats_ref, 0), three_rows(square_stats, 0))
-        square = Square(square_ref, scale_row(stats_ref, 0))
+        region = square(1, arrived_ref, foreign_ref, scales_ref)
         *parts, square_temper = gradients(
-            square, square_weight, square_towards, square_stats[0:1, :], *totals, *scratch
-        )
-        across_query, *foreign = scaled(square, parts)
+            region, square_weight, square_towards, square_stats[0:1, :], *totals, *scratch
+        )
+        across_query, *foreign = scaled(region, parts)
         for array, tiles in enumerate(foreign):
             for tile, value in enumerate(tiles):
                 across_ref[array, tile_rows(tile), :] = value.astype(jnp.bfloat16)
-        diagonal = Diagonal(arrays_ref, range(4), scale_row(stats_ref, 0))
+        region = diagonal(0, arrived_ref, scales_ref)
         *parts, temper = gradients(
-            diagonal, own_weight, own_towards, stats_ref[0:1, :], *totals, *scratch
-        )
-        query_parts, key_parts, value_parts = scaled(diagonal, parts)
-        for tile in range(square.tiles):
+            region, own_weight, own_towards, stats_ref[0:1, :], *totals, *scratch
+        )
+        query_parts, key_parts, value_parts = scaled(region, parts)
+        for tile in range(region.tiles):
             put(within_ref, 0, tile, query_parts[tile] + across_query[tile])
             put(within_ref, 1, tile, key_parts[tile])
             put(within_ref, 2, tile, value_parts[tile])
@@ -810,51 +821,70 @@
 
 
 def finish_kernel(
-    arrays_ref, square_ref, message_ref, received_ref, stats_ref, square_stats, parts_ref,
-    temper_ref, square_weight, square_towards, other_weight, other_towards, across_in, begun_ref,
-    within_ref, *refs, half_count
+    arrived_ref, scales_ref, foreign_ref, message_ref, received_ref, stats_ref, square_stats,
+    parts_ref, temper_ref, square_weight, square_towards, other_weight, other_towards,
+    across_ref, begun_ref, within_ref, *refs, half_count
 ):
-    foreign_refs = refs[:2]
-    across, temper, *scratch = refs[2:]
+    chunk_refs = refs[:2]
+    across, temper, done_sem, chunk_sem, *scratch = refs[2:]
     _, half, place = position(half_count)
     temper[...] = temper_ref[...]
+    done = pl.ds(pl.multiple_of((1 - half) * 3 * BLK, BLK), 3 * BLK)
+    finished = pltpu.make_async_copy(
+        begun_ref.at[:, done, :], within_ref.at[:, done, :], done_sem
+    )
+    finished.start()
+    totals = merged(three_rows(message_ref, 0), three_rows(received_ref, 0))
+
+    def chunks():
+        for core, chunk_ref in enumerate(chunk_refs):
+            for step in range(half_count // 2):
+                yield core, step, chunk_ref, rows_of(place ^ core ^ (2 * step))
 
     @pl.when(half == 0)
     def _():
-        totals = merged(three_rows(message_ref, 0), three_rows(received_ref, 0))
-        region = Square(square_ref, scale_row(stats_ref, 0))
+        region = square(0, arrived_ref, foreign_ref, scales_ref)
         *parts, square_temper = gradients(
             region, square_weight, square_towards, square_stats[0:1, :], *totals, *scratch
         )
         query_parts, key_parts, value_parts = scaled(region, parts)
         for tile in range(region.tiles):
             here = tile_rows(tile)
-            across[0, here, :] = query_parts[tile].astype(jnp.bfloat16)
+            across[here, :] = query_parts[tile].astype(jnp.bfloat16)
             put(within_ref, 0, tile, parts_ref[0, here, :])
             put(within_ref, 1, tile, parts_ref[1, here, :] + key_parts[tile])
             put(within_ref, 2, tile, parts_ref[2, here, :] + value_parts[tile])
-        across[1] = jnp.zeros(across.shape[1:], jnp.bfloat16)
-        within_ref[:, 3 * BLK : 6 * BLK, :] = begun_ref[:, 3 * BLK : 6 * BLK, :]
+        for _, step, chunk_ref, rows in chunks():
+            chunk_ref[step, :BLK, :] = across[rows, :]
+            chunk_ref[step, BLK : 2 * BLK, :] = jnp.zeros((BLK, HD), jnp.bfloat16)
         temper[0:1, :] = temper_ref[0:1, :] + square_temper
 
     @pl.when(half == 1)
     def _():
-        totals = merged(three_rows(message_ref, 0), three_rows(received_ref, 0))
+        copies = [
+            pltpu.make_async_copy(
+                across_ref.at[array, rows, :],
+                chunk_ref.at[step, array * BLK : (array + 1) * BLK, :],
+                chunk_sem.at[core, step, array],
+            )
+            for core, step, chunk_ref, rows in chunks()
+            for array in range(2)
+        ]
+        for copy in copies:
+            copy.start()
+        kept = (other_weight, other_towards)
         temper[1:2, :] = other_diagonal(
-            arrays_ref, (other_weight, other_towards), stats_ref, totals, scratch, within_ref
-        )
-        across[...] = across_in[...]
-        within_ref[:, : 3 * BLK, :] = begun_ref[:, : 3 * BLK, :]
+            arrived_ref, scales_ref, kept, stats_ref, totals, scratch, within_ref
+        )
+        for copy in copies:
+            copy.wait()
 
     pieces = temper_rows(temper[0:1, :], temper[1:2, :])
     for block in range(half_count):
         within_ref[block, 6 * BLK : 6 * BLK + EXTRA, :] = pieces
-    for core, foreign_ref in enumerate(foreign_refs):
-        for step in range(half_count // 2):
-            rows = rows_of(place ^ core ^ (2 * step))
-            foreign_ref[step, :BLK, :] = across[0, rows, :]
-            foreign_ref[step, BLK : 2 * BLK, :] = across[1, rows, :]
-            foreign_ref[step, 2 * BLK :, :] = pieces
+    for _, step, chunk_ref, _ in chunks():
+        chunk_ref[step, 2 * BLK :, :] = pieces
+    finished.wait()
 
 
 def temper_kernel(within_ref, *refs, half_count):
@@ -983,32 +1013,39 @@
         (probe_vectors, lookup_vectors, content_vectors, result_cotangent), half_count
     )
     arrived = exchange_within(sent)
-    foreign = crossed(*foreign, half_count)
     kept_parts = jax.ShapeDtypeStruct((3, tokens, HD), jnp.float32)
     tempers = jax.ShapeDtypeStruct((8, HD), jnp.float32)
-    (
-        arrays, stats, bias, corner, parts, temper,
-        own_weight, own_towards, other_weight, other_towards,
-    ) = call(
+    masks = call(
+        masks_kernel,
+        "scales_and_masks",
+        (),
+        [
+            jax.ShapeDtypeStruct((8, HD), jnp.float32),
+            jax.ShapeDtypeStruct((3, half_count, tokens), jnp.float32),
+            jax.ShapeDtypeStruct((2 * half_count - 1, BLK, BLK), jnp.float32),
+        ],
+        [],
+        0,
+        6,
+        settings,
+    )
+    foreign[0], *masks = lax.optimization_barrier((foreign[0], *masks))
+    foreign = crossed(*foreign, half_count)
+    scales = masks[0]
+    stats, parts, temper, own_weight, own_towards, other_weight, other_towards = call(
         within_kernel,
         "diagonal_statistics",
-        (arrived,),
-        [
-            jax.ShapeDtypeStruct((8, tokens, HD), jnp.bfloat16), rows_of_stats,
-            jax.ShapeDtypeStruct((half_count, tokens), jnp.float32),
-            jax.ShapeDtypeStruct((BLK, BLK), jnp.float32), kept_parts, tempers,
-        ]
-        + [pairs] * 4,
+        (arrived, *masks),
+        [rows_of_stats, kept_parts, tempers] + [pairs] * 4,
         lows,
         2 * pair_flops,
         20,
-        settings,
-    )
-    square, message, square_stats, square_weight, square_towards = call(
+    )
+    far, message, square_stats, square_weight, square_towards = call(
         square_kernel,
         "square_statistics",
-        (arrays, stats, bias, corner, *foreign),
-        [jax.ShapeDtypeStruct((4, tokens, HD), jnp.bfloat16)] + [rows_of_stats] * 2 + [pairs] * 2,
+        (arrived, *masks, stats, *foreign),
+        [jax.ShapeDtypeStruct((2, tokens, HD), jnp.bfloat16)] + [rows_of_stats] * 2 + [pairs] * 2,
         [],
         2 * pair_flops,
         12,
@@ -1019,7 +1056,7 @@
         first_kernel,
         "gradients_before_totals",
         (
-            arrays, square, stats, square_stats, temper, own_weight, own_towards,
+            arrived, scales, far, stats, square_stats, temper, own_weight, own_towards,
             other_weight, other_towards, square_weight, square_towards,
         ),
         [
@@ -1035,12 +1072,15 @@
         finish_kernel,
         "gradients_after_totals",
         (
-            arrays, square, message, received, stats, square_stats, parts, temper,
+            arrived, scales, far, message, received, stats, square_stats, parts, temper,
             square_weight, square_towards, other_weight, other_towards, across, begun,
         ),
         [jax.ShapeDtypeStruct((half_count, 6 * BLK + EXTRA, HD), jnp.bfloat16)]
         + [jax.ShapeDtypeStruct((half_count // 2, 2 * BLK + EXTRA, HD), jnp.bfloat16)] * 2,
-        [pltpu.VMEM((2, tokens, HD), jnp.bfloat16), pltpu.VMEM((8, HD), jnp.float32), *lows],
+        [
+            pltpu.VMEM((tokens, HD), jnp.bfloat16), pltpu.VMEM((8, HD), jnp.float32),
+            pltpu.SemaphoreType.DMA, pltpu.SemaphoreType.DMA((2, half_count // 2, 2)), *lows,
+        ],
         2 * pair_flops,
         20,
     )

time: 101 us -> 102 us (level)
  local copies, waits for them, and re-layouts: 0.03 us -> 1.21 us
    unnamed x10, local copies, waits for them, and re-layouts: 0.03 us -> 1.21 us
    ppermute x8, waiting for transfers between devices: 28.3 us -> 29.4 us  [crossed(): lax.ppermute(message, 'seq', [(source, source ^ half_count + 2 * step) fo...]
    pallas_call x8 -> x9, Pallas kernels: 15.8 us -> 16.6 us  [kernel_call(): pl.pallas_call(kernel, out_shape=out_shape, in_specs=in_specs, out_specs=...]
  transfers between devices with their start and end apart: 14 -> 14, of which waited for: 11 -> 11; matrix products, arithmetic and copies ran while one was open for 0% -> 0% of each run, Pallas kernels for 7% -> 8%
where the time goes in v11:
time: 102 us
  waiting for transfers between devices  56 us (55%)
  starting transfers between devices  26.9 us (26%)
  Pallas kernels  16.6 us (16%)
  local copies, waits for them, and re-layouts  1.21 us (1%)
    ppermute x8, waiting for transfers between devices, crossed(): lax.ppermute(message, 'seq', [(source, source ^ half_count + 2 * step) fo...  29.4 us
    all_to_all x2, waiting for transfers between devices, exchange_within(): lax.all_to_all(array_in, 'seq', split_axis=0, concat_axis=0, axis_index_g...  20.8 us
    pallas_call x9, Pallas kernels, kernel_call(): pl.pallas_call(kernel, out_shape=out_shape, in_specs=in_specs, out_specs=...  16.6 us
    ppermute x8, starting transfers between devices, crossed(): lax.ppermute(message, 'seq', [(source, source ^ half_count + 2 * step) fo...  15.4 us
    all_to_all x2, starting transfers between devices, exchange_within(): lax.all_to_all(array_in, 'seq', split_axis=0, concat_axis=0, axis_index_g...  8.98 us
    ppermute x1, waiting for transfers between devices, head_shards(): received = lax.ppermute(message, 'seq', swap)  3.31 us
  transfers between devices with their start and end apart: 14, of which 11 were waited for; matrix products, arithmetic and copies ran while one was open for 0% of the time, Pallas kernels for 8%

profile of v11, /device:TPU:0, one launch (start us, length us, event | category | flops | bytes accessed | tf_op | source)
XLA Modules:
  0.0 102.1 jit_solution(903835421187382284)
XLA Ops:
  0.7 2.9 %pack_heads.1 = (bf16[8,1024,128]{2,1,0:T(8,128)(2,1)}, bf16[4,256,128]{2,1,0:T(8,128)(2,1)}, bf16[4,256,128]{2,1,0:T(8,128)(2,1)}) custom-call(bf16[1,128,2048]{2,1,0:T(8,128)(2,1)} %refs_0_.1, bf16[1,128,2048]{2,1,0:T(8,128)(2,1)} %refs_1_.1, bf16[1,128,2048]{2,1,0:T(8,128)(2,1)} %refs_2_.1, bf16[1,128,2048]{2,1,0:T(8,128)(2,1)} %refs_3_.1), custom_call_target="tpu_custom_call" | custom-call | bytes 4718592 | tf_op jit(solution)/shard_map/pack_heads/pallas_call | solution.py:409
  3.6 5.4 %all-to-all-start = ((bf16[8,1024,128]{2,1,0:T(8,128)(2,1)}), bf16[8,1024,128]{2,1,0:T(8,128)(2,1)S(1)}, u32[]{:S(2)}, u32[]{:S(2)}) async-start(bf16[8,1024,128]{2,1,0:T(8,128)(2,1)} %get-tuple-element.43), calls=%async_computation | async-start | bytes 4194304 | tf_op jit(solution)/shard_map/all_to_all | solution.py:996
  11.9 2.6 %collective-permute-start.1 = (bf16[2,256,128]{2,1,0:T(8,128)(2,1)}, bf16[2,256,128]{2,1,0:T(8,128)(2,1)S(1)}, u32[]{:S(2)}, u32[]{:S(2)}) collective-permute-start(bf16[2,256,128]{2,1,0:T(8,128)(2,1)} %get-tuple-element.54), channel_id=1, source_target_pairs={{0,16},{2,18},{4,20},{6,22},{8,24},{10,26},{12,28},{14,30},{16,0},... | collective-permute-start | bytes 393224 | tf_op jit(solution)/shard_map/ppermute | solution.py:966
  14.5 1.5 %collective-permute-start.2 = (bf16[2,256,128]{2,1,0:T(8,128)(2,1)}, bf16[2,256,128]{2,1,0:T(8,128)(2,1)S(1)}, u32[]{:S(2)}, u32[]{:S(2)}) collective-permute-start(bf16[2,256,128]{2,1,0:T(8,128)(2,1)} %get-tuple-element.55), channel_id=1, source_target_pairs={{0,20},{2,22},{4,16},{6,18},{8,28},{10,30},{12,24},{14,26},{16,4},... | collective-permute-start | bytes 393224 | tf_op jit(solution)/shard_map/ppermute | solution.py:966
  16.0 3.5 %collective-permute-start.3 = (bf16[2,256,128]{2,1,0:T(8,128)(2,1)}, bf16[2,256,128]{2,1,0:T(8,128)(2,1)}, u32[]{:S(2)}, u32[]{:S(2)}) collective-permute-start(bf16[2,256,128]{2,1,0:T(8,128)(2,1)} %get-tuple-element.56), channel_id=1, source_target_pairs={{0,24},{2,26},{4,28},{6,30},{8,16},{10,18},{12,20},{14,22},{16,8},... | collective-permute-start | bytes 393224 | tf_op jit(solution)/shard_map/ppermute | solution.py:966
  19.6 20.7 %all-to-all-done.arrived_ref = bf16[8,1024,128]{2,1,0:T(8,128)(2,1)S(1)} async-done(((bf16[8,1024,128]{2,1,0:T(8,128)(2,1)}), bf16[8,1024,128]{2,1,0:T(8,128)(2,1)S(1)}, u32[]{:S(2)}, u32[]{:S(2)}) %all-to-all-start) | async-done | bytes 2097184 | tf_op jit(solution)/shard_map/all_to_all | solution.py:996
  40.3 3.6 %diagonal_statistics.1 = (f32[8,1024]{1,0:T(8,128)S(1)}, f32[3,1024,128]{2,1,0:T(8,128)S(1)}, f32[8,128]{1,0:T(8,128)S(1)}, f32[1024,1024]{1,0:T(8,128)S(1)}, f3...) custom-call(bf16[8,1024,128]{2,1,0:T(8,128)(2,1)S(1)} %all-to-all-done.arrived_ref, ...), custom_call_target="tpu_custom_call" | custom-call | flops 536870912 | bytes 21569536 | tf_op jit(solution)/shard_map/diagonal_statistics/pallas_call | solution.py:409
  43.9 1.8 %collective-permute-done.3.refs_2_ = bf16[2,256,128]{2,1,0:T(8,128)(2,1)} collective-permute-done((bf16[2,256,128]{2,1,0:T(8,128)(2,1)}, bf16[2,256,128]{2,1,0:T(8,128)(2,1)}, u32[]{:S(2)}, u32[]{:S(2)}) %collective-permute-start.3) | collective-permute-done | bytes 131104 | tf_op jit(solution)/shard_map/ppermute | solution.py:966
  45.8 3.2 %collective-permute-done.4.refs_3_ = bf16[2,256,128]{2,1,0:T(8,128)(2,1)} collective-permute-done((bf16[2,256,128]{2,1,0:T(8,128)(2,1)}, bf16[2,256,128]{2,1,0:T(8,128)(2,1)}, u32[]{:S(2)}, u32[]{:S(2)}) %collective-permute-start.4) | collective-permute-done | bytes 131104 | tf_op jit(solution)/shard_map/ppermute | solution.py:966
  49.0 2.9 %square_statistics.1 = (bf16[2,1024,128]{2,1,0:T(8,128)(2,1)S(1)}, f32[8,1024]{1,0:T(8,128)S(1)}, f32[8,1024]{1,0:T(8,128)S(1)}, f32[1024,1024]{1,0:T(8,128)S(1)}, f32[1024,1024]{1,0:T(8,128)S(1)}) custom-call(bf16[8,1024,128]{2,1,0:T(8,128)(2,1)S(1)} %all-to-all-done.arrived_ref, f32[8,128]{1,0:T(8,128)S(1)} %get-tuple-element.48.scales_ref, ...), custom_call_target="tpu_custom_call" | custom-call | flops 536870912 | bytes 12718080 | tf_op jit(solution)/shard_map/square_statistics/pallas_call | solution.py:409
  51.9 1.5 %gradients_before_totals.1 = (bf16[8,768,128]{2,1,0:T(8,128)(2,1)S(1)}, bf16[2,1024,128]{2,1,0:T(8,128)(2,1)S(1)}, f32[8,128]{1,0:T(8,128)S(1)}) custom-call(bf16[8,1024,128]{2,1,0:T(8,128)(2,1)S(1)} %all-to-all-done.arrived_ref, f32[8,128]{1,0:T(8,128)S(1)} %get-tuple-element.48.scales_ref, bf16[2,1024,128]{2,1,0:T(8,128)(2,1)S(1)} %get-tuple-element.58.foreign_ref, ...), custom_call_target="tpu_custom_call" | custom-call | flops 1073741824 | bytes 29962240 | tf_op jit(solution)/shard_map/gradients_before_totals/pallas_call | solution.py:409
  53.4 3.3 %collective-permute-done.5.received_ref = f32[8,1024]{1,0:T(8,128)S(1)} collective-permute-done((f32[8,1024]{1,0:T(8,128)S(1)}, f32[8,1024]{1,0:T(8,128)S(1)}, u32[]{:S(2)}, u32[]{:S(2)}) %collective-permute-start.5) | collective-permute-done | bytes 32800 | tf_op jit(solution)/shard_map/ppermute | solution.py:1054
  56.7 2.3 %gradients_after_totals.1 = (bf16[8,784,128]{2,1,0:T(8,128)(2,1)S(1)}, bf16[4,272,128]{2,1,0:T(8,128)(2,1)S(1)}, bf16[4,272,128]{2,1,0:T(8,128)(2,1)S(1)}) custom-call(bf16[8,1024,128]{2,1,0:T(8,128)(2,1)S(1)} %all-to-all-done.arrived_ref, f32[8,128]{1,0:T(8,128)S(1)} %get-tuple-element.48.scales_ref, ...), custom_call_target="tpu_custom_call" | custom-call | flops 536870912 | bytes 25370624 | tf_op jit(solution)/shard_map/gradients_after_totals/pallas_call | solution.py:409
  60.3 3.6 %all-to-all-start.1 = ((bf16[8,784,128]{2,1,0:T(8,128)(2,1)}), bf16[8,784,128]{2,1,0:T(8,128)(2,1)S(1)}, u32[]{:S(2)}, u32[]{:S(2)}) async-start(bf16[8,784,128]{2,1,0:T(8,128)(2,1)} %copy-done), calls=%async_computation.1 | async-start | bytes 3211264 | tf_op jit(solution)/shard_map/all_to_all | solution.py:996
  64.2 1.3 %collective-permute-done.6.taken_ref = bf16[4,272,128]{2,1,0:T(8,128)(2,1)S(1)} collective-permute-done((bf16[4,272,128]{2,1,0:T(8,128)(2,1)S(1)}, bf16[4,272,128]{2,1,0:T(8,128)(2,1)S(1)}, u32[]{:S(2)}, u32[]{:S(2)}) %collective-permute-start.6) | collective-permute-done | bytes 278560 | tf_op jit(solution)/shard_map/ppermute | solution.py:955
  66.9 2.9 %collective-permute-start.8 = (bf16[2,272,128]{2,1,0:T(8,128)(2,1)S(1)}, bf16[2,272,128]{2,1,0:T(8,128)(2,1)S(1)}, u32[]{:S(2)}, u32[]{:S(2)}) collective-permute-start(bf16[2,272,128]{2,1,0:T(8,128)(2,1)S(1)} %get-tuple-element.76), channel_id=1, source_target_pairs={{0,20},{2,22},{4,16},{6,18},{8,28},{10,30},{12,24},{14,26},{16,4},... | collective-permute-start | bytes 417800 | tf_op jit(solution)/shard_map/ppermute | solution.py:966
  69.8 2.1 %collective-permute-start.9 = (bf16[2,272,128]{2,1,0:T(8,128)(2,1)S(1)}, bf16[2,272,128]{2,1,0:T(8,128)(2,1)S(1)}, u32[]{:S(2)}, u32[]{:S(2)}) collective-permute-start(bf16[2,272,128]{2,1,0:T(8,128)(2,1)S(1)} %get-tuple-element.77), channel_id=1, source_target_pairs={{0,24},{2,26},{4,28},{6,30},{8,16},{10,18},{12,20},{14,22},{16,8},... | collective-permute-start | bytes 417800 | tf_op jit(solution)/shard_map/ppermute | solution.py:966
  71.9 1.4 %collective-permute-start.10 = (bf16[2,272,128]{2,1,0:T(8,128)(2,1)S(1)}, bf16[2,272,128]{2,1,0:T(8,128)(2,1)S(1)}, u32[]{:S(2)}, u32[]{:S(2)}) collective-permute-start(bf16[2,272,128]{2,1,0:T(8,128)(2,1)S(1)} %get-tuple-element.78), channel_id=1, source_target_pairs={{0,28},{2,30},{4,24},{6,26},{8,20},{10,22},{12,16},{14,18},{16,12}... | collective-permute-start | bytes 417800 | tf_op jit(solution)/shard_map/ppermute | solution.py:966
  73.3 12.0 %collective-permute-done.7.refs_0_ = bf16[2,272,128]{2,1,0:T(8,128)(2,1)S(1)} collective-permute-done((bf16[2,272,128]{2,1,0:T(8,128)(2,1)S(1)}, bf16[2,272,128]{2,1,0:T(8,128)(2,1)S(1)}, u32[]{:S(2)}, u32[]{:S(2)}) %collective-permute-start.7) | collective-permute-done | bytes 139296 | tf_op jit(solution)/shard_map/ppermute | solution.py:966
  85.3 3.0 %collective-permute-done.8.refs_1_ = bf16[2,272,128]{2,1,0:T(8,128)(2,1)S(1)} collective-permute-done((bf16[2,272,128]{2,1,0:T(8,128)(2,1)S(1)}, bf16[2,272,128]{2,1,0:T(8,128)(2,1)S(1)}, u32[]{:S(2)}, u32[]{:S(2)}) %collective-permute-start.8) | collective-permute-done | bytes 139296 | tf_op jit(solution)/shard_map/ppermute | solution.py:966
  88.3 6.0 %collective-permute-done.9.refs_2_ = bf16[2,272,128]{2,1,0:T(8,128)(2,1)S(1)} collective-permute-done((bf16[2,272,128]{2,1,0:T(8,128)(2,1)S(1)}, bf16[2,272,128]{2,1,0:T(8,128)(2,1)S(1)}, u32[]{:S(2)}, u32[]{:S(2)}) %collective-permute-start.9) | collective-permute-done | bytes 139296 | tf_op jit(solution)/shard_map/ppermute | solution.py:966
  94.3 3.4 %collective-permute-done.10.refs_3_ = bf16[2,272,128]{2,1,0:T(8,128)(2,1)S(1)} collective-permute-done((bf16[2,272,128]{2,1,0:T(8,128)(2,1)S(1)}, bf16[2,272,128]{2,1,0:T(8,128)(2,1)S(1)}, u32[]{:S(2)}, u32[]{:S(2)}) %collective-permute-start.10) | collective-permute-done | bytes 139296 | tf_op jit(solution)/shard_map/ppermute | solution.py:966
  97.7 1.6 %collective-permute-start.11 = (f32[16,128]{1,0:T(8,128)S(1)}, f32[16,128]{1,0:T(8,128)S(1)}, u32[]{:S(2)}, u32[]{:S(2)}) collective-permute-start(f32[16,128]{1,0:T(8,128)S(1)} %temper_sums.1), channel_id=1, source_target_pairs={{0,1},{1,0},{2,3},{3,2},{4,5},{5,4},{6,7},{7,6},{8,9},{9,8},{10,11... | collective-permute-start | bytes 24584 | tf_op jit(solution)/shard_map/ppermute | solution.py:1093
  99.3 1.5 %unpack_heads.1 = (bf16[1,128,2048]{2,1,0:T(8,128)(2,1)}, bf16[1,128,2048]{2,1,0:T(8,128)(2,1)}, bf16[1,128,2048]{2,1,0:T(8,128)(2,1)}) custom-call(bf16[8,784,128]{2,1,0:T(8,128)(2,1)S(1)} %all-to-all-done.1.within_ref, bf16[2,272,128]{2,1,0:T(8,128)(2,1)S(1)} %collective-permute-done.7.refs_0_, bf16[2,272,128]{2,1,0:T(8,128)(2,1)S(1)} %collective-permute-done.8.refs_1_, ...), custom_call_target="tpu_custom_call" | custom-call | bytes 3735552 | tf_op jit(solution)/shard_map/unpack_heads/pallas_call | solution.py:409
  (25 shorter events, 7.3 us)
Async XLA Ops:
  0.6 8.9 %copy-start.4 = (s32[16]{0:T(128)S(1)}, s32[16]{0:T(128)}, u32[]{:S(2)}) copy-start(s32[16]{0:T(128)} %span_ref.1) | copy-start | bytes 196
  0.6 8.9 %copy-start.2 = (s32[1,16,16,1]{2,3,1,0:T(1,128)S(1)}, s32[1,16,16,1]{2,3,1,0:T(1,128)}, u32[]{:S(2)}) copy-start(s32[1,16,16,1]{2,3,1,0:T(1,128)} %param.12) | copy-start | bytes 3076
  0.7 8.9 %copy-start.3 = (f32[16]{0:T(128)S(1)}, f32[16]{0:T(128)}, u32[]{:S(2)}) copy-start(f32[16]{0:T(128)} %softness_ref.1) | copy-start | bytes 196
  3.6 7.5 %copy-start.1 = (bf16[4,256,128]{2,1,0:T(8,128)(2,1)S(1)}, bf16[4,256,128]{2,1,0:T(8,128)(2,1)}, u32[]{:S(2)}) copy-start(bf16[4,256,128]{2,1,0:T(8,128)(2,1)} %get-tuple-element.52.kept_ref) | copy-start | bytes 786436
  3.6 36.7 %all-to-all-start = ((bf16[8,1024,128]{2,1,0:T(8,128)(2,1)}), bf16[8,1024,128]{2,1,0:T(8,128)(2,1)S(1)}, u32[]{:S(2)}, u32[]{:S(2)}) async-start(bf16[8,1024,128]{2,1,0:T(8,128)(2,1)} %get-tuple-element.43), calls=%async_computation | async-start | bytes 4194304 | tf_op jit(solution)/shard_map/all_to_all | solution.py:996
  9.0 2.1 %collective-permute-start = (bf16[4,256,128]{2,1,0:T(8,128)(2,1)}, bf16[4,256,128]{2,1,0:T(8,128)(2,1)S(1)}, u32[]{:S(2)}, u32[]{:S(2)}) collective-permute-start(bf16[4,256,128]{2,1,0:T(8,128)(2,1)} %get-tuple-element.53), channel_id=1, source_target_pairs={{0,2},{2,0},{4,6},{6,4},{8,10},{10,8},{12,14},{14,12},{16,18},{18,... | collective-permute-start | bytes 786440 | tf_op jit(solution)/shard_map/ppermute | solution.py:955
  11.9 32.0 %collective-permute-start.1 = (bf16[2,256,128]{2,1,0:T(8,128)(2,1)}, bf16[2,256,128]{2,1,0:T(8,128)(2,1)S(1)}, u32[]{:S(2)}, u32[]{:S(2)}) collective-permute-start(bf16[2,256,128]{2,1,0:T(8,128)(2,1)} %get-tuple-element.54), channel_id=1, source_target_pairs={{0,16},{2,18},{4,20},{6,22},{8,24},{10,26},{12,28},{14,30},{16,0},... | collective-permute-start | bytes 393224 | tf_op jit(solution)/shard_map/ppermute | solution.py:966
  14.5 29.4 %collective-permute-start.2 = (bf16[2,256,128]{2,1,0:T(8,128)(2,1)}, bf16[2,256,128]{2,1,0:T(8,128)(2,1)S(1)}, u32[]{:S(2)}, u32[]{:S(2)}) collective-permute-start(bf16[2,256,128]{2,1,0:T(8,128)(2,1)} %get-tuple-element.55), channel_id=1, source_target_pairs={{0,20},{2,22},{4,16},{6,18},{8,28},{10,30},{12,24},{14,26},{16,4},... | collective-permute-start | bytes 393224 | tf_op jit(solution)/shard_map/ppermute | solution.py:966
  16.0 29.8 %collective-permute-start.3 = (bf16[2,256,128]{2,1,0:T(8,128)(2,1)}, bf16[2,256,128]{2,1,0:T(8,128)(2,1)}, u32[]{:S(2)}, u32[]{:S(2)}) collective-permute-start(bf16[2,256,128]{2,1,0:T(8,128)(2,1)} %get-tuple-element.56), channel_id=1, source_target_pairs={{0,24},{2,26},{4,28},{6,30},{8,16},{10,18},{12,20},{14,22},{16,8},... | collective-permute-start | bytes 393224 | tf_op jit(solution)/shard_map/ppermute | solution.py:966
  19.5 29.5 %collective-permute-start.4 = (bf16[2,256,128]{2,1,0:T(8,128)(2,1)}, bf16[2,256,128]{2,1,0:T(8,128)(2,1)}, u32[]{:S(2)}, u32[]{:S(2)}) collective-permute-start(bf16[2,256,128]{2,1,0:T(8,128)(2,1)} %get-tuple-element.57), channel_id=1, source_target_pairs={{0,28},{2,30},{4,24},{6,26},{8,20},{10,22},{12,16},{14,18},{16,12}... | collective-permute-start | bytes 393224 | tf_op jit(solution)/shard_map/ppermute | solution.py:966
  51.9 4.9 %collective-permute-start.5 = (f32[8,1024]{1,0:T(8,128)S(1)}, f32[8,1024]{1,0:T(8,128)S(1)}, u32[]{:S(2)}, u32[]{:S(2)}) collective-permute-start(f32[8,1024]{1,0:T(8,128)S(1)} %get-tuple-element.59.message_ref), channel_id=1, source_target_pairs={{0,16},{2,18},{4,20},{6,22},{8,24},{10,26},{12,28},{14,30},{16,0},... | collective-permute-start | bytes 98312 | tf_op jit(solution)/shard_map/ppermute | solution.py:1054
  59.1 1.2 %copy-start = (bf16[8,784,128]{2,1,0:T(8,128)(2,1)}, bf16[8,784,128]{2,1,0:T(8,128)(2,1)S(1)}, u32[]{:S(2)}) copy-start(bf16[8,784,128]{2,1,0:T(8,128)(2,1)S(1)} %get-tuple-element.72) | copy-start | bytes 4816900
  60.3 37.4 %all-to-all-start.1 = ((bf16[8,784,128]{2,1,0:T(8,128)(2,1)}), bf16[8,784,128]{2,1,0:T(8,128)(2,1)S(1)}, u32[]{:S(2)}, u32[]{:S(2)}) async-start(bf16[8,784,128]{2,1,0:T(8,128)(2,1)} %copy-done), calls=%async_computation.1 | async-start | bytes 3211264 | tf_op jit(solution)/shard_map/all_to_all | solution.py:996
  63.8 1.7 %collective-permute-start.6 = (bf16[4,272,128]{2,1,0:T(8,128)(2,1)S(1)}, bf16[4,272,128]{2,1,0:T(8,128)(2,1)S(1)}, u32[]{:S(2)}, u32[]{:S(2)}) collective-permute-start(bf16[4,272,128]{2,1,0:T(8,128)(2,1)S(1)} %get-tuple-element.74), channel_id=1, source_target_pairs={{0,2},{2,0},{4,6},{6,4},{8,10},{10,8},{12,14},{14,12},{16,18},{18,... | collective-permute-start | bytes 835592 | tf_op jit(solution)/shard_map/ppermute | solution.py:955
  65.6 19.7 %collective-permute-start.7 = (bf16[2,272,128]{2,1,0:T(8,128)(2,1)S(1)}, bf16[2,272,128]{2,1,0:T(8,128)(2,1)S(1)}, u32[]{:S(2)}, u32[]{:S(2)}) collective-permute-start(bf16[2,272,128]{2,1,0:T(8,128)(2,1)S(1)} %get-tuple-element.75), channel_id=1, source_target_pairs={{0,16},{2,18},{4,20},{6,22},{8,24},{10,26},{12,28},{14,30},{16,0},... | collective-permute-start | bytes 417800 | tf_op jit(solution)/shard_map/ppermute | solution.py:966
  66.9 21.4 %collective-permute-start.8 = (bf16[2,272,128]{2,1,0:T(8,128)(2,1)S(1)}, bf16[2,272,128]{2,1,0:T(8,128)(2,1)S(1)}, u32[]{:S(2)}, u32[]{:S(2)}) collective-permute-start(bf16[2,272,128]{2,1,0:T(8,128)(2,1)S(1)} %get-tuple-element.76), channel_id=1, source_target_pairs={{0,20},{2,22},{4,16},{6,18},{8,28},{10,30},{12,24},{14,26},{16,4},... | collective-permute-start | bytes 417800 | tf_op jit(solution)/shard_map/ppermute | solution.py:966
  69.8 24.5 %collective-permute-start.9 = (bf16[2,272,128]{2,1,0:T(8,128)(2,1)S(1)}, bf16[2,272,128]{2,1,0:T(8,128)(2,1)S(1)}, u32[]{:S(2)}, u32[]{:S(2)}) collective-permute-start(bf16[2,272,128]{2,1,0:T(8,128)(2,1)S(1)} %get-tuple-element.77), channel_id=1, source_target_pairs={{0,24},{2,26},{4,28},{6,30},{8,16},{10,18},{12,20},{14,22},{16,8},... | collective-permute-start | bytes 417800 | tf_op jit(solution)/shard_map/ppermute | solution.py:966
  71.9 25.8 %collective-permute-start.10 = (bf16[2,272,128]{2,1,0:T(8,128)(2,1)S(1)}, bf16[2,272,128]{2,1,0:T(8,128)(2,1)S(1)}, u32[]{:S(2)}, u32[]{:S(2)}) collective-permute-start(bf16[2,272,128]{2,1,0:T(8,128)(2,1)S(1)} %get-tuple-element.78), channel_id=1, source_target_pairs={{0,28},{2,30},{4,24},{6,26},{8,20},{10,22},{12,16},{14,18},{16,12}... | collective-permute-start | bytes 417800 | tf_op jit(solution)/shard_map/ppermute | solution.py:966
  97.7 3.7 %collective-permute-start.11 = (f32[16,128]{1,0:T(8,128)S(1)}, f32[16,128]{1,0:T(8,128)S(1)}, u32[]{:S(2)}, u32[]{:S(2)}) collective-permute-start(f32[16,128]{1,0:T(8,128)S(1)} %temper_sums.1), channel_id=1, source_target_pairs={{0,1},{1,0},{2,3},{3,2},{4,5},{5,4},{6,7},{7,6},{8,9},{9,8},{10,11... | collective-permute-start | bytes 24584 | tf_op jit(solution)/shard_map/ppermute | solution.py:1093

commit v12 on v11

--- a/solution.py
+++ b/solution.py
@@ -401,7 +401,7 @@
 
 
 def kernel_call(
-    kernel, name, operands, in_specs, out_shape, scratch, vmem_mib, flops=0, out_space=pltpu.VMEM
+    kernel, name, operands, in_specs, out_shape, scratch, vmem_mib, flops=0, out_spaces=None
 ):
     bytes_accessed = sum(
         math.prod(item.shape) * item.dtype.itemsize for item in (*operands, *out_shape)
@@ -410,7 +410,10 @@
         kernel,
         out_shape=out_shape,
         in_specs=in_specs,
-        out_specs=[pl.BlockSpec(memory_space=out_space)] * len(out_shape),
+        out_specs=[
+            pl.BlockSpec(memory_space=space)
+            for space in out_spaces or [pltpu.VMEM] * len(out_shape)
+        ],
         scratch_shapes=scratch,
         cost_estimate=pl.CostEstimate(
             flops=flops, bytes_accessed=bytes_accessed, transcendentals=0
@@ -485,7 +488,7 @@
             pltpu.SemaphoreType.DMA((2,)),
         ],
         60,
-        out_space=pl.ANY,
+        out_spaces=[pl.ANY] * 3,
     )
 
 
@@ -568,18 +571,12 @@
     return Region(False, sources, blocks * BLK // TILE, scaling, bias, corner_ref, first)
 
 
-def square(half, arrived_ref, foreign_ref, scales_ref, bias_ref=None, corner_ref=None):
-    blocks = arrived_ref.shape[0]
-    near = [from_blocks(arrived_ref, place) for place in range(4)]
-    far = [from_array(foreign_ref, place) for place in range(2)]
-    if half == 0:
-        sources = [far[0], near[KEY], near[VALUE], far[1]]
-    else:
-        sources = [near[QUERY], far[0], far[1], near[GRAD]]
+def square(square_ref, scales_ref, bias_ref=None, corner_ref=None):
+    tiles = square_ref.shape[1] // TILE
+    sources = [from_array(square_ref, place) for place in range(4)]
     bias = None if bias_ref is None else bias_ref.at[2]
-    first = 2 * (blocks - 1)
-    scaling = scales_ref[0:1, :]
-    return Region(True, sources, blocks * BLK // TILE, scaling, bias, corner_ref, first)
+    first = 2 * (tiles * TILE // BLK - 1)
+    return Region(True, sources, tiles, scales_ref[0:1, :], bias, corner_ref, first)
 
 
 def key_minus_query():
@@ -613,7 +610,7 @@
 
 
 def gradients(
-    region, weight_ref, towards_ref, top, log_total, delta, prob_low, grad_low, keys_flat
+    region, weight_ref, towards_ref, top, log_total, delta, prob_low, grad_low, keys_flat, emit=None
 ):
     keys_flat[...] = region.rows(KEY, 0, region.tiles).T
     share = jnp.exp2(top - log_total)
@@ -636,16 +633,17 @@
             keepdims=True,
         )
         query_parts.append(query_part)
-    for tile in range(region.tiles):
-        first = 0 if region.square else tile
-        onward = slice(first * TILE, region.tiles * TILE)
-        here = tile_rows(tile)
-        key_parts.append(
-            dot_plain(grad_low[here, onward], region.rows(QUERY, first, region.tiles))
-        )
-        value_parts.append(
-            dot_plain(prob_low[here, onward], region.rows(GRAD, first, region.tiles))
-        )
+    if emit is not None:
+        emit(QUERY, query_parts)
+    for low, which, parts in ((grad_low, QUERY, key_parts), (prob_low, GRAD, value_parts)):
+        for tile in range(region.tiles):
+            first = 0 if region.square else tile
+            onward = slice(first * TILE, region.tiles * TILE)
+            parts.append(
+                dot_plain(low[tile_rows(tile), onward], region.rows(which, first, region.tiles))
+            )
+        if emit is not None:
+            emit(KEY if which == QUERY else VALUE, parts)
     return query_parts, key_parts, value_parts, temper
 
 
@@ -740,35 +738,30 @@
 
 def square_kernel(arrived_ref, scales_ref, bias_ref, corner_ref, stats_ref, *refs, half_count):
     across_refs = refs[: half_count // 2]
-    foreign_ref, message_ref, square_stats, weight, towards = refs[half_count // 2 :]
+    square_ref, message_ref, square_stats, weight, towards = refs[half_count // 2 :]
     _, half, place = position(half_count)
+    first = jnp.where(half == 0, QUERY, KEY)
+    second = jnp.where(half == 0, GRAD, VALUE)
     for step, across_ref in enumerate(across_refs):
         for core in range(2):
             rows = rows_of(place ^ core ^ (2 * step))
-            foreign_ref[0, rows, :] = across_ref[core, :BLK, :]
-            foreign_ref[1, rows, :] = across_ref[core, BLK:, :]
-
-    for role in range(2):
-
-        @pl.when(half == role)
-        def _():
-            region = square(role, arrived_ref, foreign_ref, scales_ref, bias_ref, corner_ref)
-            statistics(region, weight, towards, square_stats, 0)
-            source, first = ((square_stats, 0), (stats_ref, 3))[role]
-            message_ref[0:3, :] = source[first : first + 3, :]
-
-
-def other_diagonal(arrived_ref, scales_ref, kept, stats_ref, totals, scratch, within_ref):
-    region = diagonal(1, arrived_ref, scales_ref)
-    *parts, temper = gradients(region, *kept, stats_ref[3:4, :], *totals, *scratch)
-    for array, tiles in enumerate(scaled(region, parts)):
-        for tile, value in enumerate(tiles):
-            put(within_ref, 3 + array, tile, value)
-    return temper
+            square_ref[first, rows, :] = across_ref[core, :BLK, :]
+            square_ref[second, rows, :] = across_ref[core, BLK:, :]
+    for kept in (jnp.where(half == 0, KEY, QUERY), jnp.where(half == 0, VALUE, GRAD)):
+        for block in range(half_count):
+            square_ref[kept, block * BLK : (block + 1) * BLK, :] = arrived_ref[
+                block, rows_of(kept), :
+            ]
+    region = square(square_ref, scales_ref, bias_ref, corner_ref)
+    statistics(region, weight, towards, square_stats, 0)
+    for row in range(3):
+        message_ref[row : row + 1, :] = jnp.where(
+            half == 0, square_stats[row : row + 1, :], stats_ref[3 + row : 4 + row, :]
+        )
 
 
 def first_kernel(
-    arrived_ref, scales_ref, foreign_ref, stats_ref, square_stats, temper_in,
+    arrived_ref, scales_ref, square_ref, stats_ref, square_stats, temper_in,
     own_weight, own_towards, other_weight, other_towards, square_weight, square_towards,
     within_ref, across_ref, temper_ref, *scratch, half_count
 ):
@@ -777,16 +770,19 @@
 
     @pl.when(half == 0)
     def _():
+        region = diagonal(1, arrived_ref, scales_ref)
         totals = alone(three_rows(stats_ref, 3))
-        kept = (other_weight, other_towards)
-        temper_ref[1:2, :] = other_diagonal(
-            arrived_ref, scales_ref, kept, stats_ref, totals, scratch, within_ref
-        )
+        *parts, temper_ref[1:2, :] = gradients(
+            region, other_weight, other_towards, stats_ref[3:4, :], *totals, *scratch
+        )
+        for array, tiles in enumerate(scaled(region, parts)):
+            for tile, value in enumerate(tiles):
+                put(within_ref, array, tile, value)
 
     @pl.when(half == 1)
     def _():
         totals = merged(three_rows(stats_ref, 0), three_rows(square_stats, 0))
-        region = square(1, arrived_ref, foreign_ref, scales_ref)
+        region = square(square_ref, scales_ref)
         *parts, square_temper = gradients(
             region, square_weight, square_towards, square_stats[0:1, :], *totals, *scratch
         )
@@ -821,19 +817,25 @@
 
 
 def finish_kernel(
-    arrived_ref, scales_ref, foreign_ref, message_ref, received_ref, stats_ref, square_stats,
+    arrived_ref, scales_ref, square_ref, message_ref, received_ref, stats_ref, square_stats,
     parts_ref, temper_ref, square_weight, square_towards, other_weight, other_towards,
     across_ref, begun_ref, within_ref, *refs, half_count
 ):
     chunk_refs = refs[:2]
-    across, temper, done_sem, chunk_sem, *scratch = refs[2:]
+    across, temper, ready, tail, begun_sem, ready_sem, tail_sem, chunk_sem, *scratch = refs[2:]
     _, half, place = position(half_count)
     temper[...] = temper_ref[...]
-    done = pl.ds(pl.multiple_of((1 - half) * 3 * BLK, BLK), 3 * BLK)
-    finished = pltpu.make_async_copy(
-        begun_ref.at[:, done, :], within_ref.at[:, done, :], done_sem
-    )
-    finished.start()
+    begun_at = pl.ds(pl.multiple_of((1 - half) * 3 * BLK, BLK), 3 * BLK)
+    leaving = [pltpu.make_async_copy(begun_ref, within_ref.at[:, begun_at, :], begun_sem)]
+    leaving[0].start()
+    for array in range(3):
+        rows = slice(array * BLK, (array + 1) * BLK)
+        to = pl.ds(pl.multiple_of((half * 3 + array) * BLK, BLK), BLK)
+        leaving.append(
+            pltpu.make_async_copy(
+                ready.at[:, rows, :], within_ref.at[:, to, :], ready_sem.at[array]
+            )
+        )
     totals = merged(three_rows(message_ref, 0), three_rows(received_ref, 0))
 
     def chunks():
@@ -843,17 +845,22 @@
 
     @pl.when(half == 0)
     def _():
-        region = square(0, arrived_ref, foreign_ref, scales_ref)
-        *parts, square_temper = gradients(
-            region, square_weight, square_towards, square_stats[0:1, :], *totals, *scratch
-        )
-        query_parts, key_parts, value_parts = scaled(region, parts)
-        for tile in range(region.tiles):
-            here = tile_rows(tile)
-            across[here, :] = query_parts[tile].astype(jnp.bfloat16)
-            put(within_ref, 0, tile, parts_ref[0, here, :])
-            put(within_ref, 1, tile, parts_ref[1, here, :] + key_parts[tile])
-            put(within_ref, 2, tile, parts_ref[2, here, :] + value_parts[tile])
+        region = square(square_ref, scales_ref)
+
+        def send(array, parts):
+            for tile, part in enumerate(parts):
+                here = tile_rows(tile)
+                if array == QUERY:
+                    across[here, :] = (part * region.scaling).astype(jnp.bfloat16)
+                    put(ready, array, tile, parts_ref[array, here, :])
+                else:
+                    scale = region.scaling if array == KEY else 1.0
+                    put(ready, array, tile, parts_ref[array, here, :] + part * scale)
+            leaving[1 + array].start()
+
+        *_, square_temper = gradients(
+            region, square_weight, square_towards, square_stats[0:1, :], *totals, *scratch, emit=send
+        )
         for _, step, chunk_ref, rows in chunks():
             chunk_ref[step, :BLK, :] = across[rows, :]
             chunk_ref[step, BLK : 2 * BLK, :] = jnp.zeros((BLK, HD), jnp.bfloat16)
@@ -872,19 +879,31 @@
         ]
         for copy in copies:
             copy.start()
-        kept = (other_weight, other_towards)
-        temper[1:2, :] = other_diagonal(
-            arrived_ref, scales_ref, kept, stats_ref, totals, scratch, within_ref
+        region = diagonal(1, arrived_ref, scales_ref)
+
+        def send(array, parts):
+            scale = 1.0 if array == VALUE else region.scaling
+            for tile, part in enumerate(parts):
+                put(ready, array, tile, part * scale)
+            leaving[1 + array].start()
+
+        *_, temper[1:2, :] = gradients(
+            region, other_weight, other_towards, stats_ref[3:4, :], *totals, *scratch, emit=send
         )
         for copy in copies:
             copy.wait()
 
     pieces = temper_rows(temper[0:1, :], temper[1:2, :])
     for block in range(half_count):
-        within_ref[block, 6 * BLK : 6 * BLK + EXTRA, :] = pieces
+        tail[block] = pieces
+    leaving.append(
+        pltpu.make_async_copy(tail, within_ref.at[:, 6 * BLK : 6 * BLK + EXTRA, :], tail_sem)
+    )
+    leaving[-1].start()
     for _, step, chunk_ref, _ in chunks():
         chunk_ref[step, 2 * BLK :, :] = pieces
-    finished.wait()
+    for copy in leaving:
+        copy.wait()
 
 
 def temper_kernel(within_ref, *refs, half_count):
@@ -997,7 +1016,9 @@
             array_in, "seq", split_axis=0, concat_axis=0, axis_index_groups=groups, tiled=True
         )
 
-    def call(kernel, name, operands, out_shape, scratch, flops, vmem_mib, scalars=()):
+    def call(
+        kernel, name, operands, out_shape, scratch, flops, vmem_mib, scalars=(), out_spaces=None
+    ):
         return kernel_call(
             functools.partial(kernel, half_count=half_count),
             name,
@@ -1007,6 +1028,7 @@
             scratch,
             vmem_mib,
             flops,
+            out_spaces,
         )
 
     sent, *foreign = packed(
@@ -1041,11 +1063,11 @@
         2 * pair_flops,
         20,
     )
-    far, message, square_stats, square_weight, square_towards = call(
+    squared, message, square_stats, square_weight, square_towards = call(
         square_kernel,
         "square_statistics",
         (arrived, *masks, stats, *foreign),
-        [jax.ShapeDtypeStruct((2, tokens, HD), jnp.bfloat16)] + [rows_of_stats] * 2 + [pairs] * 2,
+        [jax.ShapeDtypeStruct((4, tokens, HD), jnp.bfloat16)] + [rows_of_stats] * 2 + [pairs] * 2,
         [],
         2 * pair_flops,
         12,
@@ -1056,11 +1078,11 @@
         first_kernel,
         "gradients_before_totals",
         (
-            arrived, scales, far, stats, square_stats, temper, own_weight, own_towards,
+            arrived, scales, squared, stats, square_stats, temper, own_weight, own_towards,
             other_weight, other_towards, square_weight, square_towards,
         ),
         [
-            jax.ShapeDtypeStruct((half_count, 6 * BLK, HD), jnp.bfloat16),
+            jax.ShapeDtypeStruct((half_count, 3 * BLK, HD), jnp.bfloat16),
             jax.ShapeDtypeStruct((2, tokens, HD), jnp.bfloat16),
             tempers,
         ],
@@ -1072,17 +1094,21 @@
         finish_kernel,
         "gradients_after_totals",
         (
-            arrived, scales, far, message, received, stats, square_stats, parts, temper,
+            arrived, scales, squared, message, received, stats, square_stats, parts, temper,
             square_weight, square_towards, other_weight, other_towards, across, begun,
         ),
-        [jax.ShapeDtypeStruct((half_count, 6 * BLK + EXTRA, HD), jnp.bfloat16)]
+        [pltpu.HBM((half_count, 6 * BLK + EXTRA, HD), jnp.bfloat16)]
         + [jax.ShapeDtypeStruct((half_count // 2, 2 * BLK + EXTRA, HD), jnp.bfloat16)] * 2,
         [
             pltpu.VMEM((tokens, HD), jnp.bfloat16), pltpu.VMEM((8, HD), jnp.float32),
-            pltpu.SemaphoreType.DMA, pltpu.SemaphoreType.DMA((2, half_count // 2, 2)), *lows,
+            pltpu.VMEM((half_count, 3 * BLK, HD), jnp.bfloat16),
+            pltpu.VMEM((half_count, EXTRA, HD), jnp.bfloat16),
+            pltpu.SemaphoreType.DMA, pltpu.SemaphoreType.DMA((3,)), pltpu.SemaphoreType.DMA,
+            pltpu.SemaphoreType.DMA((2, half_count // 2, 2)), *lows,
         ],
         2 * pair_flops,
         20,
+        out_spaces=(pl.ANY, pltpu.VMEM, pltpu.VMEM),
     )
     across = crossed(*foreign, half_count)
     within = exchange_within(within)

time: 102 us -> 102 us (level)
  local copies, waits for them, and re-layouts: 1.21 us -> 0.02 us
    unnamed x10 -> x8, local copies, waits for them, and re-layouts: 1.21 us -> 0.02 us
where the time goes in v12:
time: 102 us
  waiting for transfers between devices  56.1 us (55%)
  starting transfers between devices  26.9 us (26%)
  Pallas kernels  17.3 us (17%)
    ppermute x8, waiting for transfers between devices, crossed(): lax.ppermute(message, 'seq', [(source, source ^ half_count + 2 * step) fo...  29.4 us
    all_to_all x2, waiting for transfers between devices, exchange_within(): lax.all_to_all(array_in, 'seq', split_axis=0, concat_axis=0, axis_index_g...  20.7 us
    pallas_call x9, Pallas kernels, kernel_call(): pl.pallas_call(kernel, out_shape=out_shape, in_specs=in_specs, out_specs=...  17.3 us
    ppermute x8, starting transfers between devices, crossed(): lax.ppermute(message, 'seq', [(source, source ^ half_count + 2 * step) fo...  15.4 us
    all_to_all x2, starting transfers between devices, exchange_within(): lax.all_to_all(array_in, 'seq', split_axis=0, concat_axis=0, axis_index_g...  8.99 us
    ppermute x1, waiting for transfers between devices, head_shards(): received = lax.ppermute(message, 'seq', swap)  3.49 us
  transfers between devices with their start and end apart: 14, of which 11 were waited for; matrix products, arithmetic and copies ran while one was open for 0% of the time, Pallas kernels for 8%

profile of v12, /device:TPU:0, one launch (start us, length us, event | category | flops | bytes accessed | tf_op | source)
XLA Modules:
  0.0 101.7 jit_solution(2541989692134314507)
XLA Ops:
  0.7 2.9 %pack_heads.1 = (bf16[8,1024,128]{2,1,0:T(8,128)(2,1)}, bf16[4,256,128]{2,1,0:T(8,128)(2,1)}, bf16[4,256,128]{2,1,0:T(8,128)(2,1)}) custom-call(bf16[1,128,2048]{2,1,0:T(8,128)(2,1)} %refs_0_.1, bf16[1,128,2048]{2,1,0:T(8,128)(2,1)} %refs_1_.1, bf16[1,128,2048]{2,1,0:T(8,128)(2,1)} %refs_2_.1, bf16[1,128,2048]{2,1,0:T(8,128)(2,1)} %refs_3_.1), custom_call_target="tpu_custom_call" | custom-call | bytes 4718592 | tf_op jit(solution)/shard_map/pack_heads/pallas_call | solution.py:409
  3.6 5.4 %all-to-all-start = ((bf16[8,1024,128]{2,1,0:T(8,128)(2,1)}), bf16[8,1024,128]{2,1,0:T(8,128)(2,1)S(1)}, u32[]{:S(2)}, u32[]{:S(2)}) async-start(bf16[8,1024,128]{2,1,0:T(8,128)(2,1)} %get-tuple-element.43), calls=%async_computation | async-start | bytes 4194304 | tf_op jit(solution)/shard_map/all_to_all | solution.py:1015
  12.0 2.6 %collective-permute-start.1 = (bf16[2,256,128]{2,1,0:T(8,128)(2,1)}, bf16[2,256,128]{2,1,0:T(8,128)(2,1)S(1)}, u32[]{:S(2)}, u32[]{:S(2)}) collective-permute-start(bf16[2,256,128]{2,1,0:T(8,128)(2,1)} %get-tuple-element.54), channel_id=1, source_target_pairs={{0,16},{2,18},{4,20},{6,22},{8,24},{10,26},{12,28},{14,30},{16,0},... | collective-permute-start | bytes 393224 | tf_op jit(solution)/shard_map/ppermute | solution.py:985
  14.5 1.5 %collective-permute-start.2 = (bf16[2,256,128]{2,1,0:T(8,128)(2,1)}, bf16[2,256,128]{2,1,0:T(8,128)(2,1)S(1)}, u32[]{:S(2)}, u32[]{:S(2)}) collective-permute-start(bf16[2,256,128]{2,1,0:T(8,128)(2,1)} %get-tuple-element.55), channel_id=1, source_target_pairs={{0,20},{2,22},{4,16},{6,18},{8,28},{10,30},{12,24},{14,26},{16,4},... | collective-permute-start | bytes 393224 | tf_op jit(solution)/shard_map/ppermute | solution.py:985
  16.0 3.5 %collective-permute-start.3 = (bf16[2,256,128]{2,1,0:T(8,128)(2,1)}, bf16[2,256,128]{2,1,0:T(8,128)(2,1)}, u32[]{:S(2)}, u32[]{:S(2)}) collective-permute-start(bf16[2,256,128]{2,1,0:T(8,128)(2,1)} %get-tuple-element.56), channel_id=1, source_target_pairs={{0,24},{2,26},{4,28},{6,30},{8,16},{10,18},{12,20},{14,22},{16,8},... | collective-permute-start | bytes 393224 | tf_op jit(solution)/shard_map/ppermute | solution.py:985
  19.6 20.7 %all-to-all-done.arrived_ref = bf16[8,1024,128]{2,1,0:T(8,128)(2,1)S(1)} async-done(((bf16[8,1024,128]{2,1,0:T(8,128)(2,1)}), bf16[8,1024,128]{2,1,0:T(8,128)(2,1)S(1)}, u32[]{:S(2)}, u32[]{:S(2)}) %all-to-all-start) | async-done | bytes 2097184 | tf_op jit(solution)/shard_map/all_to_all | solution.py:1015
  40.3 3.6 %diagonal_statistics.1 = (f32[8,1024]{1,0:T(8,128)S(1)}, f32[3,1024,128]{2,1,0:T(8,128)S(1)}, f32[8,128]{1,0:T(8,128)S(1)}, f32[1024,1024]{1,0:T(8,128)S(1)}, f3...) custom-call(bf16[8,1024,128]{2,1,0:T(8,128)(2,1)S(1)} %all-to-all-done.arrived_ref, ...), custom_call_target="tpu_custom_call" | custom-call | flops 536870912 | bytes 21569536 | tf_op jit(solution)/shard_map/diagonal_statistics/pallas_call | solution.py:409
  44.0 1.8 %collective-permute-done.3.refs_2_ = bf16[2,256,128]{2,1,0:T(8,128)(2,1)} collective-permute-done((bf16[2,256,128]{2,1,0:T(8,128)(2,1)}, bf16[2,256,128]{2,1,0:T(8,128)(2,1)}, u32[]{:S(2)}, u32[]{:S(2)}) %collective-permute-start.3) | collective-permute-done | bytes 131104 | tf_op jit(solution)/shard_map/ppermute | solution.py:985
  45.8 3.2 %collective-permute-done.4.refs_3_ = bf16[2,256,128]{2,1,0:T(8,128)(2,1)} collective-permute-done((bf16[2,256,128]{2,1,0:T(8,128)(2,1)}, bf16[2,256,128]{2,1,0:T(8,128)(2,1)}, u32[]{:S(2)}, u32[]{:S(2)}) %collective-permute-start.4) | collective-permute-done | bytes 131104 | tf_op jit(solution)/shard_map/ppermute | solution.py:985
  49.0 2.9 %square_statistics.1 = (bf16[4,1024,128]{2,1,0:T(8,128)(2,1)S(1)}, f32[8,1024]{1,0:T(8,128)S(1)}, f32[8,1024]{1,0:T(8,128)S(1)}, f32[1024,1024]{1,0:T(8,128)S(1)}, f32[1024,1024]{1,0:T(8,128)S(1)}) custom-call(bf16[8,1024,128]{2,1,0:T(8,128)(2,1)S(1)} %all-to-all-done.arrived_ref, f32[8,128]{1,0:T(8,128)S(1)} %get-tuple-element.48.scales_ref, ...), custom_call_target="tpu_custom_call" | custom-call | flops 536870912 | bytes 13242368 | tf_op jit(solution)/shard_map/square_statistics/pallas_call | solution.py:409
  53.3 3.5 %collective-permute-done.5.received_ref = f32[8,1024]{1,0:T(8,128)S(1)} collective-permute-done((f32[8,1024]{1,0:T(8,128)S(1)}, f32[8,1024]{1,0:T(8,128)S(1)}, u32[]{:S(2)}, u32[]{:S(2)}) %collective-permute-start.5) | collective-permute-done | bytes 32800 | tf_op jit(solution)/shard_map/ppermute | solution.py:1076
  56.8 3.1 %gradients_after_totals.1 = (bf16[8,784,128]{2,1,0:T(8,128)(2,1)}, bf16[4,272,128]{2,1,0:T(8,128)(2,1)S(1)}, bf16[4,272,128]{2,1,0:T(8,128)(2,1)S(1)}) custom-call(bf16[8,1024,128]{2,1,0:T(8,128)(2,1)S(1)} %all-to-all-done.arrived_ref, f32[8,128]{1,0:T(8,128)S(1)} %get-tuple-element.48.scales_ref, bf16[4,1024,128]{2,1,0:T(8,128)(2,1)S(1)} %get-tuple-element.58.square_ref, ...), custom_call_target="tpu_custom_call" | custom-call | flops 536870912 | bytes 25108480 | tf_op jit(solution)/shard_map/gradients_after_totals/pallas_call | solution.py:409
  59.9 3.6 %all-to-all-start.1 = ((bf16[8,784,128]{2,1,0:T(8,128)(2,1)}), bf16[8,784,128]{2,1,0:T(8,128)(2,1)S(1)}, u32[]{:S(2)}, u32[]{:S(2)}) async-start(bf16[8,784,128]{2,1,0:T(8,128)(2,1)} %get-tuple-element.72), calls=%async_computation.1 | async-start | bytes 3211264 | tf_op jit(solution)/shard_map/all_to_all | solution.py:1015
  63.9 1.3 %collective-permute-done.6.taken_ref = bf16[4,272,128]{2,1,0:T(8,128)(2,1)S(1)} collective-permute-done((bf16[4,272,128]{2,1,0:T(8,128)(2,1)S(1)}, bf16[4,272,128]{2,1,0:T(8,128)(2,1)S(1)}, u32[]{:S(2)}, u32[]{:S(2)}) %collective-permute-start.6) | collective-permute-done | bytes 278560 | tf_op jit(solution)/shard_map/ppermute | solution.py:974
  65.3 1.3 %collective-permute-start.7 = (bf16[2,272,128]{2,1,0:T(8,128)(2,1)S(1)}, bf16[2,272,128]{2,1,0:T(8,128)(2,1)S(1)}, u32[]{:S(2)}, u32[]{:S(2)}) collective-permute-start(bf16[2,272,128]{2,1,0:T(8,128)(2,1)S(1)} %get-tuple-element.75), channel_id=1, source_target_pairs={{0,16},{2,18},{4,20},{6,22},{8,24},{10,26},{12,28},{14,30},{16,0},... | collective-permute-start | bytes 417800 | tf_op jit(solution)/shard_map/ppermute | solution.py:985
  66.6 2.9 %collective-permute-start.8 = (bf16[2,272,128]{2,1,0:T(8,128)(2,1)S(1)}, bf16[2,272,128]{2,1,0:T(8,128)(2,1)S(1)}, u32[]{:S(2)}, u32[]{:S(2)}) collective-permute-start(bf16[2,272,128]{2,1,0:T(8,128)(2,1)S(1)} %get-tuple-element.76), channel_id=1, source_target_pairs={{0,20},{2,22},{4,16},{6,18},{8,28},{10,30},{12,24},{14,26},{16,4},... | collective-permute-start | bytes 417800 | tf_op jit(solution)/shard_map/ppermute | solution.py:985
  69.4 2.1 %collective-permute-start.9 = (bf16[2,272,128]{2,1,0:T(8,128)(2,1)S(1)}, bf16[2,272,128]{2,1,0:T(8,128)(2,1)S(1)}, u32[]{:S(2)}, u32[]{:S(2)}) collective-permute-start(bf16[2,272,128]{2,1,0:T(8,128)(2,1)S(1)} %get-tuple-element.77), channel_id=1, source_target_pairs={{0,24},{2,26},{4,28},{6,30},{8,16},{10,18},{12,20},{14,22},{16,8},... | collective-permute-start | bytes 417800 | tf_op jit(solution)/shard_map/ppermute | solution.py:985
  71.6 1.4 %collective-permute-start.10 = (bf16[2,272,128]{2,1,0:T(8,128)(2,1)S(1)}, bf16[2,272,128]{2,1,0:T(8,128)(2,1)S(1)}, u32[]{:S(2)}, u32[]{:S(2)}) collective-permute-start(bf16[2,272,128]{2,1,0:T(8,128)(2,1)S(1)} %get-tuple-element.78), channel_id=1, source_target_pairs={{0,28},{2,30},{4,24},{6,26},{8,20},{10,22},{12,16},{14,18},{16,12}... | collective-permute-start | bytes 417800 | tf_op jit(solution)/shard_map/ppermute | solution.py:985
  73.0 12.0 %collective-permute-done.7.refs_0_ = bf16[2,272,128]{2,1,0:T(8,128)(2,1)S(1)} collective-permute-done((bf16[2,272,128]{2,1,0:T(8,128)(2,1)S(1)}, bf16[2,272,128]{2,1,0:T(8,128)(2,1)S(1)}, u32[]{:S(2)}, u32[]{:S(2)}) %collective-permute-start.7) | collective-permute-done | bytes 139296 | tf_op jit(solution)/shard_map/ppermute | solution.py:985
  85.0 3.0 %collective-permute-done.8.refs_1_ = bf16[2,272,128]{2,1,0:T(8,128)(2,1)S(1)} collective-permute-done((bf16[2,272,128]{2,1,0:T(8,128)(2,1)S(1)}, bf16[2,272,128]{2,1,0:T(8,128)(2,1)S(1)}, u32[]{:S(2)}, u32[]{:S(2)}) %collective-permute-start.8) | collective-permute-done | bytes 139296 | tf_op jit(solution)/shard_map/ppermute | solution.py:985
  87.9 6.0 %collective-permute-done.9.refs_2_ = bf16[2,272,128]{2,1,0:T(8,128)(2,1)S(1)} collective-permute-done((bf16[2,272,128]{2,1,0:T(8,128)(2,1)S(1)}, bf16[2,272,128]{2,1,0:T(8,128)(2,1)S(1)}, u32[]{:S(2)}, u32[]{:S(2)}) %collective-permute-start.9) | collective-permute-done | bytes 139296 | tf_op jit(solution)/shard_map/ppermute | solution.py:985
  93.9 3.4 %collective-permute-done.10.refs_3_ = bf16[2,272,128]{2,1,0:T(8,128)(2,1)S(1)} collective-permute-done((bf16[2,272,128]{2,1,0:T(8,128)(2,1)S(1)}, bf16[2,272,128]{2,1,0:T(8,128)(2,1)S(1)}, u32[]{:S(2)}, u32[]{:S(2)}) %collective-permute-start.10) | collective-permute-done | bytes 139296 | tf_op jit(solution)/shard_map/ppermute | solution.py:985
  97.4 1.6 %collective-permute-start.11 = (f32[16,128]{1,0:T(8,128)S(1)}, f32[16,128]{1,0:T(8,128)S(1)}, u32[]{:S(2)}, u32[]{:S(2)}) collective-permute-start(f32[16,128]{1,0:T(8,128)S(1)} %temper_sums.1), channel_id=1, source_target_pairs={{0,1},{1,0},{2,3},{3,2},{4,5},{5,4},{6,7},{7,6},{8,9},{9,8},{10,11... | collective-permute-start | bytes 24584 | tf_op jit(solution)/shard_map/ppermute | solution.py:1119
  98.9 1.5 %unpack_heads.1 = (bf16[1,128,2048]{2,1,0:T(8,128)(2,1)}, bf16[1,128,2048]{2,1,0:T(8,128)(2,1)}, bf16[1,128,2048]{2,1,0:T(8,128)(2,1)}) custom-call(bf16[8,784,128]{2,1,0:T(8,128)(2,1)S(1)} %all-to-all-done.1.within_ref, bf16[2,272,128]{2,1,0:T(8,128)(2,1)S(1)} %collective-permute-done.7.refs_0_, bf16[2,272,128]{2,1,0:T(8,128)(2,1)S(1)} %collective-permute-done.8.refs_1_, ...), custom_call_target="tpu_custom_call" | custom-call | bytes 3735552 | tf_op jit(solution)/shard_map/unpack_heads/pallas_call | solution.py:409
  (23 shorter events, 6.2 us)
Async XLA Ops:
  0.6 8.9 %copy-start.3 = (s32[16]{0:T(128)S(1)}, s32[16]{0:T(128)}, u32[]{:S(2)}) copy-start(s32[16]{0:T(128)} %span_ref.1) | copy-start | bytes 196
  0.6 8.9 %copy-start.1 = (s32[1,16,16,1]{2,3,1,0:T(1,128)S(1)}, s32[1,16,16,1]{2,3,1,0:T(1,128)}, u32[]{:S(2)}) copy-start(s32[1,16,16,1]{2,3,1,0:T(1,128)} %param.12) | copy-start | bytes 3076
  0.7 8.9 %copy-start.2 = (f32[16]{0:T(128)S(1)}, f32[16]{0:T(128)}, u32[]{:S(2)}) copy-start(f32[16]{0:T(128)} %softness_ref.1) | copy-start | bytes 196
  3.6 7.5 %copy-start = (bf16[4,256,128]{2,1,0:T(8,128)(2,1)S(1)}, bf16[4,256,128]{2,1,0:T(8,128)(2,1)}, u32[]{:S(2)}) copy-start(bf16[4,256,128]{2,1,0:T(8,128)(2,1)} %get-tuple-element.52.kept_ref) | copy-start | bytes 786436
  3.6 36.7 %all-to-all-start = ((bf16[8,1024,128]{2,1,0:T(8,128)(2,1)}), bf16[8,1024,128]{2,1,0:T(8,128)(2,1)S(1)}, u32[]{:S(2)}, u32[]{:S(2)}) async-start(bf16[8,1024,128]{2,1,0:T(8,128)(2,1)} %get-tuple-element.43), calls=%async_computation | async-start | bytes 4194304 | tf_op jit(solution)/shard_map/all_to_all | solution.py:1015
  9.0 2.1 %collective-permute-start = (bf16[4,256,128]{2,1,0:T(8,128)(2,1)}, bf16[4,256,128]{2,1,0:T(8,128)(2,1)S(1)}, u32[]{:S(2)}, u32[]{:S(2)}) collective-permute-start(bf16[4,256,128]{2,1,0:T(8,128)(2,1)} %get-tuple-element.53), channel_id=1, source_target_pairs={{0,2},{2,0},{4,6},{6,4},{8,10},{10,8},{12,14},{14,12},{16,18},{18,... | collective-permute-start | bytes 786440 | tf_op jit(solution)/shard_map/ppermute | solution.py:974
  12.0 32.0 %collective-permute-start.1 = (bf16[2,256,128]{2,1,0:T(8,128)(2,1)}, bf16[2,256,128]{2,1,0:T(8,128)(2,1)S(1)}, u32[]{:S(2)}, u32[]{:S(2)}) collective-permute-start(bf16[2,256,128]{2,1,0:T(8,128)(2,1)} %get-tuple-element.54), channel_id=1, source_target_pairs={{0,16},{2,18},{4,20},{6,22},{8,24},{10,26},{12,28},{14,30},{16,0},... | collective-permute-start | bytes 393224 | tf_op jit(solution)/shard_map/ppermute | solution.py:985
  14.5 29.4 %collective-permute-start.2 = (bf16[2,256,128]{2,1,0:T(8,128)(2,1)}, bf16[2,256,128]{2,1,0:T(8,128)(2,1)S(1)}, u32[]{:S(2)}, u32[]{:S(2)}) collective-permute-start(bf16[2,256,128]{2,1,0:T(8,128)(2,1)} %get-tuple-element.55), channel_id=1, source_target_pairs={{0,20},{2,22},{4,16},{6,18},{8,28},{10,30},{12,24},{14,26},{16,4},... | collective-permute-start | bytes 393224 | tf_op jit(solution)/shard_map/ppermute | solution.py:985
  16.0 29.8 %collective-permute-start.3 = (bf16[2,256,128]{2,1,0:T(8,128)(2,1)}, bf16[2,256,128]{2,1,0:T(8,128)(2,1)}, u32[]{:S(2)}, u32[]{:S(2)}) collective-permute-start(bf16[2,256,128]{2,1,0:T(8,128)(2,1)} %get-tuple-element.56), channel_id=1, source_target_pairs={{0,24},{2,26},{4,28},{6,30},{8,16},{10,18},{12,20},{14,22},{16,8},... | collective-permute-start | bytes 393224 | tf_op jit(solution)/shard_map/ppermute | solution.py:985
  19.5 29.5 %collective-permute-start.4 = (bf16[2,256,128]{2,1,0:T(8,128)(2,1)}, bf16[2,256,128]{2,1,0:T(8,128)(2,1)}, u32[]{:S(2)}, u32[]{:S(2)}) collective-permute-start(bf16[2,256,128]{2,1,0:T(8,128)(2,1)} %get-tuple-element.57), channel_id=1, source_target_pairs={{0,28},{2,30},{4,24},{6,26},{8,20},{10,22},{12,16},{14,18},{16,12}... | collective-permute-start | bytes 393224 | tf_op jit(solution)/shard_map/ppermute | solution.py:985
  51.9 4.9 %collective-permute-start.5 = (f32[8,1024]{1,0:T(8,128)S(1)}, f32[8,1024]{1,0:T(8,128)S(1)}, u32[]{:S(2)}, u32[]{:S(2)}) collective-permute-start(f32[8,1024]{1,0:T(8,128)S(1)} %get-tuple-element.59.message_ref), channel_id=1, source_target_pairs={{0,16},{2,18},{4,20},{6,22},{8,24},{10,26},{12,28},{14,30},{16,0},... | collective-permute-start | bytes 98312 | tf_op jit(solution)/shard_map/ppermute | solution.py:1076
  59.9 37.5 %all-to-all-start.1 = ((bf16[8,784,128]{2,1,0:T(8,128)(2,1)}), bf16[8,784,128]{2,1,0:T(8,128)(2,1)S(1)}, u32[]{:S(2)}, u32[]{:S(2)}) async-start(bf16[8,784,128]{2,1,0:T(8,128)(2,1)} %get-tuple-element.72), calls=%async_computation.1 | async-start | bytes 3211264 | tf_op jit(solution)/shard_map/all_to_all | solution.py:1015
  63.5 1.7 %collective-permute-start.6 = (bf16[4,272,128]{2,1,0:T(8,128)(2,1)S(1)}, bf16[4,272,128]{2,1,0:T(8,128)(2,1)S(1)}, u32[]{:S(2)}, u32[]{:S(2)}) collective-permute-start(bf16[4,272,128]{2,1,0:T(8,128)(2,1)S(1)} %get-tuple-element.74), channel_id=1, source_target_pairs={{0,2},{2,0},{4,6},{6,4},{8,10},{10,8},{12,14},{14,12},{16,18},{18,... | collective-permute-start | bytes 835592 | tf_op jit(solution)/shard_map/ppermute | solution.py:974
  65.3 19.7 %collective-permute-start.7 = (bf16[2,272,128]{2,1,0:T(8,128)(2,1)S(1)}, bf16[2,272,128]{2,1,0:T(8,128)(2,1)S(1)}, u32[]{:S(2)}, u32[]{:S(2)}) collective-permute-start(bf16[2,272,128]{2,1,0:T(8,128)(2,1)S(1)} %get-tuple-element.75), channel_id=1, source_target_pairs={{0,16},{2,18},{4,20},{6,22},{8,24},{10,26},{12,28},{14,30},{16,0},... | collective-permute-start | bytes 417800 | tf_op jit(solution)/shard_map/ppermute | solution.py:985
  66.6 21.4 %collective-permute-start.8 = (bf16[2,272,128]{2,1,0:T(8,128)(2,1)S(1)}, bf16[2,272,128]{2,1,0:T(8,128)(2,1)S(1)}, u32[]{:S(2)}, u32[]{:S(2)}) collective-permute-start(bf16[2,272,128]{2,1,0:T(8,128)(2,1)S(1)} %get-tuple-element.76), channel_id=1, source_target_pairs={{0,20},{2,22},{4,16},{6,18},{8,28},{10,30},{12,24},{14,26},{16,4},... | collective-permute-start | bytes 417800 | tf_op jit(solution)/shard_map/ppermute | solution.py:985
  69.4 24.5 %collective-permute-start.9 = (bf16[2,272,128]{2,1,0:T(8,128)(2,1)S(1)}, bf16[2,272,128]{2,1,0:T(8,128)(2,1)S(1)}, u32[]{:S(2)}, u32[]{:S(2)}) collective-permute-start(bf16[2,272,128]{2,1,0:T(8,128)(2,1)S(1)} %get-tuple-element.77), channel_id=1, source_target_pairs={{0,24},{2,26},{4,28},{6,30},{8,16},{10,18},{12,20},{14,22},{16,8},... | collective-permute-start | bytes 417800 | tf_op jit(solution)/shard_map/ppermute | solution.py:985
  71.6 25.8 %collective-permute-start.10 = (bf16[2,272,128]{2,1,0:T(8,128)(2,1)S(1)}, bf16[2,272,128]{2,1,0:T(8,128)(2,1)S(1)}, u32[]{:S(2)}, u32[]{:S(2)}) collective-permute-start(bf16[2,272,128]{2,1,0:T(8,128)(2,1)S(1)} %get-tuple-element.78), channel_id=1, source_target_pairs={{0,28},{2,30},{4,24},{6,26},{8,20},{10,22},{12,16},{14,18},{16,12}... | collective-permute-start | bytes 417800 | tf_op jit(solution)/shard_map/ppermute | solution.py:985
  97.4 3.7 %collective-permute-start.11 = (f32[16,128]{1,0:T(8,128)S(1)}, f32[16,128]{1,0:T(8,128)S(1)}, u32[]{:S(2)}, u32[]{:S(2)}) collective-permute-start(f32[16,128]{1,0:T(8,128)S(1)} %temper_sums.1), channel_id=1, source_target_pairs={{0,1},{1,0},{2,3},{3,2},{4,5},{5,4},{6,7},{7,6},{8,9},{9,8},{10,11... | collective-permute-start | bytes 24584 | tf_op jit(solution)/shard_map/ppermute | solution.py:1119

commit v13 on v12

--- a/solution.py
+++ b/solution.py
@@ -401,7 +401,8 @@
 
 
 def kernel_call(
-    kernel, name, operands, in_specs, out_shape, scratch, vmem_mib, flops=0, out_spaces=None
+    kernel, name, operands, in_specs, out_shape, scratch, vmem_mib, flops=0, out_spaces=None,
+    aliases=None,
 ):
     bytes_accessed = sum(
         math.prod(item.shape) * item.dtype.itemsize for item in (*operands, *out_shape)
@@ -415,6 +416,7 @@
             for space in out_spaces or [pltpu.VMEM] * len(out_shape)
         ],
         scratch_shapes=scratch,
+        input_output_aliases=aliases or {},
         cost_estimate=pl.CostEstimate(
             flops=flops, bytes_accessed=bytes_accessed, transcendentals=0
         ),
@@ -508,10 +510,7 @@
     def rows(start, stop):
         per_tile = TILE // BLK
         return jnp.concatenate(
-            [
-                ref[block, place * BLK : (place + 1) * BLK, :]
-                for block in range(start * per_tile, stop * per_tile)
-            ],
+            [ref[block, place] for block in range(start * per_tile, stop * per_tile)],
             axis=0,
         )
 
@@ -530,6 +529,9 @@
     def rows(self, which, start, stop):
         return self.sources[which](start, stop)
 
+    def scale_of(self, array):
+        return 1.0 if array == VALUE else self.scaling[:, :HD]
+
     def keys_of(self, tile):
         return range(self.tiles if self.square else tile + 1)
 
@@ -537,7 +539,7 @@
         per_tile = TILE // BLK
         scores = dot_rows(
             self.rows(KEY, tile_key, tile_key + 1), self.rows(QUERY, tile_query, tile_query + 1)
-        ) * (self.scaling[:, :1] * math.log2(math.e))
+        ) * (self.scaling * math.log2(math.e))
         before = self.tiles * per_tile if self.square else 0
         rows = []
         for sub_key in range(per_tile):
@@ -592,21 +594,23 @@
             raw = region.scores(other, tile)
             weight_ref[tile_rows(other), here] = raw
             top = jnp.maximum(top, jnp.max(raw, axis=0, keepdims=True))
-        total = jnp.zeros((1, TILE), jnp.float32)
-        mass = jnp.zeros((1, TILE), jnp.float32)
+        sums = [jnp.zeros((1, TILE), jnp.float32)] * 4
         for other in region.keys_of(tile):
             there = tile_rows(other)
-            weight = jnp.exp2(weight_ref[there, here] - top)
+            raw = weight_ref[there, here]
+            weight = jnp.exp2(raw - top)
             towards = dot_rows(
                 region.rows(VALUE, other, other + 1), region.rows(GRAD, tile, tile + 1)
             )
             weight_ref[there, here] = weight
             towards_ref[there, here] = towards
-            total += jnp.sum(weight, axis=0, keepdims=True)
-            mass += jnp.sum(weight * towards, axis=0, keepdims=True)
-        out_ref[first_row : first_row + 1, here] = top
-        out_ref[first_row + 1 : first_row + 2, here] = total
-        out_ref[first_row + 2 : first_row + 3, here] = mass
+            pulled, weighted = weight * towards, weight * raw
+            terms = (weight, pulled, pulled * raw, weighted)
+            sums = [
+                total + jnp.sum(term, axis=0, keepdims=True) for total, term in zip(sums, terms)
+            ]
+        for row, value in enumerate((top, *sums)):
+            out_ref[first_row + row : first_row + row + 1, here] = value
 
 
 def gradients(
@@ -614,7 +618,6 @@
 ):
     keys_flat[...] = region.rows(KEY, 0, region.tiles).T
     share = jnp.exp2(top - log_total)
-    temper = jnp.zeros((1, HD), jnp.float32)
     query_parts, key_parts, value_parts = [], [], []
     for tile in range(region.tiles):
         here = tile_rows(tile)
@@ -626,13 +629,7 @@
                 probability * (towards_ref[there, here] - delta[:, here])
             ).astype(jnp.bfloat16)
         upto = slice(0, len(region.keys_of(tile)) * TILE)
-        query_part = dot_plain(keys_flat[:, upto], grad_low[upto, here]).T
-        temper += jnp.sum(
-            query_part * region.rows(QUERY, tile, tile + 1).astype(jnp.float32),
-            axis=0,
-            keepdims=True,
-        )
-        query_parts.append(query_part)
+        query_parts.append(dot_plain(keys_flat[:, upto], grad_low[upto, here]).T)
     if emit is not None:
         emit(QUERY, query_parts)
     for low, which, parts in ((grad_low, QUERY, key_parts), (prob_low, GRAD, value_parts)):
@@ -644,7 +641,7 @@
             )
         if emit is not None:
             emit(KEY if which == QUERY else VALUE, parts)
-    return query_parts, key_parts, value_parts, temper
+    return query_parts, key_parts, value_parts
 
 
 def merged(first, second):
@@ -659,8 +656,15 @@
     return rows[0] + jnp.log2(rows[1]), rows[2] / rows[1]
 
 
-def three_rows(ref, first):
-    return [ref[first + row : first + row + 1, :] for row in range(3)]
+def rows_at(ref, first, count=5):
+    return [ref[first + row : first + row + 1, :] for row in range(count)]
+
+
+def temper_terms(rows, totals, scale_row):
+    log_total, delta = totals
+    terms = (rows[3] - delta * rows[4]) * jnp.exp2(rows[0] - log_total)
+    folded = sum(terms[:, start : start + HD] for start in range(0, terms.shape[1], HD))
+    return folded / (scale_row[:, :HD] * (math.sqrt(HD) * math.log2(math.e)))
 
 
 def put(within_ref, array, tile, value):
@@ -672,10 +676,8 @@
 
 
 def scaled(region, parts):
-    return [
-        [value * scale for value in part]
-        for part, scale in zip(parts, (region.scaling, region.scaling, 1.0))
-    ]
+    scale = region.scaling[:, :HD]
+    return [[value * scale for value in part] for part in parts[:2]] + [parts[2]]
 
 
 def masks_kernel(softness_ref, ids_ref, span_ref, scales_ref, bias_ref, corner_ref, *, half_count):
@@ -689,7 +691,7 @@
     for slot, (head, key_base, query_base) in enumerate(regions):
         if slot < 2:
             scales_ref[slot : slot + 1, :] = jnp.full(
-                (1, HD), softness_ref[head] * (1.0 / math.sqrt(HD)), jnp.float32
+                (1, TILE), softness_ref[head] * (1.0 / math.sqrt(HD)), jnp.float32
             )
 
         def same(key_block, query_block):
@@ -715,25 +717,22 @@
 
 
 def within_kernel(
-    arrived_ref, scales_ref, bias_ref, corner_ref, stats_ref, parts_ref, temper_ref,
-    own_weight, own_towards, other_weight, other_towards, *scratch, half_count
+    arrived_ref, scales_ref, bias_ref, corner_ref, stats_ref, parts_ref, own_weight, own_towards, other_weight, other_towards, *scratch, half_count
 ):
     _, half, _ = position(half_count)
     kept = ((own_weight, own_towards), (other_weight, other_towards))
     for slot in range(2):
         region = diagonal(slot, arrived_ref, scales_ref, bias_ref, corner_ref)
-        statistics(region, *kept[slot], stats_ref, slot * 3)
-    temper_ref[...] = jnp.zeros_like(temper_ref)
+        statistics(region, *kept[slot], stats_ref, slot * 5)
 
     @pl.when(half == 0)
     def _():
         region = diagonal(0, arrived_ref, scales_ref)
-        single = alone(three_rows(stats_ref, 0))
-        *parts, temper = gradients(region, *kept[0], stats_ref[0:1, :], *single, *scratch)
+        single = alone(rows_at(stats_ref, 0))
+        parts = gradients(region, *kept[0], stats_ref[0:1, :], *single, *scratch)
         for place, tiles in enumerate(scaled(region, parts)):
             for tile, value in enumerate(tiles):
                 parts_ref[place, tile_rows(tile), :] = value
-        temper_ref[0:1, :] = temper
 
 
 def square_kernel(arrived_ref, scales_ref, bias_ref, corner_ref, stats_ref, *refs, half_count):
@@ -749,41 +748,47 @@
             square_ref[second, rows, :] = across_ref[core, BLK:, :]
     for kept in (jnp.where(half == 0, KEY, QUERY), jnp.where(half == 0, VALUE, GRAD)):
         for block in range(half_count):
-            square_ref[kept, block * BLK : (block + 1) * BLK, :] = arrived_ref[
-                block, rows_of(kept), :
-            ]
+            square_ref[kept, block * BLK : (block + 1) * BLK, :] = arrived_ref[block, kept]
     region = square(square_ref, scales_ref, bias_ref, corner_ref)
     statistics(region, weight, towards, square_stats, 0)
-    for row in range(3):
-        message_ref[row : row + 1, :] = jnp.where(
-            half == 0, square_stats[row : row + 1, :], stats_ref[3 + row : 4 + row, :]
-        )
+    own, other, crossing = rows_at(stats_ref, 0), rows_at(stats_ref, 5), rows_at(square_stats, 0)
+    for row in range(5):
+        message_ref[row : row + 1, :] = jnp.where(half == 0, crossing[row], other[row])
+    own_scale, other_scale = scales_ref[0:1, :], scales_ref[1:2, :]
+    both = merged(own, crossing)
+    whole = temper_terms(own, both, own_scale) + temper_terms(crossing, both, own_scale)
+    single = temper_terms(own, alone(own), own_scale)
+    message_ref[5:6, :HD] = jnp.where(half == 0, single, whole)
+    message_ref[6:7, :HD] = temper_terms(other, alone(other), other_scale)
 
 
 def first_kernel(
-    arrived_ref, scales_ref, square_ref, stats_ref, square_stats, temper_in,
+    arrived_ref, scales_ref, square_ref, stats_ref, square_stats,
     own_weight, own_towards, other_weight, other_towards, square_weight, square_towards,
-    within_ref, across_ref, temper_ref, *scratch, half_count
+    across_ref, within_ref, ready, ready_sem, *scratch, half_count
 ):
     _, half, _ = position(half_count)
-    temper_ref[...] = temper_in[...]
+    leaving = sends(ready, within_ref, ready_sem, (1 - half) * 3)
 
     @pl.when(half == 0)
     def _():
         region = diagonal(1, arrived_ref, scales_ref)
-        totals = alone(three_rows(stats_ref, 3))
-        *parts, temper_ref[1:2, :] = gradients(
-            region, other_weight, other_towards, stats_ref[3:4, :], *totals, *scratch
-        )
-        for array, tiles in enumerate(scaled(region, parts)):
-            for tile, value in enumerate(tiles):
-                put(within_ref, array, tile, value)
+
+        def send(array, parts):
+            for tile, part in enumerate(parts):
+                put(ready, array, tile, part * region.scale_of(array))
+            leaving[array].start()
+
+        totals = alone(rows_at(stats_ref, 5))
+        gradients(
+            region, other_weight, other_towards, stats_ref[5:6, :], *totals, *scratch, emit=send
+        )
 
     @pl.when(half == 1)
     def _():
-        totals = merged(three_rows(stats_ref, 0), three_rows(square_stats, 0))
+        totals = merged(rows_at(stats_ref, 0), rows_at(square_stats, 0))
         region = square(square_ref, scales_ref)
-        *parts, square_temper = gradients(
+        parts = gradients(
             region, square_weight, square_towards, square_stats[0:1, :], *totals, *scratch
         )
         across_query, *foreign = scaled(region, parts)
@@ -791,24 +796,38 @@
             for tile, value in enumerate(tiles):
                 across_ref[array, tile_rows(tile), :] = value.astype(jnp.bfloat16)
         region = diagonal(0, arrived_ref, scales_ref)
-        *parts, temper = gradients(
-            region, own_weight, own_towards, stats_ref[0:1, :], *totals, *scratch
-        )
-        query_parts, key_parts, value_parts = scaled(region, parts)
-        for tile in range(region.tiles):
-            put(within_ref, 0, tile, query_parts[tile] + across_query[tile])
-            put(within_ref, 1, tile, key_parts[tile])
-            put(within_ref, 2, tile, value_parts[tile])
-        temper_ref[0:1, :] = temper + square_temper
+
+        def send(array, parts):
+            for tile, part in enumerate(parts):
+                value = part * region.scale_of(array)
+                put(ready, array, tile, value + across_query[tile] if array == QUERY else value)
+            leaving[array].start()
+
+        gradients(
+            region, own_weight, own_towards, stats_ref[0:1, :], *totals, *scratch, emit=send
+        )
+
+    for copy in leaving:
+        copy.wait()
+
+
+def sends(ready, within_ref, sems, first):
+    copies = []
+    for array in range(3):
+        rows = slice(array * BLK, (array + 1) * BLK)
+        copies.append(
+            pltpu.make_async_copy(
+                ready.at[:, rows, :], within_ref.at[:, rows_of(first + array), :], sems.at[array]
+            )
+        )
+    return copies
 
 
 def temper_rows(own, other):
     row = lax.broadcasted_iota(jnp.int32, (EXTRA, HD), 0)
     rows = jnp.zeros((EXTRA, HD), jnp.float32)
     for place, terms in enumerate((own, other)):
-        rest = jnp.broadcast_to(jnp.sum(terms, axis=1, keepdims=True), (EXTRA, HD)) * (
-            1.0 / math.sqrt(HD)
-        )
+        rest = jnp.broadcast_to(jnp.sum(terms, axis=1, keepdims=True), (EXTRA, HD))
         for piece in range(3):
             high = rest.astype(jnp.bfloat16).astype(jnp.float32)
             rows = jnp.where(row == place * 3 + piece, high, rows)
@@ -818,124 +837,95 @@
 
 def finish_kernel(
     arrived_ref, scales_ref, square_ref, message_ref, received_ref, stats_ref, square_stats,
-    parts_ref, temper_ref, square_weight, square_towards, other_weight, other_towards,
-    across_ref, begun_ref, within_ref, *refs, half_count
+    parts_ref, square_weight, square_towards, other_weight, other_towards, across_ref, begun_ref,
+    within_ref, *refs, half_count
 ):
+    del begun_ref
     chunk_refs = refs[:2]
-    across, temper, ready, tail, begun_sem, ready_sem, tail_sem, chunk_sem, *scratch = refs[2:]
+    across, ready, tail, ready_sem, tail_sem, *scratch = refs[2:]
     _, half, place = position(half_count)
-    temper[...] = temper_ref[...]
-    begun_at = pl.ds(pl.multiple_of((1 - half) * 3 * BLK, BLK), 3 * BLK)
-    leaving = [pltpu.make_async_copy(begun_ref, within_ref.at[:, begun_at, :], begun_sem)]
-    leaving[0].start()
-    for array in range(3):
-        rows = slice(array * BLK, (array + 1) * BLK)
-        to = pl.ds(pl.multiple_of((half * 3 + array) * BLK, BLK), BLK)
-        leaving.append(
-            pltpu.make_async_copy(
-                ready.at[:, rows, :], within_ref.at[:, to, :], ready_sem.at[array]
-            )
-        )
-    totals = merged(three_rows(message_ref, 0), three_rows(received_ref, 0))
-
-    def chunks():
-        for core, chunk_ref in enumerate(chunk_refs):
-            for step in range(half_count // 2):
-                yield core, step, chunk_ref, rows_of(place ^ core ^ (2 * step))
-
-    @pl.when(half == 0)
-    def _():
-        region = square(square_ref, scales_ref)
-
-        def send(array, parts):
-            for tile, part in enumerate(parts):
-                here = tile_rows(tile)
-                if array == QUERY:
-                    across[here, :] = (part * region.scaling).astype(jnp.bfloat16)
-                    put(ready, array, tile, parts_ref[array, here, :])
-                else:
-                    scale = region.scaling if array == KEY else 1.0
-                    put(ready, array, tile, parts_ref[array, here, :] + part * scale)
-            leaving[1 + array].start()
-
-        *_, square_temper = gradients(
-            region, square_weight, square_towards, square_stats[0:1, :], *totals, *scratch, emit=send
-        )
-        for _, step, chunk_ref, rows in chunks():
-            chunk_ref[step, :BLK, :] = across[rows, :]
-            chunk_ref[step, BLK : 2 * BLK, :] = jnp.zeros((BLK, HD), jnp.bfloat16)
-        temper[0:1, :] = temper_ref[0:1, :] + square_temper
-
-    @pl.when(half == 1)
-    def _():
-        copies = [
-            pltpu.make_async_copy(
-                across_ref.at[array, rows, :],
-                chunk_ref.at[step, array * BLK : (array + 1) * BLK, :],
-                chunk_sem.at[core, step, array],
-            )
-            for core, step, chunk_ref, rows in chunks()
-            for array in range(2)
-        ]
-        for copy in copies:
-            copy.start()
-        region = diagonal(1, arrived_ref, scales_ref)
-
-        def send(array, parts):
-            scale = 1.0 if array == VALUE else region.scaling
-            for tile, part in enumerate(parts):
-                put(ready, array, tile, part * scale)
-            leaving[1 + array].start()
-
-        *_, temper[1:2, :] = gradients(
-            region, other_weight, other_towards, stats_ref[3:4, :], *totals, *scratch, emit=send
-        )
-        for copy in copies:
-            copy.wait()
-
-    pieces = temper_rows(temper[0:1, :], temper[1:2, :])
+    leaving = sends(ready, within_ref, ready_sem, half * 3)
+    sent, came = rows_at(message_ref, 0), rows_at(received_ref, 0)
+    totals = merged(sent, came)
+    scale = jnp.where(half == 0, scales_ref[0:1, :], scales_ref[1:2, :])
+    shared = temper_terms(sent, totals, scale) + temper_terms(came, totals, scale)
+    mine, theirs = message_ref[5:6, :HD], received_ref[5:6, :HD]
+    own = mine + jnp.where(half == 0, shared, received_ref[6:7, :HD])
+    other = theirs + jnp.where(half == 0, message_ref[6:7, :HD], shared)
+    pieces = temper_rows(own, other)
     for block in range(half_count):
         tail[block] = pieces
     leaving.append(
         pltpu.make_async_copy(tail, within_ref.at[:, 6 * BLK : 6 * BLK + EXTRA, :], tail_sem)
     )
     leaving[-1].start()
-    for _, step, chunk_ref, _ in chunks():
-        chunk_ref[step, 2 * BLK :, :] = pieces
+
+    def chunks():
+        for core, chunk_ref in enumerate(chunk_refs):
+            for step in range(half_count // 2):
+                yield step, chunk_ref, rows_of(place ^ core ^ (2 * step))
+
+    @pl.when(half == 0)
+    def _():
+        region = square(square_ref, scales_ref)
+
+        def send(array, parts):
+            for tile, part in enumerate(parts):
+                here = tile_rows(tile)
+                value = part * region.scale_of(array)
+                if array == QUERY:
+                    across[here, :] = value.astype(jnp.bfloat16)
+                    put(ready, array, tile, parts_ref[array, here, :])
+                else:
+                    put(ready, array, tile, parts_ref[array, here, :] + value)
+            leaving[array].start()
+
+        gradients(
+            region, square_weight, square_towards, square_stats[0:1, :], *totals, *scratch, emit=send
+        )
+        for step, chunk_ref, rows in chunks():
+            chunk_ref[step, :BLK, :] = across[rows, :]
+            chunk_ref[step, BLK:, :] = jnp.zeros((BLK, HD), jnp.bfloat16)
+
+    @pl.when(half == 1)
+    def _():
+        region = diagonal(1, arrived_ref, scales_ref)
+
+        def send(array, parts):
+            for tile, part in enumerate(parts):
+                put(ready, array, tile, part * region.scale_of(array))
+            leaving[array].start()
+
+        gradients(
+            region, other_weight, other_towards, stats_ref[5:6, :], *totals, *scratch, emit=send
+        )
+        for step, chunk_ref, rows in chunks():
+            chunk_ref[step, :BLK, :] = across_ref[0, rows, :]
+            chunk_ref[step, BLK:, :] = across_ref[1, rows, :]
+
     for copy in leaving:
         copy.wait()
 
 
-def temper_kernel(within_ref, *refs, half_count):
-    across_refs, temper_ref = refs[: half_count // 2], refs[half_count // 2]
-    _, half, place = position(half_count)
-
-    def sums(rows):
-        return [
-            jnp.sum(rows[3 * slot : 3 * slot + 3, :].astype(jnp.float32), axis=0, keepdims=True)
-            for slot in range(2)
-        ]
-
-    for step, across_ref in enumerate(across_refs):
-        for core in range(2):
-            peer = place ^ core ^ (2 * step)
-            near, far = sums(within_ref[peer]), sums(across_ref[core])
-            temper_ref[pl.ds(half * half_count + peer, 1), :] = near[0] + far[1]
-            temper_ref[pl.ds((1 - half) * half_count + peer, 1), :] = near[1] + far[0]
-
-
-def temper_sums(within, across, half_count):
-    last = (6 * BLK // EXTRA, 2 * BLK // EXTRA)
+def temper_kernel(within_ref, temper_ref, *, half_count):
+    _, half, _ = position(half_count)
+    for peer in range(half_count):
+        for slot, base in enumerate((half * half_count, (1 - half) * half_count)):
+            rows = within_ref[peer, 3 * slot : 3 * slot + 3, :].astype(jnp.float32)
+            temper_ref[pl.ds(base + peer, 1), :] = jnp.sum(rows, axis=0, keepdims=True)
+
+
+def temper_sums(within, half_count):
+    last = 6 * BLK // EXTRA
     return pl.pallas_call(
         functools.partial(temper_kernel, half_count=half_count),
         grid=(1,),
         out_shape=jax.ShapeDtypeStruct((2 * half_count, HD), jnp.float32),
-        in_specs=[pl.BlockSpec((half_count, EXTRA, HD), lambda step: (0, last[0], 0))]
-        + [pl.BlockSpec((2, EXTRA, HD), lambda step: (0, last[1], 0))] * (half_count // 2),
+        in_specs=[pl.BlockSpec((half_count, EXTRA, HD), lambda step: (0, last, 0))],
         out_specs=pl.BlockSpec((2 * half_count, HD), lambda step: (0, 0)),
         compiler_params=pltpu.CompilerParams(vmem_limit_bytes=4 * MIB),
         name="temper_sums",
-    )(within, *across)
+    )(within)
 
 
 def unpack_kernel(within_ref, *refs, half_count):
@@ -1017,32 +1007,36 @@
         )
 
     def call(
-        kernel, name, operands, out_shape, scratch, flops, vmem_mib, scalars=(), out_spaces=None
+        kernel, name, operands, out_shape, scratch, flops, vmem_mib, scalars=(), out_spaces=None,
+        last_in_place=False,
     ):
+        in_specs = [smem] * len(scalars) + [vmem] * len(operands)
+        if last_in_place:
+            in_specs[-1] = pl.BlockSpec(memory_space=pl.ANY)
         return kernel_call(
             functools.partial(kernel, half_count=half_count),
             name,
             (*scalars, *operands),
-            [smem] * len(scalars) + [vmem] * len(operands),
+            in_specs,
             out_shape,
             scratch,
             vmem_mib,
             flops,
             out_spaces,
+            {len(operands) - 1: 0} if last_in_place else {},
         )
 
     sent, *foreign = packed(
         (probe_vectors, lookup_vectors, content_vectors, result_cotangent), half_count
     )
-    arrived = exchange_within(sent)
+    arrived = exchange_within(sent).reshape(half_count, 8, BLK, HD)
     kept_parts = jax.ShapeDtypeStruct((3, tokens, HD), jnp.float32)
-    tempers = jax.ShapeDtypeStruct((8, HD), jnp.float32)
     masks = call(
         masks_kernel,
         "scales_and_masks",
         (),
         [
-            jax.ShapeDtypeStruct((8, HD), jnp.float32),
+            jax.ShapeDtypeStruct((8, TILE), jnp.float32),
             jax.ShapeDtypeStruct((3, half_count, tokens), jnp.float32),
             jax.ShapeDtypeStruct((2 * half_count - 1, BLK, BLK), jnp.float32),
         ],
@@ -1054,11 +1048,11 @@
     foreign[0], *masks = lax.optimization_barrier((foreign[0], *masks))
     foreign = crossed(*foreign, half_count)
     scales = masks[0]
-    stats, parts, temper, own_weight, own_towards, other_weight, other_towards = call(
+    stats, parts, own_weight, own_towards, other_weight, other_towards = call(
         within_kernel,
         "diagonal_statistics",
         (arrived, *masks),
-        [rows_of_stats, kept_parts, tempers] + [pairs] * 4,
+        [jax.ShapeDtypeStruct((16, tokens), jnp.float32), kept_parts] + [pairs] * 4,
         lows,
         2 * pair_flops,
         20,
@@ -1074,45 +1068,44 @@
     )
     swap = [(source, source ^ half_count) for source in range(seq_count)]
     received = lax.ppermute(message, "seq", swap)
-    begun, across, temper = call(
+    result = pltpu.HBM((half_count, 6 * BLK + EXTRA, HD), jnp.bfloat16)
+    ready = pltpu.VMEM((half_count, 3 * BLK, HD), jnp.bfloat16)
+    across, begun = call(
         first_kernel,
         "gradients_before_totals",
         (
-            arrived, scales, squared, stats, square_stats, temper, own_weight, own_towards,
+            arrived, scales, squared, stats, square_stats, own_weight, own_towards,
             other_weight, other_towards, square_weight, square_towards,
         ),
-        [
-            jax.ShapeDtypeStruct((half_count, 3 * BLK, HD), jnp.bfloat16),
-            jax.ShapeDtypeStruct((2, tokens, HD), jnp.bfloat16),
-            tempers,
-        ],
-        lows,
+        [jax.ShapeDtypeStruct((2, tokens, HD), jnp.bfloat16), result],
+        [ready, pltpu.SemaphoreType.DMA((3,)), *lows],
         4 * pair_flops,
         14,
+        out_spaces=(pltpu.VMEM, pl.ANY),
+    )
+    operands = (
+        arrived, scales, squared, message, received, stats, square_stats, parts,
+        square_weight, square_towards, other_weight, other_towards, across, begun,
     )
     within, *foreign = call(
         finish_kernel,
         "gradients_after_totals",
-        (
-            arrived, scales, squared, message, received, stats, square_stats, parts, temper,
-            square_weight, square_towards, other_weight, other_towards, across, begun,
-        ),
-        [pltpu.HBM((half_count, 6 * BLK + EXTRA, HD), jnp.bfloat16)]
-        + [jax.ShapeDtypeStruct((half_count // 2, 2 * BLK + EXTRA, HD), jnp.bfloat16)] * 2,
+        operands,
+        [result]
+        + [jax.ShapeDtypeStruct((half_count // 2, 2 * BLK, HD), jnp.bfloat16)] * 2,
         [
-            pltpu.VMEM((tokens, HD), jnp.bfloat16), pltpu.VMEM((8, HD), jnp.float32),
-            pltpu.VMEM((half_count, 3 * BLK, HD), jnp.bfloat16),
+            pltpu.VMEM((tokens, HD), jnp.bfloat16), ready,
             pltpu.VMEM((half_count, EXTRA, HD), jnp.bfloat16),
-            pltpu.SemaphoreType.DMA, pltpu.SemaphoreType.DMA((3,)), pltpu.SemaphoreType.DMA,
-            pltpu.SemaphoreType.DMA((2, half_count // 2, 2)), *lows,
+            pltpu.SemaphoreType.DMA((3,)), pltpu.SemaphoreType.DMA, *lows,
         ],
         2 * pair_flops,
         20,
         out_spaces=(pl.ANY, pltpu.VMEM, pltpu.VMEM),
+        last_in_place=True,
     )
     across = crossed(*foreign, half_count)
     within = exchange_within(within)
-    tempers = temper_sums(within, across, half_count)
+    tempers = temper_sums(within, half_count)
     temper_total = tempers
     for step in range(1, dp_count):
         swap = [(source, (source + step) % dp_count) for source in range(dp_count)]

time: 102 us -> 99.4 us (0.975)
  waiting for transfers between devices: 56.1 us -> 51.8 us
  Pallas kernels: 17.3 us -> 19 us
    ppermute x8, waiting for transfers between devices: 29.4 us -> 9.91 us  [crossed(): lax.ppermute(message, 'seq', [(source, source ^ half_count + 2 * step) fo...]
    all_to_all x2, waiting for transfers between devices: 20.7 us -> 37.3 us  [exchange_within(): lax.all_to_all(array_in, 'seq', split_axis=0, concat_axis=0, axis_index_g...]
    pallas_call x9, Pallas kernels: 17.3 us -> 19 us  [kernel_call(): pl.pallas_call(kernel, out_shape=out_shape, in_specs=in_specs, out_specs=...]
  transfers between devices with their start and end apart: 14 -> 14, of which waited for: 11 -> 9; matrix products, arithmetic and copies ran while one was open for 0% -> 0% of each run, Pallas kernels for 8% -> 10%
where the time goes in v13:
time: 99.4 us; the launch traced here: 99.1 us
  waiting for transfers between devices  51.8 us (52%)
  starting transfers between devices  26.9 us (27%)
  Pallas kernels  19 us (19%)
    all_to_all x2, waiting for transfers between devices, exchange_within(): lax.all_to_all(array_in, 'seq', split_axis=0, concat_axis=0, axis_index_g...  37.3 us
    pallas_call x9, Pallas kernels, kernel_call(): pl.pallas_call(kernel, out_shape=out_shape, in_specs=in_specs, out_specs=...  19 us
    ppermute x8, starting transfers between devices, crossed(): lax.ppermute(message, 'seq', [(source, source ^ half_count + 2 * step) fo...  15.4 us
    ppermute x8, waiting for transfers between devices, crossed(): lax.ppermute(message, 'seq', [(source, source ^ half_count + 2 * step) fo...  9.91 us
    all_to_all x2, starting transfers between devices, exchange_within(): lax.all_to_all(array_in, 'seq', split_axis=0, concat_axis=0, axis_index_g...  8.99 us
    ppermute x1, waiting for transfers between devices, head_shards(): received = lax.ppermute(message, 'seq', swap)  2.72 us
  transfers between devices with their start and end apart: 14, of which 9 were waited for; matrix products, arithmetic and copies ran while one was open for 0% of the time, Pallas kernels for 10%

profile of v13, /device:TPU:0, one launch (start us, length us, event | category | flops | bytes accessed | tf_op | source)
XLA Modules:
  0.0 99.1 jit_solution(16580398929330294923)
XLA Ops:
  0.7 2.9 %pack_heads.1 = (bf16[8,1024,128]{2,1,0:T(8,128)(2,1)}, bf16[4,256,128]{2,1,0:T(8,128)(2,1)}, bf16[4,256,128]{2,1,0:T(8,128)(2,1)}) custom-call(bf16[1,128,2048]{2,1,0:T(8,128)(2,1)} %refs_0_.1, bf16[1,128,2048]{2,1,0:T(8,128)(2,1)} %refs_1_.1, bf16[1,128,2048]{2,1,0:T(8,128)(2,1)} %refs_2_.1, bf16[1,128,2048]{2,1,0:T(8,128)(2,1)} %refs_3_.1), custom_call_target="tpu_custom_call" | custom-call | bytes 4718592 | tf_op jit(solution)/shard_map/pack_heads/pallas_call | solution.py:410
  3.6 5.4 %all-to-all-start = ((bf16[8,1024,128]{2,1,0:T(8,128)(2,1)}), bf16[8,1024,128]{2,1,0:T(8,128)(2,1)S(1)}, u32[]{:S(2)}, u32[]{:S(2)}) async-start(bf16[8,1024,128]{2,1,0:T(8,128)(2,1)} %get-tuple-element.41), calls=%async_computation | async-start | bytes 4194304 | tf_op jit(solution)/shard_map/all_to_all | solution.py:1005
  12.0 2.6 %collective-permute-start.1 = (bf16[2,256,128]{2,1,0:T(8,128)(2,1)}, bf16[2,256,128]{2,1,0:T(8,128)(2,1)S(1)}, u32[]{:S(2)}, u32[]{:S(2)}) collective-permute-start(bf16[2,256,128]{2,1,0:T(8,128)(2,1)} %get-tuple-element.52), channel_id=1, source_target_pairs={{0,16},{2,18},{4,20},{6,22},{8,24},{10,26},{12,28},{14,30},{16,0},... | collective-permute-start | bytes 393224 | tf_op jit(solution)/shard_map/ppermute | solution.py:975
  14.5 1.5 %collective-permute-start.2 = (bf16[2,256,128]{2,1,0:T(8,128)(2,1)}, bf16[2,256,128]{2,1,0:T(8,128)(2,1)S(1)}, u32[]{:S(2)}, u32[]{:S(2)}) collective-permute-start(bf16[2,256,128]{2,1,0:T(8,128)(2,1)} %get-tuple-element.53), channel_id=1, source_target_pairs={{0,20},{2,22},{4,16},{6,18},{8,28},{10,30},{12,24},{14,26},{16,4},... | collective-permute-start | bytes 393224 | tf_op jit(solution)/shard_map/ppermute | solution.py:975
  16.0 3.5 %collective-permute-start.3 = (bf16[2,256,128]{2,1,0:T(8,128)(2,1)}, bf16[2,256,128]{2,1,0:T(8,128)(2,1)}, u32[]{:S(2)}, u32[]{:S(2)}) collective-permute-start(bf16[2,256,128]{2,1,0:T(8,128)(2,1)} %get-tuple-element.54), channel_id=1, source_target_pairs={{0,24},{2,26},{4,28},{6,30},{8,16},{10,18},{12,20},{14,22},{16,8},... | collective-permute-start | bytes 393224 | tf_op jit(solution)/shard_map/ppermute | solution.py:975
  19.6 20.7 %all-to-all-done = bf16[8,1024,128]{2,1,0:T(8,128)(2,1)S(1)} async-done(((bf16[8,1024,128]{2,1,0:T(8,128)(2,1)}), bf16[8,1024,128]{2,1,0:T(8,128)(2,1)S(1)}, u32[]{:S(2)}, u32[]{:S(2)}) %all-to-all-start) | async-done | bytes 2097184 | tf_op jit(solution)/shard_map/all_to_all | solution.py:1005
  40.3 4.2 %diagonal_statistics.1 = (f32[16,1024]{1,0:T(8,128)S(1)}, f32[3,1024,128]{2,1,0:T(8,128)S(1)}, f32[1024,1024]{1,0:T(8,128)S(1)}, f32[1024,1024]{1,0:T(8,128)S(1)...) custom-call(bf16[8,8,128,128]{3,2,1,0:T(8,128)(2,1)S(1)} %bitcast.2, f32[8,256]{1,0:T(8,128)S(1)} %get-tuple-element.46.scales_ref, ...), custom_call_target="tpu_custom_call" | custom-call | flops 536870912 | bytes 21602304 | tf_op jit(solution)/shard_map/diagonal_statistics/pallas_call | solution.py:410
  44.6 1.1 %collective-permute-done.3.refs_2_ = bf16[2,256,128]{2,1,0:T(8,128)(2,1)} collective-permute-done((bf16[2,256,128]{2,1,0:T(8,128)(2,1)}, bf16[2,256,128]{2,1,0:T(8,128)(2,1)}, u32[]{:S(2)}, u32[]{:S(2)}) %collective-permute-start.3) | collective-permute-done | bytes 131104 | tf_op jit(solution)/shard_map/ppermute | solution.py:975
  45.8 3.2 %collective-permute-done.4.refs_3_ = bf16[2,256,128]{2,1,0:T(8,128)(2,1)} collective-permute-done((bf16[2,256,128]{2,1,0:T(8,128)(2,1)}, bf16[2,256,128]{2,1,0:T(8,128)(2,1)}, u32[]{:S(2)}, u32[]{:S(2)}) %collective-permute-start.4) | collective-permute-done | bytes 131104 | tf_op jit(solution)/shard_map/ppermute | solution.py:975
  49.0 3.4 %square_statistics.1 = (bf16[4,1024,128]{2,1,0:T(8,128)(2,1)S(1)}, f32[8,1024]{1,0:T(8,128)S(1)}, f32[8,1024]{1,0:T(8,128)S(1)}, f32[1024,1024]{1,0:T(8,128)S(1)}, f32[1024,1024]{1,0:T(8,128)S(1)}) custom-call(bf16[8,8,128,128]{3,2,1,0:T(8,128)(2,1)S(1)} %bitcast.3, f32[8,256]{1,0:T(8,128)S(1)} %get-tuple-element.46.scales_ref, ...), custom_call_target="tpu_custom_call" | custom-call | flops 536870912 | bytes 13279232 | tf_op jit(solution)/shard_map/square_statistics/pallas_call | solution.py:410
  52.5 2.1 %gradients_before_totals.1 = (bf16[2,1024,128]{2,1,0:T(8,128)(2,1)S(1)}, bf16[8,784,128]{2,1,0:T(8,128)(2,1)}) custom-call(bf16[8,8,128,128]{3,2,1,0:T(8,128)(2,1)S(1)} %bitcast.4, f32[8,256]{1,0:T(8,128)S(1)} %get-tuple-element.46.scales_ref, bf16[4,1024,128]{2,1,0:T(8,128)(2,1)S(1)} %get-tuple-element.56.square_ref, ...), custom_call_target="tpu_custom_call" | custom-call | flops 1073741824 | bytes 30547968 | tf_op jit(solution)/shard_map/gradients_before_totals/pallas_call | solution.py:410
  54.6 2.7 %collective-permute-done.5.received_ref = f32[8,1024]{1,0:T(8,128)S(1)} collective-permute-done((f32[8,1024]{1,0:T(8,128)S(1)}, f32[8,1024]{1,0:T(8,128)S(1)}, u32[]{:S(2)}, u32[]{:S(2)}) %collective-permute-start.5) | collective-permute-done | bytes 32800 | tf_op jit(solution)/shard_map/ppermute | solution.py:1070
  57.3 2.9 %gradients_after_totals.1 = (bf16[8,784,128]{2,1,0:T(8,128)(2,1)}, bf16[4,256,128]{2,1,0:T(8,128)(2,1)S(1)}, bf16[4,256,128]{2,1,0:T(8,128)(2,1)S(1)}) custom-call(bf16[8,8,128,128]{3,2,1,0:T(8,128)(2,1)S(1)} %bitcast.5, f32[8,256]{1,0:T(8,128)S(1)} %get-tuple-element.46.scales_ref, ...), custom_call_target="tpu_custom_call", output_to_operand_aliasing={{0}: (13, {})} | custom-call | flops 536870912 | bytes 25927680 | tf_op jit(solution)/shard_map/gradients_after_totals/pallas_call | solution.py:410
  60.2 3.6 %all-to-all-start.1 = ((bf16[8,784,128]{2,1,0:T(8,128)(2,1)}), bf16[8,784,128]{2,1,0:T(8,128)(2,1)S(1)}, u32[]{:S(2)}, u32[]{:S(2)}) async-start(bf16[8,784,128]{2,1,0:T(8,128)(2,1)} %get-tuple-element.68), calls=%async_computation.1 | async-start | bytes 3211264 | tf_op jit(solution)/shard_map/all_to_all | solution.py:1005
  64.2 1.3 %collective-permute-done.6.taken_ref = bf16[4,256,128]{2,1,0:T(8,128)(2,1)S(1)} collective-permute-done((bf16[4,256,128]{2,1,0:T(8,128)(2,1)S(1)}, bf16[4,256,128]{2,1,0:T(8,128)(2,1)S(1)}, u32[]{:S(2)}, u32[]{:S(2)}) %collective-permute-start.6) | collective-permute-done | bytes 262176 | tf_op jit(solution)/shard_map/ppermute | solution.py:964
  65.5 1.3 %collective-permute-start.7 = (bf16[2,256,128]{2,1,0:T(8,128)(2,1)S(1)}, bf16[2,256,128]{2,1,0:T(8,128)(2,1)S(1)}, u32[]{:S(2)}, u32[]{:S(2)}) collective-permute-start(bf16[2,256,128]{2,1,0:T(8,128)(2,1)S(1)} %get-tuple-element.71), channel_id=1, source_target_pairs={{0,16},{2,18},{4,20},{6,22},{8,24},{10,26},{12,28},{14,30},{16,0},... | collective-permute-start | bytes 393224 | tf_op jit(solution)/shard_map/ppermute | solution.py:975
  66.8 2.9 %collective-permute-start.8 = (bf16[2,256,128]{2,1,0:T(8,128)(2,1)S(1)}, bf16[2,256,128]{2,1,0:T(8,128)(2,1)S(1)}, u32[]{:S(2)}, u32[]{:S(2)}) collective-permute-start(bf16[2,256,128]{2,1,0:T(8,128)(2,1)S(1)} %get-tuple-element.72), channel_id=1, source_target_pairs={{0,20},{2,22},{4,16},{6,18},{8,28},{10,30},{12,24},{14,26},{16,4},... | collective-permute-start | bytes 393224 | tf_op jit(solution)/shard_map/ppermute | solution.py:975
  69.7 2.1 %collective-permute-start.9 = (bf16[2,256,128]{2,1,0:T(8,128)(2,1)S(1)}, bf16[2,256,128]{2,1,0:T(8,128)(2,1)S(1)}, u32[]{:S(2)}, u32[]{:S(2)}) collective-permute-start(bf16[2,256,128]{2,1,0:T(8,128)(2,1)S(1)} %get-tuple-element.73), channel_id=1, source_target_pairs={{0,24},{2,26},{4,28},{6,30},{8,16},{10,18},{12,20},{14,22},{16,8},... | collective-permute-start | bytes 393224 | tf_op jit(solution)/shard_map/ppermute | solution.py:975
  71.8 1.4 %collective-permute-start.10 = (bf16[2,256,128]{2,1,0:T(8,128)(2,1)S(1)}, bf16[2,256,128]{2,1,0:T(8,128)(2,1)S(1)}, u32[]{:S(2)}, u32[]{:S(2)}) collective-permute-start(bf16[2,256,128]{2,1,0:T(8,128)(2,1)S(1)} %get-tuple-element.74), channel_id=1, source_target_pairs={{0,28},{2,30},{4,24},{6,26},{8,20},{10,22},{12,16},{14,18},{16,12}... | collective-permute-start | bytes 393224 | tf_op jit(solution)/shard_map/ppermute | solution.py:975
  73.2 16.5 %all-to-all-done.1.within_ref = bf16[8,784,128]{2,1,0:T(8,128)(2,1)S(1)} async-done(((bf16[8,784,128]{2,1,0:T(8,128)(2,1)}), bf16[8,784,128]{2,1,0:T(8,128)(2,1)S(1)}, u32[]{:S(2)}, u32[]{:S(2)}) %all-to-all-start.1) | async-done | bytes 1605664 | tf_op jit(solution)/shard_map/all_to_all | solution.py:1005
  89.8 1.6 %collective-permute-start.11 = (f32[16,128]{1,0:T(8,128)S(1)}, f32[16,128]{1,0:T(8,128)S(1)}, u32[]{:S(2)}, u32[]{:S(2)}) collective-permute-start(f32[16,128]{1,0:T(8,128)S(1)} %temper_sums.1), channel_id=1, source_target_pairs={{0,1},{1,0},{2,3},{3,2},{4,5},{5,4},{6,7},{7,6},{8,9},{9,8},{10,11... | collective-permute-start | bytes 24584 | tf_op jit(solution)/shard_map/ppermute | solution.py:1112
  91.4 2.3 %collective-permute-done.9.refs_2_ = bf16[2,256,128]{2,1,0:T(8,128)(2,1)S(1)} collective-permute-done((bf16[2,256,128]{2,1,0:T(8,128)(2,1)S(1)}, bf16[2,256,128]{2,1,0:T(8,128)(2,1)S(1)}, u32[]{:S(2)}, u32[]{:S(2)}) %collective-permute-start.9) | collective-permute-done | bytes 131104 | tf_op jit(solution)/shard_map/ppermute | solution.py:975
  93.7 3.2 %collective-permute-done.10.refs_3_ = bf16[2,256,128]{2,1,0:T(8,128)(2,1)S(1)} collective-permute-done((bf16[2,256,128]{2,1,0:T(8,128)(2,1)S(1)}, bf16[2,256,128]{2,1,0:T(8,128)(2,1)S(1)}, u32[]{:S(2)}, u32[]{:S(2)}) %collective-permute-start.10) | collective-permute-done | bytes 131104 | tf_op jit(solution)/shard_map/ppermute | solution.py:975
  96.9 1.5 %unpack_heads.1 = (bf16[1,128,2048]{2,1,0:T(8,128)(2,1)}, bf16[1,128,2048]{2,1,0:T(8,128)(2,1)}, bf16[1,128,2048]{2,1,0:T(8,128)(2,1)}) custom-call(bf16[8,784,128]{2,1,0:T(8,128)(2,1)S(1)} %all-to-all-done.1.within_ref, bf16[2,256,128]{2,1,0:T(8,128)(2,1)S(1)} %collective-permute-done.7.refs_0_, bf16[2,256,128]{2,1,0:T(8,128)(2,1)S(1)} %collective-permute-done.8.refs_1_, ...), custom_call_target="tpu_custom_call" | custom-call | bytes 3702784 | tf_op jit(solution)/shard_map/unpack_heads/pallas_call | solution.py:410
  (23 shorter events, 4.2 us)
Async XLA Ops:
  0.6 8.9 %copy-start.3 = (s32[16]{0:T(128)S(1)}, s32[16]{0:T(128)}, u32[]{:S(2)}) copy-start(s32[16]{0:T(128)} %span_ref.1) | copy-start | bytes 196
  0.6 8.9 %copy-start.1 = (s32[1,16,16,1]{2,3,1,0:T(1,128)S(1)}, s32[1,16,16,1]{2,3,1,0:T(1,128)}, u32[]{:S(2)}) copy-start(s32[1,16,16,1]{2,3,1,0:T(1,128)} %param.12) | copy-start | bytes 3076
  0.7 8.9 %copy-start.2 = (f32[16]{0:T(128)S(1)}, f32[16]{0:T(128)}, u32[]{:S(2)}) copy-start(f32[16]{0:T(128)} %softness_ref.1) | copy-start | bytes 196
  3.6 7.5 %copy-start = (bf16[4,256,128]{2,1,0:T(8,128)(2,1)S(1)}, bf16[4,256,128]{2,1,0:T(8,128)(2,1)}, u32[]{:S(2)}) copy-start(bf16[4,256,128]{2,1,0:T(8,128)(2,1)} %get-tuple-element.50.kept_ref) | copy-start | bytes 786436
  3.6 36.7 %all-to-all-start = ((bf16[8,1024,128]{2,1,0:T(8,128)(2,1)}), bf16[8,1024,128]{2,1,0:T(8,128)(2,1)S(1)}, u32[]{:S(2)}, u32[]{:S(2)}) async-start(bf16[8,1024,128]{2,1,0:T(8,128)(2,1)} %get-tuple-element.41), calls=%async_computation | async-start | bytes 4194304 | tf_op jit(solution)/shard_map/all_to_all | solution.py:1005
  9.0 2.1 %collective-permute-start = (bf16[4,256,128]{2,1,0:T(8,128)(2,1)}, bf16[4,256,128]{2,1,0:T(8,128)(2,1)S(1)}, u32[]{:S(2)}, u32[]{:S(2)}) collective-permute-start(bf16[4,256,128]{2,1,0:T(8,128)(2,1)} %get-tuple-element.51), channel_id=1, source_target_pairs={{0,2},{2,0},{4,6},{6,4},{8,10},{10,8},{12,14},{14,12},{16,18},{18,... | collective-permute-start | bytes 786440 | tf_op jit(solution)/shard_map/ppermute | solution.py:964
  12.0 32.6 %collective-permute-start.1 = (bf16[2,256,128]{2,1,0:T(8,128)(2,1)}, bf16[2,256,128]{2,1,0:T(8,128)(2,1)S(1)}, u32[]{:S(2)}, u32[]{:S(2)}) collective-permute-start(bf16[2,256,128]{2,1,0:T(8,128)(2,1)} %get-tuple-element.52), channel_id=1, source_target_pairs={{0,16},{2,18},{4,20},{6,22},{8,24},{10,26},{12,28},{14,30},{16,0},... | collective-permute-start | bytes 393224 | tf_op jit(solution)/shard_map/ppermute | solution.py:975
  14.5 30.1 %collective-permute-start.2 = (bf16[2,256,128]{2,1,0:T(8,128)(2,1)}, bf16[2,256,128]{2,1,0:T(8,128)(2,1)S(1)}, u32[]{:S(2)}, u32[]{:S(2)}) collective-permute-start(bf16[2,256,128]{2,1,0:T(8,128)(2,1)} %get-tuple-element.53), channel_id=1, source_target_pairs={{0,20},{2,22},{4,16},{6,18},{8,28},{10,30},{12,24},{14,26},{16,4},... | collective-permute-start | bytes 393224 | tf_op jit(solution)/shard_map/ppermute | solution.py:975
  16.0 29.8 %collective-permute-start.3 = (bf16[2,256,128]{2,1,0:T(8,128)(2,1)}, bf16[2,256,128]{2,1,0:T(8,128)(2,1)}, u32[]{:S(2)}, u32[]{:S(2)}) collective-permute-start(bf16[2,256,128]{2,1,0:T(8,128)(2,1)} %get-tuple-element.54), channel_id=1, source_target_pairs={{0,24},{2,26},{4,28},{6,30},{8,16},{10,18},{12,20},{14,22},{16,8},... | collective-permute-start | bytes 393224 | tf_op jit(solution)/shard_map/ppermute | solution.py:975
  19.5 29.5 %collective-permute-start.4 = (bf16[2,256,128]{2,1,0:T(8,128)(2,1)}, bf16[2,256,128]{2,1,0:T(8,128)(2,1)}, u32[]{:S(2)}, u32[]{:S(2)}) collective-permute-start(bf16[2,256,128]{2,1,0:T(8,128)(2,1)} %get-tuple-element.55), channel_id=1, source_target_pairs={{0,28},{2,30},{4,24},{6,26},{8,20},{10,22},{12,16},{14,18},{16,12}... | collective-permute-start | bytes 393224 | tf_op jit(solution)/shard_map/ppermute | solution.py:975
  52.4 4.9 %collective-permute-start.5 = (f32[8,1024]{1,0:T(8,128)S(1)}, f32[8,1024]{1,0:T(8,128)S(1)}, u32[]{:S(2)}, u32[]{:S(2)}) collective-permute-start(f32[8,1024]{1,0:T(8,128)S(1)} %get-tuple-element.57.message_ref), channel_id=1, source_target_pairs={{0,16},{2,18},{4,20},{6,22},{8,24},{10,26},{12,28},{14,30},{16,0},... | collective-permute-start | bytes 98312 | tf_op jit(solution)/shard_map/ppermute | solution.py:1070
  60.2 29.6 %all-to-all-start.1 = ((bf16[8,784,128]{2,1,0:T(8,128)(2,1)}), bf16[8,784,128]{2,1,0:T(8,128)(2,1)S(1)}, u32[]{:S(2)}, u32[]{:S(2)}) async-start(bf16[8,784,128]{2,1,0:T(8,128)(2,1)} %get-tuple-element.68), calls=%async_computation.1 | async-start | bytes 3211264 | tf_op jit(solution)/shard_map/all_to_all | solution.py:1005
  63.8 1.7 %collective-permute-start.6 = (bf16[4,256,128]{2,1,0:T(8,128)(2,1)S(1)}, bf16[4,256,128]{2,1,0:T(8,128)(2,1)S(1)}, u32[]{:S(2)}, u32[]{:S(2)}) collective-permute-start(bf16[4,256,128]{2,1,0:T(8,128)(2,1)S(1)} %get-tuple-element.70), channel_id=1, source_target_pairs={{0,2},{2,0},{4,6},{6,4},{8,10},{10,8},{12,14},{14,12},{16,18},{18,... | collective-permute-start | bytes 786440 | tf_op jit(solution)/shard_map/ppermute | solution.py:964
  65.5 25.9 %collective-permute-start.7 = (bf16[2,256,128]{2,1,0:T(8,128)(2,1)S(1)}, bf16[2,256,128]{2,1,0:T(8,128)(2,1)S(1)}, u32[]{:S(2)}, u32[]{:S(2)}) collective-permute-start(bf16[2,256,128]{2,1,0:T(8,128)(2,1)S(1)} %get-tuple-element.71), channel_id=1, source_target_pairs={{0,16},{2,18},{4,20},{6,22},{8,24},{10,26},{12,28},{14,30},{16,0},... | collective-permute-start | bytes 393224 | tf_op jit(solution)/shard_map/ppermute | solution.py:975
  66.8 24.6 %collective-permute-start.8 = (bf16[2,256,128]{2,1,0:T(8,128)(2,1)S(1)}, bf16[2,256,128]{2,1,0:T(8,128)(2,1)S(1)}, u32[]{:S(2)}, u32[]{:S(2)}) collective-permute-start(bf16[2,256,128]{2,1,0:T(8,128)(2,1)S(1)} %get-tuple-element.72), channel_id=1, source_target_pairs={{0,20},{2,22},{4,16},{6,18},{8,28},{10,30},{12,24},{14,26},{16,4},... | collective-permute-start | bytes 393224 | tf_op jit(solution)/shard_map/ppermute | solution.py:975
  69.7 24.0 %collective-permute-start.9 = (bf16[2,256,128]{2,1,0:T(8,128)(2,1)S(1)}, bf16[2,256,128]{2,1,0:T(8,128)(2,1)S(1)}, u32[]{:S(2)}, u32[]{:S(2)}) collective-permute-start(bf16[2,256,128]{2,1,0:T(8,128)(2,1)S(1)} %get-tuple-element.73), channel_id=1, source_target_pairs={{0,24},{2,26},{4,28},{6,30},{8,16},{10,18},{12,20},{14,22},{16,8},... | collective-permute-start | bytes 393224 | tf_op jit(solution)/shard_map/ppermute | solution.py:975
  71.8 25.1 %collective-permute-start.10 = (bf16[2,256,128]{2,1,0:T(8,128)(2,1)S(1)}, bf16[2,256,128]{2,1,0:T(8,128)(2,1)S(1)}, u32[]{:S(2)}, u32[]{:S(2)}) collective-permute-start(bf16[2,256,128]{2,1,0:T(8,128)(2,1)S(1)} %get-tuple-element.74), channel_id=1, source_target_pairs={{0,28},{2,30},{4,24},{6,26},{8,20},{10,22},{12,16},{14,18},{16,12}... | collective-permute-start | bytes 393224 | tf_op jit(solution)/shard_map/ppermute | solution.py:975
  89.8 8.6 %collective-permute-start.11 = (f32[16,128]{1,0:T(8,128)S(1)}, f32[16,128]{1,0:T(8,128)S(1)}, u32[]{:S(2)}, u32[]{:S(2)}) collective-permute-start(f32[16,128]{1,0:T(8,128)S(1)} %temper_sums.1), channel_id=1, source_target_pairs={{0,1},{1,0},{2,3},{3,2},{4,5},{5,4},{6,7},{7,6},{8,9},{9,8},{10,11... | collective-permute-start | bytes 24584 | tf_op jit(solution)/shard_map/ppermute | solution.py:1112

commit v14 on v13

--- a/solution.py
+++ b/solution.py
@@ -522,9 +522,9 @@
 
 
 class Region:
-    def __init__(self, square, sources, tiles, scaling, bias_ref=None, corner_ref=None, first=0):
+    def __init__(self, square, sources, tiles, scaling, bias_ref=None, least_ref=None, first=0):
         self.square, self.sources, self.tiles, self.scaling = square, sources, tiles, scaling
-        self.bias_ref, self.corner_ref, self.first = bias_ref, corner_ref, first
+        self.bias_ref, self.least_ref, self.first = bias_ref, least_ref, first
 
     def rows(self, which, start, stop):
         return self.sources[which](start, stop)
@@ -555,7 +555,9 @@
                 elif apart == 0:
                     piece = jnp.where(key_minus_query() <= 0, piece, blocked_score)
                 elif apart == 1:
-                    piece = piece + self.corner_ref[self.first + (0 if self.square else key_block)]
+                    row = self.first + (0 if self.square else key_block)
+                    least = self.least_ref[row : row + 1, :]
+                    piece = jnp.where(key_minus_query() > least, piece, blocked_score)
                 else:
                     at = slice(query_block * BLK, (query_block + 1) * BLK)
                     piece = piece + self.bias_ref[key_block : key_block + 1, at]
@@ -564,21 +566,21 @@
         return jnp.concatenate(rows, axis=0)
 
 
-def diagonal(slot, arrived_ref, scales_ref, bias_ref=None, corner_ref=None):
+def diagonal(slot, arrived_ref, scales_ref, bias_ref=None, least_ref=None):
     blocks = arrived_ref.shape[0]
     sources = [from_blocks(arrived_ref, slot * 4 + place) for place in range(4)]
     bias = None if bias_ref is None else bias_ref.at[slot]
     first = slot * (blocks - 1)
     scaling = scales_ref[slot : slot + 1, :]
-    return Region(False, sources, blocks * BLK // TILE, scaling, bias, corner_ref, first)
-
-
-def square(square_ref, scales_ref, bias_ref=None, corner_ref=None):
+    return Region(False, sources, blocks * BLK // TILE, scaling, bias, least_ref, first)
+
+
+def square(square_ref, scales_ref, bias_ref=None, least_ref=None):
     tiles = square_ref.shape[1] // TILE
     sources = [from_array(square_ref, place) for place in range(4)]
     bias = None if bias_ref is None else bias_ref.at[2]
     first = 2 * (tiles * TILE // BLK - 1)
-    return Region(True, sources, tiles, scales_ref[0:1, :], bias, corner_ref, first)
+    return Region(True, sources, tiles, scales_ref[0:1, :], bias, least_ref, first)
 
 
 def key_minus_query():
@@ -680,7 +682,7 @@
     return [[value * scale for value in part] for part in parts[:2]] + [parts[2]]
 
 
-def masks_kernel(softness_ref, ids_ref, span_ref, scales_ref, bias_ref, corner_ref, *, half_count):
+def masks_kernel(softness_ref, ids_ref, span_ref, scales_ref, bias_ref, least_ref, *, half_count):
     me, half, _ = position(half_count)
     base = half * half_count
     regions = (
@@ -711,18 +713,17 @@
             pairs = [(half_count - 1, 0)]
         for place, pair in enumerate(pairs):
             least = jnp.where(same(*pair), -BLK, BLK - span_ref[head])
-            corner_ref[slot * (half_count - 1) + place] = jnp.where(
-                key_minus_query() > least, 0.0, blocked_score
-            )
+            row = slot * (half_count - 1) + place
+            least_ref[row : row + 1, :] = jnp.full((1, BLK), least, jnp.int32)
 
 
 def within_kernel(
-    arrived_ref, scales_ref, bias_ref, corner_ref, stats_ref, parts_ref, own_weight, own_towards, other_weight, other_towards, *scratch, half_count
+    arrived_ref, scales_ref, bias_ref, least_ref, stats_ref, parts_ref, own_weight, own_towards, other_weight, other_towards, *scratch, half_count
 ):
     _, half, _ = position(half_count)
     kept = ((own_weight, own_towards), (other_weight, other_towards))
     for slot in range(2):
-        region = diagonal(slot, arrived_ref, scales_ref, bias_ref, corner_ref)
+        region = diagonal(slot, arrived_ref, scales_ref, bias_ref, least_ref)
         statistics(region, *kept[slot], stats_ref, slot * 5)
 
     @pl.when(half == 0)
@@ -735,7 +736,7 @@
                 parts_ref[place, tile_rows(tile), :] = value
 
 
-def square_kernel(arrived_ref, scales_ref, bias_ref, corner_ref, stats_ref, *refs, half_count):
+def square_kernel(arrived_ref, scales_ref, bias_ref, least_ref, stats_ref, *refs, half_count):
     across_refs = refs[: half_count // 2]
     square_ref, message_ref, square_stats, weight, towards = refs[half_count // 2 :]
     _, half, place = position(half_count)
@@ -749,7 +750,7 @@
     for kept in (jnp.where(half == 0, KEY, QUERY), jnp.where(half == 0, VALUE, GRAD)):
         for block in range(half_count):
             square_ref[kept, block * BLK : (block + 1) * BLK, :] = arrived_ref[block, kept]
-    region = square(square_ref, scales_ref, bias_ref, corner_ref)
+    region = square(square_ref, scales_ref, bias_ref, least_ref)
     statistics(region, weight, towards, square_stats, 0)
     own, other, crossing = rows_at(stats_ref, 0), rows_at(stats_ref, 5), rows_at(square_stats, 0)
     for row in range(5):
@@ -1038,11 +1039,11 @@
         [
             jax.ShapeDtypeStruct((8, TILE), jnp.float32),
             jax.ShapeDtypeStruct((3, half_count, tokens), jnp.float32),
-            jax.ShapeDtypeStruct((2 * half_count - 1, BLK, BLK), jnp.float32),
+            jax.ShapeDtypeStruct((2 * half_count, BLK), jnp.int32),
         ],
         [],
         0,
-        6,
+        2,
         settings,
     )
     foreign[0], *masks = lax.optimization_barrier((foreign[0], *masks))
@@ -1055,7 +1056,7 @@
         [jax.ShapeDtypeStruct((16, tokens), jnp.float32), kept_parts] + [pairs] * 4,
         lows,
         2 * pair_flops,
-        20,
+        14,
     )
     squared, message, square_stats, square_weight, square_towards = call(
         square_kernel,
@@ -1064,7 +1065,7 @@
         [jax.ShapeDtypeStruct((4, tokens, HD), jnp.bfloat16)] + [rows_of_stats] * 2 + [pairs] * 2,
         [],
         2 * pair_flops,
-        12,
+        8,
     )
     swap = [(source, source ^ half_count) for source in range(seq_count)]
     received = lax.ppermute(message, "seq", swap)
@@ -1099,7 +1100,7 @@
             pltpu.SemaphoreType.DMA((3,)), pltpu.SemaphoreType.DMA, *lows,
         ],
         2 * pair_flops,
-        20,
+        16,
         out_spaces=(pl.ANY, pltpu.VMEM, pltpu.VMEM),
         last_in_place=True,
     )

time: 99.4 us -> 98.4 us (0.990)
  Pallas kernels: 19 us -> 17.2 us
    pallas_call x9, Pallas kernels: 19 us -> 17.1 us  [kernel_call(): pl.pallas_call(kernel, out_shape=out_shape, in_specs=in_specs, out_specs=...]
  transfers between devices with their start and end apart: 14 -> 14, of which waited for: 9 -> 9; matrix products, arithmetic and copies ran while one was open for 0% -> 0% of each run, Pallas kernels for 10% -> 9%
where the time goes in v14:
time: 98.4 us; the launch traced here: 98.1 us
  waiting for transfers between devices  52.6 us (53%)
  starting transfers between devices  26.9 us (27%)
  Pallas kernels  17.2 us (17%)
    all_to_all x2, waiting for transfers between devices, exchange_within(): lax.all_to_all(array_in, 'seq', split_axis=0, concat_axis=0, axis_index_g...  38.2 us
    pallas_call x9, Pallas kernels, kernel_call(): pl.pallas_call(kernel, out_shape=out_shape, in_specs=in_specs, out_specs=...  17.1 us
    ppermute x8, starting transfers between devices, crossed(): lax.ppermute(message, 'seq', [(source, source ^ half_count + 2 * step) fo...  15.4 us
    ppermute x8, waiting for transfers between devices, crossed(): lax.ppermute(message, 'seq', [(source, source ^ half_count + 2 * step) fo...  9.82 us
    all_to_all x2, starting transfers between devices, exchange_within(): lax.all_to_all(array_in, 'seq', split_axis=0, concat_axis=0, axis_index_g...  8.99 us
    ppermute x1, waiting for transfers between devices, head_shards(): received = lax.ppermute(message, 'seq', swap)  2.82 us
  transfers between devices with their start and end apart: 14, of which 9 were waited for; matrix products, arithmetic and copies ran while one was open for 0% of the time, Pallas kernels for 9%

profile of v14, /device:TPU:0, one launch (start us, length us, event | category | flops | bytes accessed | tf_op | source)
XLA Modules:
  0.0 98.1 jit_solution(6272475723718061764)
XLA Ops:
  0.7 2.9 %pack_heads.1 = (bf16[8,1024,128]{2,1,0:T(8,128)(2,1)}, bf16[4,256,128]{2,1,0:T(8,128)(2,1)}, bf16[4,256,128]{2,1,0:T(8,128)(2,1)}) custom-call(bf16[1,128,2048]{2,1,0:T(8,128)(2,1)} %refs_0_.1, bf16[1,128,2048]{2,1,0:T(8,128)(2,1)} %refs_1_.1, bf16[1,128,2048]{2,1,0:T(8,128)(2,1)} %refs_2_.1, bf16[1,128,2048]{2,1,0:T(8,128)(2,1)} %refs_3_.1), custom_call_target="tpu_custom_call" | custom-call | bytes 4718592 | tf_op jit(solution)/shard_map/pack_heads/pallas_call | solution.py:410
  3.6 5.4 %all-to-all-start = ((bf16[8,1024,128]{2,1,0:T(8,128)(2,1)}), bf16[8,1024,128]{2,1,0:T(8,128)(2,1)S(1)}, u32[]{:S(2)}, u32[]{:S(2)}) async-start(bf16[8,1024,128]{2,1,0:T(8,128)(2,1)} %get-tuple-element.41), calls=%async_computation | async-start | bytes 4194304 | tf_op jit(solution)/shard_map/all_to_all | solution.py:1006
  11.0 2.7 %collective-permute-start.1 = (bf16[2,256,128]{2,1,0:T(8,128)(2,1)S(1)}, bf16[2,256,128]{2,1,0:T(8,128)(2,1)S(1)}, u32[]{:S(2)}, u32[]{:S(2)}) collective-permute-start(bf16[2,256,128]{2,1,0:T(8,128)(2,1)S(1)} %get-tuple-element.52), channel_id=1, source_target_pairs={{0,16},{2,18},{4,20},{6,22},{8,24},{10,26},{12,28},{14,30},{16,0},... | collective-permute-start | bytes 393224 | tf_op jit(solution)/shard_map/ppermute | solution.py:976
  13.6 1.5 %collective-permute-start.2 = (bf16[2,256,128]{2,1,0:T(8,128)(2,1)S(1)}, bf16[2,256,128]{2,1,0:T(8,128)(2,1)S(1)}, u32[]{:S(2)}, u32[]{:S(2)}) collective-permute-start(bf16[2,256,128]{2,1,0:T(8,128)(2,1)S(1)} %get-tuple-element.53), channel_id=1, source_target_pairs={{0,20},{2,22},{4,16},{6,18},{8,28},{10,30},{12,24},{14,26},{16,4},... | collective-permute-start | bytes 393224 | tf_op jit(solution)/shard_map/ppermute | solution.py:976
  15.1 3.5 %collective-permute-start.3 = (bf16[2,256,128]{2,1,0:T(8,128)(2,1)S(1)}, bf16[2,256,128]{2,1,0:T(8,128)(2,1)S(1)}, u32[]{:S(2)}, u32[]{:S(2)}) collective-permute-start(bf16[2,256,128]{2,1,0:T(8,128)(2,1)S(1)} %get-tuple-element.54), channel_id=1, source_target_pairs={{0,24},{2,26},{4,28},{6,30},{8,16},{10,18},{12,20},{14,22},{16,8},... | collective-permute-start | bytes 393224 | tf_op jit(solution)/shard_map/ppermute | solution.py:976
  18.7 21.7 %all-to-all-done = bf16[8,1024,128]{2,1,0:T(8,128)(2,1)S(1)} async-done(((bf16[8,1024,128]{2,1,0:T(8,128)(2,1)}), bf16[8,1024,128]{2,1,0:T(8,128)(2,1)S(1)}, u32[]{:S(2)}, u32[]{:S(2)}) %all-to-all-start) | async-done | bytes 2097184 | tf_op jit(solution)/shard_map/all_to_all | solution.py:1006
  40.4 4.3 %diagonal_statistics.1 = (f32[16,1024]{1,0:T(8,128)S(1)}, f32[3,1024,128]{2,1,0:T(8,128)S(1)}, f32[1024,1024]{1,0:T(8,128)S(1)}, f32[1024,1024]{1,0:T(8,128)S(1)...) custom-call(bf16[8,8,128,128]{3,2,1,0:T(8,128)(2,1)S(1)} %bitcast.2, f32[8,256]{1,0:T(8,128)S(1)} %get-tuple-element.46.scales_ref, ...), custom_call_target="tpu_custom_call" | custom-call | flops 536870912 | bytes 20627456 | tf_op jit(solution)/shard_map/diagonal_statistics/pallas_call | solution.py:410
  44.6 1.0 %collective-permute-done.3.refs_2_ = bf16[2,256,128]{2,1,0:T(8,128)(2,1)S(1)} collective-permute-done((bf16[2,256,128]{2,1,0:T(8,128)(2,1)S(1)}, bf16[2,256,128]{2,1,0:T(8,128)(2,1)S(1)}, u32[]{:S(2)}, u32[]{:S(2)}) %collective-permute-start.3) | collective-permute-done | bytes 131104 | tf_op jit(solution)/shard_map/ppermute | solution.py:976
  45.7 3.2 %collective-permute-done.4.refs_3_ = bf16[2,256,128]{2,1,0:T(8,128)(2,1)S(1)} collective-permute-done((bf16[2,256,128]{2,1,0:T(8,128)(2,1)S(1)}, bf16[2,256,128]{2,1,0:T(8,128)(2,1)S(1)}, u32[]{:S(2)}, u32[]{:S(2)}) %collective-permute-start.4) | collective-permute-done | bytes 131104 | tf_op jit(solution)/shard_map/ppermute | solution.py:976
  48.9 2.4 %square_statistics.1 = (bf16[4,1024,128]{2,1,0:T(8,128)(2,1)S(1)}, f32[8,1024]{1,0:T(8,128)S(1)}, f32[8,1024]{1,0:T(8,128)S(1)}, f32[1024,1024]{1,0:T(8,128)S(1)}, f32[1024,1024]{1,0:T(8,128)S(1)}) custom-call(bf16[8,8,128,128]{3,2,1,0:T(8,128)(2,1)S(1)} %bitcast.3, f32[8,256]{1,0:T(8,128)S(1)} %get-tuple-element.46.scales_ref, ...), custom_call_target="tpu_custom_call" | custom-call | flops 536870912 | bytes 12304384 | tf_op jit(solution)/shard_map/square_statistics/pallas_call | solution.py:410
  51.4 2.0 %gradients_before_totals.1 = (bf16[2,1024,128]{2,1,0:T(8,128)(2,1)S(1)}, bf16[8,784,128]{2,1,0:T(8,128)(2,1)}) custom-call(bf16[8,8,128,128]{3,2,1,0:T(8,128)(2,1)S(1)} %bitcast.4, f32[8,256]{1,0:T(8,128)S(1)} %get-tuple-element.46.scales_ref, bf16[4,1024,128]{2,1,0:T(8,128)(2,1)S(1)} %get-tuple-element.56.square_ref, ...), custom_call_target="tpu_custom_call" | custom-call | flops 1073741824 | bytes 30547968 | tf_op jit(solution)/shard_map/gradients_before_totals/pallas_call | solution.py:410
  53.4 2.8 %collective-permute-done.5.received_ref = f32[8,1024]{1,0:T(8,128)S(1)} collective-permute-done((f32[8,1024]{1,0:T(8,128)S(1)}, f32[8,1024]{1,0:T(8,128)S(1)}, u32[]{:S(2)}, u32[]{:S(2)}) %collective-permute-start.5) | collective-permute-done | bytes 32800 | tf_op jit(solution)/shard_map/ppermute | solution.py:1071
  56.3 2.9 %gradients_after_totals.1 = (bf16[8,784,128]{2,1,0:T(8,128)(2,1)}, bf16[4,256,128]{2,1,0:T(8,128)(2,1)S(1)}, bf16[4,256,128]{2,1,0:T(8,128)(2,1)S(1)}) custom-call(bf16[8,8,128,128]{3,2,1,0:T(8,128)(2,1)S(1)} %bitcast.5, f32[8,256]{1,0:T(8,128)S(1)} %get-tuple-element.46.scales_ref, ...), custom_call_target="tpu_custom_call", output_to_operand_aliasing={{0}: (13, {})} | custom-call | flops 536870912 | bytes 25927680 | tf_op jit(solution)/shard_map/gradients_after_totals/pallas_call | solution.py:410
  59.2 3.6 %all-to-all-start.1 = ((bf16[8,784,128]{2,1,0:T(8,128)(2,1)}), bf16[8,784,128]{2,1,0:T(8,128)(2,1)S(1)}, u32[]{:S(2)}, u32[]{:S(2)}) async-start(bf16[8,784,128]{2,1,0:T(8,128)(2,1)} %get-tuple-element.68), calls=%async_computation.1 | async-start | bytes 3211264 | tf_op jit(solution)/shard_map/all_to_all | solution.py:1006
  63.2 1.3 %collective-permute-done.6.taken_ref = bf16[4,256,128]{2,1,0:T(8,128)(2,1)S(1)} collective-permute-done((bf16[4,256,128]{2,1,0:T(8,128)(2,1)S(1)}, bf16[4,256,128]{2,1,0:T(8,128)(2,1)S(1)}, u32[]{:S(2)}, u32[]{:S(2)}) %collective-permute-start.6) | collective-permute-done | bytes 262176 | tf_op jit(solution)/shard_map/ppermute | solution.py:965
  64.5 1.3 %collective-permute-start.7 = (bf16[2,256,128]{2,1,0:T(8,128)(2,1)S(1)}, bf16[2,256,128]{2,1,0:T(8,128)(2,1)S(1)}, u32[]{:S(2)}, u32[]{:S(2)}) collective-permute-start(bf16[2,256,128]{2,1,0:T(8,128)(2,1)S(1)} %get-tuple-element.71), channel_id=1, source_target_pairs={{0,16},{2,18},{4,20},{6,22},{8,24},{10,26},{12,28},{14,30},{16,0},... | collective-permute-start | bytes 393224 | tf_op jit(solution)/shard_map/ppermute | solution.py:976
  65.8 2.9 %collective-permute-start.8 = (bf16[2,256,128]{2,1,0:T(8,128)(2,1)S(1)}, bf16[2,256,128]{2,1,0:T(8,128)(2,1)S(1)}, u32[]{:S(2)}, u32[]{:S(2)}) collective-permute-start(bf16[2,256,128]{2,1,0:T(8,128)(2,1)S(1)} %get-tuple-element.72), channel_id=1, source_target_pairs={{0,20},{2,22},{4,16},{6,18},{8,28},{10,30},{12,24},{14,26},{16,4},... | collective-permute-start | bytes 393224 | tf_op jit(solution)/shard_map/ppermute | solution.py:976
  68.7 2.2 %collective-permute-start.9 = (bf16[2,256,128]{2,1,0:T(8,128)(2,1)S(1)}, bf16[2,256,128]{2,1,0:T(8,128)(2,1)S(1)}, u32[]{:S(2)}, u32[]{:S(2)}) collective-permute-start(bf16[2,256,128]{2,1,0:T(8,128)(2,1)S(1)} %get-tuple-element.73), channel_id=1, source_target_pairs={{0,24},{2,26},{4,28},{6,30},{8,16},{10,18},{12,20},{14,22},{16,8},... | collective-permute-start | bytes 393224 | tf_op jit(solution)/shard_map/ppermute | solution.py:976
  70.8 1.4 %collective-permute-start.10 = (bf16[2,256,128]{2,1,0:T(8,128)(2,1)S(1)}, bf16[2,256,128]{2,1,0:T(8,128)(2,1)S(1)}, u32[]{:S(2)}, u32[]{:S(2)}) collective-permute-start(bf16[2,256,128]{2,1,0:T(8,128)(2,1)S(1)} %get-tuple-element.74), channel_id=1, source_target_pairs={{0,28},{2,30},{4,24},{6,26},{8,20},{10,22},{12,16},{14,18},{16,12}... | collective-permute-start | bytes 393224 | tf_op jit(solution)/shard_map/ppermute | solution.py:976
  72.2 16.5 %all-to-all-done.1.within_ref = bf16[8,784,128]{2,1,0:T(8,128)(2,1)S(1)} async-done(((bf16[8,784,128]{2,1,0:T(8,128)(2,1)}), bf16[8,784,128]{2,1,0:T(8,128)(2,1)S(1)}, u32[]{:S(2)}, u32[]{:S(2)}) %all-to-all-start.1) | async-done | bytes 1605664 | tf_op jit(solution)/shard_map/all_to_all | solution.py:1006
  88.8 1.5 %collective-permute-start.11 = (f32[16,128]{1,0:T(8,128)S(1)}, f32[16,128]{1,0:T(8,128)S(1)}, u32[]{:S(2)}, u32[]{:S(2)}) collective-permute-start(f32[16,128]{1,0:T(8,128)S(1)} %temper_sums.1), channel_id=1, source_target_pairs={{0,1},{1,0},{2,3},{3,2},{4,5},{5,4},{6,7},{7,6},{8,9},{9,8},{10,11... | collective-permute-start | bytes 24584 | tf_op jit(solution)/shard_map/ppermute | solution.py:1113
  90.4 2.3 %collective-permute-done.9.refs_2_ = bf16[2,256,128]{2,1,0:T(8,128)(2,1)S(1)} collective-permute-done((bf16[2,256,128]{2,1,0:T(8,128)(2,1)S(1)}, bf16[2,256,128]{2,1,0:T(8,128)(2,1)S(1)}, u32[]{:S(2)}, u32[]{:S(2)}) %collective-permute-start.9) | collective-permute-done | bytes 131104 | tf_op jit(solution)/shard_map/ppermute | solution.py:976
  92.7 3.2 %collective-permute-done.10.refs_3_ = bf16[2,256,128]{2,1,0:T(8,128)(2,1)S(1)} collective-permute-done((bf16[2,256,128]{2,1,0:T(8,128)(2,1)S(1)}, bf16[2,256,128]{2,1,0:T(8,128)(2,1)S(1)}, u32[]{:S(2)}, u32[]{:S(2)}) %collective-permute-start.10) | collective-permute-done | bytes 131104 | tf_op jit(solution)/shard_map/ppermute | solution.py:976
  95.9 1.5 %unpack_heads.1 = (bf16[1,128,2048]{2,1,0:T(8,128)(2,1)}, bf16[1,128,2048]{2,1,0:T(8,128)(2,1)}, bf16[1,128,2048]{2,1,0:T(8,128)(2,1)}) custom-call(bf16[8,784,128]{2,1,0:T(8,128)(2,1)S(1)} %all-to-all-done.1.within_ref, bf16[2,256,128]{2,1,0:T(8,128)(2,1)S(1)} %collective-permute-done.7.refs_0_, bf16[2,256,128]{2,1,0:T(8,128)(2,1)S(1)} %collective-permute-done.8.refs_1_, ...), custom_call_target="tpu_custom_call" | custom-call | bytes 3702784 | tf_op jit(solution)/shard_map/unpack_heads/pallas_call | solution.py:410
  (25 shorter events, 3.2 us)
Async XLA Ops:
  0.6 8.9 %copy-start.3 = (s32[16]{0:T(128)S(1)}, s32[16]{0:T(128)}, u32[]{:S(2)}) copy-start(s32[16]{0:T(128)} %span_ref.1) | copy-start | bytes 196
  0.6 8.9 %copy-start.1 = (s32[1,16,16,1]{2,3,1,0:T(1,128)S(1)}, s32[1,16,16,1]{2,3,1,0:T(1,128)}, u32[]{:S(2)}) copy-start(s32[1,16,16,1]{2,3,1,0:T(1,128)} %param.12) | copy-start | bytes 3076
  0.7 8.9 %copy-start.2 = (f32[16]{0:T(128)S(1)}, f32[16]{0:T(128)}, u32[]{:S(2)}) copy-start(f32[16]{0:T(128)} %softness_ref.1) | copy-start | bytes 196
  3.6 5.4 %copy-start.4 = (bf16[4,256,128]{2,1,0:T(8,128)(2,1)S(1)}, bf16[4,256,128]{2,1,0:T(8,128)(2,1)}, u32[]{:S(2)}) copy-start(bf16[4,256,128]{2,1,0:T(8,128)(2,1)} %get-tuple-element.51) | copy-start | bytes 786436
  3.6 7.3 %copy-start = (bf16[4,256,128]{2,1,0:T(8,128)(2,1)S(1)}, bf16[4,256,128]{2,1,0:T(8,128)(2,1)}, u32[]{:S(2)}) copy-start(bf16[4,256,128]{2,1,0:T(8,128)(2,1)} %get-tuple-element.50.kept_ref) | copy-start | bytes 786436
  3.6 36.7 %all-to-all-start = ((bf16[8,1024,128]{2,1,0:T(8,128)(2,1)}), bf16[8,1024,128]{2,1,0:T(8,128)(2,1)S(1)}, u32[]{:S(2)}, u32[]{:S(2)}) async-start(bf16[8,1024,128]{2,1,0:T(8,128)(2,1)} %get-tuple-element.41), calls=%async_computation | async-start | bytes 4194304 | tf_op jit(solution)/shard_map/all_to_all | solution.py:1006
  9.0 1.9 %collective-permute-start = (bf16[4,256,128]{2,1,0:T(8,128)(2,1)S(1)}, bf16[4,256,128]{2,1,0:T(8,128)(2,1)S(1)}, u32[]{:S(2)}, u32[]{:S(2)}) collective-permute-start(bf16[4,256,128]{2,1,0:T(8,128)(2,1)S(1)} %copy-done.4), channel_id=1, source_target_pairs={{0,2},{2,0},{4,6},{6,4},{8,10},{10,8},{12,14},{14,12},{16,18},{18,... | collective-permute-start | bytes 786440 | tf_op jit(solution)/shard_map/ppermute | solution.py:965
  11.0 33.6 %collective-permute-start.1 = (bf16[2,256,128]{2,1,0:T(8,128)(2,1)S(1)}, bf16[2,256,128]{2,1,0:T(8,128)(2,1)S(1)}, u32[]{:S(2)}, u32[]{:S(2)}) collective-permute-start(bf16[2,256,128]{2,1,0:T(8,128)(2,1)S(1)} %get-tuple-element.52), channel_id=1, source_target_pairs={{0,16},{2,18},{4,20},{6,22},{8,24},{10,26},{12,28},{14,30},{16,0},... | collective-permute-start | bytes 393224 | tf_op jit(solution)/shard_map/ppermute | solution.py:976
  13.6 31.0 %collective-permute-start.2 = (bf16[2,256,128]{2,1,0:T(8,128)(2,1)S(1)}, bf16[2,256,128]{2,1,0:T(8,128)(2,1)S(1)}, u32[]{:S(2)}, u32[]{:S(2)}) collective-permute-start(bf16[2,256,128]{2,1,0:T(8,128)(2,1)S(1)} %get-tuple-element.53), channel_id=1, source_target_pairs={{0,20},{2,22},{4,16},{6,18},{8,28},{10,30},{12,24},{14,26},{16,4},... | collective-permute-start | bytes 393224 | tf_op jit(solution)/shard_map/ppermute | solution.py:976
  15.1 30.6 %collective-permute-start.3 = (bf16[2,256,128]{2,1,0:T(8,128)(2,1)S(1)}, bf16[2,256,128]{2,1,0:T(8,128)(2,1)S(1)}, u32[]{:S(2)}, u32[]{:S(2)}) collective-permute-start(bf16[2,256,128]{2,1,0:T(8,128)(2,1)S(1)} %get-tuple-element.54), channel_id=1, source_target_pairs={{0,24},{2,26},{4,28},{6,30},{8,16},{10,18},{12,20},{14,22},{16,8},... | collective-permute-start | bytes 393224 | tf_op jit(solution)/shard_map/ppermute | solution.py:976
  18.6 30.3 %collective-permute-start.4 = (bf16[2,256,128]{2,1,0:T(8,128)(2,1)S(1)}, bf16[2,256,128]{2,1,0:T(8,128)(2,1)S(1)}, u32[]{:S(2)}, u32[]{:S(2)}) collective-permute-start(bf16[2,256,128]{2,1,0:T(8,128)(2,1)S(1)} %get-tuple-element.55), channel_id=1, source_target_pairs={{0,28},{2,30},{4,24},{6,26},{8,20},{10,22},{12,16},{14,18},{16,12}... | collective-permute-start | bytes 393224 | tf_op jit(solution)/shard_map/ppermute | solution.py:976
  51.3 4.9 %collective-permute-start.5 = (f32[8,1024]{1,0:T(8,128)S(1)}, f32[8,1024]{1,0:T(8,128)S(1)}, u32[]{:S(2)}, u32[]{:S(2)}) collective-permute-start(f32[8,1024]{1,0:T(8,128)S(1)} %get-tuple-element.57.message_ref), channel_id=1, source_target_pairs={{0,16},{2,18},{4,20},{6,22},{8,24},{10,26},{12,28},{14,30},{16,0},... | collective-permute-start | bytes 98312 | tf_op jit(solution)/shard_map/ppermute | solution.py:1071
  59.2 29.6 %all-to-all-start.1 = ((bf16[8,784,128]{2,1,0:T(8,128)(2,1)}), bf16[8,784,128]{2,1,0:T(8,128)(2,1)S(1)}, u32[]{:S(2)}, u32[]{:S(2)}) async-start(bf16[8,784,128]{2,1,0:T(8,128)(2,1)} %get-tuple-element.68), calls=%async_computation.1 | async-start | bytes 3211264 | tf_op jit(solution)/shard_map/all_to_all | solution.py:1006
  62.8 1.7 %collective-permute-start.6 = (bf16[4,256,128]{2,1,0:T(8,128)(2,1)S(1)}, bf16[4,256,128]{2,1,0:T(8,128)(2,1)S(1)}, u32[]{:S(2)}, u32[]{:S(2)}) collective-permute-start(bf16[4,256,128]{2,1,0:T(8,128)(2,1)S(1)} %get-tuple-element.70), channel_id=1, source_target_pairs={{0,2},{2,0},{4,6},{6,4},{8,10},{10,8},{12,14},{14,12},{16,18},{18,... | collective-permute-start | bytes 786440 | tf_op jit(solution)/shard_map/ppermute | solution.py:965
  64.5 25.8 %collective-permute-start.7 = (bf16[2,256,128]{2,1,0:T(8,128)(2,1)S(1)}, bf16[2,256,128]{2,1,0:T(8,128)(2,1)S(1)}, u32[]{:S(2)}, u32[]{:S(2)}) collective-permute-start(bf16[2,256,128]{2,1,0:T(8,128)(2,1)S(1)} %get-tuple-element.71), channel_id=1, source_target_pairs={{0,16},{2,18},{4,20},{6,22},{8,24},{10,26},{12,28},{14,30},{16,0},... | collective-permute-start | bytes 393224 | tf_op jit(solution)/shard_map/ppermute | solution.py:976
  65.8 24.5 %collective-permute-start.8 = (bf16[2,256,128]{2,1,0:T(8,128)(2,1)S(1)}, bf16[2,256,128]{2,1,0:T(8,128)(2,1)S(1)}, u32[]{:S(2)}, u32[]{:S(2)}) collective-permute-start(bf16[2,256,128]{2,1,0:T(8,128)(2,1)S(1)} %get-tuple-element.72), channel_id=1, source_target_pairs={{0,20},{2,22},{4,16},{6,18},{8,28},{10,30},{12,24},{14,26},{16,4},... | collective-permute-start | bytes 393224 | tf_op jit(solution)/shard_map/ppermute | solution.py:976
  68.7 24.0 %collective-permute-start.9 = (bf16[2,256,128]{2,1,0:T(8,128)(2,1)S(1)}, bf16[2,256,128]{2,1,0:T(8,128)(2,1)S(1)}, u32[]{:S(2)}, u32[]{:S(2)}) collective-permute-start(bf16[2,256,128]{2,1,0:T(8,128)(2,1)S(1)} %get-tuple-element.73), channel_id=1, source_target_pairs={{0,24},{2,26},{4,28},{6,30},{8,16},{10,18},{12,20},{14,22},{16,8},... | collective-permute-start | bytes 393224 | tf_op jit(solution)/shard_map/ppermute | solution.py:976
  70.8 25.1 %collective-permute-start.10 = (bf16[2,256,128]{2,1,0:T(8,128)(2,1)S(1)}, bf16[2,256,128]{2,1,0:T(8,128)(2,1)S(1)}, u32[]{:S(2)}, u32[]{:S(2)}) collective-permute-start(bf16[2,256,128]{2,1,0:T(8,128)(2,1)S(1)} %get-tuple-element.74), channel_id=1, source_target_pairs={{0,28},{2,30},{4,24},{6,26},{8,20},{10,22},{12,16},{14,18},{16,12}... | collective-permute-start | bytes 393224 | tf_op jit(solution)/shard_map/ppermute | solution.py:976
  88.8 8.7 %collective-permute-start.11 = (f32[16,128]{1,0:T(8,128)S(1)}, f32[16,128]{1,0:T(8,128)S(1)}, u32[]{:S(2)}, u32[]{:S(2)}) collective-permute-start(f32[16,128]{1,0:T(8,128)S(1)} %temper_sums.1), channel_id=1, source_target_pairs={{0,1},{1,0},{2,3},{3,2},{4,5},{5,4},{6,7},{7,6},{8,9},{9,8},{10,11... | collective-permute-start | bytes 24584 | tf_op jit(solution)/shard_map/ppermute | solution.py:1113

commit v15 on v14

--- a/solution.py
+++ b/solution.py
@@ -929,28 +929,74 @@
     )(within)
 
 
-def unpack_kernel(within_ref, *refs, half_count):
-    across_refs = refs[: half_count // 2]
-    out_refs = refs[half_count // 2 :]
+def own_columns_kernel(within_ref, *refs, half_count):
+    out_refs, (staged, sems) = refs[:3], refs[3:]
+    _, half, _ = position(half_count)
+    width = half_count * HD
+    for array in range(6):
+        for peer in range(half_count):
+            staged[array, :, peer * HD : (peer + 1) * HD] = within_ref[
+                peer, array * BLK : (array + 1) * BLK, :
+            ]
+
+    def copies(arrays):
+        return [
+            pltpu.make_async_copy(
+                staged.at[array],
+                out_refs[array % 3].at[0, :, side(half if array < 3 else 1 - half, width)],
+                sems.at[array],
+            )
+            for array in arrays
+        ]
+
+    for role, arrays in enumerate(((0, 1, 2, 3), (0, 1, 2, 4, 5))):
+
+        @pl.when(half == role)
+        def _():
+            leaving = copies(arrays)
+            for copy in leaving:
+                copy.start()
+            for copy in leaving:
+                copy.wait()
+
+
+def side(half, width):
+    return pl.ds(pl.multiple_of(half * width, width), width)
+
+
+def other_columns_kernel(within_ref, *refs, half_count):
+    messages = half_count // 2
+    across_refs = refs[:messages]
+    out_refs, (staged, sems) = refs[messages + 3 : messages + 6], refs[messages + 6 :]
     _, half, place = position(half_count)
-    for step, across_ref in enumerate(across_refs):
-        for core in range(2):
-            peer = place ^ core ^ (2 * step)
-            other = columns_of((1 - half) * half_count + peer)
-            own = columns_of(half * half_count + peer)
-            first = across_ref[core, :BLK, :].astype(jnp.float32)
-            second = across_ref[core, BLK : 2 * BLK, :].astype(jnp.float32)
-            added = (
-                jnp.where(half == 0, 0.0, first),
-                jnp.where(half == 0, first, 0.0),
-                jnp.where(half == 0, second, 0.0),
-            )
-            for array, out_ref in enumerate(out_refs):
-                out_ref[0, :, own] = within_ref[peer, array * BLK : (array + 1) * BLK, :]
-                kept = within_ref[peer, (3 + array) * BLK : (4 + array) * BLK, :]
-                out_ref[0, :, other] = (kept.astype(jnp.float32) + added[array]).astype(
-                    jnp.bfloat16
-                )
+
+    for role, arrays in enumerate(((1, 2), (0,))):
+
+        @pl.when(half == role)
+        def _():
+            leaving = []
+            for step, across_ref in enumerate(across_refs):
+                pair = (place ^ (2 * step)) >> 1
+                for part, array in enumerate(arrays):
+                    rows = slice(part * BLK, (part + 1) * BLK)
+                    for core in range(2):
+                        peer = place ^ core ^ (2 * step)
+                        kept = within_ref[peer, (3 + array) * BLK : (4 + array) * BLK, :]
+                        total = kept.astype(jnp.float32) + across_ref[core, rows, :].astype(
+                            jnp.float32
+                        )
+                        staged[part, :, columns_of(peer)] = total.astype(jnp.bfloat16)
+                    start = (1 - role) * messages + pair
+                    leaving.append(
+                        pltpu.make_async_copy(
+                            staged.at[part, :, side(pair, 2 * HD)],
+                            out_refs[array].at[0, :, side(start, 2 * HD)],
+                            sems.at[step, part],
+                        )
+                    )
+                    leaving[-1].start()
+            for copy in leaving:
+                copy.wait()
 
 
 def join_kernel(kept_ref, taken_ref, *out_refs):
@@ -1111,16 +1157,32 @@
     for step in range(1, dp_count):
         swap = [(source, (source + step) % dp_count) for source in range(dp_count)]
         temper_total = temper_total + lax.ppermute(tempers, "dp", swap)
+    temper = temper_total[:, 0] / (dp_count * BLK * seq_count)
+    result = [pltpu.HBM(probe_vectors.shape, jnp.bfloat16)] * 3
+    width = half_count * HD
     outs = kernel_call(
-        functools.partial(unpack_kernel, half_count=half_count),
-        "unpack_heads",
-        (within, *across),
-        [vmem] * (1 + len(across)),
-        [jax.ShapeDtypeStruct(probe_vectors.shape, jnp.bfloat16)] * 3,
-        [],
-        10,
-    )
-    return (*outs, temper_total[:, 0] / (dp_count * BLK * seq_count))
+        functools.partial(own_columns_kernel, half_count=half_count),
+        "unpack_own",
+        (within,),
+        [vmem],
+        result,
+        [pltpu.VMEM((6, BLK, width), jnp.bfloat16), pltpu.SemaphoreType.DMA((6,))],
+        6,
+        out_spaces=[pl.ANY] * 3,
+    )
+    across[0], temper = lax.optimization_barrier((across[0], temper))
+    outs = kernel_call(
+        functools.partial(other_columns_kernel, half_count=half_count),
+        "unpack_other",
+        (within, *across, *outs),
+        [vmem] * (1 + len(across)) + [pl.BlockSpec(memory_space=pl.ANY)] * 3,
+        result,
+        [pltpu.VMEM((2, BLK, width), jnp.bfloat16), pltpu.SemaphoreType.DMA((len(across), 2))],
+        6,
+        out_spaces=[pl.ANY] * 3,
+        aliases={1 + len(across) + array: array for array in range(3)},
+    )
+    return (*outs, temper)
 
 
 def shards(

time: 98.4 us -> 97.3 us (0.989)
  waiting for transfers between devices: 52.6 us -> 50.5 us
    ppermute x8, waiting for transfers between devices: 9.82 us -> 7.07 us  [crossed(): lax.ppermute(message, 'seq', [(source, source ^ half_count + 2 * step) fo...]
    pallas_call x9 -> x10, Pallas kernels: 17.1 us -> 17.9 us  [kernel_call(): pl.pallas_call(kernel, out_shape=out_shape, in_specs=in_specs, out_specs=...]
  transfers between devices with their start and end apart: 14 -> 14, of which waited for: 9 -> 9; matrix products, arithmetic and copies ran while one was open for 0% -> 1% of each run, Pallas kernels for 9% -> 9%
where the time goes in v15:
time: 97.3 us; the launch traced here: 97 us
  waiting for transfers between devices  50.5 us (52%)
  starting transfers between devices  27 us (28%)
  Pallas kernels  17.9 us (18%)
    all_to_all x2, waiting for transfers between devices, exchange_within(): lax.all_to_all(array_in, 'seq', split_axis=0, concat_axis=0, axis_index_g...  38.2 us
    pallas_call x10, Pallas kernels, kernel_call(): pl.pallas_call(kernel, out_shape=out_shape, in_specs=in_specs, out_specs=...  17.9 us
    ppermute x8, starting transfers between devices, crossed(): lax.ppermute(message, 'seq', [(source, source ^ half_count + 2 * step) fo...  15.4 us
    all_to_all x2, starting transfers between devices, exchange_within(): lax.all_to_all(array_in, 'seq', split_axis=0, concat_axis=0, axis_index_g...  8.99 us
    ppermute x8, waiting for transfers between devices, crossed(): lax.ppermute(message, 'seq', [(source, source ^ half_count + 2 * step) fo...  7.07 us
    ppermute x1, waiting for transfers between devices, head_shards(): received = lax.ppermute(message, 'seq', swap)  2.81 us
  transfers between devices with their start and end apart: 14, of which 9 were waited for; matrix products, arithmetic and copies ran while one was open for 1% of the time, Pallas kernels for 9%

profile of v15, /device:TPU:0, one launch (start us, length us, event | category | flops | bytes accessed | tf_op | source)
XLA Modules:
  0.0 97.0 jit_solution(2434252749129237036)
XLA Ops:
  0.7 2.9 %pack_heads.1 = (bf16[8,1024,128]{2,1,0:T(8,128)(2,1)}, bf16[4,256,128]{2,1,0:T(8,128)(2,1)}, bf16[4,256,128]{2,1,0:T(8,128)(2,1)}) custom-call(bf16[1,128,2048]{2,1,0:T(8,128)(2,1)} %refs_0_.1, bf16[1,128,2048]{2,1,0:T(8,128)(2,1)} %refs_1_.1, bf16[1,128,2048]{2,1,0:T(8,128)(2,1)} %refs_2_.1, bf16[1,128,2048]{2,1,0:T(8,128)(2,1)} %refs_3_.1), custom_call_target="tpu_custom_call" | custom-call | bytes 4718592 | tf_op jit(solution)/shard_map/pack_heads/pallas_call | solution.py:410
  3.6 5.4 %all-to-all-start = ((bf16[8,1024,128]{2,1,0:T(8,128)(2,1)}), bf16[8,1024,128]{2,1,0:T(8,128)(2,1)S(1)}, u32[]{:S(2)}, u32[]{:S(2)}) async-start(bf16[8,1024,128]{2,1,0:T(8,128)(2,1)} %get-tuple-element.46), calls=%async_computation | async-start | bytes 4194304 | tf_op jit(solution)/shard_map/all_to_all | solution.py:1052
  9.6 1.0 %scales_and_masks.1 = (f32[8,256]{1,0:T(8,128)S(1)}, f32[3,8,1024]{2,1,0:T(8,128)S(1)}, s32[16,128]{1,0:T(8,128)S(1)}) custom-call(f32[16]{0:T(128)S(1)} %copy-done.2, s32[16,16]{1,0:T(8,128)S(1)} %bitcast.6, s32[16]{0:T(128)S(1)} %copy-done.3), custom_call_target="tpu_custom_call" | custom-call | bytes 115840 | tf_op jit(solution)/shard_map/scales_and_masks/pallas_call | solution.py:410
  11.0 2.7 %collective-permute-start.1 = (bf16[2,256,128]{2,1,0:T(8,128)(2,1)S(1)}, bf16[2,256,128]{2,1,0:T(8,128)(2,1)S(1)}, u32[]{:S(2)}, u32[]{:S(2)}) collective-permute-start(bf16[2,256,128]{2,1,0:T(8,128)(2,1)S(1)} %get-tuple-element.57), channel_id=1, source_target_pairs={{0,16},{2,18},{4,20},{6,22},{8,24},{10,26},{12,28},{14,30},{16,0},... | collective-permute-start | bytes 393224 | tf_op jit(solution)/shard_map/ppermute | solution.py:1022
  13.6 1.5 %collective-permute-start.2 = (bf16[2,256,128]{2,1,0:T(8,128)(2,1)S(1)}, bf16[2,256,128]{2,1,0:T(8,128)(2,1)S(1)}, u32[]{:S(2)}, u32[]{:S(2)}) collective-permute-start(bf16[2,256,128]{2,1,0:T(8,128)(2,1)S(1)} %get-tuple-element.58), channel_id=1, source_target_pairs={{0,20},{2,22},{4,16},{6,18},{8,28},{10,30},{12,24},{14,26},{16,4},... | collective-permute-start | bytes 393224 | tf_op jit(solution)/shard_map/ppermute | solution.py:1022
  15.1 3.5 %collective-permute-start.3 = (bf16[2,256,128]{2,1,0:T(8,128)(2,1)S(1)}, bf16[2,256,128]{2,1,0:T(8,128)(2,1)S(1)}, u32[]{:S(2)}, u32[]{:S(2)}) collective-permute-start(bf16[2,256,128]{2,1,0:T(8,128)(2,1)S(1)} %get-tuple-element.59), channel_id=1, source_target_pairs={{0,24},{2,26},{4,28},{6,30},{8,16},{10,18},{12,20},{14,22},{16,8},... | collective-permute-start | bytes 393224 | tf_op jit(solution)/shard_map/ppermute | solution.py:1022
  18.7 21.7 %all-to-all-done = bf16[8,1024,128]{2,1,0:T(8,128)(2,1)S(1)} async-done(((bf16[8,1024,128]{2,1,0:T(8,128)(2,1)}), bf16[8,1024,128]{2,1,0:T(8,128)(2,1)S(1)}, u32[]{:S(2)}, u32[]{:S(2)}) %all-to-all-start) | async-done | bytes 2097184 | tf_op jit(solution)/shard_map/all_to_all | solution.py:1052
  40.4 4.3 %diagonal_statistics.1 = (f32[16,1024]{1,0:T(8,128)S(1)}, f32[3,1024,128]{2,1,0:T(8,128)S(1)}, f32[1024,1024]{1,0:T(8,128)S(1)}, f32[1024,1024]{1,0:T(8,128)S(1)...) custom-call(bf16[8,8,128,128]{3,2,1,0:T(8,128)(2,1)S(1)} %bitcast.2, f32[8,256]{1,0:T(8,128)S(1)} %get-tuple-element.51.scales_ref, ...), custom_call_target="tpu_custom_call" | custom-call | flops 536870912 | bytes 20627456 | tf_op jit(solution)/shard_map/diagonal_statistics/pallas_call | solution.py:410
  44.6 1.0 %collective-permute-done.3.refs_2_ = bf16[2,256,128]{2,1,0:T(8,128)(2,1)S(1)} collective-permute-done((bf16[2,256,128]{2,1,0:T(8,128)(2,1)S(1)}, bf16[2,256,128]{2,1,0:T(8,128)(2,1)S(1)}, u32[]{:S(2)}, u32[]{:S(2)}) %collective-permute-start.3) | collective-permute-done | bytes 131104 | tf_op jit(solution)/shard_map/ppermute | solution.py:1022
  45.7 3.2 %collective-permute-done.4.refs_3_ = bf16[2,256,128]{2,1,0:T(8,128)(2,1)S(1)} collective-permute-done((bf16[2,256,128]{2,1,0:T(8,128)(2,1)S(1)}, bf16[2,256,128]{2,1,0:T(8,128)(2,1)S(1)}, u32[]{:S(2)}, u32[]{:S(2)}) %collective-permute-start.4) | collective-permute-done | bytes 131104 | tf_op jit(solution)/shard_map/ppermute | solution.py:1022
  48.9 2.4 %square_statistics.1 = (bf16[4,1024,128]{2,1,0:T(8,128)(2,1)S(1)}, f32[8,1024]{1,0:T(8,128)S(1)}, f32[8,1024]{1,0:T(8,128)S(1)}, f32[1024,1024]{1,0:T(8,128)S(1)}, f32[1024,1024]{1,0:T(8,128)S(1)}) custom-call(bf16[8,8,128,128]{3,2,1,0:T(8,128)(2,1)S(1)} %bitcast.3, f32[8,256]{1,0:T(8,128)S(1)} %get-tuple-element.51.scales_ref, ...), custom_call_target="tpu_custom_call" | custom-call | flops 536870912 | bytes 12304384 | tf_op jit(solution)/shard_map/square_statistics/pallas_call | solution.py:410
  51.4 2.0 %gradients_before_totals.1 = (bf16[2,1024,128]{2,1,0:T(8,128)(2,1)S(1)}, bf16[8,784,128]{2,1,0:T(8,128)(2,1)}) custom-call(bf16[8,8,128,128]{3,2,1,0:T(8,128)(2,1)S(1)} %bitcast.4, f32[8,256]{1,0:T(8,128)S(1)} %get-tuple-element.51.scales_ref, bf16[4,1024,128]{2,1,0:T(8,128)(2,1)S(1)} %get-tuple-element.61.square_ref, ...), custom_call_target="tpu_custom_call" | custom-call | flops 1073741824 | bytes 30547968 | tf_op jit(solution)/shard_map/gradients_before_totals/pallas_call | solution.py:410
  53.4 2.8 %collective-permute-done.5.received_ref = f32[8,1024]{1,0:T(8,128)S(1)} collective-permute-done((f32[8,1024]{1,0:T(8,128)S(1)}, f32[8,1024]{1,0:T(8,128)S(1)}, u32[]{:S(2)}, u32[]{:S(2)}) %collective-permute-start.5) | collective-permute-done | bytes 32800 | tf_op jit(solution)/shard_map/ppermute | solution.py:1117
  56.2 2.9 %gradients_after_totals.1 = (bf16[8,784,128]{2,1,0:T(8,128)(2,1)}, bf16[4,256,128]{2,1,0:T(8,128)(2,1)S(1)}, bf16[4,256,128]{2,1,0:T(8,128)(2,1)S(1)}) custom-call(bf16[8,8,128,128]{3,2,1,0:T(8,128)(2,1)S(1)} %bitcast.5, f32[8,256]{1,0:T(8,128)S(1)} %get-tuple-element.51.scales_ref, ...), custom_call_target="tpu_custom_call", output_to_operand_aliasing={{0}: (13, {})} | custom-call | flops 536870912 | bytes 25927680 | tf_op jit(solution)/shard_map/gradients_after_totals/pallas_call | solution.py:410
  59.1 3.6 %all-to-all-start.1 = ((bf16[8,784,128]{2,1,0:T(8,128)(2,1)}), bf16[8,784,128]{2,1,0:T(8,128)(2,1)S(1)}, u32[]{:S(2)}, u32[]{:S(2)}) async-start(bf16[8,784,128]{2,1,0:T(8,128)(2,1)} %get-tuple-element.73), calls=%async_computation.1 | async-start | bytes 3211264 | tf_op jit(solution)/shard_map/all_to_all | solution.py:1052
  63.1 1.3 %collective-permute-done.6.taken_ref = bf16[4,256,128]{2,1,0:T(8,128)(2,1)S(1)} collective-permute-done((bf16[4,256,128]{2,1,0:T(8,128)(2,1)S(1)}, bf16[4,256,128]{2,1,0:T(8,128)(2,1)S(1)}, u32[]{:S(2)}, u32[]{:S(2)}) %collective-permute-start.6) | collective-permute-done | bytes 262176 | tf_op jit(solution)/shard_map/ppermute | solution.py:1011
  64.5 1.4 %collective-permute-start.7 = (bf16[2,256,128]{2,1,0:T(8,128)(2,1)S(1)}, bf16[2,256,128]{2,1,0:T(8,128)(2,1)S(1)}, u32[]{:S(2)}, u32[]{:S(2)}) collective-permute-start(bf16[2,256,128]{2,1,0:T(8,128)(2,1)S(1)} %get-tuple-element.76), channel_id=1, source_target_pairs={{0,16},{2,18},{4,20},{6,22},{8,24},{10,26},{12,28},{14,30},{16,0},... | collective-permute-start | bytes 393224 | tf_op jit(solution)/shard_map/ppermute | solution.py:1022
  65.8 2.8 %collective-permute-start.9 = (bf16[2,256,128]{2,1,0:T(8,128)(2,1)S(1)}, bf16[2,256,128]{2,1,0:T(8,128)(2,1)S(1)}, u32[]{:S(2)}, u32[]{:S(2)}) collective-permute-start(bf16[2,256,128]{2,1,0:T(8,128)(2,1)S(1)} %get-tuple-element.78), channel_id=1, source_target_pairs={{0,20},{2,22},{4,16},{6,18},{8,28},{10,30},{12,24},{14,26},{16,4},... | collective-permute-start | bytes 393224 | tf_op jit(solution)/shard_map/ppermute | solution.py:1022
  68.6 2.2 %collective-permute-start.10 = (bf16[2,256,128]{2,1,0:T(8,128)(2,1)S(1)}, bf16[2,256,128]{2,1,0:T(8,128)(2,1)S(1)}, u32[]{:S(2)}, u32[]{:S(2)}) collective-permute-start(bf16[2,256,128]{2,1,0:T(8,128)(2,1)S(1)} %get-tuple-element.79), channel_id=1, source_target_pairs={{0,24},{2,26},{4,28},{6,30},{8,16},{10,18},{12,20},{14,22},{16,8},... | collective-permute-start | bytes 393224 | tf_op jit(solution)/shard_map/ppermute | solution.py:1022
  70.9 1.3 %collective-permute-start.11 = (bf16[2,256,128]{2,1,0:T(8,128)(2,1)S(1)}, bf16[2,256,128]{2,1,0:T(8,128)(2,1)S(1)}, u32[]{:S(2)}, u32[]{:S(2)}) collective-permute-start(bf16[2,256,128]{2,1,0:T(8,128)(2,1)S(1)} %get-tuple-element.80), channel_id=1, source_target_pairs={{0,28},{2,30},{4,24},{6,26},{8,20},{10,22},{12,16},{14,18},{16,12}... | collective-permute-start | bytes 393224 | tf_op jit(solution)/shard_map/ppermute | solution.py:1022
  72.2 16.5 %all-to-all-done.1.within_ref = bf16[8,784,128]{2,1,0:T(8,128)(2,1)S(1)} async-done(((bf16[8,784,128]{2,1,0:T(8,128)(2,1)}), bf16[8,784,128]{2,1,0:T(8,128)(2,1)S(1)}, u32[]{:S(2)}, u32[]{:S(2)}) %all-to-all-start.1) | async-done | bytes 1605664 | tf_op jit(solution)/shard_map/all_to_all | solution.py:1052
  88.8 1.6 %collective-permute-start.8 = (f32[16,128]{1,0:T(8,128)S(1)}, f32[16,128]{1,0:T(8,128)S(1)}, u32[]{:S(2)}, u32[]{:S(2)}) collective-permute-start(f32[16,128]{1,0:T(8,128)S(1)} %temper_sums.1), channel_id=1, source_target_pairs={{0,1},{1,0},{2,3},{3,2},{4,5},{5,4},{6,7},{7,6},{8,9},{9,8},{10,11... | collective-permute-start | bytes 24584 | tf_op jit(solution)/shard_map/ppermute | solution.py:1159
  90.3 1.4 %unpack_own.1 = (bf16[1,128,2048]{2,1,0:T(8,128)(2,1)}, bf16[1,128,2048]{2,1,0:T(8,128)(2,1)}, bf16[1,128,2048]{2,1,0:T(8,128)(2,1)}) custom-call(bf16[8,784,128]{2,1,0:T(8,128)(2,1)S(1)} %all-to-all-done.1.within_ref), custom_call_target="tpu_custom_call" | custom-call | bytes 3178496 | tf_op jit(solution)/shard_map/unpack_own/pallas_call | solution.py:410
  93.1 2.8 %collective-permute-done.11.refs_3_ = bf16[2,256,128]{2,1,0:T(8,128)(2,1)S(1)} collective-permute-done((bf16[2,256,128]{2,1,0:T(8,128)(2,1)S(1)}, bf16[2,256,128]{2,1,0:T(8,128)(2,1)S(1)}, u32[]{:S(2)}, u32[]{:S(2)}) %collective-permute-start.11) | collective-permute-done | bytes 131104 | tf_op jit(solution)/shard_map/ppermute | solution.py:1022
  (26 shorter events, 3.9 us)
Async XLA Ops:
  0.6 8.9 %copy-start.3 = (s32[16]{0:T(128)S(1)}, s32[16]{0:T(128)}, u32[]{:S(2)}) copy-start(s32[16]{0:T(128)} %span_ref.1) | copy-start | bytes 196
  0.6 8.9 %copy-start.1 = (s32[1,16,16,1]{2,3,1,0:T(1,128)S(1)}, s32[1,16,16,1]{2,3,1,0:T(1,128)}, u32[]{:S(2)}) copy-start(s32[1,16,16,1]{2,3,1,0:T(1,128)} %param.12) | copy-start | bytes 3076
  0.7 8.9 %copy-start.2 = (f32[16]{0:T(128)S(1)}, f32[16]{0:T(128)}, u32[]{:S(2)}) copy-start(f32[16]{0:T(128)} %softness_ref.1) | copy-start | bytes 196
  3.6 5.4 %copy-start.4 = (bf16[4,256,128]{2,1,0:T(8,128)(2,1)S(1)}, bf16[4,256,128]{2,1,0:T(8,128)(2,1)}, u32[]{:S(2)}) copy-start(bf16[4,256,128]{2,1,0:T(8,128)(2,1)} %get-tuple-element.56) | copy-start | bytes 786436
  3.6 7.3 %copy-start = (bf16[4,256,128]{2,1,0:T(8,128)(2,1)S(1)}, bf16[4,256,128]{2,1,0:T(8,128)(2,1)}, u32[]{:S(2)}) copy-start(bf16[4,256,128]{2,1,0:T(8,128)(2,1)} %get-tuple-element.55.kept_ref) | copy-start | bytes 786436
  3.6 36.7 %all-to-all-start = ((bf16[8,1024,128]{2,1,0:T(8,128)(2,1)}), bf16[8,1024,128]{2,1,0:T(8,128)(2,1)S(1)}, u32[]{:S(2)}, u32[]{:S(2)}) async-start(bf16[8,1024,128]{2,1,0:T(8,128)(2,1)} %get-tuple-element.46), calls=%async_computation | async-start | bytes 4194304 | tf_op jit(solution)/shard_map/all_to_all | solution.py:1052
  9.0 1.9 %collective-permute-start = (bf16[4,256,128]{2,1,0:T(8,128)(2,1)S(1)}, bf16[4,256,128]{2,1,0:T(8,128)(2,1)S(1)}, u32[]{:S(2)}, u32[]{:S(2)}) collective-permute-start(bf16[4,256,128]{2,1,0:T(8,128)(2,1)S(1)} %copy-done.4), channel_id=1, source_target_pairs={{0,2},{2,0},{4,6},{6,4},{8,10},{10,8},{12,14},{14,12},{16,18},{18,... | collective-permute-start | bytes 786440 | tf_op jit(solution)/shard_map/ppermute | solution.py:1011
  11.0 33.6 %collective-permute-start.1 = (bf16[2,256,128]{2,1,0:T(8,128)(2,1)S(1)}, bf16[2,256,128]{2,1,0:T(8,128)(2,1)S(1)}, u32[]{:S(2)}, u32[]{:S(2)}) collective-permute-start(bf16[2,256,128]{2,1,0:T(8,128)(2,1)S(1)} %get-tuple-element.57), channel_id=1, source_target_pairs={{0,16},{2,18},{4,20},{6,22},{8,24},{10,26},{12,28},{14,30},{16,0},... | collective-permute-start | bytes 393224 | tf_op jit(solution)/shard_map/ppermute | solution.py:1022
  13.6 31.0 %collective-permute-start.2 = (bf16[2,256,128]{2,1,0:T(8,128)(2,1)S(1)}, bf16[2,256,128]{2,1,0:T(8,128)(2,1)S(1)}, u32[]{:S(2)}, u32[]{:S(2)}) collective-permute-start(bf16[2,256,128]{2,1,0:T(8,128)(2,1)S(1)} %get-tuple-element.58), channel_id=1, source_target_pairs={{0,20},{2,22},{4,16},{6,18},{8,28},{10,30},{12,24},{14,26},{16,4},... | collective-permute-start | bytes 393224 | tf_op jit(solution)/shard_map/ppermute | solution.py:1022
  15.1 30.6 %collective-permute-start.3 = (bf16[2,256,128]{2,1,0:T(8,128)(2,1)S(1)}, bf16[2,256,128]{2,1,0:T(8,128)(2,1)S(1)}, u32[]{:S(2)}, u32[]{:S(2)}) collective-permute-start(bf16[2,256,128]{2,1,0:T(8,128)(2,1)S(1)} %get-tuple-element.59), channel_id=1, source_target_pairs={{0,24},{2,26},{4,28},{6,30},{8,16},{10,18},{12,20},{14,22},{16,8},... | collective-permute-start | bytes 393224 | tf_op jit(solution)/shard_map/ppermute | solution.py:1022
  18.6 30.3 %collective-permute-start.4 = (bf16[2,256,128]{2,1,0:T(8,128)(2,1)S(1)}, bf16[2,256,128]{2,1,0:T(8,128)(2,1)S(1)}, u32[]{:S(2)}, u32[]{:S(2)}) collective-permute-start(bf16[2,256,128]{2,1,0:T(8,128)(2,1)S(1)} %get-tuple-element.60), channel_id=1, source_target_pairs={{0,28},{2,30},{4,24},{6,26},{8,20},{10,22},{12,16},{14,18},{16,12}... | collective-permute-start | bytes 393224 | tf_op jit(solution)/shard_map/ppermute | solution.py:1022
  51.3 4.9 %collective-permute-start.5 = (f32[8,1024]{1,0:T(8,128)S(1)}, f32[8,1024]{1,0:T(8,128)S(1)}, u32[]{:S(2)}, u32[]{:S(2)}) collective-permute-start(f32[8,1024]{1,0:T(8,128)S(1)} %get-tuple-element.62.message_ref), channel_id=1, source_target_pairs={{0,16},{2,18},{4,20},{6,22},{8,24},{10,26},{12,28},{14,30},{16,0},... | collective-permute-start | bytes 98312 | tf_op jit(solution)/shard_map/ppermute | solution.py:1117
  59.1 29.6 %all-to-all-start.1 = ((bf16[8,784,128]{2,1,0:T(8,128)(2,1)}), bf16[8,784,128]{2,1,0:T(8,128)(2,1)S(1)}, u32[]{:S(2)}, u32[]{:S(2)}) async-start(bf16[8,784,128]{2,1,0:T(8,128)(2,1)} %get-tuple-element.73), calls=%async_computation.1 | async-start | bytes 3211264 | tf_op jit(solution)/shard_map/all_to_all | solution.py:1052
  62.7 1.7 %collective-permute-start.6 = (bf16[4,256,128]{2,1,0:T(8,128)(2,1)S(1)}, bf16[4,256,128]{2,1,0:T(8,128)(2,1)S(1)}, u32[]{:S(2)}, u32[]{:S(2)}) collective-permute-start(bf16[4,256,128]{2,1,0:T(8,128)(2,1)S(1)} %get-tuple-element.75), channel_id=1, source_target_pairs={{0,2},{2,0},{4,6},{6,4},{8,10},{10,8},{12,14},{14,12},{16,18},{18,... | collective-permute-start | bytes 786440 | tf_op jit(solution)/shard_map/ppermute | solution.py:1011
  64.5 28.6 %collective-permute-start.7 = (bf16[2,256,128]{2,1,0:T(8,128)(2,1)S(1)}, bf16[2,256,128]{2,1,0:T(8,128)(2,1)S(1)}, u32[]{:S(2)}, u32[]{:S(2)}) collective-permute-start(bf16[2,256,128]{2,1,0:T(8,128)(2,1)S(1)} %get-tuple-element.76), channel_id=1, source_target_pairs={{0,16},{2,18},{4,20},{6,22},{8,24},{10,26},{12,28},{14,30},{16,0},... | collective-permute-start | bytes 393224 | tf_op jit(solution)/shard_map/ppermute | solution.py:1022
  65.8 27.3 %collective-permute-start.9 = (bf16[2,256,128]{2,1,0:T(8,128)(2,1)S(1)}, bf16[2,256,128]{2,1,0:T(8,128)(2,1)S(1)}, u32[]{:S(2)}, u32[]{:S(2)}) collective-permute-start(bf16[2,256,128]{2,1,0:T(8,128)(2,1)S(1)} %get-tuple-element.78), channel_id=1, source_target_pairs={{0,20},{2,22},{4,16},{6,18},{8,28},{10,30},{12,24},{14,26},{16,4},... | collective-permute-start | bytes 393224 | tf_op jit(solution)/shard_map/ppermute | solution.py:1022
  68.6 24.5 %collective-permute-start.10 = (bf16[2,256,128]{2,1,0:T(8,128)(2,1)S(1)}, bf16[2,256,128]{2,1,0:T(8,128)(2,1)S(1)}, u32[]{:S(2)}, u32[]{:S(2)}) collective-permute-start(bf16[2,256,128]{2,1,0:T(8,128)(2,1)S(1)} %get-tuple-element.79), channel_id=1, source_target_pairs={{0,24},{2,26},{4,28},{6,30},{8,16},{10,18},{12,20},{14,22},{16,8},... | collective-permute-start | bytes 393224 | tf_op jit(solution)/shard_map/ppermute | solution.py:1022
  70.9 25.1 %collective-permute-start.11 = (bf16[2,256,128]{2,1,0:T(8,128)(2,1)S(1)}, bf16[2,256,128]{2,1,0:T(8,128)(2,1)S(1)}, u32[]{:S(2)}, u32[]{:S(2)}) collective-permute-start(bf16[2,256,128]{2,1,0:T(8,128)(2,1)S(1)} %get-tuple-element.80), channel_id=1, source_target_pairs={{0,28},{2,30},{4,24},{6,26},{8,20},{10,22},{12,16},{14,18},{16,12}... | collective-permute-start | bytes 393224 | tf_op jit(solution)/shard_map/ppermute | solution.py:1022
  88.8 3.7 %collective-permute-start.8 = (f32[16,128]{1,0:T(8,128)S(1)}, f32[16,128]{1,0:T(8,128)S(1)}, u32[]{:S(2)}, u32[]{:S(2)}) collective-permute-start(f32[16,128]{1,0:T(8,128)S(1)} %temper_sums.1), channel_id=1, source_target_pairs={{0,1},{1,0},{2,3},{3,2},{4,5},{5,4},{6,7},{7,6},{8,9},{9,8},{10,11... | collective-permute-start | bytes 24584 | tf_op jit(solution)/shard_map/ppermute | solution.py:1159

commit v16 on v14

--- a/solution.py
+++ b/solution.py
@@ -843,7 +843,7 @@
 ):
     del begun_ref
     chunk_refs = refs[:2]
-    across, ready, tail, ready_sem, tail_sem, *scratch = refs[2:]
+    across, ready, ready_sem, *scratch = refs[2:]
     _, half, place = position(half_count)
     leaving = sends(ready, within_ref, ready_sem, half * 3)
     sent, came = rows_at(message_ref, 0), rows_at(received_ref, 0)
@@ -854,12 +854,6 @@
     own = mine + jnp.where(half == 0, shared, received_ref[6:7, :HD])
     other = theirs + jnp.where(half == 0, message_ref[6:7, :HD], shared)
     pieces = temper_rows(own, other)
-    for block in range(half_count):
-        tail[block] = pieces
-    leaving.append(
-        pltpu.make_async_copy(tail, within_ref.at[:, 6 * BLK : 6 * BLK + EXTRA, :], tail_sem)
-    )
-    leaving[-1].start()
 
     def chunks():
         for core, chunk_ref in enumerate(chunk_refs):
@@ -886,7 +880,7 @@
         )
         for step, chunk_ref, rows in chunks():
             chunk_ref[step, :BLK, :] = across[rows, :]
-            chunk_ref[step, BLK:, :] = jnp.zeros((BLK, HD), jnp.bfloat16)
+            chunk_ref[step, BLK : 2 * BLK, :] = jnp.zeros((BLK, HD), jnp.bfloat16)
 
     @pl.when(half == 1)
     def _():
@@ -902,31 +896,36 @@
         )
         for step, chunk_ref, rows in chunks():
             chunk_ref[step, :BLK, :] = across_ref[0, rows, :]
-            chunk_ref[step, BLK:, :] = across_ref[1, rows, :]
-
+            chunk_ref[step, BLK : 2 * BLK, :] = across_ref[1, rows, :]
+
+    for step, chunk_ref, _ in chunks():
+        chunk_ref[step, 2 * BLK :, :] = pieces
     for copy in leaving:
         copy.wait()
 
 
-def temper_kernel(within_ref, temper_ref, *, half_count):
-    _, half, _ = position(half_count)
-    for peer in range(half_count):
-        for slot, base in enumerate((half * half_count, (1 - half) * half_count)):
-            rows = within_ref[peer, 3 * slot : 3 * slot + 3, :].astype(jnp.float32)
-            temper_ref[pl.ds(base + peer, 1), :] = jnp.sum(rows, axis=0, keepdims=True)
-
-
-def temper_sums(within, half_count):
-    last = 6 * BLK // EXTRA
+def temper_kernel(*refs, half_count):
+    across_refs, temper_ref = refs[:-1], refs[-1]
+    _, half, place = position(half_count)
+    for step, across_ref in enumerate(across_refs):
+        for core in range(2):
+            peer = place ^ core ^ (2 * step)
+            for slot, base in enumerate(((1 - half) * half_count, half * half_count)):
+                rows = across_ref[core, 3 * slot : 3 * slot + 3, :].astype(jnp.float32)
+                temper_ref[pl.ds(base + peer, 1), :] = jnp.sum(rows, axis=0, keepdims=True)
+
+
+def temper_sums(across, half_count):
+    last = 2 * BLK // EXTRA
     return pl.pallas_call(
         functools.partial(temper_kernel, half_count=half_count),
         grid=(1,),
         out_shape=jax.ShapeDtypeStruct((2 * half_count, HD), jnp.float32),
-        in_specs=[pl.BlockSpec((half_count, EXTRA, HD), lambda step: (0, last, 0))],
+        in_specs=[pl.BlockSpec((2, EXTRA, HD), lambda step: (0, last, 0))] * len(across),
         out_specs=pl.BlockSpec((2 * half_count, HD), lambda step: (0, 0)),
         compiler_params=pltpu.CompilerParams(vmem_limit_bytes=4 * MIB),
         name="temper_sums",
-    )(within)
+    )(*across)
 
 
 def unpack_kernel(within_ref, *refs, half_count):
@@ -1069,7 +1068,7 @@
     )
     swap = [(source, source ^ half_count) for source in range(seq_count)]
     received = lax.ppermute(message, "seq", swap)
-    result = pltpu.HBM((half_count, 6 * BLK + EXTRA, HD), jnp.bfloat16)
+    result = pltpu.HBM((half_count, 6 * BLK, HD), jnp.bfloat16)
     ready = pltpu.VMEM((half_count, 3 * BLK, HD), jnp.bfloat16)
     across, begun = call(
         first_kernel,
@@ -1093,11 +1092,10 @@
         "gradients_after_totals",
         operands,
         [result]
-        + [jax.ShapeDtypeStruct((half_count // 2, 2 * BLK, HD), jnp.bfloat16)] * 2,
+        + [jax.ShapeDtypeStruct((half_count // 2, 2 * BLK + EXTRA, HD), jnp.bfloat16)] * 2,
         [
             pltpu.VMEM((tokens, HD), jnp.bfloat16), ready,
-            pltpu.VMEM((half_count, EXTRA, HD), jnp.bfloat16),
-            pltpu.SemaphoreType.DMA((3,)), pltpu.SemaphoreType.DMA, *lows,
+            pltpu.SemaphoreType.DMA((3,)), *lows,
         ],
         2 * pair_flops,
         16,
@@ -1105,12 +1103,15 @@
         last_in_place=True,
     )
     across = crossed(*foreign, half_count)
+    across[0], within = lax.optimization_barrier((across[0], within))
     within = exchange_within(within)
-    tempers = temper_sums(within, half_count)
+    tempers = temper_sums(across, half_count)
     temper_total = tempers
     for step in range(1, dp_count):
         swap = [(source, (source + step) % dp_count) for source in range(dp_count)]
         temper_total = temper_total + lax.ppermute(tempers, "dp", swap)
+    temper = temper_total[:, 0] / (dp_count * BLK * seq_count)
+    within, temper = lax.optimization_barrier((within, temper))
     outs = kernel_call(
         functools.partial(unpack_kernel, half_count=half_count),
         "unpack_heads",
@@ -1120,7 +1121,7 @@
         [],
         10,
     )
-    return (*outs, temper_total[:, 0] / (dp_count * BLK * seq_count))
+    return (*outs, temper)
 
 
 def shards(

time: 98.4 us -> 111 us (1.13)
  waiting for transfers between devices: 52.6 us -> 67.2 us
  starting transfers between devices: 26.9 us -> 25.2 us
    ppermute x8, waiting for transfers between devices: 9.82 us -> 38.7 us  [crossed(): lax.ppermute(message, 'seq', [(source, source ^ half_count + 2 * step) fo...]
    all_to_all x2, waiting for transfers between devices: 38.2 us -> 21.7 us  [exchange_within(): lax.all_to_all(array_in, 'seq', split_axis=0, concat_axis=0, axis_index_g...]
    ppermute x1, waiting for transfers between devices: 0.01 us -> 2.16 us  [head_shards(): temper_total = temper_total + lax.ppermute(tempers, 'dp', swap)]
    ppermute x8, starting transfers between devices: 15.4 us -> 14 us  [crossed(): lax.ppermute(message, 'seq', [(source, source ^ half_count + 2 * step) fo...]
  transfers between devices with their start and end apart: 14 -> 14, of which waited for: 9 -> 11; matrix products, arithmetic and copies ran while one was open for 0% -> 1% of each run, Pallas kernels for 9% -> 7%
where the time goes in v16:
time: 111 us
  waiting for transfers between devices  67.2 us (61%)
  starting transfers between devices  25.2 us (23%)
  Pallas kernels  17.1 us (15%)
    ppermute x8, waiting for transfers between devices, crossed(): lax.ppermute(message, 'seq', [(source, source ^ half_count + 2 * step) fo...  38.7 us
    all_to_all x2, waiting for transfers between devices, exchange_within(): lax.all_to_all(array_in, 'seq', split_axis=0, concat_axis=0, axis_index_g...  21.7 us
    pallas_call x9, Pallas kernels, kernel_call(): pl.pallas_call(kernel, out_shape=out_shape, in_specs=in_specs, out_specs=...  17.1 us
    ppermute x8, starting transfers between devices, crossed(): lax.ppermute(message, 'seq', [(source, source ^ half_count + 2 * step) fo...  14 us
    all_to_all x2, starting transfers between devices, exchange_within(): lax.all_to_all(array_in, 'seq', split_axis=0, concat_axis=0, axis_index_g...  8.98 us
    ppermute x1, waiting for transfers between devices, head_shards(): received = lax.ppermute(message, 'seq', swap)  2.82 us
  transfers between devices with their start and end apart: 14, of which 11 were waited for; matrix products, arithmetic and copies ran while one was open for 1% of the time, Pallas kernels for 7%

profile of v16, /device:TPU:0, one launch (start us, length us, event | category | flops | bytes accessed | tf_op | source)
XLA Modules:
  0.0 111.0 jit_solution(10043114730966174604)
XLA Ops:
  0.7 2.9 %pack_heads.1 = (bf16[8,1024,128]{2,1,0:T(8,128)(2,1)}, bf16[4,256,128]{2,1,0:T(8,128)(2,1)}, bf16[4,256,128]{2,1,0:T(8,128)(2,1)}) custom-call(bf16[1,128,2048]{2,1,0:T(8,128)(2,1)} %refs_0_.1, bf16[1,128,2048]{2,1,0:T(8,128)(2,1)} %refs_1_.1, bf16[1,128,2048]{2,1,0:T(8,128)(2,1)} %refs_2_.1, bf16[1,128,2048]{2,1,0:T(8,128)(2,1)} %refs_3_.1), custom_call_target="tpu_custom_call" | custom-call | bytes 4718592 | tf_op jit(solution)/shard_map/pack_heads/pallas_call | solution.py:410
  3.6 5.4 %all-to-all-start = ((bf16[8,1024,128]{2,1,0:T(8,128)(2,1)}), bf16[8,1024,128]{2,1,0:T(8,128)(2,1)S(1)}, u32[]{:S(2)}, u32[]{:S(2)}) async-start(bf16[8,1024,128]{2,1,0:T(8,128)(2,1)} %get-tuple-element.45), calls=%async_computation | async-start | bytes 4194304 | tf_op jit(solution)/shard_map/all_to_all | solution.py:1005
  11.0 2.7 %collective-permute-start.1 = (bf16[2,256,128]{2,1,0:T(8,128)(2,1)S(1)}, bf16[2,256,128]{2,1,0:T(8,128)(2,1)S(1)}, u32[]{:S(2)}, u32[]{:S(2)}) collective-permute-start(bf16[2,256,128]{2,1,0:T(8,128)(2,1)S(1)} %get-tuple-element.56), channel_id=1, source_target_pairs={{0,16},{2,18},{4,20},{6,22},{8,24},{10,26},{12,28},{14,30},{16,0},... | collective-permute-start | bytes 393224 | tf_op jit(solution)/shard_map/ppermute | solution.py:975
  13.6 1.5 %collective-permute-start.2 = (bf16[2,256,128]{2,1,0:T(8,128)(2,1)S(1)}, bf16[2,256,128]{2,1,0:T(8,128)(2,1)S(1)}, u32[]{:S(2)}, u32[]{:S(2)}) collective-permute-start(bf16[2,256,128]{2,1,0:T(8,128)(2,1)S(1)} %get-tuple-element.57), channel_id=1, source_target_pairs={{0,20},{2,22},{4,16},{6,18},{8,28},{10,30},{12,24},{14,26},{16,4},... | collective-permute-start | bytes 393224 | tf_op jit(solution)/shard_map/ppermute | solution.py:975
  15.1 3.5 %collective-permute-start.3 = (bf16[2,256,128]{2,1,0:T(8,128)(2,1)S(1)}, bf16[2,256,128]{2,1,0:T(8,128)(2,1)S(1)}, u32[]{:S(2)}, u32[]{:S(2)}) collective-permute-start(bf16[2,256,128]{2,1,0:T(8,128)(2,1)S(1)} %get-tuple-element.58), channel_id=1, source_target_pairs={{0,24},{2,26},{4,28},{6,30},{8,16},{10,18},{12,20},{14,22},{16,8},... | collective-permute-start | bytes 393224 | tf_op jit(solution)/shard_map/ppermute | solution.py:975
  18.7 21.7 %all-to-all-done = bf16[8,1024,128]{2,1,0:T(8,128)(2,1)S(1)} async-done(((bf16[8,1024,128]{2,1,0:T(8,128)(2,1)}), bf16[8,1024,128]{2,1,0:T(8,128)(2,1)S(1)}, u32[]{:S(2)}, u32[]{:S(2)}) %all-to-all-start) | async-done | bytes 2097184 | tf_op jit(solution)/shard_map/all_to_all | solution.py:1005
  40.4 4.3 %diagonal_statistics.1 = (f32[16,1024]{1,0:T(8,128)S(1)}, f32[3,1024,128]{2,1,0:T(8,128)S(1)}, f32[1024,1024]{1,0:T(8,128)S(1)}, f32[1024,1024]{1,0:T(8,128)S(1)...) custom-call(bf16[8,8,128,128]{3,2,1,0:T(8,128)(2,1)S(1)} %bitcast.2, f32[8,256]{1,0:T(8,128)S(1)} %get-tuple-element.50.scales_ref, ...), custom_call_target="tpu_custom_call" | custom-call | flops 536870912 | bytes 20627456 | tf_op jit(solution)/shard_map/diagonal_statistics/pallas_call | solution.py:410
  45.7 3.2 %collective-permute-done.4.refs_3_ = bf16[2,256,128]{2,1,0:T(8,128)(2,1)S(1)} collective-permute-done((bf16[2,256,128]{2,1,0:T(8,128)(2,1)S(1)}, bf16[2,256,128]{2,1,0:T(8,128)(2,1)S(1)}, u32[]{:S(2)}, u32[]{:S(2)}) %collective-permute-start.4) | collective-permute-done | bytes 131104 | tf_op jit(solution)/shard_map/ppermute | solution.py:975
  48.9 2.4 %square_statistics.1 = (bf16[4,1024,128]{2,1,0:T(8,128)(2,1)S(1)}, f32[8,1024]{1,0:T(8,128)S(1)}, f32[8,1024]{1,0:T(8,128)S(1)}, f32[1024,1024]{1,0:T(8,128)S(1)}, f32[1024,1024]{1,0:T(8,128)S(1)}) custom-call(bf16[8,8,128,128]{3,2,1,0:T(8,128)(2,1)S(1)} %bitcast.3, f32[8,256]{1,0:T(8,128)S(1)} %get-tuple-element.50.scales_ref, ...), custom_call_target="tpu_custom_call" | custom-call | flops 536870912 | bytes 12304384 | tf_op jit(solution)/shard_map/square_statistics/pallas_call | solution.py:410
  51.4 2.0 %gradients_before_totals.1 = (bf16[2,1024,128]{2,1,0:T(8,128)(2,1)S(1)}, bf16[8,768,128]{2,1,0:T(8,128)(2,1)}) custom-call(bf16[8,8,128,128]{3,2,1,0:T(8,128)(2,1)S(1)} %bitcast.4, f32[8,256]{1,0:T(8,128)S(1)} %get-tuple-element.50.scales_ref, bf16[4,1024,128]{2,1,0:T(8,128)(2,1)S(1)} %get-tuple-element.60.square_ref, ...), custom_call_target="tpu_custom_call" | custom-call | flops 1073741824 | bytes 30515200 | tf_op jit(solution)/shard_map/gradients_before_totals/pallas_call | solution.py:410
  53.4 2.8 %collective-permute-done.5.received_ref = f32[8,1024]{1,0:T(8,128)S(1)} collective-permute-done((f32[8,1024]{1,0:T(8,128)S(1)}, f32[8,1024]{1,0:T(8,128)S(1)}, u32[]{:S(2)}, u32[]{:S(2)}) %collective-permute-start.5) | collective-permute-done | bytes 32800 | tf_op jit(solution)/shard_map/ppermute | solution.py:1070
  56.3 2.8 %gradients_after_totals.1 = (bf16[8,768,128]{2,1,0:T(8,128)(2,1)}, bf16[4,272,128]{2,1,0:T(8,128)(2,1)S(1)}, bf16[4,272,128]{2,1,0:T(8,128)(2,1)S(1)}) custom-call(bf16[8,8,128,128]{3,2,1,0:T(8,128)(2,1)S(1)} %bitcast.5, f32[8,256]{1,0:T(8,128)S(1)} %get-tuple-element.50.scales_ref, ...), custom_call_target="tpu_custom_call", output_to_operand_aliasing={{0}: (13, {})} | custom-call | flops 536870912 | bytes 25894912 | tf_op jit(solution)/shard_map/gradients_after_totals/pallas_call | solution.py:410
  59.2 1.5 %collective-permute-done.6.taken_ref = bf16[4,272,128]{2,1,0:T(8,128)(2,1)S(1)} collective-permute-done((bf16[4,272,128]{2,1,0:T(8,128)(2,1)S(1)}, bf16[4,272,128]{2,1,0:T(8,128)(2,1)S(1)}, u32[]{:S(2)}, u32[]{:S(2)}) %collective-permute-start.6) | collective-permute-done | bytes 278560 | tf_op jit(solution)/shard_map/ppermute | solution.py:964
  60.8 1.1 %collective-permute-start.7 = (bf16[2,272,128]{2,1,0:T(8,128)(2,1)S(1)}, bf16[2,272,128]{2,1,0:T(8,128)(2,1)S(1)}, u32[]{:S(2)}, u32[]{:S(2)}) collective-permute-start(bf16[2,272,128]{2,1,0:T(8,128)(2,1)S(1)} %get-tuple-element.74), channel_id=1, source_target_pairs={{0,16},{2,18},{4,20},{6,22},{8,24},{10,26},{12,28},{14,30},{16,0},... | collective-permute-start | bytes 417800 | tf_op jit(solution)/shard_map/ppermute | solution.py:975
  61.9 8.3 %collective-permute-done.7.refs_0_ = bf16[2,272,128]{2,1,0:T(8,128)(2,1)S(1)} collective-permute-done((bf16[2,272,128]{2,1,0:T(8,128)(2,1)S(1)}, bf16[2,272,128]{2,1,0:T(8,128)(2,1)S(1)}, u32[]{:S(2)}, u32[]{:S(2)}) %collective-permute-start.7) | collective-permute-done | bytes 139296 | tf_op jit(solution)/shard_map/ppermute | solution.py:975
  70.2 3.6 %all-to-all-start.1 = ((bf16[8,768,128]{2,1,0:T(8,128)(2,1)}), bf16[8,768,128]{2,1,0:T(8,128)(2,1)S(1)}, u32[]{:S(2)}, u32[]{:S(2)}) async-start(bf16[8,768,128]{2,1,0:T(8,128)(2,1)} %get-tuple-element.76), calls=%async_computation.1 | async-start | bytes 3145728 | tf_op jit(solution)/shard_map/all_to_all | solution.py:1005
  73.8 1.9 %collective-permute-start.8 = (bf16[2,272,128]{2,1,0:T(8,128)(2,1)S(1)}, bf16[2,272,128]{2,1,0:T(8,128)(2,1)S(1)}, u32[]{:S(2)}, u32[]{:S(2)}) collective-permute-start(bf16[2,272,128]{2,1,0:T(8,128)(2,1)S(1)} %get-tuple-element.78), channel_id=1, source_target_pairs={{0,20},{2,22},{4,16},{6,18},{8,28},{10,30},{12,24},{14,26},{16,4},... | collective-permute-start | bytes 417800 | tf_op jit(solution)/shard_map/ppermute | solution.py:975
  75.7 3.4 %collective-permute-start.9 = (bf16[2,272,128]{2,1,0:T(8,128)(2,1)S(1)}, bf16[2,272,128]{2,1,0:T(8,128)(2,1)S(1)}, u32[]{:S(2)}, u32[]{:S(2)}) collective-permute-start(bf16[2,272,128]{2,1,0:T(8,128)(2,1)S(1)} %get-tuple-element.79), channel_id=1, source_target_pairs={{0,24},{2,26},{4,28},{6,30},{8,16},{10,18},{12,20},{14,22},{16,8},... | collective-permute-start | bytes 417800 | tf_op jit(solution)/shard_map/ppermute | solution.py:975
  79.0 16.1 %collective-permute-done.8.refs_1_ = bf16[2,272,128]{2,1,0:T(8,128)(2,1)S(1)} collective-permute-done((bf16[2,272,128]{2,1,0:T(8,128)(2,1)S(1)}, bf16[2,272,128]{2,1,0:T(8,128)(2,1)S(1)}, u32[]{:S(2)}, u32[]{:S(2)}) %collective-permute-start.8) | collective-permute-done | bytes 139296 | tf_op jit(solution)/shard_map/ppermute | solution.py:975
  95.2 5.8 %collective-permute-done.9.refs_2_ = bf16[2,272,128]{2,1,0:T(8,128)(2,1)S(1)} collective-permute-done((bf16[2,272,128]{2,1,0:T(8,128)(2,1)S(1)}, bf16[2,272,128]{2,1,0:T(8,128)(2,1)S(1)}, u32[]{:S(2)}, u32[]{:S(2)}) %collective-permute-start.9) | collective-permute-done | bytes 139296 | tf_op jit(solution)/shard_map/ppermute | solution.py:975
  100.9 4.2 %collective-permute-done.10.refs_3_ = bf16[2,272,128]{2,1,0:T(8,128)(2,1)S(1)} collective-permute-done((bf16[2,272,128]{2,1,0:T(8,128)(2,1)S(1)}, bf16[2,272,128]{2,1,0:T(8,128)(2,1)S(1)}, u32[]{:S(2)}, u32[]{:S(2)}) %collective-permute-start.10) | collective-permute-done | bytes 139296 | tf_op jit(solution)/shard_map/ppermute | solution.py:975
  105.1 1.6 %collective-permute-start.11 = (f32[16,128]{1,0:T(8,128)S(1)}, f32[16,128]{1,0:T(8,128)S(1)}, u32[]{:S(2)}, u32[]{:S(2)}) collective-permute-start(f32[16,128]{1,0:T(8,128)S(1)} %temper_sums.1), channel_id=1, source_target_pairs={{0,1},{1,0},{2,3},{3,2},{4,5},{5,4},{6,7},{7,6},{8,9},{9,8},{10,11... | collective-permute-start | bytes 24584 | tf_op jit(solution)/shard_map/ppermute | solution.py:1112
  106.7 2.2 %collective-permute-done.11 = f32[16,128]{1,0:T(8,128)S(1)} collective-permute-done((f32[16,128]{1,0:T(8,128)S(1)}, f32[16,128]{1,0:T(8,128)S(1)}, u32[]{:S(2)}, u32[]{:S(2)}) %collective-permute-start.11) | collective-permute-done | bytes 8224 | tf_op jit(solution)/shard_map/ppermute | solution.py:1112
  109.5 1.5 %unpack_heads.1 = (bf16[1,128,2048]{2,1,0:T(8,128)(2,1)}, bf16[1,128,2048]{2,1,0:T(8,128)(2,1)}, bf16[1,128,2048]{2,1,0:T(8,128)(2,1)}) custom-call(bf16[8,768,128]{2,1,0:T(8,128)(2,1)S(1)} %all-to-all-done.1.within_ref, bf16[2,272,128]{2,1,0:T(8,128)(2,1)S(1)} %collective-permute-done.7.refs_0_, bf16[2,272,128]{2,1,0:T(8,128)(2,1)S(1)} %collective-permute-done.8.refs_1_, ...), custom_call_target="tpu_custom_call" | custom-call | bytes 3702784 | tf_op jit(solution)/shard_map/unpack_heads/pallas_call | solution.py:410
  (25 shorter events, 3.9 us)
Async XLA Ops:
  0.6 8.9 %copy-start.3 = (s32[16]{0:T(128)S(1)}, s32[16]{0:T(128)}, u32[]{:S(2)}) copy-start(s32[16]{0:T(128)} %span_ref.1) | copy-start | bytes 196
  0.6 8.9 %copy-start.1 = (s32[1,16,16,1]{2,3,1,0:T(1,128)S(1)}, s32[1,16,16,1]{2,3,1,0:T(1,128)}, u32[]{:S(2)}) copy-start(s32[1,16,16,1]{2,3,1,0:T(1,128)} %param.12) | copy-start | bytes 3076
  0.7 8.9 %copy-start.2 = (f32[16]{0:T(128)S(1)}, f32[16]{0:T(128)}, u32[]{:S(2)}) copy-start(f32[16]{0:T(128)} %softness_ref.1) | copy-start | bytes 196
  3.6 5.4 %copy-start.4 = (bf16[4,256,128]{2,1,0:T(8,128)(2,1)S(1)}, bf16[4,256,128]{2,1,0:T(8,128)(2,1)}, u32[]{:S(2)}) copy-start(bf16[4,256,128]{2,1,0:T(8,128)(2,1)} %get-tuple-element.55) | copy-start | bytes 786436
  3.6 7.3 %copy-start = (bf16[4,256,128]{2,1,0:T(8,128)(2,1)S(1)}, bf16[4,256,128]{2,1,0:T(8,128)(2,1)}, u32[]{:S(2)}) copy-start(bf16[4,256,128]{2,1,0:T(8,128)(2,1)} %get-tuple-element.54.kept_ref) | copy-start | bytes 786436
  3.6 36.7 %all-to-all-start = ((bf16[8,1024,128]{2,1,0:T(8,128)(2,1)}), bf16[8,1024,128]{2,1,0:T(8,128)(2,1)S(1)}, u32[]{:S(2)}, u32[]{:S(2)}) async-start(bf16[8,1024,128]{2,1,0:T(8,128)(2,1)} %get-tuple-element.45), calls=%async_computation | async-start | bytes 4194304 | tf_op jit(solution)/shard_map/all_to_all | solution.py:1005
  9.0 1.9 %collective-permute-start = (bf16[4,256,128]{2,1,0:T(8,128)(2,1)S(1)}, bf16[4,256,128]{2,1,0:T(8,128)(2,1)S(1)}, u32[]{:S(2)}, u32[]{:S(2)}) collective-permute-start(bf16[4,256,128]{2,1,0:T(8,128)(2,1)S(1)} %copy-done.4), channel_id=1, source_target_pairs={{0,2},{2,0},{4,6},{6,4},{8,10},{10,8},{12,14},{14,12},{16,18},{18,... | collective-permute-start | bytes 786440 | tf_op jit(solution)/shard_map/ppermute | solution.py:964
  11.0 33.6 %collective-permute-start.1 = (bf16[2,256,128]{2,1,0:T(8,128)(2,1)S(1)}, bf16[2,256,128]{2,1,0:T(8,128)(2,1)S(1)}, u32[]{:S(2)}, u32[]{:S(2)}) collective-permute-start(bf16[2,256,128]{2,1,0:T(8,128)(2,1)S(1)} %get-tuple-element.56), channel_id=1, source_target_pairs={{0,16},{2,18},{4,20},{6,22},{8,24},{10,26},{12,28},{14,30},{16,0},... | collective-permute-start | bytes 393224 | tf_op jit(solution)/shard_map/ppermute | solution.py:975
  13.6 31.0 %collective-permute-start.2 = (bf16[2,256,128]{2,1,0:T(8,128)(2,1)S(1)}, bf16[2,256,128]{2,1,0:T(8,128)(2,1)S(1)}, u32[]{:S(2)}, u32[]{:S(2)}) collective-permute-start(bf16[2,256,128]{2,1,0:T(8,128)(2,1)S(1)} %get-tuple-element.57), channel_id=1, source_target_pairs={{0,20},{2,22},{4,16},{6,18},{8,28},{10,30},{12,24},{14,26},{16,4},... | collective-permute-start | bytes 393224 | tf_op jit(solution)/shard_map/ppermute | solution.py:975
  15.1 30.6 %collective-permute-start.3 = (bf16[2,256,128]{2,1,0:T(8,128)(2,1)S(1)}, bf16[2,256,128]{2,1,0:T(8,128)(2,1)S(1)}, u32[]{:S(2)}, u32[]{:S(2)}) collective-permute-start(bf16[2,256,128]{2,1,0:T(8,128)(2,1)S(1)} %get-tuple-element.58), channel_id=1, source_target_pairs={{0,24},{2,26},{4,28},{6,30},{8,16},{10,18},{12,20},{14,22},{16,8},... | collective-permute-start | bytes 393224 | tf_op jit(solution)/shard_map/ppermute | solution.py:975
  18.6 30.3 %collective-permute-start.4 = (bf16[2,256,128]{2,1,0:T(8,128)(2,1)S(1)}, bf16[2,256,128]{2,1,0:T(8,128)(2,1)S(1)}, u32[]{:S(2)}, u32[]{:S(2)}) collective-permute-start(bf16[2,256,128]{2,1,0:T(8,128)(2,1)S(1)} %get-tuple-element.59), channel_id=1, source_target_pairs={{0,28},{2,30},{4,24},{6,26},{8,20},{10,22},{12,16},{14,18},{16,12}... | collective-permute-start | bytes 393224 | tf_op jit(solution)/shard_map/ppermute | solution.py:975
  51.3 4.9 %collective-permute-start.5 = (f32[8,1024]{1,0:T(8,128)S(1)}, f32[8,1024]{1,0:T(8,128)S(1)}, u32[]{:S(2)}, u32[]{:S(2)}) collective-permute-start(f32[8,1024]{1,0:T(8,128)S(1)} %get-tuple-element.61.message_ref), channel_id=1, source_target_pairs={{0,16},{2,18},{4,20},{6,22},{8,24},{10,26},{12,28},{14,30},{16,0},... | collective-permute-start | bytes 98312 | tf_op jit(solution)/shard_map/ppermute | solution.py:1070
  59.1 1.6 %collective-permute-start.6 = (bf16[4,272,128]{2,1,0:T(8,128)(2,1)S(1)}, bf16[4,272,128]{2,1,0:T(8,128)(2,1)S(1)}, u32[]{:S(2)}, u32[]{:S(2)}) collective-permute-start(bf16[4,272,128]{2,1,0:T(8,128)(2,1)S(1)} %get-tuple-element.73), channel_id=1, source_target_pairs={{0,2},{2,0},{4,6},{6,4},{8,10},{10,8},{12,14},{14,12},{16,18},{18,... | collective-permute-start | bytes 835592 | tf_op jit(solution)/shard_map/ppermute | solution.py:964
  60.8 9.5 %collective-permute-start.7 = (bf16[2,272,128]{2,1,0:T(8,128)(2,1)S(1)}, bf16[2,272,128]{2,1,0:T(8,128)(2,1)S(1)}, u32[]{:S(2)}, u32[]{:S(2)}) collective-permute-start(bf16[2,272,128]{2,1,0:T(8,128)(2,1)S(1)} %get-tuple-element.74), channel_id=1, source_target_pairs={{0,16},{2,18},{4,20},{6,22},{8,24},{10,26},{12,28},{14,30},{16,0},... | collective-permute-start | bytes 417800 | tf_op jit(solution)/shard_map/ppermute | solution.py:975
  70.2 39.2 %all-to-all-start.1 = ((bf16[8,768,128]{2,1,0:T(8,128)(2,1)}), bf16[8,768,128]{2,1,0:T(8,128)(2,1)S(1)}, u32[]{:S(2)}, u32[]{:S(2)}) async-start(bf16[8,768,128]{2,1,0:T(8,128)(2,1)} %get-tuple-element.76), calls=%async_computation.1 | async-start | bytes 3145728 | tf_op jit(solution)/shard_map/all_to_all | solution.py:1005
  73.8 21.3 %collective-permute-start.8 = (bf16[2,272,128]{2,1,0:T(8,128)(2,1)S(1)}, bf16[2,272,128]{2,1,0:T(8,128)(2,1)S(1)}, u32[]{:S(2)}, u32[]{:S(2)}) collective-permute-start(bf16[2,272,128]{2,1,0:T(8,128)(2,1)S(1)} %get-tuple-element.78), channel_id=1, source_target_pairs={{0,20},{2,22},{4,16},{6,18},{8,28},{10,30},{12,24},{14,26},{16,4},... | collective-permute-start | bytes 417800 | tf_op jit(solution)/shard_map/ppermute | solution.py:975
  75.7 25.2 %collective-permute-start.9 = (bf16[2,272,128]{2,1,0:T(8,128)(2,1)S(1)}, bf16[2,272,128]{2,1,0:T(8,128)(2,1)S(1)}, u32[]{:S(2)}, u32[]{:S(2)}) collective-permute-start(bf16[2,272,128]{2,1,0:T(8,128)(2,1)S(1)} %get-tuple-element.79), channel_id=1, source_target_pairs={{0,24},{2,26},{4,28},{6,30},{8,16},{10,18},{12,20},{14,22},{16,8},... | collective-permute-start | bytes 417800 | tf_op jit(solution)/shard_map/ppermute | solution.py:975
  79.0 26.1 %collective-permute-start.10 = (bf16[2,272,128]{2,1,0:T(8,128)(2,1)S(1)}, bf16[2,272,128]{2,1,0:T(8,128)(2,1)S(1)}, u32[]{:S(2)}, u32[]{:S(2)}) collective-permute-start(bf16[2,272,128]{2,1,0:T(8,128)(2,1)S(1)} %get-tuple-element.80), channel_id=1, source_target_pairs={{0,28},{2,30},{4,24},{6,26},{8,20},{10,22},{12,16},{14,18},{16,12}... | collective-permute-start | bytes 417800 | tf_op jit(solution)/shard_map/ppermute | solution.py:975
  105.1 3.7 %collective-permute-start.11 = (f32[16,128]{1,0:T(8,128)S(1)}, f32[16,128]{1,0:T(8,128)S(1)}, u32[]{:S(2)}, u32[]{:S(2)}) collective-permute-start(f32[16,128]{1,0:T(8,128)S(1)} %temper_sums.1), channel_id=1, source_target_pairs={{0,1},{1,0},{2,3},{3,2},{4,5},{5,4},{6,7},{7,6},{8,9},{9,8},{10,11... | collective-permute-start | bytes 24584 | tf_op jit(solution)/shard_map/ppermute | solution.py:1112

commit v17 on v15

--- a/solution.py
+++ b/solution.py
@@ -1018,12 +1018,11 @@
         [],
         4,
     )
-    return [
-        lax.ppermute(
-            message, "seq", [(source, source ^ (half_count + 2 * step)) for source in devices]
-        )
-        for step, message in enumerate(messages)
-    ]
+    received = {}
+    for step in reversed(range(steps)):
+        pairs = [(source, source ^ (half_count + 2 * step)) for source in devices]
+        received[step] = lax.ppermute(messages[step], "seq", pairs)
+    return [received[step] for step in range(steps)]
 
 
 def head_shards(

time: 97.3 us -> 97.3 us (level)
  no operation moved by 1% of the time
where the time goes in v17:
time: 97.3 us; the launch traced here: 97 us
  waiting for transfers between devices  50.5 us (52%)
  starting transfers between devices  27 us (28%)
  Pallas kernels  17.9 us (18%)
    all_to_all x2, waiting for transfers between devices, exchange_within(): lax.all_to_all(array_in, 'seq', split_axis=0, concat_axis=0, axis_index_g...  38.2 us
    pallas_call x10, Pallas kernels, kernel_call(): pl.pallas_call(kernel, out_shape=out_shape, in_specs=in_specs, out_specs=...  17.9 us
    ppermute x8, starting transfers between devices, crossed(): received[step] = lax.ppermute(messages[step], 'seq', pairs)  15.4 us
    all_to_all x2, starting transfers between devices, exchange_within(): lax.all_to_all(array_in, 'seq', split_axis=0, concat_axis=0, axis_index_g...  8.99 us
    ppermute x8, waiting for transfers between devices, crossed(): received[step] = lax.ppermute(messages[step], 'seq', pairs)  7.07 us
    ppermute x1, waiting for transfers between devices, head_shards(): received = lax.ppermute(message, 'seq', swap)  2.81 us
  transfers between devices with their start and end apart: 14, of which 9 were waited for; matrix products, arithmetic and copies ran while one was open for 1% of the time, Pallas kernels for 9%

profile of v17, /device:TPU:0, one launch (start us, length us, event | category | flops | bytes accessed | tf_op | source)
XLA Modules:
  0.0 97.0 jit_solution(2434252749129237036)
XLA Ops:
  0.7 2.9 %pack_heads.1 = (bf16[8,1024,128]{2,1,0:T(8,128)(2,1)}, bf16[4,256,128]{2,1,0:T(8,128)(2,1)}, bf16[4,256,128]{2,1,0:T(8,128)(2,1)}) custom-call(bf16[1,128,2048]{2,1,0:T(8,128)(2,1)} %refs_0_.1, bf16[1,128,2048]{2,1,0:T(8,128)(2,1)} %refs_1_.1, bf16[1,128,2048]{2,1,0:T(8,128)(2,1)} %refs_2_.1, bf16[1,128,2048]{2,1,0:T(8,128)(2,1)} %refs_3_.1), custom_call_target="tpu_custom_call" | custom-call | bytes 4718592 | tf_op jit(solution)/shard_map/pack_heads/pallas_call | solution.py:410
  3.6 5.4 %all-to-all-start = ((bf16[8,1024,128]{2,1,0:T(8,128)(2,1)}), bf16[8,1024,128]{2,1,0:T(8,128)(2,1)S(1)}, u32[]{:S(2)}, u32[]{:S(2)}) async-start(bf16[8,1024,128]{2,1,0:T(8,128)(2,1)} %get-tuple-element.46), calls=%async_computation | async-start | bytes 4194304 | tf_op jit(solution)/shard_map/all_to_all | solution.py:1051
  9.6 1.0 %scales_and_masks.1 = (f32[8,256]{1,0:T(8,128)S(1)}, f32[3,8,1024]{2,1,0:T(8,128)S(1)}, s32[16,128]{1,0:T(8,128)S(1)}) custom-call(f32[16]{0:T(128)S(1)} %copy-done.2, s32[16,16]{1,0:T(8,128)S(1)} %bitcast.6, s32[16]{0:T(128)S(1)} %copy-done.3), custom_call_target="tpu_custom_call" | custom-call | bytes 115840 | tf_op jit(solution)/shard_map/scales_and_masks/pallas_call | solution.py:410
  11.0 2.7 %collective-permute-start.1 = (bf16[2,256,128]{2,1,0:T(8,128)(2,1)S(1)}, bf16[2,256,128]{2,1,0:T(8,128)(2,1)S(1)}, u32[]{:S(2)}, u32[]{:S(2)}) collective-permute-start(bf16[2,256,128]{2,1,0:T(8,128)(2,1)S(1)} %get-tuple-element.57), channel_id=1, source_target_pairs={{0,16},{2,18},{4,20},{6,22},{8,24},{10,26},{12,28},{14,30},{16,0},... | collective-permute-start | bytes 393224 | tf_op jit(solution)/shard_map/ppermute | solution.py:1024
  13.6 1.5 %collective-permute-start.2 = (bf16[2,256,128]{2,1,0:T(8,128)(2,1)S(1)}, bf16[2,256,128]{2,1,0:T(8,128)(2,1)S(1)}, u32[]{:S(2)}, u32[]{:S(2)}) collective-permute-start(bf16[2,256,128]{2,1,0:T(8,128)(2,1)S(1)} %get-tuple-element.58), channel_id=1, source_target_pairs={{0,20},{2,22},{4,16},{6,18},{8,28},{10,30},{12,24},{14,26},{16,4},... | collective-permute-start | bytes 393224 | tf_op jit(solution)/shard_map/ppermute | solution.py:1024
  15.1 3.5 %collective-permute-start.3 = (bf16[2,256,128]{2,1,0:T(8,128)(2,1)S(1)}, bf16[2,256,128]{2,1,0:T(8,128)(2,1)S(1)}, u32[]{:S(2)}, u32[]{:S(2)}) collective-permute-start(bf16[2,256,128]{2,1,0:T(8,128)(2,1)S(1)} %get-tuple-element.59), channel_id=1, source_target_pairs={{0,24},{2,26},{4,28},{6,30},{8,16},{10,18},{12,20},{14,22},{16,8},... | collective-permute-start | bytes 393224 | tf_op jit(solution)/shard_map/ppermute | solution.py:1024
  18.7 21.7 %all-to-all-done = bf16[8,1024,128]{2,1,0:T(8,128)(2,1)S(1)} async-done(((bf16[8,1024,128]{2,1,0:T(8,128)(2,1)}), bf16[8,1024,128]{2,1,0:T(8,128)(2,1)S(1)}, u32[]{:S(2)}, u32[]{:S(2)}) %all-to-all-start) | async-done | bytes 2097184 | tf_op jit(solution)/shard_map/all_to_all | solution.py:1051
  40.4 4.3 %diagonal_statistics.1 = (f32[16,1024]{1,0:T(8,128)S(1)}, f32[3,1024,128]{2,1,0:T(8,128)S(1)}, f32[1024,1024]{1,0:T(8,128)S(1)}, f32[1024,1024]{1,0:T(8,128)S(1)...) custom-call(bf16[8,8,128,128]{3,2,1,0:T(8,128)(2,1)S(1)} %bitcast.2, f32[8,256]{1,0:T(8,128)S(1)} %get-tuple-element.51.scales_ref, ...), custom_call_target="tpu_custom_call" | custom-call | flops 536870912 | bytes 20627456 | tf_op jit(solution)/shard_map/diagonal_statistics/pallas_call | solution.py:410
  44.6 1.0 %collective-permute-done.3.refs_2_ = bf16[2,256,128]{2,1,0:T(8,128)(2,1)S(1)} collective-permute-done((bf16[2,256,128]{2,1,0:T(8,128)(2,1)S(1)}, bf16[2,256,128]{2,1,0:T(8,128)(2,1)S(1)}, u32[]{:S(2)}, u32[]{:S(2)}) %collective-permute-start.3) | collective-permute-done | bytes 131104 | tf_op jit(solution)/shard_map/ppermute | solution.py:1024
  45.7 3.2 %collective-permute-done.4.refs_3_ = bf16[2,256,128]{2,1,0:T(8,128)(2,1)S(1)} collective-permute-done((bf16[2,256,128]{2,1,0:T(8,128)(2,1)S(1)}, bf16[2,256,128]{2,1,0:T(8,128)(2,1)S(1)}, u32[]{:S(2)}, u32[]{:S(2)}) %collective-permute-start.4) | collective-permute-done | bytes 131104 | tf_op jit(solution)/shard_map/ppermute | solution.py:1024
  48.9 2.4 %square_statistics.1 = (bf16[4,1024,128]{2,1,0:T(8,128)(2,1)S(1)}, f32[8,1024]{1,0:T(8,128)S(1)}, f32[8,1024]{1,0:T(8,128)S(1)}, f32[1024,1024]{1,0:T(8,128)S(1)}, f32[1024,1024]{1,0:T(8,128)S(1)}) custom-call(bf16[8,8,128,128]{3,2,1,0:T(8,128)(2,1)S(1)} %bitcast.3, f32[8,256]{1,0:T(8,128)S(1)} %get-tuple-element.51.scales_ref, ...), custom_call_target="tpu_custom_call" | custom-call | flops 536870912 | bytes 12304384 | tf_op jit(solution)/shard_map/square_statistics/pallas_call | solution.py:410
  51.4 2.0 %gradients_before_totals.1 = (bf16[2,1024,128]{2,1,0:T(8,128)(2,1)S(1)}, bf16[8,784,128]{2,1,0:T(8,128)(2,1)}) custom-call(bf16[8,8,128,128]{3,2,1,0:T(8,128)(2,1)S(1)} %bitcast.4, f32[8,256]{1,0:T(8,128)S(1)} %get-tuple-element.51.scales_ref, bf16[4,1024,128]{2,1,0:T(8,128)(2,1)S(1)} %get-tuple-element.61.square_ref, ...), custom_call_target="tpu_custom_call" | custom-call | flops 1073741824 | bytes 30547968 | tf_op jit(solution)/shard_map/gradients_before_totals/pallas_call | solution.py:410
  53.4 2.8 %collective-permute-done.5.received_ref = f32[8,1024]{1,0:T(8,128)S(1)} collective-permute-done((f32[8,1024]{1,0:T(8,128)S(1)}, f32[8,1024]{1,0:T(8,128)S(1)}, u32[]{:S(2)}, u32[]{:S(2)}) %collective-permute-start.5) | collective-permute-done | bytes 32800 | tf_op jit(solution)/shard_map/ppermute | solution.py:1116
  56.2 2.9 %gradients_after_totals.1 = (bf16[8,784,128]{2,1,0:T(8,128)(2,1)}, bf16[4,256,128]{2,1,0:T(8,128)(2,1)S(1)}, bf16[4,256,128]{2,1,0:T(8,128)(2,1)S(1)}) custom-call(bf16[8,8,128,128]{3,2,1,0:T(8,128)(2,1)S(1)} %bitcast.5, f32[8,256]{1,0:T(8,128)S(1)} %get-tuple-element.51.scales_ref, ...), custom_call_target="tpu_custom_call", output_to_operand_aliasing={{0}: (13, {})} | custom-call | flops 536870912 | bytes 25927680 | tf_op jit(solution)/shard_map/gradients_after_totals/pallas_call | solution.py:410
  59.1 3.6 %all-to-all-start.1 = ((bf16[8,784,128]{2,1,0:T(8,128)(2,1)}), bf16[8,784,128]{2,1,0:T(8,128)(2,1)S(1)}, u32[]{:S(2)}, u32[]{:S(2)}) async-start(bf16[8,784,128]{2,1,0:T(8,128)(2,1)} %get-tuple-element.73), calls=%async_computation.1 | async-start | bytes 3211264 | tf_op jit(solution)/shard_map/all_to_all | solution.py:1051
  63.1 1.3 %collective-permute-done.6.taken_ref = bf16[4,256,128]{2,1,0:T(8,128)(2,1)S(1)} collective-permute-done((bf16[4,256,128]{2,1,0:T(8,128)(2,1)S(1)}, bf16[4,256,128]{2,1,0:T(8,128)(2,1)S(1)}, u32[]{:S(2)}, u32[]{:S(2)}) %collective-permute-start.6) | collective-permute-done | bytes 262176 | tf_op jit(solution)/shard_map/ppermute | solution.py:1011
  64.5 1.4 %collective-permute-start.7 = (bf16[2,256,128]{2,1,0:T(8,128)(2,1)S(1)}, bf16[2,256,128]{2,1,0:T(8,128)(2,1)S(1)}, u32[]{:S(2)}, u32[]{:S(2)}) collective-permute-start(bf16[2,256,128]{2,1,0:T(8,128)(2,1)S(1)} %get-tuple-element.76), channel_id=1, source_target_pairs={{0,16},{2,18},{4,20},{6,22},{8,24},{10,26},{12,28},{14,30},{16,0},... | collective-permute-start | bytes 393224 | tf_op jit(solution)/shard_map/ppermute | solution.py:1024
  65.8 2.8 %collective-permute-start.9 = (bf16[2,256,128]{2,1,0:T(8,128)(2,1)S(1)}, bf16[2,256,128]{2,1,0:T(8,128)(2,1)S(1)}, u32[]{:S(2)}, u32[]{:S(2)}) collective-permute-start(bf16[2,256,128]{2,1,0:T(8,128)(2,1)S(1)} %get-tuple-element.78), channel_id=1, source_target_pairs={{0,20},{2,22},{4,16},{6,18},{8,28},{10,30},{12,24},{14,26},{16,4},... | collective-permute-start | bytes 393224 | tf_op jit(solution)/shard_map/ppermute | solution.py:1024
  68.6 2.2 %collective-permute-start.10 = (bf16[2,256,128]{2,1,0:T(8,128)(2,1)S(1)}, bf16[2,256,128]{2,1,0:T(8,128)(2,1)S(1)}, u32[]{:S(2)}, u32[]{:S(2)}) collective-permute-start(bf16[2,256,128]{2,1,0:T(8,128)(2,1)S(1)} %get-tuple-element.79), channel_id=1, source_target_pairs={{0,24},{2,26},{4,28},{6,30},{8,16},{10,18},{12,20},{14,22},{16,8},... | collective-permute-start | bytes 393224 | tf_op jit(solution)/shard_map/ppermute | solution.py:1024
  70.9 1.3 %collective-permute-start.11 = (bf16[2,256,128]{2,1,0:T(8,128)(2,1)S(1)}, bf16[2,256,128]{2,1,0:T(8,128)(2,1)S(1)}, u32[]{:S(2)}, u32[]{:S(2)}) collective-permute-start(bf16[2,256,128]{2,1,0:T(8,128)(2,1)S(1)} %get-tuple-element.80), channel_id=1, source_target_pairs={{0,28},{2,30},{4,24},{6,26},{8,20},{10,22},{12,16},{14,18},{16,12}... | collective-permute-start | bytes 393224 | tf_op jit(solution)/shard_map/ppermute | solution.py:1024
  72.2 16.5 %all-to-all-done.1.within_ref = bf16[8,784,128]{2,1,0:T(8,128)(2,1)S(1)} async-done(((bf16[8,784,128]{2,1,0:T(8,128)(2,1)}), bf16[8,784,128]{2,1,0:T(8,128)(2,1)S(1)}, u32[]{:S(2)}, u32[]{:S(2)}) %all-to-all-start.1) | async-done | bytes 1605664 | tf_op jit(solution)/shard_map/all_to_all | solution.py:1051
  88.8 1.6 %collective-permute-start.8 = (f32[16,128]{1,0:T(8,128)S(1)}, f32[16,128]{1,0:T(8,128)S(1)}, u32[]{:S(2)}, u32[]{:S(2)}) collective-permute-start(f32[16,128]{1,0:T(8,128)S(1)} %temper_sums.1), channel_id=1, source_target_pairs={{0,1},{1,0},{2,3},{3,2},{4,5},{5,4},{6,7},{7,6},{8,9},{9,8},{10,11... | collective-permute-start | bytes 24584 | tf_op jit(solution)/shard_map/ppermute | solution.py:1158
  90.3 1.4 %unpack_own.1 = (bf16[1,128,2048]{2,1,0:T(8,128)(2,1)}, bf16[1,128,2048]{2,1,0:T(8,128)(2,1)}, bf16[1,128,2048]{2,1,0:T(8,128)(2,1)}) custom-call(bf16[8,784,128]{2,1,0:T(8,128)(2,1)S(1)} %all-to-all-done.1.within_ref), custom_call_target="tpu_custom_call" | custom-call | bytes 3178496 | tf_op jit(solution)/shard_map/unpack_own/pallas_call | solution.py:410
  93.1 2.8 %collective-permute-done.11.refs_3_ = bf16[2,256,128]{2,1,0:T(8,128)(2,1)S(1)} collective-permute-done((bf16[2,256,128]{2,1,0:T(8,128)(2,1)S(1)}, bf16[2,256,128]{2,1,0:T(8,128)(2,1)S(1)}, u32[]{:S(2)}, u32[]{:S(2)}) %collective-permute-start.11) | collective-permute-done | bytes 131104 | tf_op jit(solution)/shard_map/ppermute | solution.py:1024
  (26 shorter events, 3.9 us)
Async XLA Ops:
  0.6 8.9 %copy-start.3 = (s32[16]{0:T(128)S(1)}, s32[16]{0:T(128)}, u32[]{:S(2)}) copy-start(s32[16]{0:T(128)} %span_ref.1) | copy-start | bytes 196
  0.6 8.9 %copy-start.1 = (s32[1,16,16,1]{2,3,1,0:T(1,128)S(1)}, s32[1,16,16,1]{2,3,1,0:T(1,128)}, u32[]{:S(2)}) copy-start(s32[1,16,16,1]{2,3,1,0:T(1,128)} %param.12) | copy-start | bytes 3076
  0.7 8.9 %copy-start.2 = (f32[16]{0:T(128)S(1)}, f32[16]{0:T(128)}, u32[]{:S(2)}) copy-start(f32[16]{0:T(128)} %softness_ref.1) | copy-start | bytes 196
  3.6 5.4 %copy-start.4 = (bf16[4,256,128]{2,1,0:T(8,128)(2,1)S(1)}, bf16[4,256,128]{2,1,0:T(8,128)(2,1)}, u32[]{:S(2)}) copy-start(bf16[4,256,128]{2,1,0:T(8,128)(2,1)} %get-tuple-element.56) | copy-start | bytes 786436
  3.6 7.3 %copy-start = (bf16[4,256,128]{2,1,0:T(8,128)(2,1)S(1)}, bf16[4,256,128]{2,1,0:T(8,128)(2,1)}, u32[]{:S(2)}) copy-start(bf16[4,256,128]{2,1,0:T(8,128)(2,1)} %get-tuple-element.55.kept_ref) | copy-start | bytes 786436
  3.6 36.7 %all-to-all-start = ((bf16[8,1024,128]{2,1,0:T(8,128)(2,1)}), bf16[8,1024,128]{2,1,0:T(8,128)(2,1)S(1)}, u32[]{:S(2)}, u32[]{:S(2)}) async-start(bf16[8,1024,128]{2,1,0:T(8,128)(2,1)} %get-tuple-element.46), calls=%async_computation | async-start | bytes 4194304 | tf_op jit(solution)/shard_map/all_to_all | solution.py:1051
  9.0 1.9 %collective-permute-start = (bf16[4,256,128]{2,1,0:T(8,128)(2,1)S(1)}, bf16[4,256,128]{2,1,0:T(8,128)(2,1)S(1)}, u32[]{:S(2)}, u32[]{:S(2)}) collective-permute-start(bf16[4,256,128]{2,1,0:T(8,128)(2,1)S(1)} %copy-done.4), channel_id=1, source_target_pairs={{0,2},{2,0},{4,6},{6,4},{8,10},{10,8},{12,14},{14,12},{16,18},{18,... | collective-permute-start | bytes 786440 | tf_op jit(solution)/shard_map/ppermute | solution.py:1011
  11.0 33.6 %collective-permute-start.1 = (bf16[2,256,128]{2,1,0:T(8,128)(2,1)S(1)}, bf16[2,256,128]{2,1,0:T(8,128)(2,1)S(1)}, u32[]{:S(2)}, u32[]{:S(2)}) collective-permute-start(bf16[2,256,128]{2,1,0:T(8,128)(2,1)S(1)} %get-tuple-element.57), channel_id=1, source_target_pairs={{0,16},{2,18},{4,20},{6,22},{8,24},{10,26},{12,28},{14,30},{16,0},... | collective-permute-start | bytes 393224 | tf_op jit(solution)/shard_map/ppermute | solution.py:1024
  13.6 31.0 %collective-permute-start.2 = (bf16[2,256,128]{2,1,0:T(8,128)(2,1)S(1)}, bf16[2,256,128]{2,1,0:T(8,128)(2,1)S(1)}, u32[]{:S(2)}, u32[]{:S(2)}) collective-permute-start(bf16[2,256,128]{2,1,0:T(8,128)(2,1)S(1)} %get-tuple-element.58), channel_id=1, source_target_pairs={{0,20},{2,22},{4,16},{6,18},{8,28},{10,30},{12,24},{14,26},{16,4},... | collective-permute-start | bytes 393224 | tf_op jit(solution)/shard_map/ppermute | solution.py:1024
  15.1 30.6 %collective-permute-start.3 = (bf16[2,256,128]{2,1,0:T(8,128)(2,1)S(1)}, bf16[2,256,128]{2,1,0:T(8,128)(2,1)S(1)}, u32[]{:S(2)}, u32[]{:S(2)}) collective-permute-start(bf16[2,256,128]{2,1,0:T(8,128)(2,1)S(1)} %get-tuple-element.59), channel_id=1, source_target_pairs={{0,24},{2,26},{4,28},{6,30},{8,16},{10,18},{12,20},{14,22},{16,8},... | collective-permute-start | bytes 393224 | tf_op jit(solution)/shard_map/ppermute | solution.py:1024
  18.6 30.3 %collective-permute-start.4 = (bf16[2,256,128]{2,1,0:T(8,128)(2,1)S(1)}, bf16[2,256,128]{2,1,0:T(8,128)(2,1)S(1)}, u32[]{:S(2)}, u32[]{:S(2)}) collective-permute-start(bf16[2,256,128]{2,1,0:T(8,128)(2,1)S(1)} %get-tuple-element.60), channel_id=1, source_target_pairs={{0,28},{2,30},{4,24},{6,26},{8,20},{10,22},{12,16},{14,18},{16,12}... | collective-permute-start | bytes 393224 | tf_op jit(solution)/shard_map/ppermute | solution.py:1024
  51.3 4.9 %collective-permute-start.5 = (f32[8,1024]{1,0:T(8,128)S(1)}, f32[8,1024]{1,0:T(8,128)S(1)}, u32[]{:S(2)}, u32[]{:S(2)}) collective-permute-start(f32[8,1024]{1,0:T(8,128)S(1)} %get-tuple-element.62.message_ref), channel_id=1, source_target_pairs={{0,16},{2,18},{4,20},{6,22},{8,24},{10,26},{12,28},{14,30},{16,0},... | collective-permute-start | bytes 98312 | tf_op jit(solution)/shard_map/ppermute | solution.py:1116
  59.1 29.6 %all-to-all-start.1 = ((bf16[8,784,128]{2,1,0:T(8,128)(2,1)}), bf16[8,784,128]{2,1,0:T(8,128)(2,1)S(1)}, u32[]{:S(2)}, u32[]{:S(2)}) async-start(bf16[8,784,128]{2,1,0:T(8,128)(2,1)} %get-tuple-element.73), calls=%async_computation.1 | async-start | bytes 3211264 | tf_op jit(solution)/shard_map/all_to_all | solution.py:1051
  62.7 1.7 %collective-permute-start.6 = (bf16[4,256,128]{2,1,0:T(8,128)(2,1)S(1)}, bf16[4,256,128]{2,1,0:T(8,128)(2,1)S(1)}, u32[]{:S(2)}, u32[]{:S(2)}) collective-permute-start(bf16[4,256,128]{2,1,0:T(8,128)(2,1)S(1)} %get-tuple-element.75), channel_id=1, source_target_pairs={{0,2},{2,0},{4,6},{6,4},{8,10},{10,8},{12,14},{14,12},{16,18},{18,... | collective-permute-start | bytes 786440 | tf_op jit(solution)/shard_map/ppermute | solution.py:1011
  64.5 28.6 %collective-permute-start.7 = (bf16[2,256,128]{2,1,0:T(8,128)(2,1)S(1)}, bf16[2,256,128]{2,1,0:T(8,128)(2,1)S(1)}, u32[]{:S(2)}, u32[]{:S(2)}) collective-permute-start(bf16[2,256,128]{2,1,0:T(8,128)(2,1)S(1)} %get-tuple-element.76), channel_id=1, source_target_pairs={{0,16},{2,18},{4,20},{6,22},{8,24},{10,26},{12,28},{14,30},{16,0},... | collective-permute-start | bytes 393224 | tf_op jit(solution)/shard_map/ppermute | solution.py:1024
  65.8 27.3 %collective-permute-start.9 = (bf16[2,256,128]{2,1,0:T(8,128)(2,1)S(1)}, bf16[2,256,128]{2,1,0:T(8,128)(2,1)S(1)}, u32[]{:S(2)}, u32[]{:S(2)}) collective-permute-start(bf16[2,256,128]{2,1,0:T(8,128)(2,1)S(1)} %get-tuple-element.78), channel_id=1, source_target_pairs={{0,20},{2,22},{4,16},{6,18},{8,28},{10,30},{12,24},{14,26},{16,4},... | collective-permute-start | bytes 393224 | tf_op jit(solution)/shard_map/ppermute | solution.py:1024
  68.6 24.5 %collective-permute-start.10 = (bf16[2,256,128]{2,1,0:T(8,128)(2,1)S(1)}, bf16[2,256,128]{2,1,0:T(8,128)(2,1)S(1)}, u32[]{:S(2)}, u32[]{:S(2)}) collective-permute-start(bf16[2,256,128]{2,1,0:T(8,128)(2,1)S(1)} %get-tuple-element.79), channel_id=1, source_target_pairs={{0,24},{2,26},{4,28},{6,30},{8,16},{10,18},{12,20},{14,22},{16,8},... | collective-permute-start | bytes 393224 | tf_op jit(solution)/shard_map/ppermute | solution.py:1024
  70.9 25.1 %collective-permute-start.11 = (bf16[2,256,128]{2,1,0:T(8,128)(2,1)S(1)}, bf16[2,256,128]{2,1,0:T(8,128)(2,1)S(1)}, u32[]{:S(2)}, u32[]{:S(2)}) collective-permute-start(bf16[2,256,128]{2,1,0:T(8,128)(2,1)S(1)} %get-tuple-element.80), channel_id=1, source_target_pairs={{0,28},{2,30},{4,24},{6,26},{8,20},{10,22},{12,16},{14,18},{16,12}... | collective-permute-start | bytes 393224 | tf_op jit(solution)/shard_map/ppermute | solution.py:1024
  88.8 3.7 %collective-permute-start.8 = (f32[16,128]{1,0:T(8,128)S(1)}, f32[16,128]{1,0:T(8,128)S(1)}, u32[]{:S(2)}, u32[]{:S(2)}) collective-permute-start(f32[16,128]{1,0:T(8,128)S(1)} %temper_sums.1), channel_id=1, source_target_pairs={{0,1},{1,0},{2,3},{3,2},{4,5},{5,4},{6,7},{7,6},{8,9},{9,8},{10,11... | collective-permute-start | bytes 24584 | tf_op jit(solution)/shard_map/ppermute | solution.py:1158

commit v18 on v15

--- a/solution.py
+++ b/solution.py
@@ -400,6 +400,10 @@
     return me, half, me - half * half_count
 
 
+def hop(step, half_count):
+    return half_count - 2 - 2 * step
+
+
 def kernel_call(
     kernel, name, operands, in_specs, out_shape, scratch, vmem_mib, flops=0, out_spaces=None,
     aliases=None,
@@ -462,7 +466,7 @@
     second = jnp.where(half == 0, VALUE, GRAD)
     for core, foreign_ref in enumerate(foreign_refs):
         for step in range(half_count // 2):
-            columns = columns_of(me ^ core ^ (half_count + 2 * step))
+            columns = columns_of(me ^ core ^ (half_count + hop(step, half_count)))
             across[core, step, :BLK, :] = held[first, :, columns]
             across[core, step, BLK:, :] = held[second, :, columns]
         leaving.append(pltpu.make_async_copy(across.at[core], foreign_ref, left_across.at[core]))
@@ -744,7 +748,7 @@
     second = jnp.where(half == 0, GRAD, VALUE)
     for step, across_ref in enumerate(across_refs):
         for core in range(2):
-            rows = rows_of(place ^ core ^ (2 * step))
+            rows = rows_of(place ^ core ^ hop(step, half_count))
             square_ref[first, rows, :] = across_ref[core, :BLK, :]
             square_ref[second, rows, :] = across_ref[core, BLK:, :]
     for kept in (jnp.where(half == 0, KEY, QUERY), jnp.where(half == 0, VALUE, GRAD)):
@@ -864,7 +868,7 @@
     def chunks():
         for core, chunk_ref in enumerate(chunk_refs):
             for step in range(half_count // 2):
-                yield step, chunk_ref, rows_of(place ^ core ^ (2 * step))
+                yield step, chunk_ref, rows_of(place ^ core ^ hop(step, half_count))
 
     @pl.when(half == 0)
     def _():
@@ -976,11 +980,11 @@
         def _():
             leaving = []
             for step, across_ref in enumerate(across_refs):
-                pair = (place ^ (2 * step)) >> 1
+                pair = (place ^ hop(step, half_count)) >> 1
                 for part, array in enumerate(arrays):
                     rows = slice(part * BLK, (part + 1) * BLK)
                     for core in range(2):
-                        peer = place ^ core ^ (2 * step)
+                        peer = place ^ core ^ hop(step, half_count)
                         kept = within_ref[peer, (3 + array) * BLK : (4 + array) * BLK, :]
                         total = kept.astype(jnp.float32) + across_ref[core, rows, :].astype(
                             jnp.float32
@@ -1020,7 +1024,7 @@
     )
     return [
         lax.ppermute(
-            message, "seq", [(source, source ^ (half_count + 2 * step)) for source in devices]
+            message, "seq", [(source, source ^ (half_count + hop(step, half_count))) for source in devices]
         )
         for step, message in enumerate(messages)
     ]

time: 97.3 us -> 101 us (1.038)
  waiting for transfers between devices: 50.5 us -> 54.6 us
    all_to_all x2, waiting for transfers between devices: 38.2 us -> 49.4 us  [exchange_within(): lax.all_to_all(array_in, 'seq', split_axis=0, concat_axis=0, axis_index_g...]
    ppermute x8, waiting for transfers between devices: 7.07 us -> 0.02 us  [crossed(): lax.ppermute(message, 'seq', [(source, source ^ half_count + hop(step, ha...]
  transfers between devices with their start and end apart: 14 -> 14, of which waited for: 9 -> 6; matrix products, arithmetic and copies ran while one was open for 1% -> 1% of each run, Pallas kernels for 9% -> 9%
where the time goes in v18:
time: 101 us
  waiting for transfers between devices  54.6 us (54%)
  starting transfers between devices  27 us (27%)
  Pallas kernels  17.9 us (18%)
    all_to_all x2, waiting for transfers between devices, exchange_within(): lax.all_to_all(array_in, 'seq', split_axis=0, concat_axis=0, axis_index_g...  49.4 us
    pallas_call x10, Pallas kernels, kernel_call(): pl.pallas_call(kernel, out_shape=out_shape, in_specs=in_specs, out_specs=...  17.9 us
    ppermute x8, starting transfers between devices, crossed(): lax.ppermute(message, 'seq', [(source, source ^ half_count + hop(step, ha...  15.4 us
    all_to_all x2, starting transfers between devices, exchange_within(): lax.all_to_all(array_in, 'seq', split_axis=0, concat_axis=0, axis_index_g...  8.99 us
    ppermute x1, waiting for transfers between devices, head_shards(): received = lax.ppermute(message, 'seq', swap)  2.75 us
  transfers between devices with their start and end apart: 14, of which 6 were waited for; matrix products, arithmetic and copies ran while one was open for 1% of the time, Pallas kernels for 9%

profile of v18, /device:TPU:0, one launch (start us, length us, event | category | flops | bytes accessed | tf_op | source)
XLA Modules:
  0.0 101.1 jit_solution(16549361241760780057)
XLA Ops:
  0.7 2.9 %pack_heads.1 = (bf16[8,1024,128]{2,1,0:T(8,128)(2,1)}, bf16[4,256,128]{2,1,0:T(8,128)(2,1)}, bf16[4,256,128]{2,1,0:T(8,128)(2,1)}) custom-call(bf16[1,128,2048]{2,1,0:T(8,128)(2,1)} %refs_0_.1, bf16[1,128,2048]{2,1,0:T(8,128)(2,1)} %refs_1_.1, bf16[1,128,2048]{2,1,0:T(8,128)(2,1)} %refs_2_.1, bf16[1,128,2048]{2,1,0:T(8,128)(2,1)} %refs_3_.1), custom_call_target="tpu_custom_call" | custom-call | bytes 4718592 | tf_op jit(solution)/shard_map/pack_heads/pallas_call | solution.py:414
  3.6 5.4 %all-to-all-start = ((bf16[8,1024,128]{2,1,0:T(8,128)(2,1)}), bf16[8,1024,128]{2,1,0:T(8,128)(2,1)S(1)}, u32[]{:S(2)}, u32[]{:S(2)}) async-start(bf16[8,1024,128]{2,1,0:T(8,128)(2,1)} %get-tuple-element.46), calls=%async_computation | async-start | bytes 4194304 | tf_op jit(solution)/shard_map/all_to_all | solution.py:1056
  9.0 0.5 collective-permute-start
  9.6 1.0 scales_and_masks.1
  11.0 4.7 %collective-permute-start.1 = (bf16[2,256,128]{2,1,0:T(8,128)(2,1)S(1)}, bf16[2,256,128]{2,1,0:T(8,128)(2,1)S(1)}, u32[]{:S(2)}, u32[]{:S(2)}) collective-permute-start(bf16[2,256,128]{2,1,0:T(8,128)(2,1)S(1)} %get-tuple-element.57), channel_id=1, source_target_pairs={{0,28},{2,30},{4,24},{6,26},{8,20},{10,22},{12,16},{14,18},{16,12}... | collective-permute-start | bytes 393224 | tf_op jit(solution)/shard_map/ppermute | solution.py:1026
  16.0 0.6 collective-permute-start.3
  16.6 2.1 %collective-permute-start.4 = (bf16[2,256,128]{2,1,0:T(8,128)(2,1)S(1)}, bf16[2,256,128]{2,1,0:T(8,128)(2,1)S(1)}, u32[]{:S(2)}, u32[]{:S(2)}) collective-permute-start(bf16[2,256,128]{2,1,0:T(8,128)(2,1)S(1)} %get-tuple-element.60), channel_id=1, source_target_pairs={{0,16},{2,18},{4,20},{6,22},{8,24},{10,26},{12,28},{14,30},{16,0},... | collective-permute-start | bytes 393224 | tf_op jit(solution)/shard_map/ppermute | solution.py:1026
  18.7 27.3 %all-to-all-done = bf16[8,1024,128]{2,1,0:T(8,128)(2,1)S(1)} async-done(((bf16[8,1024,128]{2,1,0:T(8,128)(2,1)}), bf16[8,1024,128]{2,1,0:T(8,128)(2,1)S(1)}, u32[]{:S(2)}, u32[]{:S(2)}) %all-to-all-start) | async-done | bytes 2097184 | tf_op jit(solution)/shard_map/all_to_all | solution.py:1056
  46.0 4.3 %diagonal_statistics.1 = (f32[16,1024]{1,0:T(8,128)S(1)}, f32[3,1024,128]{2,1,0:T(8,128)S(1)}, f32[1024,1024]{1,0:T(8,128)S(1)}, f32[1024,1024]{1,0:T(8,128)S(1)...) custom-call(bf16[8,8,128,128]{3,2,1,0:T(8,128)(2,1)S(1)} %bitcast.2, f32[8,256]{1,0:T(8,128)S(1)} %get-tuple-element.51.scales_ref, ...), custom_call_target="tpu_custom_call" | custom-call | flops 536870912 | bytes 20627456 | tf_op jit(solution)/shard_map/diagonal_statistics/pallas_call | solution.py:414
  50.3 2.4 %square_statistics.1 = (bf16[4,1024,128]{2,1,0:T(8,128)(2,1)S(1)}, f32[8,1024]{1,0:T(8,128)S(1)}, f32[8,1024]{1,0:T(8,128)S(1)}, f32[1024,1024]{1,0:T(8,128)S(1)}, f32[1024,1024]{1,0:T(8,128)S(1)}) custom-call(bf16[8,8,128,128]{3,2,1,0:T(8,128)(2,1)S(1)} %bitcast.3, f32[8,256]{1,0:T(8,128)S(1)} %get-tuple-element.51.scales_ref, ...), custom_call_target="tpu_custom_call" | custom-call | flops 536870912 | bytes 12304384 | tf_op jit(solution)/shard_map/square_statistics/pallas_call | solution.py:414
  52.8 2.0 %gradients_before_totals.1 = (bf16[2,1024,128]{2,1,0:T(8,128)(2,1)S(1)}, bf16[8,784,128]{2,1,0:T(8,128)(2,1)}) custom-call(bf16[8,8,128,128]{3,2,1,0:T(8,128)(2,1)S(1)} %bitcast.4, f32[8,256]{1,0:T(8,128)S(1)} %get-tuple-element.51.scales_ref, bf16[4,1024,128]{2,1,0:T(8,128)(2,1)S(1)} %get-tuple-element.61.square_ref, ...), custom_call_target="tpu_custom_call" | custom-call | flops 1073741824 | bytes 30547968 | tf_op jit(solution)/shard_map/gradients_before_totals/pallas_call | solution.py:414
  54.9 2.8 %collective-permute-done.5.received_ref = f32[8,1024]{1,0:T(8,128)S(1)} collective-permute-done((f32[8,1024]{1,0:T(8,128)S(1)}, f32[8,1024]{1,0:T(8,128)S(1)}, u32[]{:S(2)}, u32[]{:S(2)}) %collective-permute-start.5) | collective-permute-done | bytes 32800 | tf_op jit(solution)/shard_map/ppermute | solution.py:1121
  57.6 2.9 %gradients_after_totals.1 = (bf16[8,784,128]{2,1,0:T(8,128)(2,1)}, bf16[4,256,128]{2,1,0:T(8,128)(2,1)S(1)}, bf16[4,256,128]{2,1,0:T(8,128)(2,1)S(1)}) custom-call(bf16[8,8,128,128]{3,2,1,0:T(8,128)(2,1)S(1)} %bitcast.5, f32[8,256]{1,0:T(8,128)S(1)} %get-tuple-element.51.scales_ref, ...), custom_call_target="tpu_custom_call", output_to_operand_aliasing={{0}: (13, {})} | custom-call | flops 536870912 | bytes 25927680 | tf_op jit(solution)/shard_map/gradients_after_totals/pallas_call | solution.py:414
  60.5 3.6 %all-to-all-start.1 = ((bf16[8,784,128]{2,1,0:T(8,128)(2,1)}), bf16[8,784,128]{2,1,0:T(8,128)(2,1)S(1)}, u32[]{:S(2)}, u32[]{:S(2)}) async-start(bf16[8,784,128]{2,1,0:T(8,128)(2,1)} %get-tuple-element.73), calls=%async_computation.1 | async-start | bytes 3211264 | tf_op jit(solution)/shard_map/all_to_all | solution.py:1056
  64.5 1.3 %collective-permute-done.6.taken_ref = bf16[4,256,128]{2,1,0:T(8,128)(2,1)S(1)} collective-permute-done((bf16[4,256,128]{2,1,0:T(8,128)(2,1)S(1)}, bf16[4,256,128]{2,1,0:T(8,128)(2,1)S(1)}, u32[]{:S(2)}, u32[]{:S(2)}) %collective-permute-start.6) | collective-permute-done | bytes 262176 | tf_op jit(solution)/shard_map/ppermute | solution.py:1015
  65.8 3.3 %collective-permute-start.7 = (bf16[2,256,128]{2,1,0:T(8,128)(2,1)S(1)}, bf16[2,256,128]{2,1,0:T(8,128)(2,1)S(1)}, u32[]{:S(2)}, u32[]{:S(2)}) collective-permute-start(bf16[2,256,128]{2,1,0:T(8,128)(2,1)S(1)} %get-tuple-element.76), channel_id=1, source_target_pairs={{0,28},{2,30},{4,24},{6,26},{8,20},{10,22},{12,16},{14,18},{16,12}... | collective-permute-start | bytes 393224 | tf_op jit(solution)/shard_map/ppermute | solution.py:1026
  69.1 1.8 %collective-permute-start.9 = (bf16[2,256,128]{2,1,0:T(8,128)(2,1)S(1)}, bf16[2,256,128]{2,1,0:T(8,128)(2,1)S(1)}, u32[]{:S(2)}, u32[]{:S(2)}) collective-permute-start(bf16[2,256,128]{2,1,0:T(8,128)(2,1)S(1)} %get-tuple-element.78), channel_id=1, source_target_pairs={{0,24},{2,26},{4,28},{6,30},{8,16},{10,18},{12,20},{14,22},{16,8},... | collective-permute-start | bytes 393224 | tf_op jit(solution)/shard_map/ppermute | solution.py:1026
  70.9 2.6 %collective-permute-start.11 = (bf16[2,256,128]{2,1,0:T(8,128)(2,1)S(1)}, bf16[2,256,128]{2,1,0:T(8,128)(2,1)S(1)}, u32[]{:S(2)}, u32[]{:S(2)}) collective-permute-start(bf16[2,256,128]{2,1,0:T(8,128)(2,1)S(1)} %get-tuple-element.80), channel_id=1, source_target_pairs={{0,16},{2,18},{4,20},{6,22},{8,24},{10,26},{12,28},{14,30},{16,0},... | collective-permute-start | bytes 393224 | tf_op jit(solution)/shard_map/ppermute | solution.py:1026
  73.6 22.1 %all-to-all-done.1.within_ref = bf16[8,784,128]{2,1,0:T(8,128)(2,1)S(1)} async-done(((bf16[8,784,128]{2,1,0:T(8,128)(2,1)}), bf16[8,784,128]{2,1,0:T(8,128)(2,1)S(1)}, u32[]{:S(2)}, u32[]{:S(2)}) %all-to-all-start.1) | async-done | bytes 1605664 | tf_op jit(solution)/shard_map/all_to_all | solution.py:1056
  95.7 1.6 %collective-permute-start.8 = (f32[16,128]{1,0:T(8,128)S(1)}, f32[16,128]{1,0:T(8,128)S(1)}, u32[]{:S(2)}, u32[]{:S(2)}) collective-permute-start(f32[16,128]{1,0:T(8,128)S(1)} %temper_sums.1), channel_id=1, source_target_pairs={{0,1},{1,0},{2,3},{3,2},{4,5},{5,4},{6,7},{7,6},{8,9},{9,8},{10,11... | collective-permute-start | bytes 24584 | tf_op jit(solution)/shard_map/ppermute | solution.py:1163
  97.3 1.4 %unpack_own.1 = (bf16[1,128,2048]{2,1,0:T(8,128)(2,1)}, bf16[1,128,2048]{2,1,0:T(8,128)(2,1)}, bf16[1,128,2048]{2,1,0:T(8,128)(2,1)}) custom-call(bf16[8,784,128]{2,1,0:T(8,128)(2,1)S(1)} %all-to-all-done.1.within_ref), custom_call_target="tpu_custom_call" | custom-call | bytes 3178496 | tf_op jit(solution)/shard_map/unpack_own/pallas_call | solution.py:414
  98.7 0.7 collective-permute-done.8
  99.4 0.6 fusion.1
  100.1 0.9 unpack_other.1
  (26 shorter events, 1.4 us)
Async XLA Ops:
  0.6 8.9 %copy-start.3 = (s32[16]{0:T(128)S(1)}, s32[16]{0:T(128)}, u32[]{:S(2)}) copy-start(s32[16]{0:T(128)} %span_ref.1) | copy-start | bytes 196
  0.6 8.9 %copy-start.1 = (s32[1,16,16,1]{2,3,1,0:T(1,128)S(1)}, s32[1,16,16,1]{2,3,1,0:T(1,128)}, u32[]{:S(2)}) copy-start(s32[1,16,16,1]{2,3,1,0:T(1,128)} %param.12) | copy-start | bytes 3076
  0.7 8.9 %copy-start.2 = (f32[16]{0:T(128)S(1)}, f32[16]{0:T(128)}, u32[]{:S(2)}) copy-start(f32[16]{0:T(128)} %softness_ref.1) | copy-start | bytes 196
  3.6 5.4 %copy-start.4 = (bf16[4,256,128]{2,1,0:T(8,128)(2,1)S(1)}, bf16[4,256,128]{2,1,0:T(8,128)(2,1)}, u32[]{:S(2)}) copy-start(bf16[4,256,128]{2,1,0:T(8,128)(2,1)} %get-tuple-element.56) | copy-start | bytes 786436
  3.6 7.3 %copy-start = (bf16[4,256,128]{2,1,0:T(8,128)(2,1)S(1)}, bf16[4,256,128]{2,1,0:T(8,128)(2,1)}, u32[]{:S(2)}) copy-start(bf16[4,256,128]{2,1,0:T(8,128)(2,1)} %get-tuple-element.55.kept_ref) | copy-start | bytes 786436
  3.6 42.4 %all-to-all-start = ((bf16[8,1024,128]{2,1,0:T(8,128)(2,1)}), bf16[8,1024,128]{2,1,0:T(8,128)(2,1)S(1)}, u32[]{:S(2)}, u32[]{:S(2)}) async-start(bf16[8,1024,128]{2,1,0:T(8,128)(2,1)} %get-tuple-element.46), calls=%async_computation | async-start | bytes 4194304 | tf_op jit(solution)/shard_map/all_to_all | solution.py:1056
  9.0 1.9 %collective-permute-start = (bf16[4,256,128]{2,1,0:T(8,128)(2,1)S(1)}, bf16[4,256,128]{2,1,0:T(8,128)(2,1)S(1)}, u32[]{:S(2)}, u32[]{:S(2)}) collective-permute-start(bf16[4,256,128]{2,1,0:T(8,128)(2,1)S(1)} %copy-done.4), channel_id=1, source_target_pairs={{0,2},{2,0},{4,6},{6,4},{8,10},{10,8},{12,14},{14,12},{16,18},{18,... | collective-permute-start | bytes 786440 | tf_op jit(solution)/shard_map/ppermute | solution.py:1015
  11.0 39.3 %collective-permute-start.1 = (bf16[2,256,128]{2,1,0:T(8,128)(2,1)S(1)}, bf16[2,256,128]{2,1,0:T(8,128)(2,1)S(1)}, u32[]{:S(2)}, u32[]{:S(2)}) collective-permute-start(bf16[2,256,128]{2,1,0:T(8,128)(2,1)S(1)} %get-tuple-element.57), channel_id=1, source_target_pairs={{0,28},{2,30},{4,24},{6,26},{8,20},{10,22},{12,16},{14,18},{16,12}... | collective-permute-start | bytes 393224 | tf_op jit(solution)/shard_map/ppermute | solution.py:1026
  15.7 34.6 %collective-permute-start.2 = (bf16[2,256,128]{2,1,0:T(8,128)(2,1)S(1)}, bf16[2,256,128]{2,1,0:T(8,128)(2,1)S(1)}, u32[]{:S(2)}, u32[]{:S(2)}) collective-permute-start(bf16[2,256,128]{2,1,0:T(8,128)(2,1)S(1)} %get-tuple-element.58), channel_id=1, source_target_pairs={{0,24},{2,26},{4,28},{6,30},{8,16},{10,18},{12,20},{14,22},{16,8},... | collective-permute-start | bytes 393224 | tf_op jit(solution)/shard_map/ppermute | solution.py:1026
  16.0 34.3 %collective-permute-start.3 = (bf16[2,256,128]{2,1,0:T(8,128)(2,1)S(1)}, bf16[2,256,128]{2,1,0:T(8,128)(2,1)S(1)}, u32[]{:S(2)}, u32[]{:S(2)}) collective-permute-start(bf16[2,256,128]{2,1,0:T(8,128)(2,1)S(1)} %get-tuple-element.59), channel_id=1, source_target_pairs={{0,20},{2,22},{4,16},{6,18},{8,28},{10,30},{12,24},{14,26},{16,4},... | collective-permute-start | bytes 393224 | tf_op jit(solution)/shard_map/ppermute | solution.py:1026
  16.6 33.8 %collective-permute-start.4 = (bf16[2,256,128]{2,1,0:T(8,128)(2,1)S(1)}, bf16[2,256,128]{2,1,0:T(8,128)(2,1)S(1)}, u32[]{:S(2)}, u32[]{:S(2)}) collective-permute-start(bf16[2,256,128]{2,1,0:T(8,128)(2,1)S(1)} %get-tuple-element.60), channel_id=1, source_target_pairs={{0,16},{2,18},{4,20},{6,22},{8,24},{10,26},{12,28},{14,30},{16,0},... | collective-permute-start | bytes 393224 | tf_op jit(solution)/shard_map/ppermute | solution.py:1026
  52.7 4.9 %collective-permute-start.5 = (f32[8,1024]{1,0:T(8,128)S(1)}, f32[8,1024]{1,0:T(8,128)S(1)}, u32[]{:S(2)}, u32[]{:S(2)}) collective-permute-start(f32[8,1024]{1,0:T(8,128)S(1)} %get-tuple-element.62.message_ref), channel_id=1, source_target_pairs={{0,16},{2,18},{4,20},{6,22},{8,24},{10,26},{12,28},{14,30},{16,0},... | collective-permute-start | bytes 98312 | tf_op jit(solution)/shard_map/ppermute | solution.py:1121
  60.5 35.2 %all-to-all-start.1 = ((bf16[8,784,128]{2,1,0:T(8,128)(2,1)}), bf16[8,784,128]{2,1,0:T(8,128)(2,1)S(1)}, u32[]{:S(2)}, u32[]{:S(2)}) async-start(bf16[8,784,128]{2,1,0:T(8,128)(2,1)} %get-tuple-element.73), calls=%async_computation.1 | async-start | bytes 3211264 | tf_op jit(solution)/shard_map/all_to_all | solution.py:1056
  64.1 1.7 %collective-permute-start.6 = (bf16[4,256,128]{2,1,0:T(8,128)(2,1)S(1)}, bf16[4,256,128]{2,1,0:T(8,128)(2,1)S(1)}, u32[]{:S(2)}, u32[]{:S(2)}) collective-permute-start(bf16[4,256,128]{2,1,0:T(8,128)(2,1)S(1)} %get-tuple-element.75), channel_id=1, source_target_pairs={{0,2},{2,0},{4,6},{6,4},{8,10},{10,8},{12,14},{14,12},{16,18},{18,... | collective-permute-start | bytes 786440 | tf_op jit(solution)/shard_map/ppermute | solution.py:1015
  65.8 34.2 %collective-permute-start.7 = (bf16[2,256,128]{2,1,0:T(8,128)(2,1)S(1)}, bf16[2,256,128]{2,1,0:T(8,128)(2,1)S(1)}, u32[]{:S(2)}, u32[]{:S(2)}) collective-permute-start(bf16[2,256,128]{2,1,0:T(8,128)(2,1)S(1)} %get-tuple-element.76), channel_id=1, source_target_pairs={{0,28},{2,30},{4,24},{6,26},{8,20},{10,22},{12,16},{14,18},{16,12}... | collective-permute-start | bytes 393224 | tf_op jit(solution)/shard_map/ppermute | solution.py:1026
  69.1 30.9 %collective-permute-start.9 = (bf16[2,256,128]{2,1,0:T(8,128)(2,1)S(1)}, bf16[2,256,128]{2,1,0:T(8,128)(2,1)S(1)}, u32[]{:S(2)}, u32[]{:S(2)}) collective-permute-start(bf16[2,256,128]{2,1,0:T(8,128)(2,1)S(1)} %get-tuple-element.78), channel_id=1, source_target_pairs={{0,24},{2,26},{4,28},{6,30},{8,16},{10,18},{12,20},{14,22},{16,8},... | collective-permute-start | bytes 393224 | tf_op jit(solution)/shard_map/ppermute | solution.py:1026
  70.9 29.1 %collective-permute-start.10 = (bf16[2,256,128]{2,1,0:T(8,128)(2,1)S(1)}, bf16[2,256,128]{2,1,0:T(8,128)(2,1)S(1)}, u32[]{:S(2)}, u32[]{:S(2)}) collective-permute-start(bf16[2,256,128]{2,1,0:T(8,128)(2,1)S(1)} %get-tuple-element.79), channel_id=1, source_target_pairs={{0,20},{2,22},{4,16},{6,18},{8,28},{10,30},{12,24},{14,26},{16,4},... | collective-permute-start | bytes 393224 | tf_op jit(solution)/shard_map/ppermute | solution.py:1026
  70.9 29.1 %collective-permute-start.11 = (bf16[2,256,128]{2,1,0:T(8,128)(2,1)S(1)}, bf16[2,256,128]{2,1,0:T(8,128)(2,1)S(1)}, u32[]{:S(2)}, u32[]{:S(2)}) collective-permute-start(bf16[2,256,128]{2,1,0:T(8,128)(2,1)S(1)} %get-tuple-element.80), channel_id=1, source_target_pairs={{0,16},{2,18},{4,20},{6,22},{8,24},{10,26},{12,28},{14,30},{16,0},... | collective-permute-start | bytes 393224 | tf_op jit(solution)/shard_map/ppermute | solution.py:1026
  95.7 3.7 %collective-permute-start.8 = (f32[16,128]{1,0:T(8,128)S(1)}, f32[16,128]{1,0:T(8,128)S(1)}, u32[]{:S(2)}, u32[]{:S(2)}) collective-permute-start(f32[16,128]{1,0:T(8,128)S(1)} %temper_sums.1), channel_id=1, source_target_pairs={{0,1},{1,0},{2,3},{3,2},{4,5},{5,4},{6,7},{7,6},{8,9},{9,8},{10,11... | collective-permute-start | bytes 24584 | tf_op jit(solution)/shard_map/ppermute | solution.py:1163

commit v19 on v18

--- a/solution.py
+++ b/solution.py
@@ -401,7 +401,7 @@
 
 
 def hop(step, half_count):
-    return half_count - 2 - 2 * step
+    return half_count - 1 - step if step % 2 else step
 
 
 def kernel_call(

time: 101 us -> 101 us (level)
  starting transfers between devices: 27 us -> 25.9 us
    ppermute x8, waiting for transfers between devices: 0.02 us -> 10.4 us  [crossed(): lax.ppermute(message, 'seq', [(source, source ^ half_count + hop(step, ha...]
    all_to_all x2, waiting for transfers between devices: 49.4 us -> 39.4 us  [exchange_within(): lax.all_to_all(array_in, 'seq', split_axis=0, concat_axis=0, axis_index_g...]
    ppermute x8, starting transfers between devices: 15.4 us -> 14.4 us  [crossed(): lax.ppermute(message, 'seq', [(source, source ^ half_count + hop(step, ha...]
  transfers between devices with their start and end apart: 14 -> 14, of which waited for: 6 -> 10; matrix products, arithmetic and copies ran while one was open for 1% -> 1% of each run, Pallas kernels for 9% -> 9%
where the time goes in v19:
time: 101 us; the launch traced here: 100 us
  waiting for transfers between devices  54.9 us (54%)
  starting transfers between devices  25.9 us (26%)
  Pallas kernels  17.9 us (18%)
    all_to_all x2, waiting for transfers between devices, exchange_within(): lax.all_to_all(array_in, 'seq', split_axis=0, concat_axis=0, axis_index_g...  39.4 us
    pallas_call x10, Pallas kernels, kernel_call(): pl.pallas_call(kernel, out_shape=out_shape, in_specs=in_specs, out_specs=...  17.9 us
    ppermute x8, starting transfers between devices, crossed(): lax.ppermute(message, 'seq', [(source, source ^ half_count + hop(step, ha...  14.4 us
    ppermute x8, waiting for transfers between devices, crossed(): lax.ppermute(message, 'seq', [(source, source ^ half_count + hop(step, ha...  10.4 us
    all_to_all x2, starting transfers between devices, exchange_within(): lax.all_to_all(array_in, 'seq', split_axis=0, concat_axis=0, axis_index_g...  8.99 us
    ppermute x1, waiting for transfers between devices, head_shards(): received = lax.ppermute(message, 'seq', swap)  2.75 us
  transfers between devices with their start and end apart: 14, of which 10 were waited for; matrix products, arithmetic and copies ran while one was open for 1% of the time, Pallas kernels for 9%

profile of v19, /device:TPU:0, one launch (start us, length us, event | category | flops | bytes accessed | tf_op | source)
XLA Modules:
  0.0 100.4 jit_solution(8054144414846804492)
XLA Ops:
  0.7 2.9 %pack_heads.1 = (bf16[8,1024,128]{2,1,0:T(8,128)(2,1)}, bf16[4,256,128]{2,1,0:T(8,128)(2,1)}, bf16[4,256,128]{2,1,0:T(8,128)(2,1)}) custom-call(bf16[1,128,2048]{2,1,0:T(8,128)(2,1)} %refs_0_.1, bf16[1,128,2048]{2,1,0:T(8,128)(2,1)} %refs_1_.1, bf16[1,128,2048]{2,1,0:T(8,128)(2,1)} %refs_2_.1, bf16[1,128,2048]{2,1,0:T(8,128)(2,1)} %refs_3_.1), custom_call_target="tpu_custom_call" | custom-call | bytes 4718592 | tf_op jit(solution)/shard_map/pack_heads/pallas_call | solution.py:414
  3.6 5.4 %all-to-all-start = ((bf16[8,1024,128]{2,1,0:T(8,128)(2,1)}), bf16[8,1024,128]{2,1,0:T(8,128)(2,1)S(1)}, u32[]{:S(2)}, u32[]{:S(2)}) async-start(bf16[8,1024,128]{2,1,0:T(8,128)(2,1)} %get-tuple-element.46), calls=%async_computation | async-start | bytes 4194304 | tf_op jit(solution)/shard_map/all_to_all | solution.py:1056
  9.6 1.0 scales_and_masks.1
  11.0 2.7 %collective-permute-start.1 = (bf16[2,256,128]{2,1,0:T(8,128)(2,1)S(1)}, bf16[2,256,128]{2,1,0:T(8,128)(2,1)S(1)}, u32[]{:S(2)}, u32[]{:S(2)}) collective-permute-start(bf16[2,256,128]{2,1,0:T(8,128)(2,1)S(1)} %get-tuple-element.57), channel_id=1, source_target_pairs={{0,16},{2,18},{4,20},{6,22},{8,24},{10,26},{12,28},{14,30},{16,0},... | collective-permute-start | bytes 393224 | tf_op jit(solution)/shard_map/ppermute | solution.py:1026
  13.6 2.4 %collective-permute-start.2 = (bf16[2,256,128]{2,1,0:T(8,128)(2,1)S(1)}, bf16[2,256,128]{2,1,0:T(8,128)(2,1)S(1)}, u32[]{:S(2)}, u32[]{:S(2)}) collective-permute-start(bf16[2,256,128]{2,1,0:T(8,128)(2,1)S(1)} %get-tuple-element.58), channel_id=1, source_target_pairs={{0,28},{2,30},{4,24},{6,26},{8,20},{10,22},{12,16},{14,18},{16,12}... | collective-permute-start | bytes 393224 | tf_op jit(solution)/shard_map/ppermute | solution.py:1026
  16.0 1.7 %collective-permute-start.3 = (bf16[2,256,128]{2,1,0:T(8,128)(2,1)S(1)}, bf16[2,256,128]{2,1,0:T(8,128)(2,1)S(1)}, u32[]{:S(2)}, u32[]{:S(2)}) collective-permute-start(bf16[2,256,128]{2,1,0:T(8,128)(2,1)S(1)} %get-tuple-element.59), channel_id=1, source_target_pairs={{0,20},{2,22},{4,16},{6,18},{8,28},{10,30},{12,24},{14,26},{16,4},... | collective-permute-start | bytes 393224 | tf_op jit(solution)/shard_map/ppermute | solution.py:1026
  17.7 0.9 collective-permute-start.4
  18.6 21.8 %all-to-all-done = bf16[8,1024,128]{2,1,0:T(8,128)(2,1)S(1)} async-done(((bf16[8,1024,128]{2,1,0:T(8,128)(2,1)}), bf16[8,1024,128]{2,1,0:T(8,128)(2,1)S(1)}, u32[]{:S(2)}, u32[]{:S(2)}) %all-to-all-start) | async-done | bytes 2097184 | tf_op jit(solution)/shard_map/all_to_all | solution.py:1056
  40.4 4.3 %diagonal_statistics.1 = (f32[16,1024]{1,0:T(8,128)S(1)}, f32[3,1024,128]{2,1,0:T(8,128)S(1)}, f32[1024,1024]{1,0:T(8,128)S(1)}, f32[1024,1024]{1,0:T(8,128)S(1)...) custom-call(bf16[8,8,128,128]{3,2,1,0:T(8,128)(2,1)S(1)} %bitcast.2, f32[8,256]{1,0:T(8,128)S(1)} %get-tuple-element.51.scales_ref, ...), custom_call_target="tpu_custom_call" | custom-call | flops 536870912 | bytes 20627456 | tf_op jit(solution)/shard_map/diagonal_statistics/pallas_call | solution.py:414
  44.7 1.8 %collective-permute-done.2.refs_1_ = bf16[2,256,128]{2,1,0:T(8,128)(2,1)S(1)} collective-permute-done((bf16[2,256,128]{2,1,0:T(8,128)(2,1)S(1)}, bf16[2,256,128]{2,1,0:T(8,128)(2,1)S(1)}, u32[]{:S(2)}, u32[]{:S(2)}) %collective-permute-start.2) | collective-permute-done | bytes 131104 | tf_op jit(solution)/shard_map/ppermute | solution.py:1026
  46.5 4.2 %collective-permute-done.4.refs_3_ = bf16[2,256,128]{2,1,0:T(8,128)(2,1)S(1)} collective-permute-done((bf16[2,256,128]{2,1,0:T(8,128)(2,1)S(1)}, bf16[2,256,128]{2,1,0:T(8,128)(2,1)S(1)}, u32[]{:S(2)}, u32[]{:S(2)}) %collective-permute-start.4) | collective-permute-done | bytes 131104 | tf_op jit(solution)/shard_map/ppermute | solution.py:1026
  50.8 2.4 %square_statistics.1 = (bf16[4,1024,128]{2,1,0:T(8,128)(2,1)S(1)}, f32[8,1024]{1,0:T(8,128)S(1)}, f32[8,1024]{1,0:T(8,128)S(1)}, f32[1024,1024]{1,0:T(8,128)S(1)}, f32[1024,1024]{1,0:T(8,128)S(1)}) custom-call(bf16[8,8,128,128]{3,2,1,0:T(8,128)(2,1)S(1)} %bitcast.3, f32[8,256]{1,0:T(8,128)S(1)} %get-tuple-element.51.scales_ref, ...), custom_call_target="tpu_custom_call" | custom-call | flops 536870912 | bytes 12304384 | tf_op jit(solution)/shard_map/square_statistics/pallas_call | solution.py:414
  53.2 2.0 %gradients_before_totals.1 = (bf16[2,1024,128]{2,1,0:T(8,128)(2,1)S(1)}, bf16[8,784,128]{2,1,0:T(8,128)(2,1)}) custom-call(bf16[8,8,128,128]{3,2,1,0:T(8,128)(2,1)S(1)} %bitcast.4, f32[8,256]{1,0:T(8,128)S(1)} %get-tuple-element.51.scales_ref, bf16[4,1024,128]{2,1,0:T(8,128)(2,1)S(1)} %get-tuple-element.61.square_ref, ...), custom_call_target="tpu_custom_call" | custom-call | flops 1073741824 | bytes 30547968 | tf_op jit(solution)/shard_map/gradients_before_totals/pallas_call | solution.py:414
  55.3 2.8 %collective-permute-done.5.received_ref = f32[8,1024]{1,0:T(8,128)S(1)} collective-permute-done((f32[8,1024]{1,0:T(8,128)S(1)}, f32[8,1024]{1,0:T(8,128)S(1)}, u32[]{:S(2)}, u32[]{:S(2)}) %collective-permute-start.5) | collective-permute-done | bytes 32800 | tf_op jit(solution)/shard_map/ppermute | solution.py:1121
  58.0 2.9 %gradients_after_totals.1 = (bf16[8,784,128]{2,1,0:T(8,128)(2,1)}, bf16[4,256,128]{2,1,0:T(8,128)(2,1)S(1)}, bf16[4,256,128]{2,1,0:T(8,128)(2,1)S(1)}) custom-call(bf16[8,8,128,128]{3,2,1,0:T(8,128)(2,1)S(1)} %bitcast.5, f32[8,256]{1,0:T(8,128)S(1)} %get-tuple-element.51.scales_ref, ...), custom_call_target="tpu_custom_call", output_to_operand_aliasing={{0}: (13, {})} | custom-call | flops 536870912 | bytes 25927680 | tf_op jit(solution)/shard_map/gradients_after_totals/pallas_call | solution.py:414
  60.9 3.6 %all-to-all-start.1 = ((bf16[8,784,128]{2,1,0:T(8,128)(2,1)}), bf16[8,784,128]{2,1,0:T(8,128)(2,1)S(1)}, u32[]{:S(2)}, u32[]{:S(2)}) async-start(bf16[8,784,128]{2,1,0:T(8,128)(2,1)} %get-tuple-element.73), calls=%async_computation.1 | async-start | bytes 3211264 | tf_op jit(solution)/shard_map/all_to_all | solution.py:1056
  64.9 1.3 %collective-permute-done.6.taken_ref = bf16[4,256,128]{2,1,0:T(8,128)(2,1)S(1)} collective-permute-done((bf16[4,256,128]{2,1,0:T(8,128)(2,1)S(1)}, bf16[4,256,128]{2,1,0:T(8,128)(2,1)S(1)}, u32[]{:S(2)}, u32[]{:S(2)}) %collective-permute-start.6) | collective-permute-done | bytes 262176 | tf_op jit(solution)/shard_map/ppermute | solution.py:1015
  66.3 1.2 %collective-permute-start.7 = (bf16[2,256,128]{2,1,0:T(8,128)(2,1)S(1)}, bf16[2,256,128]{2,1,0:T(8,128)(2,1)S(1)}, u32[]{:S(2)}, u32[]{:S(2)}) collective-permute-start(bf16[2,256,128]{2,1,0:T(8,128)(2,1)S(1)} %get-tuple-element.76), channel_id=1, source_target_pairs={{0,16},{2,18},{4,20},{6,22},{8,24},{10,26},{12,28},{14,30},{16,0},... | collective-permute-start | bytes 393224 | tf_op jit(solution)/shard_map/ppermute | solution.py:1026
  67.5 3.9 %collective-permute-start.9 = (bf16[2,256,128]{2,1,0:T(8,128)(2,1)S(1)}, bf16[2,256,128]{2,1,0:T(8,128)(2,1)S(1)}, u32[]{:S(2)}, u32[]{:S(2)}) collective-permute-start(bf16[2,256,128]{2,1,0:T(8,128)(2,1)S(1)} %get-tuple-element.78), channel_id=1, source_target_pairs={{0,28},{2,30},{4,24},{6,26},{8,20},{10,22},{12,16},{14,18},{16,12}... | collective-permute-start | bytes 393224 | tf_op jit(solution)/shard_map/ppermute | solution.py:1026
  71.6 1.5 %collective-permute-start.11 = (bf16[2,256,128]{2,1,0:T(8,128)(2,1)S(1)}, bf16[2,256,128]{2,1,0:T(8,128)(2,1)S(1)}, u32[]{:S(2)}, u32[]{:S(2)}) collective-permute-start(bf16[2,256,128]{2,1,0:T(8,128)(2,1)S(1)} %get-tuple-element.80), channel_id=1, source_target_pairs={{0,24},{2,26},{4,28},{6,30},{8,16},{10,18},{12,20},{14,22},{16,8},... | collective-permute-start | bytes 393224 | tf_op jit(solution)/shard_map/ppermute | solution.py:1026
  73.1 17.6 %all-to-all-done.1.within_ref = bf16[8,784,128]{2,1,0:T(8,128)(2,1)S(1)} async-done(((bf16[8,784,128]{2,1,0:T(8,128)(2,1)}), bf16[8,784,128]{2,1,0:T(8,128)(2,1)S(1)}, u32[]{:S(2)}, u32[]{:S(2)}) %all-to-all-start.1) | async-done | bytes 1605664 | tf_op jit(solution)/shard_map/all_to_all | solution.py:1056
  90.7 1.6 %collective-permute-start.8 = (f32[16,128]{1,0:T(8,128)S(1)}, f32[16,128]{1,0:T(8,128)S(1)}, u32[]{:S(2)}, u32[]{:S(2)}) collective-permute-start(f32[16,128]{1,0:T(8,128)S(1)} %temper_sums.1), channel_id=1, source_target_pairs={{0,1},{1,0},{2,3},{3,2},{4,5},{5,4},{6,7},{7,6},{8,9},{9,8},{10,11... | collective-permute-start | bytes 24584 | tf_op jit(solution)/shard_map/ppermute | solution.py:1163
  92.2 1.4 %unpack_own.1 = (bf16[1,128,2048]{2,1,0:T(8,128)(2,1)}, bf16[1,128,2048]{2,1,0:T(8,128)(2,1)}, bf16[1,128,2048]{2,1,0:T(8,128)(2,1)}) custom-call(bf16[8,784,128]{2,1,0:T(8,128)(2,1)S(1)} %all-to-all-done.1.within_ref), custom_call_target="tpu_custom_call" | custom-call | bytes 3178496 | tf_op jit(solution)/shard_map/unpack_own/pallas_call | solution.py:414
  95.1 4.2 %collective-permute-done.11.refs_3_ = bf16[2,256,128]{2,1,0:T(8,128)(2,1)S(1)} collective-permute-done((bf16[2,256,128]{2,1,0:T(8,128)(2,1)S(1)}, bf16[2,256,128]{2,1,0:T(8,128)(2,1)S(1)}, u32[]{:S(2)}, u32[]{:S(2)}) %collective-permute-start.11) | collective-permute-done | bytes 131104 | tf_op jit(solution)/shard_map/ppermute | solution.py:1026
  (26 shorter events, 4.0 us)
Async XLA Ops:
  0.6 8.9 %copy-start.3 = (s32[16]{0:T(128)S(1)}, s32[16]{0:T(128)}, u32[]{:S(2)}) copy-start(s32[16]{0:T(128)} %span_ref.1) | copy-start | bytes 196
  0.6 8.9 %copy-start.1 = (s32[1,16,16,1]{2,3,1,0:T(1,128)S(1)}, s32[1,16,16,1]{2,3,1,0:T(1,128)}, u32[]{:S(2)}) copy-start(s32[1,16,16,1]{2,3,1,0:T(1,128)} %param.12) | copy-start | bytes 3076
  0.7 8.9 %copy-start.2 = (f32[16]{0:T(128)S(1)}, f32[16]{0:T(128)}, u32[]{:S(2)}) copy-start(f32[16]{0:T(128)} %softness_ref.1) | copy-start | bytes 196
  3.6 5.4 %copy-start.4 = (bf16[4,256,128]{2,1,0:T(8,128)(2,1)S(1)}, bf16[4,256,128]{2,1,0:T(8,128)(2,1)}, u32[]{:S(2)}) copy-start(bf16[4,256,128]{2,1,0:T(8,128)(2,1)} %get-tuple-element.56) | copy-start | bytes 786436
  3.6 7.3 %copy-start = (bf16[4,256,128]{2,1,0:T(8,128)(2,1)S(1)}, bf16[4,256,128]{2,1,0:T(8,128)(2,1)}, u32[]{:S(2)}) copy-start(bf16[4,256,128]{2,1,0:T(8,128)(2,1)} %get-tuple-element.55.kept_ref) | copy-start | bytes 786436
  3.6 36.8 %all-to-all-start = ((bf16[8,1024,128]{2,1,0:T(8,128)(2,1)}), bf16[8,1024,128]{2,1,0:T(8,128)(2,1)S(1)}, u32[]{:S(2)}, u32[]{:S(2)}) async-start(bf16[8,1024,128]{2,1,0:T(8,128)(2,1)} %get-tuple-element.46), calls=%async_computation | async-start | bytes 4194304 | tf_op jit(solution)/shard_map/all_to_all | solution.py:1056
  9.0 1.9 %collective-permute-start = (bf16[4,256,128]{2,1,0:T(8,128)(2,1)S(1)}, bf16[4,256,128]{2,1,0:T(8,128)(2,1)S(1)}, u32[]{:S(2)}, u32[]{:S(2)}) collective-permute-start(bf16[4,256,128]{2,1,0:T(8,128)(2,1)S(1)} %copy-done.4), channel_id=1, source_target_pairs={{0,2},{2,0},{4,6},{6,4},{8,10},{10,8},{12,14},{14,12},{16,18},{18,... | collective-permute-start | bytes 786440 | tf_op jit(solution)/shard_map/ppermute | solution.py:1015
  11.0 33.7 %collective-permute-start.1 = (bf16[2,256,128]{2,1,0:T(8,128)(2,1)S(1)}, bf16[2,256,128]{2,1,0:T(8,128)(2,1)S(1)}, u32[]{:S(2)}, u32[]{:S(2)}) collective-permute-start(bf16[2,256,128]{2,1,0:T(8,128)(2,1)S(1)} %get-tuple-element.57), channel_id=1, source_target_pairs={{0,16},{2,18},{4,20},{6,22},{8,24},{10,26},{12,28},{14,30},{16,0},... | collective-permute-start | bytes 393224 | tf_op jit(solution)/shard_map/ppermute | solution.py:1026
  13.6 32.9 %collective-permute-start.2 = (bf16[2,256,128]{2,1,0:T(8,128)(2,1)S(1)}, bf16[2,256,128]{2,1,0:T(8,128)(2,1)S(1)}, u32[]{:S(2)}, u32[]{:S(2)}) collective-permute-start(bf16[2,256,128]{2,1,0:T(8,128)(2,1)S(1)} %get-tuple-element.58), channel_id=1, source_target_pairs={{0,28},{2,30},{4,24},{6,26},{8,20},{10,22},{12,16},{14,18},{16,12}... | collective-permute-start | bytes 393224 | tf_op jit(solution)/shard_map/ppermute | solution.py:1026
  16.0 30.5 %collective-permute-start.3 = (bf16[2,256,128]{2,1,0:T(8,128)(2,1)S(1)}, bf16[2,256,128]{2,1,0:T(8,128)(2,1)S(1)}, u32[]{:S(2)}, u32[]{:S(2)}) collective-permute-start(bf16[2,256,128]{2,1,0:T(8,128)(2,1)S(1)} %get-tuple-element.59), channel_id=1, source_target_pairs={{0,20},{2,22},{4,16},{6,18},{8,28},{10,30},{12,24},{14,26},{16,4},... | collective-permute-start | bytes 393224 | tf_op jit(solution)/shard_map/ppermute | solution.py:1026
  17.7 33.1 %collective-permute-start.4 = (bf16[2,256,128]{2,1,0:T(8,128)(2,1)S(1)}, bf16[2,256,128]{2,1,0:T(8,128)(2,1)S(1)}, u32[]{:S(2)}, u32[]{:S(2)}) collective-permute-start(bf16[2,256,128]{2,1,0:T(8,128)(2,1)S(1)} %get-tuple-element.60), channel_id=1, source_target_pairs={{0,24},{2,26},{4,28},{6,30},{8,16},{10,18},{12,20},{14,22},{16,8},... | collective-permute-start | bytes 393224 | tf_op jit(solution)/shard_map/ppermute | solution.py:1026
  53.2 4.9 %collective-permute-start.5 = (f32[8,1024]{1,0:T(8,128)S(1)}, f32[8,1024]{1,0:T(8,128)S(1)}, u32[]{:S(2)}, u32[]{:S(2)}) collective-permute-start(f32[8,1024]{1,0:T(8,128)S(1)} %get-tuple-element.62.message_ref), channel_id=1, source_target_pairs={{0,16},{2,18},{4,20},{6,22},{8,24},{10,26},{12,28},{14,30},{16,0},... | collective-permute-start | bytes 98312 | tf_op jit(solution)/shard_map/ppermute | solution.py:1121
  60.9 29.7 %all-to-all-start.1 = ((bf16[8,784,128]{2,1,0:T(8,128)(2,1)}), bf16[8,784,128]{2,1,0:T(8,128)(2,1)S(1)}, u32[]{:S(2)}, u32[]{:S(2)}) async-start(bf16[8,784,128]{2,1,0:T(8,128)(2,1)} %get-tuple-element.73), calls=%async_computation.1 | async-start | bytes 3211264 | tf_op jit(solution)/shard_map/all_to_all | solution.py:1056
  64.5 1.7 %collective-permute-start.6 = (bf16[4,256,128]{2,1,0:T(8,128)(2,1)S(1)}, bf16[4,256,128]{2,1,0:T(8,128)(2,1)S(1)}, u32[]{:S(2)}, u32[]{:S(2)}) collective-permute-start(bf16[4,256,128]{2,1,0:T(8,128)(2,1)S(1)} %get-tuple-element.75), channel_id=1, source_target_pairs={{0,2},{2,0},{4,6},{6,4},{8,10},{10,8},{12,14},{14,12},{16,18},{18,... | collective-permute-start | bytes 786440 | tf_op jit(solution)/shard_map/ppermute | solution.py:1015
  66.3 28.7 %collective-permute-start.7 = (bf16[2,256,128]{2,1,0:T(8,128)(2,1)S(1)}, bf16[2,256,128]{2,1,0:T(8,128)(2,1)S(1)}, u32[]{:S(2)}, u32[]{:S(2)}) collective-permute-start(bf16[2,256,128]{2,1,0:T(8,128)(2,1)S(1)} %get-tuple-element.76), channel_id=1, source_target_pairs={{0,16},{2,18},{4,20},{6,22},{8,24},{10,26},{12,28},{14,30},{16,0},... | collective-permute-start | bytes 393224 | tf_op jit(solution)/shard_map/ppermute | solution.py:1026
  67.5 27.6 %collective-permute-start.9 = (bf16[2,256,128]{2,1,0:T(8,128)(2,1)S(1)}, bf16[2,256,128]{2,1,0:T(8,128)(2,1)S(1)}, u32[]{:S(2)}, u32[]{:S(2)}) collective-permute-start(bf16[2,256,128]{2,1,0:T(8,128)(2,1)S(1)} %get-tuple-element.78), channel_id=1, source_target_pairs={{0,28},{2,30},{4,24},{6,26},{8,20},{10,22},{12,16},{14,18},{16,12}... | collective-permute-start | bytes 393224 | tf_op jit(solution)/shard_map/ppermute | solution.py:1026
  71.4 23.7 %collective-permute-start.10 = (bf16[2,256,128]{2,1,0:T(8,128)(2,1)S(1)}, bf16[2,256,128]{2,1,0:T(8,128)(2,1)S(1)}, u32[]{:S(2)}, u32[]{:S(2)}) collective-permute-start(bf16[2,256,128]{2,1,0:T(8,128)(2,1)S(1)} %get-tuple-element.79), channel_id=1, source_target_pairs={{0,20},{2,22},{4,16},{6,18},{8,28},{10,30},{12,24},{14,26},{16,4},... | collective-permute-start | bytes 393224 | tf_op jit(solution)/shard_map/ppermute | solution.py:1026
  71.6 27.7 %collective-permute-start.11 = (bf16[2,256,128]{2,1,0:T(8,128)(2,1)S(1)}, bf16[2,256,128]{2,1,0:T(8,128)(2,1)S(1)}, u32[]{:S(2)}, u32[]{:S(2)}) collective-permute-start(bf16[2,256,128]{2,1,0:T(8,128)(2,1)S(1)} %get-tuple-element.80), channel_id=1, source_target_pairs={{0,24},{2,26},{4,28},{6,30},{8,16},{10,18},{12,20},{14,22},{16,8},... | collective-permute-start | bytes 393224 | tf_op jit(solution)/shard_map/ppermute | solution.py:1026
  90.7 3.7 %collective-permute-start.8 = (f32[16,128]{1,0:T(8,128)S(1)}, f32[16,128]{1,0:T(8,128)S(1)}, u32[]{:S(2)}, u32[]{:S(2)}) collective-permute-start(f32[16,128]{1,0:T(8,128)S(1)} %temper_sums.1), channel_id=1, source_target_pairs={{0,1},{1,0},{2,3},{3,2},{4,5},{5,4},{6,7},{7,6},{8,9},{9,8},{10,11... | collective-permute-start | bytes 24584 | tf_op jit(solution)/shard_map/ppermute | solution.py:1163

commit v20 on v19

--- a/solution.py
+++ b/solution.py
@@ -401,7 +401,8 @@
 
 
 def hop(step, half_count):
-    return half_count - 1 - step if step % 2 else step
+    near = half_count // 4
+    return 2 * step if step < near else 2 * (half_count // 2 - 1 - (step - near))
 
 
 def kernel_call(

time: 101 us -> 97.7 us (0.967)
  waiting for transfers between devices: 54.9 us -> 51 us
  starting transfers between devices: 25.9 us -> 27 us
    ppermute x8, waiting for transfers between devices: 10.4 us -> 7.56 us  [crossed(): lax.ppermute(message, 'seq', [(source, source ^ half_count + hop(step, ha...]
    all_to_all x2, waiting for transfers between devices: 39.4 us -> 38.2 us  [exchange_within(): lax.all_to_all(array_in, 'seq', split_axis=0, concat_axis=0, axis_index_g...]
    ppermute x8, starting transfers between devices: 14.4 us -> 15.4 us  [crossed(): lax.ppermute(message, 'seq', [(source, source ^ half_count + hop(step, ha...]
where the time goes in v20:
time: 97.7 us; the launch traced here: 97.4 us
  waiting for transfers between devices  51 us (52%)
  starting transfers between devices  27 us (28%)
  Pallas kernels  17.9 us (18%)
    all_to_all x2, waiting for transfers between devices, exchange_within(): lax.all_to_all(array_in, 'seq', split_axis=0, concat_axis=0, axis_index_g...  38.2 us
    pallas_call x10, Pallas kernels, kernel_call(): pl.pallas_call(kernel, out_shape=out_shape, in_specs=in_specs, out_specs=...  17.9 us
    ppermute x8, starting transfers between devices, crossed(): lax.ppermute(message, 'seq', [(source, source ^ half_count + hop(step, ha...  15.4 us
    all_to_all x2, starting transfers between devices, exchange_within(): lax.all_to_all(array_in, 'seq', split_axis=0, concat_axis=0, axis_index_g...  8.99 us
    ppermute x8, waiting for transfers between devices, crossed(): lax.ppermute(message, 'seq', [(source, source ^ half_count + hop(step, ha...  7.56 us
    ppermute x1, waiting for transfers between devices, head_shards(): received = lax.ppermute(message, 'seq', swap)  2.75 us
  transfers between devices with their start and end apart: 14, of which 10 were waited for; matrix products, arithmetic and copies ran while one was open for 1% of the time, Pallas kernels for 9%

profile of v20, /device:TPU:0, one launch (start us, length us, event | category | flops | bytes accessed | tf_op | source)
XLA Modules:
  0.0 97.4 jit_solution(10940966760701252671)
XLA Ops:
  0.7 2.9 %pack_heads.1 = (bf16[8,1024,128]{2,1,0:T(8,128)(2,1)}, bf16[4,256,128]{2,1,0:T(8,128)(2,1)}, bf16[4,256,128]{2,1,0:T(8,128)(2,1)}) custom-call(bf16[1,128,2048]{2,1,0:T(8,128)(2,1)} %refs_0_.1, bf16[1,128,2048]{2,1,0:T(8,128)(2,1)} %refs_1_.1, bf16[1,128,2048]{2,1,0:T(8,128)(2,1)} %refs_2_.1, bf16[1,128,2048]{2,1,0:T(8,128)(2,1)} %refs_3_.1), custom_call_target="tpu_custom_call" | custom-call | bytes 4718592 | tf_op jit(solution)/shard_map/pack_heads/pallas_call | solution.py:415
  3.6 5.4 %all-to-all-start = ((bf16[8,1024,128]{2,1,0:T(8,128)(2,1)}), bf16[8,1024,128]{2,1,0:T(8,128)(2,1)S(1)}, u32[]{:S(2)}, u32[]{:S(2)}) async-start(bf16[8,1024,128]{2,1,0:T(8,128)(2,1)} %get-tuple-element.46), calls=%async_computation | async-start | bytes 4194304 | tf_op jit(solution)/shard_map/all_to_all | solution.py:1057
  9.6 1.0 %scales_and_masks.1 = (f32[8,256]{1,0:T(8,128)S(1)}, f32[3,8,1024]{2,1,0:T(8,128)S(1)}, s32[16,128]{1,0:T(8,128)S(1)}) custom-call(f32[16]{0:T(128)S(1)} %copy-done.2, s32[16,16]{1,0:T(8,128)S(1)} %bitcast.6, s32[16]{0:T(128)S(1)} %copy-done.3), custom_call_target="tpu_custom_call" | custom-call | bytes 115840 | tf_op jit(solution)/shard_map/scales_and_masks/pallas_call | solution.py:415
  11.0 2.7 %collective-permute-start.1 = (bf16[2,256,128]{2,1,0:T(8,128)(2,1)S(1)}, bf16[2,256,128]{2,1,0:T(8,128)(2,1)S(1)}, u32[]{:S(2)}, u32[]{:S(2)}) collective-permute-start(bf16[2,256,128]{2,1,0:T(8,128)(2,1)S(1)} %get-tuple-element.57), channel_id=1, source_target_pairs={{0,16},{2,18},{4,20},{6,22},{8,24},{10,26},{12,28},{14,30},{16,0},... | collective-permute-start | bytes 393224 | tf_op jit(solution)/shard_map/ppermute | solution.py:1027
  13.6 1.5 %collective-permute-start.2 = (bf16[2,256,128]{2,1,0:T(8,128)(2,1)S(1)}, bf16[2,256,128]{2,1,0:T(8,128)(2,1)S(1)}, u32[]{:S(2)}, u32[]{:S(2)}) collective-permute-start(bf16[2,256,128]{2,1,0:T(8,128)(2,1)S(1)} %get-tuple-element.58), channel_id=1, source_target_pairs={{0,20},{2,22},{4,16},{6,18},{8,28},{10,30},{12,24},{14,26},{16,4},... | collective-permute-start | bytes 393224 | tf_op jit(solution)/shard_map/ppermute | solution.py:1027
  15.1 3.5 %collective-permute-start.3 = (bf16[2,256,128]{2,1,0:T(8,128)(2,1)S(1)}, bf16[2,256,128]{2,1,0:T(8,128)(2,1)S(1)}, u32[]{:S(2)}, u32[]{:S(2)}) collective-permute-start(bf16[2,256,128]{2,1,0:T(8,128)(2,1)S(1)} %get-tuple-element.59), channel_id=1, source_target_pairs={{0,28},{2,30},{4,24},{6,26},{8,20},{10,22},{12,16},{14,18},{16,12}... | collective-permute-start | bytes 393224 | tf_op jit(solution)/shard_map/ppermute | solution.py:1027
  18.7 21.7 %all-to-all-done = bf16[8,1024,128]{2,1,0:T(8,128)(2,1)S(1)} async-done(((bf16[8,1024,128]{2,1,0:T(8,128)(2,1)}), bf16[8,1024,128]{2,1,0:T(8,128)(2,1)S(1)}, u32[]{:S(2)}, u32[]{:S(2)}) %all-to-all-start) | async-done | bytes 2097184 | tf_op jit(solution)/shard_map/all_to_all | solution.py:1057
  40.4 4.3 %diagonal_statistics.1 = (f32[16,1024]{1,0:T(8,128)S(1)}, f32[3,1024,128]{2,1,0:T(8,128)S(1)}, f32[1024,1024]{1,0:T(8,128)S(1)}, f32[1024,1024]{1,0:T(8,128)S(1)...) custom-call(bf16[8,8,128,128]{3,2,1,0:T(8,128)(2,1)S(1)} %bitcast.2, f32[8,256]{1,0:T(8,128)S(1)} %get-tuple-element.51.scales_ref, ...), custom_call_target="tpu_custom_call" | custom-call | flops 536870912 | bytes 20627456 | tf_op jit(solution)/shard_map/diagonal_statistics/pallas_call | solution.py:415
  44.6 4.3 %collective-permute-done.3.refs_2_ = bf16[2,256,128]{2,1,0:T(8,128)(2,1)S(1)} collective-permute-done((bf16[2,256,128]{2,1,0:T(8,128)(2,1)S(1)}, bf16[2,256,128]{2,1,0:T(8,128)(2,1)S(1)}, u32[]{:S(2)}, u32[]{:S(2)}) %collective-permute-start.3) | collective-permute-done | bytes 131104 | tf_op jit(solution)/shard_map/ppermute | solution.py:1027
  48.9 1.4 %collective-permute-done.4.refs_3_ = bf16[2,256,128]{2,1,0:T(8,128)(2,1)S(1)} collective-permute-done((bf16[2,256,128]{2,1,0:T(8,128)(2,1)S(1)}, bf16[2,256,128]{2,1,0:T(8,128)(2,1)S(1)}, u32[]{:S(2)}, u32[]{:S(2)}) %collective-permute-start.4) | collective-permute-done | bytes 131104 | tf_op jit(solution)/shard_map/ppermute | solution.py:1027
  50.4 2.4 %square_statistics.1 = (bf16[4,1024,128]{2,1,0:T(8,128)(2,1)S(1)}, f32[8,1024]{1,0:T(8,128)S(1)}, f32[8,1024]{1,0:T(8,128)S(1)}, f32[1024,1024]{1,0:T(8,128)S(1)}, f32[1024,1024]{1,0:T(8,128)S(1)}) custom-call(bf16[8,8,128,128]{3,2,1,0:T(8,128)(2,1)S(1)} %bitcast.3, f32[8,256]{1,0:T(8,128)S(1)} %get-tuple-element.51.scales_ref, ...), custom_call_target="tpu_custom_call" | custom-call | flops 536870912 | bytes 12304384 | tf_op jit(solution)/shard_map/square_statistics/pallas_call | solution.py:415
  52.8 2.0 %gradients_before_totals.1 = (bf16[2,1024,128]{2,1,0:T(8,128)(2,1)S(1)}, bf16[8,784,128]{2,1,0:T(8,128)(2,1)}) custom-call(bf16[8,8,128,128]{3,2,1,0:T(8,128)(2,1)S(1)} %bitcast.4, f32[8,256]{1,0:T(8,128)S(1)} %get-tuple-element.51.scales_ref, bf16[4,1024,128]{2,1,0:T(8,128)(2,1)S(1)} %get-tuple-element.61.square_ref, ...), custom_call_target="tpu_custom_call" | custom-call | flops 1073741824 | bytes 30547968 | tf_op jit(solution)/shard_map/gradients_before_totals/pallas_call | solution.py:415
  54.9 2.8 %collective-permute-done.5.received_ref = f32[8,1024]{1,0:T(8,128)S(1)} collective-permute-done((f32[8,1024]{1,0:T(8,128)S(1)}, f32[8,1024]{1,0:T(8,128)S(1)}, u32[]{:S(2)}, u32[]{:S(2)}) %collective-permute-start.5) | collective-permute-done | bytes 32800 | tf_op jit(solution)/shard_map/ppermute | solution.py:1122
  57.6 2.9 %gradients_after_totals.1 = (bf16[8,784,128]{2,1,0:T(8,128)(2,1)}, bf16[4,256,128]{2,1,0:T(8,128)(2,1)S(1)}, bf16[4,256,128]{2,1,0:T(8,128)(2,1)S(1)}) custom-call(bf16[8,8,128,128]{3,2,1,0:T(8,128)(2,1)S(1)} %bitcast.5, f32[8,256]{1,0:T(8,128)S(1)} %get-tuple-element.51.scales_ref, ...), custom_call_target="tpu_custom_call", output_to_operand_aliasing={{0}: (13, {})} | custom-call | flops 536870912 | bytes 25927680 | tf_op jit(solution)/shard_map/gradients_after_totals/pallas_call | solution.py:415
  60.5 3.6 %all-to-all-start.1 = ((bf16[8,784,128]{2,1,0:T(8,128)(2,1)}), bf16[8,784,128]{2,1,0:T(8,128)(2,1)S(1)}, u32[]{:S(2)}, u32[]{:S(2)}) async-start(bf16[8,784,128]{2,1,0:T(8,128)(2,1)} %get-tuple-element.73), calls=%async_computation.1 | async-start | bytes 3211264 | tf_op jit(solution)/shard_map/all_to_all | solution.py:1057
  64.5 1.3 %collective-permute-done.6.taken_ref = bf16[4,256,128]{2,1,0:T(8,128)(2,1)S(1)} collective-permute-done((bf16[4,256,128]{2,1,0:T(8,128)(2,1)S(1)}, bf16[4,256,128]{2,1,0:T(8,128)(2,1)S(1)}, u32[]{:S(2)}, u32[]{:S(2)}) %collective-permute-start.6) | collective-permute-done | bytes 262176 | tf_op jit(solution)/shard_map/ppermute | solution.py:1016
  65.9 1.2 %collective-permute-start.7 = (bf16[2,256,128]{2,1,0:T(8,128)(2,1)S(1)}, bf16[2,256,128]{2,1,0:T(8,128)(2,1)S(1)}, u32[]{:S(2)}, u32[]{:S(2)}) collective-permute-start(bf16[2,256,128]{2,1,0:T(8,128)(2,1)S(1)} %get-tuple-element.76), channel_id=1, source_target_pairs={{0,16},{2,18},{4,20},{6,22},{8,24},{10,26},{12,28},{14,30},{16,0},... | collective-permute-start | bytes 393224 | tf_op jit(solution)/shard_map/ppermute | solution.py:1027
  67.1 3.0 %collective-permute-start.9 = (bf16[2,256,128]{2,1,0:T(8,128)(2,1)S(1)}, bf16[2,256,128]{2,1,0:T(8,128)(2,1)S(1)}, u32[]{:S(2)}, u32[]{:S(2)}) collective-permute-start(bf16[2,256,128]{2,1,0:T(8,128)(2,1)S(1)} %get-tuple-element.78), channel_id=1, source_target_pairs={{0,20},{2,22},{4,16},{6,18},{8,28},{10,30},{12,24},{14,26},{16,4},... | collective-permute-start | bytes 393224 | tf_op jit(solution)/shard_map/ppermute | solution.py:1027
  70.1 2.0 %collective-permute-start.10 = (bf16[2,256,128]{2,1,0:T(8,128)(2,1)S(1)}, bf16[2,256,128]{2,1,0:T(8,128)(2,1)S(1)}, u32[]{:S(2)}, u32[]{:S(2)}) collective-permute-start(bf16[2,256,128]{2,1,0:T(8,128)(2,1)S(1)} %get-tuple-element.79), channel_id=1, source_target_pairs={{0,28},{2,30},{4,24},{6,26},{8,20},{10,22},{12,16},{14,18},{16,12}... | collective-permute-start | bytes 393224 | tf_op jit(solution)/shard_map/ppermute | solution.py:1027
  72.1 1.5 %collective-permute-start.11 = (bf16[2,256,128]{2,1,0:T(8,128)(2,1)S(1)}, bf16[2,256,128]{2,1,0:T(8,128)(2,1)S(1)}, u32[]{:S(2)}, u32[]{:S(2)}) collective-permute-start(bf16[2,256,128]{2,1,0:T(8,128)(2,1)S(1)} %get-tuple-element.80), channel_id=1, source_target_pairs={{0,24},{2,26},{4,28},{6,30},{8,16},{10,18},{12,20},{14,22},{16,8},... | collective-permute-start | bytes 393224 | tf_op jit(solution)/shard_map/ppermute | solution.py:1027
  73.6 16.5 %all-to-all-done.1.within_ref = bf16[8,784,128]{2,1,0:T(8,128)(2,1)S(1)} async-done(((bf16[8,784,128]{2,1,0:T(8,128)(2,1)}), bf16[8,784,128]{2,1,0:T(8,128)(2,1)S(1)}, u32[]{:S(2)}, u32[]{:S(2)}) %all-to-all-start.1) | async-done | bytes 1605664 | tf_op jit(solution)/shard_map/all_to_all | solution.py:1057
  90.2 1.6 %collective-permute-start.8 = (f32[16,128]{1,0:T(8,128)S(1)}, f32[16,128]{1,0:T(8,128)S(1)}, u32[]{:S(2)}, u32[]{:S(2)}) collective-permute-start(f32[16,128]{1,0:T(8,128)S(1)} %temper_sums.1), channel_id=1, source_target_pairs={{0,1},{1,0},{2,3},{3,2},{4,5},{5,4},{6,7},{7,6},{8,9},{9,8},{10,11... | collective-permute-start | bytes 24584 | tf_op jit(solution)/shard_map/ppermute | solution.py:1164
  91.7 1.4 %unpack_own.1 = (bf16[1,128,2048]{2,1,0:T(8,128)(2,1)}, bf16[1,128,2048]{2,1,0:T(8,128)(2,1)}, bf16[1,128,2048]{2,1,0:T(8,128)(2,1)}) custom-call(bf16[8,784,128]{2,1,0:T(8,128)(2,1)S(1)} %all-to-all-done.1.within_ref), custom_call_target="tpu_custom_call" | custom-call | bytes 3178496 | tf_op jit(solution)/shard_map/unpack_own/pallas_call | solution.py:415
  95.0 1.4 %collective-permute-done.11.refs_3_ = bf16[2,256,128]{2,1,0:T(8,128)(2,1)S(1)} collective-permute-done((bf16[2,256,128]{2,1,0:T(8,128)(2,1)S(1)}, bf16[2,256,128]{2,1,0:T(8,128)(2,1)S(1)}, u32[]{:S(2)}, u32[]{:S(2)}) %collective-permute-start.11) | collective-permute-done | bytes 131104 | tf_op jit(solution)/shard_map/ppermute | solution.py:1027
  (26 shorter events, 4.4 us)
Async XLA Ops:
  0.6 8.9 %copy-start.3 = (s32[16]{0:T(128)S(1)}, s32[16]{0:T(128)}, u32[]{:S(2)}) copy-start(s32[16]{0:T(128)} %span_ref.1) | copy-start | bytes 196
  0.6 8.9 %copy-start.1 = (s32[1,16,16,1]{2,3,1,0:T(1,128)S(1)}, s32[1,16,16,1]{2,3,1,0:T(1,128)}, u32[]{:S(2)}) copy-start(s32[1,16,16,1]{2,3,1,0:T(1,128)} %param.12) | copy-start | bytes 3076
  0.7 8.9 %copy-start.2 = (f32[16]{0:T(128)S(1)}, f32[16]{0:T(128)}, u32[]{:S(2)}) copy-start(f32[16]{0:T(128)} %softness_ref.1) | copy-start | bytes 196
  3.6 5.4 %copy-start.4 = (bf16[4,256,128]{2,1,0:T(8,128)(2,1)S(1)}, bf16[4,256,128]{2,1,0:T(8,128)(2,1)}, u32[]{:S(2)}) copy-start(bf16[4,256,128]{2,1,0:T(8,128)(2,1)} %get-tuple-element.56) | copy-start | bytes 786436
  3.6 7.3 %copy-start = (bf16[4,256,128]{2,1,0:T(8,128)(2,1)S(1)}, bf16[4,256,128]{2,1,0:T(8,128)(2,1)}, u32[]{:S(2)}) copy-start(bf16[4,256,128]{2,1,0:T(8,128)(2,1)} %get-tuple-element.55.kept_ref) | copy-start | bytes 786436
  3.6 36.7 %all-to-all-start = ((bf16[8,1024,128]{2,1,0:T(8,128)(2,1)}), bf16[8,1024,128]{2,1,0:T(8,128)(2,1)S(1)}, u32[]{:S(2)}, u32[]{:S(2)}) async-start(bf16[8,1024,128]{2,1,0:T(8,128)(2,1)} %get-tuple-element.46), calls=%async_computation | async-start | bytes 4194304 | tf_op jit(solution)/shard_map/all_to_all | solution.py:1057
  9.0 1.9 %collective-permute-start = (bf16[4,256,128]{2,1,0:T(8,128)(2,1)S(1)}, bf16[4,256,128]{2,1,0:T(8,128)(2,1)S(1)}, u32[]{:S(2)}, u32[]{:S(2)}) collective-permute-start(bf16[4,256,128]{2,1,0:T(8,128)(2,1)S(1)} %copy-done.4), channel_id=1, source_target_pairs={{0,2},{2,0},{4,6},{6,4},{8,10},{10,8},{12,14},{14,12},{16,18},{18,... | collective-permute-start | bytes 786440 | tf_op jit(solution)/shard_map/ppermute | solution.py:1016
  11.0 33.6 %collective-permute-start.1 = (bf16[2,256,128]{2,1,0:T(8,128)(2,1)S(1)}, bf16[2,256,128]{2,1,0:T(8,128)(2,1)S(1)}, u32[]{:S(2)}, u32[]{:S(2)}) collective-permute-start(bf16[2,256,128]{2,1,0:T(8,128)(2,1)S(1)} %get-tuple-element.57), channel_id=1, source_target_pairs={{0,16},{2,18},{4,20},{6,22},{8,24},{10,26},{12,28},{14,30},{16,0},... | collective-permute-start | bytes 393224 | tf_op jit(solution)/shard_map/ppermute | solution.py:1027
  13.6 31.0 %collective-permute-start.2 = (bf16[2,256,128]{2,1,0:T(8,128)(2,1)S(1)}, bf16[2,256,128]{2,1,0:T(8,128)(2,1)S(1)}, u32[]{:S(2)}, u32[]{:S(2)}) collective-permute-start(bf16[2,256,128]{2,1,0:T(8,128)(2,1)S(1)} %get-tuple-element.58), channel_id=1, source_target_pairs={{0,20},{2,22},{4,16},{6,18},{8,28},{10,30},{12,24},{14,26},{16,4},... | collective-permute-start | bytes 393224 | tf_op jit(solution)/shard_map/ppermute | solution.py:1027
  15.1 33.8 %collective-permute-start.3 = (bf16[2,256,128]{2,1,0:T(8,128)(2,1)S(1)}, bf16[2,256,128]{2,1,0:T(8,128)(2,1)S(1)}, u32[]{:S(2)}, u32[]{:S(2)}) collective-permute-start(bf16[2,256,128]{2,1,0:T(8,128)(2,1)S(1)} %get-tuple-element.59), channel_id=1, source_target_pairs={{0,28},{2,30},{4,24},{6,26},{8,20},{10,22},{12,16},{14,18},{16,12}... | collective-permute-start | bytes 393224 | tf_op jit(solution)/shard_map/ppermute | solution.py:1027
  18.6 31.8 %collective-permute-start.4 = (bf16[2,256,128]{2,1,0:T(8,128)(2,1)S(1)}, bf16[2,256,128]{2,1,0:T(8,128)(2,1)S(1)}, u32[]{:S(2)}, u32[]{:S(2)}) collective-permute-start(bf16[2,256,128]{2,1,0:T(8,128)(2,1)S(1)} %get-tuple-element.60), channel_id=1, source_target_pairs={{0,24},{2,26},{4,28},{6,30},{8,16},{10,18},{12,20},{14,22},{16,8},... | collective-permute-start | bytes 393224 | tf_op jit(solution)/shard_map/ppermute | solution.py:1027
  52.8 4.9 %collective-permute-start.5 = (f32[8,1024]{1,0:T(8,128)S(1)}, f32[8,1024]{1,0:T(8,128)S(1)}, u32[]{:S(2)}, u32[]{:S(2)}) collective-permute-start(f32[8,1024]{1,0:T(8,128)S(1)} %get-tuple-element.62.message_ref), channel_id=1, source_target_pairs={{0,16},{2,18},{4,20},{6,22},{8,24},{10,26},{12,28},{14,30},{16,0},... | collective-permute-start | bytes 98312 | tf_op jit(solution)/shard_map/ppermute | solution.py:1122
  60.5 29.6 %all-to-all-start.1 = ((bf16[8,784,128]{2,1,0:T(8,128)(2,1)}), bf16[8,784,128]{2,1,0:T(8,128)(2,1)S(1)}, u32[]{:S(2)}, u32[]{:S(2)}) async-start(bf16[8,784,128]{2,1,0:T(8,128)(2,1)} %get-tuple-element.73), calls=%async_computation.1 | async-start | bytes 3211264 | tf_op jit(solution)/shard_map/all_to_all | solution.py:1057
  64.1 1.7 %collective-permute-start.6 = (bf16[4,256,128]{2,1,0:T(8,128)(2,1)S(1)}, bf16[4,256,128]{2,1,0:T(8,128)(2,1)S(1)}, u32[]{:S(2)}, u32[]{:S(2)}) collective-permute-start(bf16[4,256,128]{2,1,0:T(8,128)(2,1)S(1)} %get-tuple-element.75), channel_id=1, source_target_pairs={{0,2},{2,0},{4,6},{6,4},{8,10},{10,8},{12,14},{14,12},{16,18},{18,... | collective-permute-start | bytes 786440 | tf_op jit(solution)/shard_map/ppermute | solution.py:1016
  65.9 28.6 %collective-permute-start.7 = (bf16[2,256,128]{2,1,0:T(8,128)(2,1)S(1)}, bf16[2,256,128]{2,1,0:T(8,128)(2,1)S(1)}, u32[]{:S(2)}, u32[]{:S(2)}) collective-permute-start(bf16[2,256,128]{2,1,0:T(8,128)(2,1)S(1)} %get-tuple-element.76), channel_id=1, source_target_pairs={{0,16},{2,18},{4,20},{6,22},{8,24},{10,26},{12,28},{14,30},{16,0},... | collective-permute-start | bytes 393224 | tf_op jit(solution)/shard_map/ppermute | solution.py:1027
  67.1 27.5 %collective-permute-start.9 = (bf16[2,256,128]{2,1,0:T(8,128)(2,1)S(1)}, bf16[2,256,128]{2,1,0:T(8,128)(2,1)S(1)}, u32[]{:S(2)}, u32[]{:S(2)}) collective-permute-start(bf16[2,256,128]{2,1,0:T(8,128)(2,1)S(1)} %get-tuple-element.78), channel_id=1, source_target_pairs={{0,20},{2,22},{4,16},{6,18},{8,28},{10,30},{12,24},{14,26},{16,4},... | collective-permute-start | bytes 393224 | tf_op jit(solution)/shard_map/ppermute | solution.py:1027
  70.1 24.9 %collective-permute-start.10 = (bf16[2,256,128]{2,1,0:T(8,128)(2,1)S(1)}, bf16[2,256,128]{2,1,0:T(8,128)(2,1)S(1)}, u32[]{:S(2)}, u32[]{:S(2)}) collective-permute-start(bf16[2,256,128]{2,1,0:T(8,128)(2,1)S(1)} %get-tuple-element.79), channel_id=1, source_target_pairs={{0,28},{2,30},{4,24},{6,26},{8,20},{10,22},{12,16},{14,18},{16,12}... | collective-permute-start | bytes 393224 | tf_op jit(solution)/shard_map/ppermute | solution.py:1027
  72.1 24.3 %collective-permute-start.11 = (bf16[2,256,128]{2,1,0:T(8,128)(2,1)S(1)}, bf16[2,256,128]{2,1,0:T(8,128)(2,1)S(1)}, u32[]{:S(2)}, u32[]{:S(2)}) collective-permute-start(bf16[2,256,128]{2,1,0:T(8,128)(2,1)S(1)} %get-tuple-element.80), channel_id=1, source_target_pairs={{0,24},{2,26},{4,28},{6,30},{8,16},{10,18},{12,20},{14,22},{16,8},... | collective-permute-start | bytes 393224 | tf_op jit(solution)/shard_map/ppermute | solution.py:1027
  90.2 3.7 %collective-permute-start.8 = (f32[16,128]{1,0:T(8,128)S(1)}, f32[16,128]{1,0:T(8,128)S(1)}, u32[]{:S(2)}, u32[]{:S(2)}) collective-permute-start(f32[16,128]{1,0:T(8,128)S(1)} %temper_sums.1), channel_id=1, source_target_pairs={{0,1},{1,0},{2,3},{3,2},{4,5},{5,4},{6,7},{7,6},{8,9},{9,8},{10,11... | collective-permute-start | bytes 24584 | tf_op jit(solution)/shard_map/ppermute | solution.py:1164
